TPU v7x, 128 devices: a whole 4x4x4 slice. The times are simulated.
128 devices in a mesh: segment: 2 (over core), mp: 4 (over x), dp: 16 (over z, y).
Axes of the slice: x: 4, y: 4, z: 4, core: 2. Of those that a mesh axis runs over, the one named last changes fastest.
Arguments:
- patches: bfloat16 [128, 32, 2560], P(('segment', 'dp')), may hold values from -6 to 6
- merger_weight: bfloat16 [2560, 4096], P(None, 'mp'), may hold values from -0.125 to 0.125
- image_counts: int32 [128], replicated, may hold values from 1 to 32, as said below
- routing: int32 [128], replicated, may hold values from 0 to 127, as said below
- text_embed: bfloat16 [2, 2048, 4096], P(None, 'dp', 'mp'), may hold values from -6 to 6
- llm_weight: bfloat16 [2, 4096, 4096], P('segment', None, 'mp'), may hold values from -0.046875 to 0.046875
- upstream: bfloat16 [2, 2048, 4096], P(None, 'dp', 'mp'), may hold values from -0.4375 to 0.4375
Outputs:
- llm_grad: float32 [2, 4096, 4096], P('segment', 'dp', 'mp')
- merger_grad: float32 [2560, 4096], P(('segment', 'dp'), 'mp')
Inputs may be any that keep to these rules, and one draw needn't show every extreme that they name: Sample k has image_counts[k] image rows; one sample of every draw has all 32. `routing`: each slot is named by exactly one sample; the 4 samples k that share k // 4 name slots of 4 different replicas.
All inputs are finite; a program needn't handle non-finite values.
Results may differ from a plain program's by a relative error of at most 0.022.
Values may be sent and summed in bfloat16 or wider, within the bound.
No kernel may reach another device: no remote copies, remote signals or barrier semaphores. Data moves between devices by JAX's collectives and lax.ppermute only.
A program may use at most 192 MiB of HBM per device.

v0:
```python
import jax
import jax.numpy as jnp
from jax import lax
from jax.sharding import PartitionSpec as P


def shifted(block, axis, distance):
    devices = range(lax.axis_size(axis))
    route = [(i - distance, i) for i in devices if i - distance in devices]
    return lax.ppermute(block, axis, route)


def spread(shard, axis, root):
    mine = lax.axis_index(axis) == root
    return lax.psum(jnp.where(mine, shard, jnp.zeros_like(shard)), axis)


def gelu_back(preact, cotangent):
    _, pullback = jax.vjp(jax.nn.gelu, preact)
    return pullback(cotangent)[0]


def on_device(patches, merger_weight, image_counts, routing, text_embed, llm_weight, upstream):
    phases = lax.axis_size("segment")
    replicas = lax.axis_size("dp")
    phase_index = lax.axis_index("segment")
    replica = lax.axis_index("dp")
    group_index = phase_index * replicas + replica
    encoded = patches.shape[0]
    slot_rows = patches.shape[1]
    micro_count = text_embed.shape[0]
    token_rows = text_embed.shape[1]
    per_micro = token_rows // slot_rows
    per_replica = micro_count * per_micro
    columns = merger_weight.shape[1]
    features = llm_weight.shape[1]
    weight = llm_weight[0]
    position = jnp.arange(slot_rows)
    activated = jax.nn.gelu(patches.astype(jnp.float32)).astype(jnp.bfloat16)
    flat_act = activated.reshape(encoded * slot_rows, patches.shape[2])
    embeds = jnp.dot(flat_act, merger_weight, preferred_element_type=jnp.float32).astype(
        jnp.bfloat16
    )
    embeds = embeds.reshape(encoded, slot_rows, columns)
    slot_owner = jnp.argsort(routing)
    my_samples = lax.dynamic_slice_in_dim(slot_owner, replica * per_replica, per_replica)
    target = lax.dynamic_slice_in_dim(routing, group_index * encoded, encoded)
    every_embed = lax.all_gather(embeds, ("segment", "dp"), axis=0, tiled=True)
    picked = jnp.take(every_embed, my_samples, axis=0)
    image_mask = position[None, :] < jnp.take(image_counts, my_samples)[:, None]
    text_slots = text_embed.reshape(per_replica, slot_rows, columns)
    start_rows = jnp.where(image_mask[:, :, None], picked, text_slots)
    pieces = 1
    unit_count = micro_count * pieces
    piece_rows = token_rows // pieces
    start_units = start_rows.reshape(unit_count, piece_rows, columns)
    tick_count = phases + unit_count - 1

    def forward_tick(tick_number, state_carry):
        incoming, saved_rows, saved_pre = state_carry
        micro_unit = tick_number - phase_index
        active = (micro_unit >= 0) & (micro_unit < unit_count)
        slot_index = jnp.clip(micro_unit, 0, unit_count - 1)
        first_rows = lax.dynamic_index_in_dim(
            start_units, jnp.minimum(tick_number, unit_count - 1), 0, keepdims=False
        )
        current = jnp.where(phase_index == 0, first_rows, incoming)
        gathered = lax.all_gather(current, "mp", axis=1, tiled=True)
        preact = jnp.dot(gathered, weight, preferred_element_type=jnp.float32)
        result = (current.astype(jnp.float32) + jax.nn.gelu(preact)).astype(jnp.bfloat16)
        old_rows = lax.dynamic_index_in_dim(saved_rows, slot_index, 0, keepdims=False)
        old_pre = lax.dynamic_index_in_dim(saved_pre, slot_index, 0, keepdims=False)
        saved_rows = lax.dynamic_update_index_in_dim(
            saved_rows, jnp.where(active, gathered, old_rows), slot_index, 0
        )
        saved_pre = lax.dynamic_update_index_in_dim(
            saved_pre, jnp.where(active, preact, old_pre), slot_index, 0
        )
        passed = shifted(result, "segment", 1)
        return (passed, saved_rows, saved_pre)

    forward_init = (
        jnp.zeros((piece_rows, columns), jnp.bfloat16),
        jnp.zeros((unit_count, piece_rows, features), jnp.bfloat16),
        jnp.zeros((unit_count, piece_rows, columns), jnp.float32),
    )
    _, saved_rows, saved_pre = lax.fori_loop(0, tick_count, forward_tick, forward_init)

    def backward_tick(tick_number, state_carry):
        incoming, weight_grad, start_grad = state_carry
        micro_unit = tick_number - (phases - 1 - phase_index)
        active = (micro_unit >= 0) & (micro_unit < unit_count)
        slot_index = jnp.clip(micro_unit, 0, unit_count - 1)
        top_grad = lax.dynamic_index_in_dim(
            upstream, jnp.minimum(tick_number, unit_count - 1), 0, keepdims=False
        )
        current = jnp.where(phase_index == phases - 1, top_grad, incoming)
        gathered = lax.dynamic_index_in_dim(saved_rows, slot_index, 0, keepdims=False)
        preact = lax.dynamic_index_in_dim(saved_pre, slot_index, 0, keepdims=False)
        local_grad = gelu_back(preact, current.astype(jnp.float32)).astype(jnp.bfloat16)

        def add_grad(running):
            return running + lax.dot_general(
                gathered, local_grad, (((0,), (0,)), ((), ())), preferred_element_type=jnp.float32
            )

        def keep_grad(running):
            return running

        weight_grad = lax.cond(active, add_grad, keep_grad, weight_grad)
        partial_value = lax.dot_general(
            local_grad, weight, (((1,), (1,)), ((), ())), preferred_element_type=jnp.float32
        )
        inner_grad = lax.psum_scatter(
            partial_value.astype(jnp.bfloat16), "mp", scatter_dimension=1, tiled=True
        ).astype(jnp.float32)
        result = (current.astype(jnp.float32) + inner_grad).astype(jnp.bfloat16)
        old_rows = lax.dynamic_index_in_dim(start_grad, slot_index, 0, keepdims=False)
        start_grad = lax.dynamic_update_index_in_dim(
            start_grad, jnp.where(active, result, old_rows), slot_index, 0
        )
        passed = shifted(result, "segment", -1)
        return (passed, weight_grad, start_grad)

    backward_init = (
        jnp.zeros((piece_rows, columns), jnp.bfloat16),
        jnp.zeros((features, columns), jnp.float32),
        jnp.zeros((unit_count, piece_rows, columns), jnp.bfloat16),
    )
    _, weight_grad, start_grad = lax.fori_loop(0, tick_count, backward_tick, backward_init)
    replica_part = lax.psum_scatter(
        weight_grad.astype(jnp.bfloat16), "dp", scatter_dimension=0, tiled=True
    ).astype(jnp.float32)
    llm_grad = replica_part[None]
    counts_here = lax.dynamic_slice_in_dim(image_counts, group_index * encoded, encoded)
    sample_mask = position[None, :] < counts_here[:, None]
    rooted = spread(start_grad, "segment", 0)
    owners = lax.all_gather(rooted, "dp", axis=0, tiled=True)
    owners = owners.reshape(replicas * per_replica, slot_rows, columns)
    chosen_grads = jnp.take(owners, target, axis=0)
    image_grad = jnp.where(sample_mask[:, :, None], chosen_grads, jnp.zeros((), jnp.bfloat16))
    merger_part = lax.dot_general(
        flat_act,
        image_grad.reshape(encoded * slot_rows, columns),
        (((0,), (0,)), ((), ())),
        preferred_element_type=jnp.float32,
    )
    merger_grad = lax.psum_scatter(
        merger_part.astype(jnp.bfloat16), ("segment", "dp"), scatter_dimension=0, tiled=True
    ).astype(jnp.float32)
    return (llm_grad, merger_grad)


def solution(mesh):
    return jax.shard_map(
        on_device,
        mesh=mesh,
        in_specs=(
            P(("segment", "dp"), None, None),
            P(None, "mp"),
            P(),
            P(),
            P(None, "dp", "mp"),
            P("segment", None, "mp"),
            P(None, "dp", "mp"),
        ),
        out_specs=(P("segment", "dp", "mp"), P(("segment", "dp"), "mp")),
        check_vma=False,
    )
```

profile of v0, /device:TPU:0, one launch (start us, length us, event | category | flops | bytes accessed | tf_op | source)
XLA Modules:
  0.0 625.7 jit_solution(14714405157802074775)
XLA Ops:
  7.2 1.5 fusion.28
  8.8 4.1 convolution_convert_fusion.1
  13.0 2.5 sort.17
  15.6 0.6 gather_fusion
  16.8 51.7 %all-gather.4.cloned.1.call-done = bf16[128,32,1024]{2,1,0:T(8,128)(2,1)} async-done(((bf16[4,32,1024]{2,1,0:T(8,128)(2,1)}), bf16[128,32,1024]{2,1,0:T(8,128)(2,1)}) %all-gather.4.cloned.1.call-update) | async-done | bytes 8388624 | tf_op jit(solution)/shard_map/all_gather | solution.py:48
  68.6 4.0 gather_fusion.1
  72.6 0.9 fusion.29
  73.8 1.1 broadcast_in_dim.104
  74.9 104.7 %while.40 = (s32[]{:T(128)}, bf16[128,1024]{1,0:T(8,128)(2,1)S(1)}, bf16[2,128,4096]{2,1,0:T(8,128)(2,1)S(1)}, f32[2,128,1024]{2,1,0:T(8,128)}, pred[]{:T(512)},...) while((s32[]{:T(128)}, bf16[128,1024]{1,0:T(8,128)(2,1)S(1)}, ...), condition=%wide.region_2.3_spmd, body=%wide.region_1.2_spmd.sunk | while | flops 1075970048 | bytes 31457676 | solution.py:87
  74.9 1.7 bitcast_select_fusion.7
  76.7 1.9 constant_dynamic-slice_fusion.7
  78.7 22.7 %all-gather.8.cloned.1.call-done = bf16[128,4096]{1,0:T(8,128)(2,1)} async-done(((bf16[128,1024]{1,0:T(8,128)(2,1)}), bf16[128,4096]{1,0:T(8,128)(2,1)}) %all-gather.8.cloned.1.call-update) | async-done | bytes 1048592 | tf_op jit(solution)/shard_map/while/body/eval_jaxpr/all_gather | solution.py:68
  101.4 5.2 fusion.55
  106.7 1.4 collective-permute-start
  108.5 0.9 bitcast_dynamic-update-slice_fusion.7
  109.4 1.7 bitcast_select_fusion.7
  111.1 1.9 constant_dynamic-slice_fusion.7
  113.1 23.6 %all-gather.8.cloned.1.call-done = bf16[128,4096]{1,0:T(8,128)(2,1)} async-done(((bf16[128,1024]{1,0:T(8,128)(2,1)}), bf16[128,4096]{1,0:T(8,128)(2,1)}) %all-gather.8.cloned.1.call-update) | async-done | bytes 1048592 | tf_op jit(solution)/shard_map/while/body/eval_jaxpr/all_gather | solution.py:68
  136.7 5.2 fusion.55
  142.0 1.4 collective-permute-start
  143.8 0.9 bitcast_dynamic-update-slice_fusion.7
  144.6 1.7 bitcast_select_fusion.7
  146.4 1.9 constant_dynamic-slice_fusion.7
  148.4 23.3 %all-gather.8.cloned.1.call-done = bf16[128,4096]{1,0:T(8,128)(2,1)} async-done(((bf16[128,1024]{1,0:T(8,128)(2,1)}), bf16[128,4096]{1,0:T(8,128)(2,1)}) %all-gather.8.cloned.1.call-update) | async-done | bytes 1048592 | tf_op jit(solution)/shard_map/while/body/eval_jaxpr/all_gather | solution.py:68
  171.7 5.2 fusion.55
  177.0 1.4 collective-permute-start
  178.8 0.9 bitcast_dynamic-update-slice_fusion.7
  179.6 7.9 %broadcast_in_dim.102 = f32[4096,1024]{1,0:T(8,128)} broadcast(f32[]{:T(128)} %constant.237.clone.1), dimensions={} | broadcast | bytes 16777220 | tf_op jit(solution)/shard_map/broadcast_in_dim | solution.py:127
  187.5 0.9 broadcast.162
  188.4 150.0 %while.41 = (s32[]{:T(128)}, bf16[128,1024]{1,0:T(8,128)(2,1)S(1)}, f32[4096,1024]{1,0:T(8,128)}, bf16[2,128,1024]{2,1,0:T(8,128)(2,1)}, pred[]{:T(512)}, /*inde...) while((s32[]{:T(128)}, bf16[128,1024]{1,0:T(8,128)(2,1)S(1)}, ...), condition=%wide.region_7.8_spmd, body=%wide.region_3.7_spmd.sunk | while | flops 2155872256 | bytes 52954484 | solution.py:130
  188.5 1.5 fusion.58
  189.9 7.3 %convolution_convert_fusion.3 = bf16[128,4096]{1,0:T(8,128)(2,1)} fusion(bf16[128,1024]{1,0:T(8,128)(2,1)S(1)} %fusion.58, bf16[4096,1024]{1,0:T(8,128)(2,1)} %get-tuple-element.657), kind=kOutput, calls=%fused_computation.24.clone.1 | convolution fusion | flops 1074266112 | bytes 9699328 | tf_op jit(solution)/shard_map/while/body/eval_jaxpr/dot_general | solution.py:111
  197.2 1.0 constant_dynamic-slice_fusion.8
  198.2 23.0 %reduce-scatter.8.cloned.1.call-done = bf16[128,1024]{1,0:T(8,128)(2,1)} async-done(((bf16[128,4096]{1,0:T(8,128)(2,1)}), bf16[128,1024]{1,0:T(8,128)(2,1)}) %reduce-scatter.8.cloned.1.call-update) | async-done | bytes 262160 | tf_op jit(solution)/shard_map/while/body/eval_jaxpr/reduce_scatter | solution.py:114
  221.2 1.9 bitcast_dynamic-update-slice_fusion.8
  223.2 1.3 collective-permute-start.1
  224.5 2.3 collective-permute-done.1
  226.8 1.4 fusion.58
  228.2 7.3 %convolution_convert_fusion.3 = bf16[128,4096]{1,0:T(8,128)(2,1)} fusion(bf16[128,1024]{1,0:T(8,128)(2,1)S(1)} %fusion.58, bf16[4096,1024]{1,0:T(8,128)(2,1)} %get-tuple-element.657), kind=kOutput, calls=%fused_computation.24.clone.1 | convolution fusion | flops 1074266112 | bytes 9699328 | tf_op jit(solution)/shard_map/while/body/eval_jaxpr/dot_general | solution.py:111
  235.5 1.0 constant_dynamic-slice_fusion.8
  236.5 34.8 %reduce-scatter.8.cloned.1.call-done = bf16[128,1024]{1,0:T(8,128)(2,1)} async-done(((bf16[128,4096]{1,0:T(8,128)(2,1)}), bf16[128,1024]{1,0:T(8,128)(2,1)}) %reduce-scatter.8.cloned.1.call-update) | async-done | bytes 262160 | tf_op jit(solution)/shard_map/while/body/eval_jaxpr/reduce_scatter | solution.py:114
  271.3 1.9 bitcast_dynamic-update-slice_fusion.8
  273.2 1.3 collective-permute-start.1
  274.5 13.9 %conditional.2 = (f32[4096,1024]{1,0:T(8,128)}) conditional(s32[]{:T(128)} %convert_element_type.164, f32[4096,1024]{1,0:T(8,128)} %get-tuple-element.638, (bf16[2,128,4096]{2,1,0:T(8,128)(2,1)S(1)}, s32[]{:T(128)}, bf16[128,1024]{1,0:T(8,128)(2,1)S(1)}, f32[4096,1024]{1,0:T(8,128)}) %tuple.91), branch_computations={%region_5.5_spmd, %region_6.6_spmd} | conditional | flops 1077936128 | bytes 34865164 | solution.py:110
  274.5 13.9 %convolution_add_fusion = f32[4096,1024]{1,0:T(8,128)} fusion(f32[4096,1024]{1,0:T(8,128)} %get-tuple-element.401, bf16[128,1024]{1,0:T(8,128)(2,1)S(1)} %get-tuple-element.404, bf16[2,128,4096]{2,1,0:T(8,128)(2,1)S(1)} %get-tuple-element.402, s32[]{:T(128)} %get-tuple-element.403), kind=kOutput, calls=%fused_computation.20 | convolution fusion | flops 1077936128 | bytes 34865156 | tf_op jit(solution)/shard_map/while/body/eval_jaxpr/cond/branch_1_fun/dot_general | solution.py:103
  288.4 1.4 fusion.58
  289.8 7.3 %convolution_convert_fusion.3 = bf16[128,4096]{1,0:T(8,128)(2,1)} fusion(bf16[128,1024]{1,0:T(8,128)(2,1)S(1)} %fusion.58, bf16[4096,1024]{1,0:T(8,128)(2,1)} %get-tuple-element.657), kind=kOutput, calls=%fused_computation.24.clone.1 | convolution fusion | flops 1074266112 | bytes 9699328 | tf_op jit(solution)/shard_map/while/body/eval_jaxpr/dot_general | solution.py:111
  297.1 1.0 constant_dynamic-slice_fusion.8
  298.1 23.2 %reduce-scatter.8.cloned.1.call-done = bf16[128,1024]{1,0:T(8,128)(2,1)} async-done(((bf16[128,4096]{1,0:T(8,128)(2,1)}), bf16[128,1024]{1,0:T(8,128)(2,1)}) %reduce-scatter.8.cloned.1.call-update) | async-done | bytes 262160 | tf_op jit(solution)/shard_map/while/body/eval_jaxpr/reduce_scatter | solution.py:114
  321.3 1.9 bitcast_dynamic-update-slice_fusion.8
  323.2 1.3 collective-permute-start.1
  324.5 13.9 %conditional.2 = (f32[4096,1024]{1,0:T(8,128)}) conditional(s32[]{:T(128)} %convert_element_type.164, f32[4096,1024]{1,0:T(8,128)} %get-tuple-element.638, (bf16[2,128,4096]{2,1,0:T(8,128)(2,1)S(1)}, s32[]{:T(128)}, bf16[128,1024]{1,0:T(8,128)(2,1)S(1)}, f32[4096,1024]{1,0:T(8,128)}) %tuple.91), branch_computations={%region_5.5_spmd, %region_6.6_spmd} | conditional | flops 1077936128 | bytes 34865164 | solution.py:110
  324.5 13.9 %convolution_add_fusion = f32[4096,1024]{1,0:T(8,128)} fusion(f32[4096,1024]{1,0:T(8,128)} %get-tuple-element.401, bf16[128,1024]{1,0:T(8,128)(2,1)S(1)} %get-tuple-element.404, bf16[2,128,4096]{2,1,0:T(8,128)(2,1)S(1)} %get-tuple-element.402, s32[]{:T(128)} %get-tuple-element.403), kind=kOutput, calls=%fused_computation.20 | convolution fusion | flops 1077936128 | bytes 34865156 | tf_op jit(solution)/shard_map/while/body/eval_jaxpr/cond/branch_1_fun/dot_general | solution.py:103
  338.4 1.9 broadcast_select_fusion
  340.4 26.0 %all-reduce.2.cloned.1.call-done = bf16[2,128,1024]{2,1,0:T(8,128)(2,1)} async-done(((bf16[2,128,1024]{2,1,0:T(8,128)(2,1)}), bf16[2,128,1024]{2,1,0:T(8,128)(2,1)}) %all-reduce.2.cloned.1.call-update) | async-done | bytes 524304 | tf_op jit(solution)/shard_map/psum | solution.py:15
  366.4 9.1 %convert_element_type.99 = bf16[4096,1024]{1,0:T(8,128)(2,1)} convert(f32[4096,1024]{1,0:T(8,128)} %get-tuple-element.426) | non-fusion elementwise | flops 4194304 | bytes 25165824 | tf_op jit(solution)/shard_map/convert_element_type | solution.py:132
  375.6 0.6 copy-done.1
  376.4 64.6 %all-gather.6.cloned.1.call-done = bf16[32,128,1024]{2,1,0:T(8,128)(2,1)} async-done(((bf16[2,128,1024]{2,1,0:T(8,128)(2,1)}), bf16[32,128,1024]{2,1,0:T(8,128)(2,1)}) %all-gather.6.cloned.1.call-update) | async-done | bytes 8388624 | tf_op jit(solution)/shard_map/all_gather | solution.py:138
  440.9 3.9 gather_fusion.2
  444.9 3.9 bitcast_convert_fusion
  448.9 80.4 %reduce-scatter.4.cloned.1.call-done = bf16[256,1024]{1,0:T(8,128)(2,1)} async-done(((bf16[4096,1024]{1,0:T(8,128)(2,1)}), bf16[256,1024]{1,0:T(8,128)(2,1)}) %reduce-scatter.4.cloned.1.call-update) | async-done | bytes 524304 | tf_op jit(solution)/shard_map/reduce_scatter | solution.py:131
  529.3 2.1 bitcast_convert_fusion.1
  531.4 86.1 %reduce-scatter.6.cloned.1.call-done = bf16[80,1024]{1,0:T(8,128)(2,1)} async-done(((bf16[2560,1024]{1,0:T(8,128)(2,1)}), bf16[80,1024]{1,0:T(8,128)(2,1)}) %reduce-scatter.6.cloned.1.call-update) | async-done | bytes 163856 | tf_op jit(solution)/shard_map/reduce_scatter | solution.py:148
  617.5 1.7 convert_element_type.101
  (85 shorter events, 3.0 us)
Async XLA Ops:
  7.2 61.4 %all-gather.4.cloned.1.call-start = ((), (), s32[]{:S(2)}) async-start(), calls=%async_computation.3 | async-start | bytes 8650752 | tf_op jit(solution)/shard_map/all_gather | solution.py:48
  8.8 4.2 copy-start.8
  8.8 6.8 %copy-start = (s32[128]{0:T(128)S(1)}, s32[128]{0:T(128)}, u32[]{:S(2)}) copy-start(s32[128]{0:T(128)} %param.15) | copy-start | bytes 1540
  12.9 59.7 %copy-start.7 = (bf16[2,128,1024]{2,1,0:T(8,128)(2,1)S(1)}, bf16[2,128,1024]{2,1,0:T(8,128)(2,1)}, u32[]{:S(2)}) copy-start(bf16[2,128,1024]{2,1,0:T(8,128)(2,1)} %param.17) | copy-start | bytes 1572868
  74.9 26.5 %all-gather.8.cloned.1.call-start = ((), (), s32[]{:S(2)}) async-start(), calls=%async_computation.8 | async-start | bytes 1310720 | tf_op jit(solution)/shard_map/while/body/eval_jaxpr/all_gather | solution.py:68
  76.6 24.8 %copy-start.3 = (bf16[128,1024]{1,0:T(8,128)(2,1)S(1)}, bf16[128,1024]{1,0:T(8,128)(2,1)}, u32[]{:S(2)}) copy-start(bf16[128,1024]{1,0:T(8,128)(2,1)} %bitcast_select_fusion.7) | copy-start | bytes 786436 | tf_op jit(solution)/shard_map/while
  101.4 6.7 %copy-start.2 = (bf16[128,4096]{1,0:T(8,128)(2,1)S(1)}, bf16[128,4096]{1,0:T(8,128)(2,1)}, u32[]{:S(2)}) copy-start(bf16[128,4096]{1,0:T(8,128)(2,1)} %all-gather.8.cloned.1.call-done) | copy-start | bytes 3145732 | tf_op jit(solution)/shard_map/while
  106.7 1.8 copy-start.4
  106.7 2.7 collective-permute-start
  109.4 27.4 %all-gather.8.cloned.1.call-start = ((), (), s32[]{:S(2)}) async-start(), calls=%async_computation.8 | async-start | bytes 1310720 | tf_op jit(solution)/shard_map/while/body/eval_jaxpr/all_gather | solution.py:68
  111.0 25.7 %copy-start.3 = (bf16[128,1024]{1,0:T(8,128)(2,1)S(1)}, bf16[128,1024]{1,0:T(8,128)(2,1)}, u32[]{:S(2)}) copy-start(bf16[128,1024]{1,0:T(8,128)(2,1)} %bitcast_select_fusion.7) | copy-start | bytes 786436 | tf_op jit(solution)/shard_map/while
  136.7 6.7 %copy-start.2 = (bf16[128,4096]{1,0:T(8,128)(2,1)S(1)}, bf16[128,4096]{1,0:T(8,128)(2,1)}, u32[]{:S(2)}) copy-start(bf16[128,4096]{1,0:T(8,128)(2,1)} %all-gather.8.cloned.1.call-done) | copy-start | bytes 3145732 | tf_op jit(solution)/shard_map/while
  142.0 1.8 copy-start.4
  142.0 2.7 collective-permute-start
  144.6 27.1 %all-gather.8.cloned.1.call-start = ((), (), s32[]{:S(2)}) async-start(), calls=%async_computation.8 | async-start | bytes 1310720 | tf_op jit(solution)/shard_map/while/body/eval_jaxpr/all_gather | solution.py:68
  146.3 25.4 %copy-start.3 = (bf16[128,1024]{1,0:T(8,128)(2,1)S(1)}, bf16[128,1024]{1,0:T(8,128)(2,1)}, u32[]{:S(2)}) copy-start(bf16[128,1024]{1,0:T(8,128)(2,1)} %bitcast_select_fusion.7) | copy-start | bytes 786436 | tf_op jit(solution)/shard_map/while
  171.7 6.7 %copy-start.2 = (bf16[128,4096]{1,0:T(8,128)(2,1)S(1)}, bf16[128,4096]{1,0:T(8,128)(2,1)}, u32[]{:S(2)}) copy-start(bf16[128,4096]{1,0:T(8,128)(2,1)} %all-gather.8.cloned.1.call-done) | copy-start | bytes 3145732 | tf_op jit(solution)/shard_map/while
  176.9 1.8 copy-start.4
  177.0 2.7 collective-permute-start
  179.6 8.8 %copy-start.5 = (bf16[2,128,1024]{2,1,0:T(8,128)(2,1)S(1)}, bf16[2,128,1024]{2,1,0:T(8,128)(2,1)}, u32[]{:S(2)}) copy-start(bf16[2,128,1024]{2,1,0:T(8,128)(2,1)} %param.19) | copy-start | bytes 1572868
  188.4 32.8 %reduce-scatter.8.cloned.1.call-start = ((), (), s32[]{:S(2)}) async-start(), calls=%async_computation.9 | async-start | bytes 1310720 | tf_op jit(solution)/shard_map/while/body/eval_jaxpr/reduce_scatter | solution.py:114
  223.2 3.6 collective-permute-start.1
  226.8 44.5 %reduce-scatter.8.cloned.1.call-start = ((), (), s32[]{:S(2)}) async-start(), calls=%async_computation.9 | async-start | bytes 1310720 | tf_op jit(solution)/shard_map/while/body/eval_jaxpr/reduce_scatter | solution.py:114
  273.2 15.2 %collective-permute-start.1 = (bf16[128,1024]{1,0:T(8,128)(2,1)}, bf16[128,1024]{1,0:T(8,128)(2,1)S(1)}, u32[]{:S(2)}, u32[]{:S(2)}) collective-permute-start(bf16[128,1024]{1,0:T(8,128)(2,1)} %get-tuple-element.588), channel_id=1, source_target_pairs={{64,0},{65,1},{66,2},{67,3},{68,4},{69,5},{70,6},{71,7},{72,8},{73... | collective-permute-start | bytes 786440 | tf_op jit(solution)/shard_map/while/body/eval_jaxpr/ppermute | solution.py:10
  288.4 32.9 %reduce-scatter.8.cloned.1.call-start = ((), (), s32[]{:S(2)}) async-start(), calls=%async_computation.9 | async-start | bytes 1310720 | tf_op jit(solution)/shard_map/while/body/eval_jaxpr/reduce_scatter | solution.py:114
  323.2 15.2 %collective-permute-start.1 = (bf16[128,1024]{1,0:T(8,128)(2,1)}, bf16[128,1024]{1,0:T(8,128)(2,1)S(1)}, u32[]{:S(2)}, u32[]{:S(2)}) collective-permute-start(bf16[128,1024]{1,0:T(8,128)(2,1)} %get-tuple-element.588), channel_id=1, source_target_pairs={{64,0},{65,1},{66,2},{67,3},{68,4},{69,5},{70,6},{71,7},{72,8},{73... | collective-permute-start | bytes 786440 | tf_op jit(solution)/shard_map/while/body/eval_jaxpr/ppermute | solution.py:10
  338.4 27.9 %all-reduce.2.cloned.1.call-start = ((), (), s32[]{:S(2)}) async-start(), calls=%async_computation.5 | async-start | bytes 1048576 | tf_op jit(solution)/shard_map/psum | solution.py:15
  340.3 100.6 %all-gather.6.cloned.1.call-start = ((), (), s32[]{:S(2)}) async-start(), calls=%async_computation.6 | async-start | bytes 8912896 | tf_op jit(solution)/shard_map/all_gather | solution.py:138
  366.3 162.9 %reduce-scatter.4.cloned.1.call-start = ((), (), s32[]{:S(2)}) async-start(), calls=%async_computation.4 | async-start | bytes 8912896 | tf_op jit(solution)/shard_map/reduce_scatter | solution.py:131
  375.5 0.7 copy-start.1
  375.5 0.7 copy-start.9
  375.5 69.4 %copy-start.6 = (bf16[4,32,2560]{2,1,0:T(8,128)(2,1)S(1)}, bf16[4,32,2560]{2,1,0:T(8,128)(2,1)}, u32[]{:S(2)}) copy-start(bf16[4,32,2560]{2,1,0:T(8,128)(2,1)} %param.13) | copy-start | bytes 1966084
  375.5 242.0 %reduce-scatter.6.cloned.1.call-start = ((), (), s32[]{:S(2)}) async-start(), calls=%async_computation.7 | async-start | bytes 5406720 | tf_op jit(solution)/shard_map/reduce_scatter | solution.py:148
Sparse Core Ops, SparseCore 0:
  13.0 55.4 all-gather.3
  78.0 23.4 all-gather.7
  112.4 24.2 all-gather.7
  147.4 24.2 all-gather.7
  197.3 23.8 reduce-scatter.7
  235.6 35.5 reduce-scatter.7
  297.3 23.9 reduce-scatter.7
  342.3 24.0 all-reduce.1
  368.7 72.2 all-gather.5
  444.6 84.6 reduce-scatter.3
  533.5 83.9 reduce-scatter.5
where the time goes:
time: 627 us; the launch traced here: 626 us
  waiting for transfers between devices  462 us (74%)
  matrix products  73.3 us (12%)
  other arithmetic  38.8 us (6%)
  local copies, waits for them, and re-layouts  29 us (5%)
  between operations  13.9 us (2%)
  starting transfers between devices  8.41 us (1%)
    reduce_scatter x1, waiting for transfers between devices, on_device(): lax.psum_scatter(merger_part.astype(jnp.bfloat16), ('segment', 'dp'), sca...  86.1 us
    reduce_scatter x3, waiting for transfers between devices, backward_tick(): lax.psum_scatter(partial_value.astype(jnp.bfloat16), 'mp', scatter_dimens...  81 us
    reduce_scatter x1, waiting for transfers between devices, on_device(): lax.psum_scatter(weight_grad.astype(jnp.bfloat16), 'dp', scatter_dimensio...  80.4 us
    all_gather x3, waiting for transfers between devices, forward_tick(): gathered = lax.all_gather(current, 'mp', axis=1, tiled=True)  69.6 us
    all_gather x1, waiting for transfers between devices, on_device(): owners = lax.all_gather(rooted, 'dp', axis=0, tiled=True)  64.6 us
    all_gather x1, waiting for transfers between devices, on_device(): every_embed = lax.all_gather(embeds, ('segment', 'dp'), axis=0, tiled=True)  51.7 us
    dot_general x2, matrix products, add_grad(): lax.dot_general(gathered, local_grad, (((0,), (0,)), ((), ())), preferred...  27.7 us
    psum x1, waiting for transfers between devices, spread(): return lax.psum(jnp.where(mine, shard, jnp.zeros_like(shard)), axis)  26 us
  transfers between devices with their start and end apart: 17, of which 12 were waited for; matrix products, arithmetic and copies ran while one was open for 10% of the time, Pallas kernels for 0%

commit v1 on v0

v1 whole, which is shorter than its diff:
```python
import jax
import jax.numpy as jnp
from jax import lax
from jax.experimental import pallas as pl
from jax.experimental.pallas import tpu as pltpu
from jax.sharding import PartitionSpec as P

BF = jnp.bfloat16
F32 = jnp.float32
SIDE = 4
SLOTS = 8
ROWS = 32
MINE = 4
ANY = pl.BlockSpec(memory_space=pl.ANY)


def dot(a, b):
    return jnp.dot(a, b, preferred_element_type=F32)


def dot_nt(a, b):
    return lax.dot_general(a, b, (((1,), (1,)), ((), ())), preferred_element_type=F32)


def dot_tn(a, b):
    return lax.dot_general(a, b, (((0,), (0,)), ((), ())), preferred_element_type=F32)


def along_x(block, distance):
    return lax.ppermute(block, "mp", [(i, (i + distance) % SIDE) for i in range(SIDE)])


def along_z(block, distance):
    pairs = [
        (z * SIDE + y, (z + distance) % SIDE * SIDE + y) for z in range(SIDE) for y in range(SIDE)
    ]
    return lax.ppermute(block, "dp", pairs)


def along_y(block, distance):
    pairs = [
        (z * SIDE + y, z * SIDE + (y + distance) % SIDE) for z in range(SIDE) for y in range(SIDE)
    ]
    return lax.ppermute(block, "dp", pairs)


def along_y_of(core, block, distance):
    size = SIDE * SIDE
    pairs = [
        (core * size + z * SIDE + y, core * size + z * SIDE + (y + distance) % SIDE)
        for z in range(SIDE)
        for y in range(SIDE)
    ]
    return lax.ppermute(block, ("segment", "dp"), pairs)


def spread_kernel(routing, place, text, ups, out_text, out_ups, sems):
    core, replica = place[0], place[1]
    copies = []
    for group in range(16):
        slot = jnp.int32(0)
        for j in range(MINE):
            q = routing[(core * 16 + group) * MINE + j]
            slot = jnp.where(lax.shift_right_logical(q, 3) == replica, q & 7, slot)
        for n, (src, dst) in enumerate(((text, out_text), (ups, out_ups))):
            copy = pltpu.make_async_copy(src.at[slot], dst.at[group], sems.at[n, group])
            copy.start()
            copies.append(copy)
    for copy in copies:
        copy.wait()


def spread(routing, place, text, ups):
    shape = jax.ShapeDtypeStruct((16,) + text.shape[1:], text.dtype)
    return pl.pallas_call(
        spread_kernel,
        grid_spec=pltpu.PrefetchScalarGridSpec(
            num_scalar_prefetch=2,
            grid=(1,),
            in_specs=[ANY, ANY],
            out_specs=[ANY, ANY],
            scratch_shapes=[pltpu.SemaphoreType.DMA((2, 16))],
        ),
        out_shape=[shape, shape],
    )(routing, place, text, ups)


def merge_kernel(source, counts, text, image, out):
    row = lax.broadcasted_iota(jnp.int32, (ROWS, text.shape[2]), 0)
    out[0] = jnp.where(row < counts[pl.program_id(0)], image[0], text[0])


def merge(source, counts, text, image):
    columns = text.shape[2]
    block = (1, ROWS, columns)
    return pl.pallas_call(
        merge_kernel,
        grid_spec=pltpu.PrefetchScalarGridSpec(
            num_scalar_prefetch=2,
            grid=(MINE,),
            in_specs=[
                pl.BlockSpec(block, lambda j, source, counts: (source[j], 0, 0)),
                pl.BlockSpec(block, lambda j, source, counts: (j, 0, 0)),
            ],
            out_specs=pl.BlockSpec(block, lambda j, source, counts: (j, 0, 0)),
        ),
        out_shape=jax.ShapeDtypeStruct((MINE, ROWS, columns), text.dtype),
    )(source, counts, text, image).reshape(MINE * ROWS, columns)


def pick_kernel(source, arrived, out):
    out[...] = arrived[...]


def pick(source, arrived):
    columns = arrived.shape[2]
    block = (1, ROWS, columns)
    return pl.pallas_call(
        pick_kernel,
        grid_spec=pltpu.PrefetchScalarGridSpec(
            num_scalar_prefetch=1,
            grid=(MINE,),
            in_specs=[pl.BlockSpec(block, lambda j, source: (source[j], 0, 0))],
            out_specs=pl.BlockSpec(block, lambda j, source: (j, 0, 0)),
        ),
        out_shape=jax.ShapeDtypeStruct((MINE, ROWS, columns), arrived.dtype),
    )(source, arrived).reshape(MINE * ROWS, columns)


def turn_kernel(place, own, other, out, sems):
    core, x = place[0], place[2]
    size = out.shape[2]

    def copy(source, section, d):
        block = lax.rem(x - d + SIDE, SIDE)
        start = pl.multiple_of(block * size, size)
        return pltpu.make_async_copy(
            source.at[pl.ds(start, size)], out.at[section, d], sems.at[section, d]
        )

    for section in range(2):
        for d in range(SIDE):

            @pl.when(core == section)
            def _():
                copy(own, section, d).start()

            @pl.when(core != section)
            def _():
                copy(other, section, d).start()

    for section in range(2):
        for d in range(SIDE):
            copy(own, section, d).wait()


def turn(place, own, other):
    rows, columns = own.shape
    return pl.pallas_call(
        turn_kernel,
        grid_spec=pltpu.PrefetchScalarGridSpec(
            num_scalar_prefetch=1,
            grid=(1,),
            in_specs=[ANY, ANY],
            out_specs=ANY,
            scratch_shapes=[pltpu.SemaphoreType.DMA((2, SIDE))],
        ),
        out_shape=jax.ShapeDtypeStruct((2, SIDE, rows // SIDE, columns), own.dtype),
    )(place, own, other)


def order_kernel(place, in0, in1, in2, in3, out0, out1, out2, out3, sems):
    x, y, z = place[2], place[3], place[4]
    blocks = (in0, in1, in2, in3)
    outs = (out0, out1, out2, out3)
    part = in0.shape[1] // SIDE

    def copy(d, e, j):
        start = pl.multiple_of(lax.rem(y + j, SIDE) * part, part)
        return pltpu.make_async_copy(
            blocks[d].at[:, pl.ds(start, part)],
            outs[e].at[:, pl.ds(j * part, part)],
            sems.at[e, j],
        )

    for e in range(SIDE):
        for d in range(SIDE):

            @pl.when(lax.rem(x - z - e + 2 * SIDE, SIDE) == d)
            def _():
                for j in range(SIDE):
                    copy(d, e, j).start()

    for e in range(SIDE):
        for j in range(SIDE):
            copy(0, e, j).wait()


def order(place, blocks):
    shape = jax.ShapeDtypeStruct(blocks[0].shape, blocks[0].dtype)
    return pl.pallas_call(
        order_kernel,
        grid_spec=pltpu.PrefetchScalarGridSpec(
            num_scalar_prefetch=1,
            grid=(1,),
            in_specs=[ANY] * 4,
            out_specs=[ANY] * 4,
            scratch_shapes=[pltpu.SemaphoreType.DMA((SIDE, SIDE))],
        ),
        out_shape=[shape] * 4,
    )(place, *blocks)


def line_up_kernel(place, arrived, out, sems):
    core, z = place[0], place[4]
    copies = []
    for other in range(2):
        for e in range(SIDE):
            block = lax.rem(core + other, 2) * SIDE + lax.rem(z - e + SIDE, SIDE)
            copy = pltpu.make_async_copy(
                arrived.at[block], out.at[other * SIDE + e], sems.at[other, e]
            )
            copy.start()
            copies.append(copy)
    for copy in copies:
        copy.wait()


def line_up(place, arrived):
    return pl.pallas_call(
        line_up_kernel,
        grid_spec=pltpu.PrefetchScalarGridSpec(
            num_scalar_prefetch=1,
            grid=(1,),
            in_specs=[ANY],
            out_specs=ANY,
            scratch_shapes=[pltpu.SemaphoreType.DMA((2, SIDE))],
        ),
        out_shape=jax.ShapeDtypeStruct(arrived.shape, arrived.dtype),
    )(place, arrived)


def gelu_back(preact, cotangent):
    _, pullback = jax.vjp(jax.nn.gelu, preact)
    return pullback(cotangent)[0]


def on_device(patches, merger_weight, image_counts, routing, text_embed, llm_weight, upstream):
    core = lax.axis_index("segment")
    x = lax.axis_index("mp")
    replica = lax.axis_index("dp")
    z, y = replica // SIDE, replica % SIDE
    place = jnp.stack([core, replica, x, y, z]).astype(jnp.int32)
    group = core * 16 + replica
    columns = merger_weight.shape[1]
    merger = patches.shape[2]

    send_text, send_ups = spread(
        routing,
        place,
        text_embed.reshape(SLOTS, ROWS, columns),
        upstream.reshape(SLOTS, ROWS, columns),
    )
    arrived_text = lax.all_to_all(send_text, "dp", 0, 0, tiled=True)
    own_weight = llm_weight[0]
    other_weight = lax.ppermute(own_weight, "segment", [(0, 1), (1, 0)])
    source = lax.dynamic_slice_in_dim(routing, group * MINE, MINE) // SLOTS
    counts = lax.dynamic_slice_in_dim(image_counts, group * MINE, MINE)

    activated = jax.nn.gelu(patches.astype(F32)).astype(BF).reshape(MINE * ROWS, merger)
    embeds = dot(activated, merger_weight).astype(BF).reshape(MINE, ROWS, columns)
    weights = turn(place, own_weight, other_weight)
    hidden = merge(source, counts, arrived_text, embeds)
    arrived_ups = lax.all_to_all(send_ups, "dp", 0, 0, tiled=True)

    parts = activated.reshape(MINE * ROWS, 8, merger // 8).transpose(1, 0, 2)
    eights = [
        [c * 16 + zz * SIDE + yy for c in range(2) for zz in range(SIDE)] for yy in range(SIDE)
    ]
    act_cols = lax.all_to_all(
        parts, ("segment", "dp"), 0, 0, tiled=True, axis_index_groups=eights
    )
    act_cols = line_up(place, act_cols).reshape(8 * MINE * ROWS, merger // 8)

    saved = []
    rows_of = []
    for section in range(2):
        blocks = [hidden] + [along_x(hidden, d) for d in (1, 2, 3)]
        preact = dot(blocks[0], weights[section, 0])
        for d in (1, 3, 2):
            preact = preact + dot(blocks[d], weights[section, d])
        saved.append(preact)
        ordered = order(place, blocks)
        tokens = [ordered[0]] + [along_z(ordered[e], e) for e in (1, 2, 3)]
        tokens = jnp.concatenate(tokens, axis=0)
        hop = lax.ppermute(tokens, "segment", [(1 - section, section)])
        rows_of.append((tokens, hop))
        if section == 0:
            hidden = (hidden.astype(F32) + jax.nn.gelu(preact)).astype(BF)

    cotangent = pick(source, arrived_ups)
    partials = []
    for section in (1, 0):
        local = gelu_back(saved[section], cotangent.astype(F32)).astype(BF)
        terms = [
            along_x(dot_nt(local, weights[section, SIDE - d]).astype(BF), d) for d in (2, 1, 3)
        ]
        terms.append(dot_nt(local, weights[section, 0]).astype(BF))
        inner = sum(term.astype(F32) for term in terms)
        cotangent = (cotangent.astype(F32) + inner).astype(BF)
        locals_here = [local] + [along_z(local, e) for e in (1, 2, 3)]
        locals_here = jnp.concatenate(locals_here, axis=0)
        hop = lax.ppermute(locals_here, "segment", [(1 - section, section)])
        tokens, tokens_hop = rows_of[section]
        part = dot_tn(tokens, locals_here) + dot_tn(tokens_hop, hop)
        part = part.astype(BF).reshape(SIDE, -1, columns)
        own = part[0].astype(F32)
        for j in (1, 2, 3):
            own = own + along_y_of(section, part[j], j).astype(F32)
        partials.append(own)
    llm_grad = jnp.where(core == 0, partials[1], partials[0])[None]

    position = jnp.arange(MINE * ROWS) % ROWS
    image_rows = position < jnp.repeat(counts, ROWS)
    image_grad = jnp.where(image_rows[:, None], cotangent, jnp.zeros((), BF))
    grads = [image_grad] + [along_z(image_grad, e) for e in (1, 2, 3)]
    grads = jnp.concatenate(grads, axis=0)
    grads_hop = lax.ppermute(grads, "segment", [(0, 1), (1, 0)])
    half = grads.shape[0]
    part = dot_tn(act_cols[:half], grads) + dot_tn(act_cols[half:], grads_hop)
    part = part.astype(BF).reshape(SIDE, -1, columns)

    def toward(j):
        return lax.dynamic_index_in_dim(part, (y + j) % SIDE, 0, keepdims=False)

    merger_grad = toward(0).astype(F32)
    for j in (1, 2, 3):
        merger_grad = merger_grad + along_y(toward(j), j).astype(F32)
    return (llm_grad, merger_grad)


def solution(mesh):
    return jax.shard_map(
        on_device,
        mesh=mesh,
        in_specs=(
            P(("segment", "dp"), None, None),
            P(None, "mp"),
            P(),
            P(),
            P(None, "dp", "mp"),
            P("segment", None, "mp"),
            P(None, "dp", "mp"),
        ),
        out_specs=(P("segment", "dp", "mp"), P(("segment", "dp"), "mp")),
        check_vma=False,
    )
```

time: 627 us -> 879 us (1.40)
  Pallas kernels: 0 us -> 676 us
  waiting for transfers between devices: 462 us -> 37.5 us
  starting transfers between devices: 8.41 us -> 91.5 us
  other arithmetic: 38.8 us -> 7.06 us
  matrix products: 73.3 us -> 50.5 us
  local copies, waits for them, and re-layouts: 29 us -> 10.6 us
  between operations: 13.9 us -> 1.55 us
    pallas_call x0 -> x7, Pallas kernels: none -> 676 us  [the longest x1 510 us: turn(): pl.pallas_call(turn_kernel, grid_spec=pltpu.PrefetchScalarGridSpec(num_sc...]
    reduce_scatter x5 -> x0, waiting for transfers between devices: 247 us -> none  [the longest x1 86.1 us: on_device(): lax.psum_scatter(merger_part.astype(jnp.bfloat16), ('segment', 'dp'), sca...]
    all_gather x5 -> x0, waiting for transfers between devices: 186 us -> none  [the longest x3 69.6 us: forward_tick(): gathered = lax.all_gather(current, 'mp', axis=1, tiled=True)]
    ppermute x6 -> x42, starting transfers between devices: 8.15 us -> 75 us  [the longest x15 23.6 us: along_z(): return lax.ppermute(block, 'dp', pairs)]
    psum x1 -> x0, waiting for transfers between devices: 26 us -> none  [spread(): return lax.psum(jnp.where(mine, shard, jnp.zeros_like(shard)), axis)]
    ppermute x6 -> x42, waiting for transfers between devices: 2.33 us -> 25.4 us  [the longest x15 10.2 us: along_z(): return lax.ppermute(block, 'dp', pairs)]
    dot_general x10 -> x23, matrix products: 73.3 us -> 50.5 us  [the longest x9 22.1 us: dot(): return jnp.dot(a, b, preferred_element_type=F32)]
    all_to_all x0 -> x3, starting transfers between devices: none -> 16.5 us  [the longest x1 8.14 us: on_device(): arrived_text = lax.all_to_all(send_text, 'dp', 0, 0, tiled=True)]
  transfers between devices with their start and end apart: 17 -> 45, of which waited for: 12 -> 10; matrix products, arithmetic and copies ran while one was open for 10% -> 6% of each run, Pallas kernels for 0% -> 77%
where the time goes in v1:
time: 879 us; the launch traced here: 875 us
  Pallas kernels  676 us (77%)
  starting transfers between devices  91.5 us (10%)
  matrix products  50.5 us (6%)
  waiting for transfers between devices  37.5 us (4%)
  local copies, waits for them, and re-layouts  10.6 us (1%)
    pallas_call x1, Pallas kernels, turn(): pl.pallas_call(turn_kernel, grid_spec=pltpu.PrefetchScalarGridSpec(num_sc...  510 us
    pallas_call x2, Pallas kernels, order(): pl.pallas_call(order_kernel, grid_spec=pltpu.PrefetchScalarGridSpec(num_s...  67.4 us
    pallas_call x1, Pallas kernels, spread(): pl.pallas_call(spread_kernel, grid_spec=pltpu.PrefetchScalarGridSpec(num_...  65.6 us
    pallas_call x1, Pallas kernels, line_up(): pl.pallas_call(line_up_kernel, grid_spec=pltpu.PrefetchScalarGridSpec(num...  25.7 us
    ppermute x15, starting transfers between devices, along_z(): return lax.ppermute(block, 'dp', pairs)  23.6 us
    dot_general x9, matrix products, dot(): return jnp.dot(a, b, preferred_element_type=F32)  22.1 us
    dot_general x8, matrix products, dot_nt(): lax.dot_general(a, b, (((1,), (1,)), ((), ())), preferred_element_type=F32)  21 us
    ppermute x6, starting transfers between devices, along_y_of(): return lax.ppermute(block, ('segment', 'dp'), pairs)  19.6 us
  transfers between devices with their start and end apart: 45, of which 10 were waited for; matrix products, arithmetic and copies ran while one was open for 6% of the time, Pallas kernels for 77%

profile of v1, /device:TPU:0, one launch (start us, length us, event | category | flops | bytes accessed | tf_op | source)
XLA Modules:
  0.0 874.7 jit_solution(463224726732257456)
XLA Ops:
  1.4 65.6 %shard_map.86 = (bf16[16,32,1024]{2,1,0:T(8,128)(2,1)}, bf16[16,32,1024]{2,1,0:T(8,128)(2,1)}) custom-call(s32[128]{0:T(128)} %routing.1, s32[5]{0:T(128)} %stack.23.place, bf16[8,32,1024]{2,1,0:T(8,128)(2,1)} %bitcast.143, bf16[8,32,1024]{2,1,0:T(8,128)(2,1)} %bitcast.144), custom_call_target="tpu_custom_call" | custom-call | tf_op jit(solution)/shard_map/pallas_call | solution.py:75
  67.0 8.1 all-to-all-start
  77.6 4.1 convolution_convert_fusion
  81.6 12.1 %all-to-all-done.text = bf16[16,32,1024]{2,1,0:T(8,128)(2,1)S(1)} async-done(((bf16[16,32,1024]{2,1,0:T(8,128)(2,1)}), bf16[16,32,1024]{2,1,0:T(8,128)(2,1)S(1)}, u32[]{:S(2)}, u32[]{:S(2)}) %all-to-all-start) | async-done | bytes 1048608 | tf_op jit(solution)/shard_map/all_to_all | solution.py:264
  93.7 3.5 all-to-all-start.2
  98.6 3.7 shard_map.87
  102.3 1.5 collective-permute-start
  103.8 1.7 collective-permute-start.2
  105.5 1.8 collective-permute-start.1
  107.3 510.1 %shard_map.90 = bf16[2,4,1024,1024]{3,2,1,0:T(8,128)(2,1)} custom-call(s32[5]{0:T(128)} %stack.23.place, bf16[4096,1024]{1,0:T(8,128)(2,1)} %bitcast.131, bf16[4096,1024]{1,0:T(8,128)(2,1)} %collective-permute-done.6.other), custom_call_target="tpu_custom_call" | custom-call | tf_op jit(solution)/shard_map/pallas_call | solution.py:159
  617.4 2.1 fusion.3
  619.6 4.8 all-to-all-start.1
  624.4 2.1 fusion.5
  627.3 2.0 fusion.7
  629.3 2.3 add_convert_fusion.2
  633.6 25.7 %shard_map.92 = bf16[8,128,320]{2,1,0:T(8,128)(2,1)} custom-call(s32[5]{0:T(128)} %stack.23.place, bf16[8,128,320]{2,1,0:T(8,128)(2,1)} %copy.11.arrived), custom_call_target="tpu_custom_call" | custom-call | tf_op jit(solution)/shard_map/pallas_call | solution.py:230
  660.2 3.6 shard_map.89
  663.9 2.6 collective-permute-start.8
  667.0 2.1 fusion.11
  669.1 7.5 collective-permute-done.8.in3
  676.6 2.1 fusion.13
  678.8 2.1 fusion.15
  681.0 3.1 fusion.52
  684.1 3.2 fusion.29
  687.3 2.5 fusion.30
  689.8 2.6 fusion.31
  692.5 4.5 collective-permute-start.11
  697.1 33.7 %shard_map.88 = (bf16[128,1024]{1,0:T(8,128)(2,1)}, bf16[128,1024]{1,0:T(8,128)(2,1)}, bf16[128,1024]{1,0:T(8,128)(2,1)}, bf16[128,1024]{1,0:T(8,128)(2,1)}) custom-call(s32[5]{0:T(128)} %stack.23.place, bf16[128,1024]{1,0:T(8,128)(2,1)} %bitcast.136, bf16[128,1024]{1,0:T(8,128)(2,1)} %copy-done.10, bf16[128,1024]{1,0:T(8,128)(2,1)} %copy-done.12, ...), custom_call_target="tpu_custom_call" | custom-call | tf_op jit(solution)/shard_map/pallas_call | solution.py:201
  730.8 1.8 collective-permute-start.24
  732.6 2.7 collective-permute-start.25
  735.2 33.7 %shard_map.91 = (bf16[128,1024]{1,0:T(8,128)(2,1)}, bf16[128,1024]{1,0:T(8,128)(2,1)}, bf16[128,1024]{1,0:T(8,128)(2,1)}, bf16[128,1024]{1,0:T(8,128)(2,1)}) custom-call(s32[5]{0:T(128)} %stack.23.place, bf16[128,1024]{1,0:T(8,128)(2,1)} %copy-done.5, bf16[128,1024]{1,0:T(8,128)(2,1)} %copy-done.13, bf16[128,1024]{1,0:T(8,128)(2,1)} %copy-done.15, ...), custom_call_target="tpu_custom_call" | custom-call | tf_op jit(solution)/shard_map/pallas_call | solution.py:201
  769.9 1.6 collective-permute-start.26
  773.0 2.8 fusion.45
  775.8 2.4 fusion.34
  778.3 2.4 fusion.35
  780.8 2.5 fusion.36
  783.3 2.6 collective-permute-start.3
  786.7 1.5 collective-permute-start.4
  788.3 2.6 collective-permute-start.5
  790.9 2.6 collective-permute-start.32
  794.8 3.2 collective-permute-start.34
  798.0 1.4 collective-permute-start.28
  799.4 1.7 collective-permute-done.5
  801.0 1.3 collective-permute-start.27
  802.6 5.3 collective-permute-start.14
  807.8 2.5 fusion.63
  810.3 2.4 collective-permute-done.13
  812.8 2.8 collective-permute-done.14
  816.7 2.7 collective-permute-start.37
  821.7 1.8 collective-permute-done.36
  824.9 1.5 collective-permute-start.38
  827.7 2.4 add_convert_fusion
  831.9 1.5 collective-permute-start.30
  834.6 1.4 add_convert_fusion.1
  837.2 1.5 collective-permute-start.39
  838.7 2.7 collective-permute-start.40
  841.4 1.5 collective-permute-start.41
  844.8 1.4 collective-permute-start.31
  846.3 6.9 collective-permute-start.18
  853.2 4.6 collective-permute-start.19
  857.8 4.5 collective-permute-start.20
  863.2 5.7 collective-permute-done.19
  869.0 1.9 collective-permute-done.20
  870.9 3.8 select_bitcast_fusion
  (137 shorter events, 26.5 us)
Async XLA Ops:
  0.6 74.6 %copy-start.6 = (bf16[4,32,2560]{2,1,0:T(8,128)(2,1)S(1)}, bf16[4,32,2560]{2,1,0:T(8,128)(2,1)}, u32[]{:S(2)}) copy-start(bf16[4,32,2560]{2,1,0:T(8,128)(2,1)} %param.7) | copy-start | bytes 1966084
  0.6 106.7 %collective-permute-start.6 = (bf16[4096,1024]{1,0:T(8,128)(2,1)}, bf16[4096,1024]{1,0:T(8,128)(2,1)}, u32[]{:S(2)}, u32[]{:S(2)}) collective-permute-start(bf16[4096,1024]{1,0:T(8,128)(2,1)} %bitcast.130), channel_id=1, source_target_pairs={{0,64},{64,0},{1,65},{65,1},{2,66},{66,2},{3,67},{67,3},{4,68},{68... | collective-permute-start | bytes 25165832 | tf_op jit(solution)/shard_map/ppermute | solution.py:266
  67.0 26.7 %all-to-all-start = ((bf16[16,32,1024]{2,1,0:T(8,128)(2,1)}), bf16[16,32,1024]{2,1,0:T(8,128)(2,1)S(1)}, u32[]{:S(2)}, u32[]{:S(2)}) async-start(bf16[16,32,1024]{2,1,0:T(8,128)(2,1)} %get-tuple-element.12), calls=%async_computation | async-start | bytes 2097152 | tf_op jit(solution)/shard_map/all_to_all | solution.py:264
  77.6 19.7 %copy-start.21 = (s32[128]{0:T(128)S(1)}, s32[128]{0:T(128)}, u32[]{:S(2)}) copy-start(s32[128]{0:T(128)} %routing.1) | copy-start | bytes 1540
  77.6 20.4 %copy-start.26 = (s32[128]{0:T(128)S(1)}, s32[128]{0:T(128)}, u32[]{:S(2)}) copy-start(s32[128]{0:T(128)} %param.9) | copy-start | bytes 1540
  93.7 4.8 copy-start.1
  93.7 525.8 %all-to-all-start.2 = ((bf16[8,128,320]{1,2,0:T(8,128)(2,1)}), bf16[8,128,320]{1,2,0:T(8,128)(2,1)S(1)}, u32[]{:S(2)}, u32[]{:S(2)}) async-start(bf16[8,128,320]{1,2,0:T(8,128)(2,1)} %copy.10), calls=%async_computation.2 | async-start | bytes 1310720 | tf_op jit(solution)/shard_map/all_to_all | solution.py:280
  102.3 515.1 %collective-permute-start = (bf16[128,1024]{1,0:T(8,128)(2,1)}, bf16[128,1024]{1,0:T(8,128)(2,1)S(1)}, u32[]{:S(2)}, u32[]{:S(2)}) collective-permute-start(bf16[128,1024]{1,0:T(8,128)(2,1)} %bitcast.133), channel_id=1, source_target_pairs={{0,16},{16,32},{32,48},{48,0},{1,17},{17,33},{33,49},{49,1},{2,18}... | collective-permute-start | bytes 786440 | tf_op jit(solution)/shard_map/ppermute | solution.py:30
  103.8 520.6 %collective-permute-start.2 = (bf16[128,1024]{1,0:T(8,128)(2,1)}, bf16[128,1024]{1,0:T(8,128)(2,1)S(1)}, u32[]{:S(2)}, u32[]{:S(2)}) collective-permute-start(bf16[128,1024]{1,0:T(8,128)(2,1)} %bitcast.134), channel_id=1, source_target_pairs={{0,48},{16,0},{32,16},{48,32},{1,49},{17,1},{33,17},{49,33},{2,50}... | collective-permute-start | bytes 786440 | tf_op jit(solution)/shard_map/ppermute | solution.py:30
  105.5 521.1 %collective-permute-start.1 = (bf16[128,1024]{1,0:T(8,128)(2,1)}, bf16[128,1024]{1,0:T(8,128)(2,1)S(1)}, u32[]{:S(2)}, u32[]{:S(2)}) collective-permute-start(bf16[128,1024]{1,0:T(8,128)(2,1)} %bitcast.135), channel_id=1, source_target_pairs={{0,32},{16,48},{32,0},{48,16},{1,33},{17,49},{33,1},{49,17},{2,34}... | collective-permute-start | bytes 786440 | tf_op jit(solution)/shard_map/ppermute | solution.py:30
  619.6 39.7 %all-to-all-start.1 = ((bf16[16,32,1024]{2,1,0:T(8,128)(2,1)}), bf16[16,32,1024]{2,1,0:T(8,128)(2,1)S(1)}, u32[]{:S(2)}, u32[]{:S(2)}) async-start(bf16[16,32,1024]{2,1,0:T(8,128)(2,1)} %get-tuple-element.17), calls=%async_computation.1 | async-start | bytes 2097152 | tf_op jit(solution)/shard_map/all_to_all | solution.py:274
  626.5 2.8 copy-start.2
  629.3 3.0 copy-start.20
  631.6 49.4 %copy-start.5 = (bf16[128,1024]{1,0:T(8,128)(2,1)}, bf16[128,1024]{1,0:T(8,128)(2,1)S(1)}, u32[]{:S(2)}) copy-start(bf16[128,1024]{1,0:T(8,128)(2,1)S(1)} %get-tuple-element.35.in0) | copy-start | bytes 786436
  631.6 35.4 %collective-permute-start.7 = (bf16[128,1024]{1,0:T(8,128)(2,1)S(1)}, bf16[128,1024]{1,0:T(8,128)(2,1)S(1)}, u32[]{:S(2)}, u32[]{:S(2)}) collective-permute-start(bf16[128,1024]{1,0:T(8,128)(2,1)S(1)} %get-tuple-element.35.in0), channel_id=1, source_target_pairs={{0,16},{16,32},{32,48},{48,0},{1,17},{17,33},{33,49},{49,1},{2,18}... | collective-permute-start | bytes 786440 | tf_op jit(solution)/shard_map/ppermute | solution.py:30
  663.9 12.8 %collective-permute-start.8 = (bf16[128,1024]{1,0:T(8,128)(2,1)S(1)}, bf16[128,1024]{1,0:T(8,128)(2,1)S(1)}, u32[]{:S(2)}, u32[]{:S(2)}) collective-permute-start(bf16[128,1024]{1,0:T(8,128)(2,1)S(1)} %get-tuple-element.35.in0), channel_id=1, source_target_pairs={{0,48},{16,0},{32,16},{48,32},{1,49},{17,1},{33,17},{49,33},{2,50}... | collective-permute-start | bytes 786440 | tf_op jit(solution)/shard_map/ppermute | solution.py:30
  666.5 12.3 %collective-permute-start.9 = (bf16[128,1024]{1,0:T(8,128)(2,1)S(1)}, bf16[128,1024]{1,0:T(8,128)(2,1)S(1)}, u32[]{:S(2)}, u32[]{:S(2)}) collective-permute-start(bf16[128,1024]{1,0:T(8,128)(2,1)S(1)} %get-tuple-element.35.in0), channel_id=1, source_target_pairs={{0,32},{16,48},{32,0},{48,16},{1,33},{17,49},{33,1},{49,17},{2,34}... | collective-permute-start | bytes 786440 | tf_op jit(solution)/shard_map/ppermute | solution.py:30
  667.0 11.8 %copy-start.13 = (bf16[128,1024]{1,0:T(8,128)(2,1)}, bf16[128,1024]{1,0:T(8,128)(2,1)S(1)}, u32[]{:S(2)}) copy-start(bf16[128,1024]{1,0:T(8,128)(2,1)S(1)} %collective-permute-done.7.in1) | copy-start | bytes 786436
  676.6 4.3 copy-start.14
  678.8 5.3 copy-start.15
  689.8 7.2 copy-start.3
  692.4 77.5 %collective-permute-start.10 = (bf16[128,1024]{1,0:T(8,128)(2,1)}, bf16[128,1024]{1,0:T(8,128)(2,1)S(1)}, u32[]{:S(2)}, u32[]{:S(2)}) collective-permute-start(bf16[128,1024]{1,0:T(8,128)(2,1)} %fusion.29), channel_id=1, source_target_pairs={{0,32},{16,48},{32,0},{48,16},{1,33},{17,49},{33,1},{49,17},{2,34}... | collective-permute-start | bytes 786440 | tf_op jit(solution)/shard_map/ppermute | solution.py:30
  692.5 78.9 %collective-permute-start.11 = (bf16[128,1024]{1,0:T(8,128)(2,1)S(1)}, bf16[128,1024]{1,0:T(8,128)(2,1)S(1)}, u32[]{:S(2)}, u32[]{:S(2)}) collective-permute-start(bf16[128,1024]{1,0:T(8,128)(2,1)S(1)} %fusion.30), channel_id=1, source_target_pairs={{0,16},{16,32},{32,48},{48,0},{1,17},{17,33},{33,49},{49,1},{2,18}... | collective-permute-start | bytes 786440 | tf_op jit(solution)/shard_map/ppermute | solution.py:30
  697.0 75.0 %collective-permute-start.12 = (bf16[128,1024]{1,0:T(8,128)(2,1)S(1)}, bf16[128,1024]{1,0:T(8,128)(2,1)S(1)}, u32[]{:S(2)}, u32[]{:S(2)}) collective-permute-start(bf16[128,1024]{1,0:T(8,128)(2,1)S(1)} %fusion.31), channel_id=1, source_target_pairs={{0,48},{16,0},{32,16},{48,32},{1,49},{17,1},{33,17},{49,33},{2,50}... | collective-permute-start | bytes 786440 | tf_op jit(solution)/shard_map/ppermute | solution.py:30
  730.8 52.5 %collective-permute-start.24 = (bf16[128,1024]{1,0:T(8,128)(2,1)}, bf16[128,1024]{1,0:T(8,128)(2,1)S(1)}, u32[]{:S(2)}, u32[]{:S(2)}) collective-permute-start(bf16[128,1024]{1,0:T(8,128)(2,1)} %fusion.52), channel_id=1, source_target_pairs={{0,4},{1,5},{2,6},{3,7},{4,8},{5,9},{6,10},{7,11},{8,12},{9,13},{1... | collective-permute-start | bytes 786440 | tf_op jit(solution)/shard_map/ppermute | solution.py:37
  732.6 54.1 %collective-permute-start.25 = (bf16[128,1024]{1,0:T(8,128)(2,1)}, bf16[128,1024]{1,0:T(8,128)(2,1)S(1)}, u32[]{:S(2)}, u32[]{:S(2)}) collective-permute-start(bf16[128,1024]{1,0:T(8,128)(2,1)} %fusion.52), channel_id=1, source_target_pairs={{0,8},{1,9},{2,10},{3,11},{4,12},{5,13},{6,14},{7,15},{8,0},{9,1},... | collective-permute-start | bytes 786440 | tf_op jit(solution)/shard_map/ppermute | solution.py:37
  769.9 21.0 %collective-permute-start.26 = (bf16[128,1024]{1,0:T(8,128)(2,1)}, bf16[128,1024]{1,0:T(8,128)(2,1)S(1)}, u32[]{:S(2)}, u32[]{:S(2)}) collective-permute-start(bf16[128,1024]{1,0:T(8,128)(2,1)} %fusion.52), channel_id=1, source_target_pairs={{0,12},{1,13},{2,14},{3,15},{4,0},{5,1},{6,2},{7,3},{8,4},{9,5},{1... | collective-permute-start | bytes 786440 | tf_op jit(solution)/shard_map/ppermute | solution.py:37
  771.5 14.5 %collective-permute-start.21 = (bf16[128,1024]{1,0:T(8,128)(2,1)}, bf16[128,1024]{1,0:T(8,128)(2,1)S(1)}, u32[]{:S(2)}, u32[]{:S(2)}) collective-permute-start(bf16[128,1024]{1,0:T(8,128)(2,1)} %get-tuple-element.19), channel_id=1, source_target_pairs={{0,4},{1,5},{2,6},{3,7},{4,8},{5,9},{6,10},{7,11},{8,12},{9,13},{1... | collective-permute-start | bytes 786440 | tf_op jit(solution)/shard_map/ppermute | solution.py:37
  772.0 16.3 %collective-permute-start.22 = (bf16[128,1024]{1,0:T(8,128)(2,1)}, bf16[128,1024]{1,0:T(8,128)(2,1)S(1)}, u32[]{:S(2)}, u32[]{:S(2)}) collective-permute-start(bf16[128,1024]{1,0:T(8,128)(2,1)} %get-tuple-element.20), channel_id=1, source_target_pairs={{0,8},{1,9},{2,10},{3,11},{4,12},{5,13},{6,14},{7,15},{8,0},{9,1},... | collective-permute-start | bytes 786440 | tf_op jit(solution)/shard_map/ppermute | solution.py:37
  780.7 5.2 copy-start.25
  780.8 6.0 copy-start.23
  780.8 7.5 copy-start.22
  783.3 19.1 %copy-start.9 = (bf16[128,1024]{1,0:T(8,128)(2,1)S(1)}, bf16[128,1024]{1,0:T(8,128)(2,1)}, u32[]{:S(2)}) copy-start(bf16[128,1024]{1,0:T(8,128)(2,1)} %get-tuple-element.13) | copy-start | bytes 786436
  783.3 3.4 copy-start.16
  783.3 11.3 %collective-permute-start.3 = (bf16[128,1024]{1,0:T(8,128)(2,1)S(1)}, bf16[128,1024]{1,0:T(8,128)(2,1)S(1)}, u32[]{:S(2)}, u32[]{:S(2)}) collective-permute-start(bf16[128,1024]{1,0:T(8,128)(2,1)S(1)} %copy-done.24), channel_id=1, source_target_pairs={{0,4},{1,5},{2,6},{3,7},{4,8},{5,9},{6,10},{7,11},{8,12},{9,13},{1... | collective-permute-start | bytes 786440 | tf_op jit(solution)/shard_map/ppermute | solution.py:37
  786.0 8.8 %collective-permute-start.23 = (bf16[128,1024]{1,0:T(8,128)(2,1)S(1)}, bf16[128,1024]{1,0:T(8,128)(2,1)S(1)}, u32[]{:S(2)}, u32[]{:S(2)}) collective-permute-start(bf16[128,1024]{1,0:T(8,128)(2,1)S(1)} %copy-done.25), channel_id=1, source_target_pairs={{0,12},{1,13},{2,14},{3,15},{4,0},{5,1},{6,2},{7,3},{8,4},{9,5},{1... | collective-permute-start | bytes 786440 | tf_op jit(solution)/shard_map/ppermute | solution.py:37
  786.7 11.3 %collective-permute-start.4 = (bf16[128,1024]{1,0:T(8,128)(2,1)S(1)}, bf16[128,1024]{1,0:T(8,128)(2,1)S(1)}, u32[]{:S(2)}, u32[]{:S(2)}) collective-permute-start(bf16[128,1024]{1,0:T(8,128)(2,1)S(1)} %copy-done.23), channel_id=1, source_target_pairs={{0,8},{1,9},{2,10},{3,11},{4,12},{5,13},{6,14},{7,15},{8,0},{9,1},... | collective-permute-start | bytes 786440 | tf_op jit(solution)/shard_map/ppermute | solution.py:37
  788.3 12.8 %collective-permute-start.5 = (bf16[128,1024]{1,0:T(8,128)(2,1)S(1)}, bf16[128,1024]{1,0:T(8,128)(2,1)S(1)}, u32[]{:S(2)}, u32[]{:S(2)}) collective-permute-start(bf16[128,1024]{1,0:T(8,128)(2,1)S(1)} %copy-done.22), channel_id=1, source_target_pairs={{0,12},{1,13},{2,14},{3,15},{4,0},{5,1},{6,2},{7,3},{8,4},{9,5},{1... | collective-permute-start | bytes 786440 | tf_op jit(solution)/shard_map/ppermute | solution.py:37
  790.9 11.6 %collective-permute-start.32 = (bf16[128,1024]{1,0:T(8,128)(2,1)S(1)}, bf16[128,1024]{1,0:T(8,128)(2,1)S(1)}, u32[]{:S(2)}, u32[]{:S(2)}) collective-permute-start(bf16[128,1024]{1,0:T(8,128)(2,1)S(1)} %fusion.34), channel_id=1, source_target_pairs={{0,32},{16,48},{32,0},{48,16},{1,33},{17,49},{33,1},{49,17},{2,34}... | collective-permute-start | bytes 786440 | tf_op jit(solution)/shard_map/ppermute | solution.py:30
  794.7 7.9 collective-permute-start.33
  794.8 13.1 %collective-permute-start.34 = (bf16[128,1024]{1,0:T(8,128)(2,1)S(1)}, bf16[128,1024]{1,0:T(8,128)(2,1)S(1)}, u32[]{:S(2)}, u32[]{:S(2)}) collective-permute-start(bf16[128,1024]{1,0:T(8,128)(2,1)S(1)} %fusion.36), channel_id=1, source_target_pairs={{0,48},{16,0},{32,16},{48,32},{1,49},{17,1},{33,17},{49,33},{2,50}... | collective-permute-start | bytes 786440 | tf_op jit(solution)/shard_map/ppermute | solution.py:30
  798.0 28.4 %collective-permute-start.28 = (bf16[512,1024]{1,0:T(8,128)(2,1)S(1)}, bf16[512,1024]{1,0:T(8,128)(2,1)S(1)}, u32[]{:S(2)}, u32[]{:S(2)}) collective-permute-start(bf16[512,1024]{1,0:T(8,128)(2,1)S(1)} %pad_maximum_fusion.1), channel_id=1, source_target_pairs={{0,64},{1,65},{2,66},{3,67},{4,68},{5,69},{6,70},{7,71},{8,72},{9,... | collective-permute-start | bytes 3145736 | tf_op jit(solution)/shard_map/ppermute | solution.py:313
  801.0 25.3 %collective-permute-start.27 = (bf16[512,1024]{1,0:T(8,128)(2,1)S(1)}, bf16[512,1024]{1,0:T(8,128)(2,1)S(1)}, u32[]{:S(2)}, u32[]{:S(2)}) collective-permute-start(bf16[512,1024]{1,0:T(8,128)(2,1)S(1)} %constant_dynamic-update-slice_fusion.4), channel_id=1, source_target_pairs={{0,64},{1,65},{2,66},{3,67},{4,68},{5,69},{6,70},{7,71},{8,72},{9,... | collective-permute-start | bytes 3145736 | tf_op jit(solution)/shard_map/ppermute | solution.py:296
  802.5 10.3 %collective-permute-start.13 = (bf16[128,1024]{1,0:T(8,128)(2,1)S(1)}, bf16[128,1024]{1,0:T(8,128)(2,1)S(1)}, u32[]{:S(2)}, u32[]{:S(2)}) collective-permute-start(bf16[128,1024]{1,0:T(8,128)(2,1)S(1)} %get-tuple-element.22), channel_id=1, source_target_pairs={{0,4},{1,5},{2,6},{3,7},{4,8},{5,9},{6,10},{7,11},{8,12},{9,13},{1... | collective-permute-start | bytes 786440 | tf_op jit(solution)/shard_map/ppermute | solution.py:37
  802.6 13.0 %collective-permute-start.14 = (bf16[128,1024]{1,0:T(8,128)(2,1)S(1)}, bf16[128,1024]{1,0:T(8,128)(2,1)S(1)}, u32[]{:S(2)}, u32[]{:S(2)}) collective-permute-start(bf16[128,1024]{1,0:T(8,128)(2,1)S(1)} %get-tuple-element.22), channel_id=1, source_target_pairs={{0,8},{1,9},{2,10},{3,11},{4,12},{5,13},{6,14},{7,15},{8,0},{9,1},... | collective-permute-start | bytes 786440 | tf_op jit(solution)/shard_map/ppermute | solution.py:37
  807.8 8.8 %collective-permute-start.15 = (bf16[128,1024]{1,0:T(8,128)(2,1)S(1)}, bf16[128,1024]{1,0:T(8,128)(2,1)S(1)}, u32[]{:S(2)}, u32[]{:S(2)}) collective-permute-start(bf16[128,1024]{1,0:T(8,128)(2,1)S(1)} %get-tuple-element.22), channel_id=1, source_target_pairs={{0,12},{1,13},{2,14},{3,15},{4,0},{5,1},{6,2},{7,3},{8,4},{9,5},{1... | collective-permute-start | bytes 786440 | tf_op jit(solution)/shard_map/ppermute | solution.py:37
  812.8 7.6 collective-permute-start.35
  815.6 7.9 collective-permute-start.36
  816.7 8.1 collective-permute-start.37
  820.4 12.9 %collective-permute-start.16 = (bf16[512,1024]{1,0:T(8,128)(2,1)S(1)}, bf16[512,1024]{1,0:T(8,128)(2,1)S(1)}, u32[]{:S(2)}, u32[]{:S(2)}) collective-permute-start(bf16[512,1024]{1,0:T(8,128)(2,1)S(1)} %constant_dynamic-update-slice_fusion), channel_id=1, source_target_pairs={{64,0},{65,1},{66,2},{67,3},{68,4},{69,5},{70,6},{71,7},{72,8},{73... | collective-permute-start | bytes 3145736 | tf_op jit(solution)/shard_map/ppermute | solution.py:296
  823.5 9.8 %collective-permute-start.17 = (bf16[512,1024]{1,0:T(8,128)(2,1)S(1)}, bf16[512,1024]{1,0:T(8,128)(2,1)S(1)}, u32[]{:S(2)}, u32[]{:S(2)}) collective-permute-start(bf16[512,1024]{1,0:T(8,128)(2,1)S(1)} %pad_maximum_fusion), channel_id=1, source_target_pairs={{64,0},{65,1},{66,2},{67,3},{68,4},{69,5},{70,6},{71,7},{72,8},{73... | collective-permute-start | bytes 3145736 | tf_op jit(solution)/shard_map/ppermute | solution.py:313
  824.9 2.8 copy-start.17
  824.9 2.8 copy-start.19
  824.9 11.2 %collective-permute-start.38 = (bf16[512,1024]{1,0:T(8,128)(2,1)S(1)}, bf16[512,1024]{1,0:T(8,128)(2,1)S(1)}, u32[]{:S(2)}, u32[]{:S(2)}) collective-permute-start(bf16[512,1024]{1,0:T(8,128)(2,1)S(1)} %pad_maximum_fusion.2), channel_id=1, source_target_pairs={{0,64},{64,0},{1,65},{65,1},{2,66},{66,2},{3,67},{67,3},{4,68},{68... | collective-permute-start | bytes 3145736 | tf_op jit(solution)/shard_map/ppermute | solution.py:328
  831.2 12.9 %collective-permute-start.29 = (bf16[256,1024]{1,0:T(8,128)(2,1)S(1)}, bf16[256,1024]{1,0:T(8,128)(2,1)S(1)}, u32[]{:S(2)}, u32[]{:S(2)}) collective-permute-start(bf16[256,1024]{1,0:T(8,128)(2,1)S(1)} %get-tuple-element.27), channel_id=1, source_target_pairs={{64,65},{65,66},{66,67},{67,64},{68,69},{69,70},{70,71},{71,68},{7... | collective-permute-start | bytes 1572872 | tf_op jit(solution)/shard_map/ppermute | solution.py:54
  831.9 31.4 %collective-permute-start.30 = (bf16[256,1024]{1,0:T(8,128)(2,1)}, bf16[256,1024]{1,0:T(8,128)(2,1)}, u32[]{:S(2)}, u32[]{:S(2)}) collective-permute-start(bf16[256,1024]{1,0:T(8,128)(2,1)} %get-tuple-element.29), channel_id=1, source_target_pairs={{64,66},{65,67},{66,64},{67,65},{68,70},{69,71},{70,68},{71,69},{7... | collective-permute-start | bytes 1572872 | tf_op jit(solution)/shard_map/ppermute | solution.py:54
  836.0 6.8 copy-start.4
  837.2 9.1 %collective-permute-start.39 = (bf16[80,1024]{1,0:T(8,128)(2,1)S(1)}, bf16[80,1024]{1,0:T(8,128)(2,1)S(1)}, u32[]{:S(2)}, u32[]{:S(2)}) collective-permute-start(bf16[80,1024]{1,0:T(8,128)(2,1)S(1)} %get-tuple-element.32), channel_id=1, source_target_pairs={{0,1},{1,2},{2,3},{3,0},{4,5},{5,6},{6,7},{7,4},{8,9},{9,10},{10,1... | collective-permute-start | bytes 491528 | tf_op jit(solution)/shard_map/ppermute | solution.py:44
  838.7 14.5 %collective-permute-start.40 = (bf16[80,1024]{1,0:T(8,128)(2,1)S(1)}, bf16[80,1024]{1,0:T(8,128)(2,1)S(1)}, u32[]{:S(2)}, u32[]{:S(2)}) collective-permute-start(bf16[80,1024]{1,0:T(8,128)(2,1)S(1)} %get-tuple-element.34), channel_id=1, source_target_pairs={{0,2},{1,3},{2,0},{3,1},{4,6},{5,7},{6,4},{7,5},{8,10},{9,11},{10,... | collective-permute-start | bytes 491528 | tf_op jit(solution)/shard_map/ppermute | solution.py:44
  841.4 16.5 %collective-permute-start.41 = (bf16[80,1024]{1,0:T(8,128)(2,1)S(1)}, bf16[80,1024]{1,0:T(8,128)(2,1)S(1)}, u32[]{:S(2)}, u32[]{:S(2)}) collective-permute-start(bf16[80,1024]{1,0:T(8,128)(2,1)S(1)} %get-tuple-element.33), channel_id=1, source_target_pairs={{0,3},{1,0},{2,1},{3,2},{4,7},{5,4},{6,5},{7,6},{8,11},{9,8},{10,9... | collective-permute-start | bytes 491528 | tf_op jit(solution)/shard_map/ppermute | solution.py:44
  844.8 18.4 %collective-permute-start.31 = (bf16[256,1024]{1,0:T(8,128)(2,1)}, bf16[256,1024]{1,0:T(8,128)(2,1)}, u32[]{:S(2)}, u32[]{:S(2)}) collective-permute-start(bf16[256,1024]{1,0:T(8,128)(2,1)} %get-tuple-element.28), channel_id=1, source_target_pairs={{64,67},{65,64},{66,65},{67,66},{68,71},{69,68},{70,69},{71,70},{7... | collective-permute-start | bytes 1572872 | tf_op jit(solution)/shard_map/ppermute | solution.py:54
  846.3 16.9 %collective-permute-start.18 = (bf16[256,1024]{1,0:T(8,128)(2,1)}, bf16[256,1024]{1,0:T(8,128)(2,1)}, u32[]{:S(2)}, u32[]{:S(2)}) collective-permute-start(bf16[256,1024]{1,0:T(8,128)(2,1)} %get-tuple-element.24), channel_id=1, source_target_pairs={{0,1},{1,2},{2,3},{3,0},{4,5},{5,6},{6,7},{7,4},{8,9},{9,10},{10,1... | collective-permute-start | bytes 1572872 | tf_op jit(solution)/shard_map/ppermute | solution.py:54
  853.2 15.7 %collective-permute-start.19 = (bf16[256,1024]{1,0:T(8,128)(2,1)}, bf16[256,1024]{1,0:T(8,128)(2,1)}, u32[]{:S(2)}, u32[]{:S(2)}) collective-permute-start(bf16[256,1024]{1,0:T(8,128)(2,1)} %get-tuple-element.26), channel_id=1, source_target_pairs={{0,2},{1,3},{2,0},{3,1},{4,6},{5,7},{6,4},{7,5},{8,10},{9,11},{10,... | collective-permute-start | bytes 1572872 | tf_op jit(solution)/shard_map/ppermute | solution.py:54
  857.8 13.0 %collective-permute-start.20 = (bf16[256,1024]{1,0:T(8,128)(2,1)}, bf16[256,1024]{1,0:T(8,128)(2,1)}, u32[]{:S(2)}, u32[]{:S(2)}) collective-permute-start(bf16[256,1024]{1,0:T(8,128)(2,1)} %get-tuple-element.25), channel_id=1, source_target_pairs={{0,3},{1,0},{2,1},{3,2},{4,7},{5,4},{6,5},{7,6},{8,11},{9,8},{10,9... | collective-permute-start | bytes 1572872 | tf_op jit(solution)/shard_map/ppermute | solution.py:54
  (8 other events, 13.2 us)

commit v2 on v1

--- a/solution.py
+++ b/solution.py
@@ -54,35 +54,28 @@
     return lax.ppermute(block, ("segment", "dp"), pairs)
 
 
-def spread_kernel(routing, place, text, ups, out_text, out_ups, sems):
+def spread_kernel(routing, place, slots, out):
     core, replica = place[0], place[1]
-    copies = []
     for group in range(16):
         slot = jnp.int32(0)
         for j in range(MINE):
             q = routing[(core * 16 + group) * MINE + j]
             slot = jnp.where(lax.shift_right_logical(q, 3) == replica, q & 7, slot)
-        for n, (src, dst) in enumerate(((text, out_text), (ups, out_ups))):
-            copy = pltpu.make_async_copy(src.at[slot], dst.at[group], sems.at[n, group])
-            copy.start()
-            copies.append(copy)
-    for copy in copies:
-        copy.wait()
-
-
-def spread(routing, place, text, ups):
-    shape = jax.ShapeDtypeStruct((16,) + text.shape[1:], text.dtype)
+        out[group] = slots[slot]
+
+
+def spread(routing, place, slots):
+    shape = (16,) + slots.shape[1:]
     return pl.pallas_call(
         spread_kernel,
         grid_spec=pltpu.PrefetchScalarGridSpec(
             num_scalar_prefetch=2,
             grid=(1,),
-            in_specs=[ANY, ANY],
-            out_specs=[ANY, ANY],
-            scratch_shapes=[pltpu.SemaphoreType.DMA((2, 16))],
+            in_specs=[pl.BlockSpec(slots.shape, lambda i, *_: (0, 0, 0))],
+            out_specs=pl.BlockSpec(shape, lambda i, *_: (0, 0, 0)),
         ),
-        out_shape=[shape, shape],
-    )(routing, place, text, ups)
+        out_shape=jax.ShapeDtypeStruct(shape, slots.dtype),
+    )(routing, place, slots)
 
 
 def merge_kernel(source, counts, text, image, out):
@@ -127,115 +120,83 @@
     )(source, arrived).reshape(MINE * ROWS, columns)
 
 
-def turn_kernel(place, own, other, out, sems):
+def turn_kernel(place, own, other, *outs_and_sems):
+    outs, sems = outs_and_sems[:-1], outs_and_sems[-1]
     core, x = place[0], place[2]
-    size = out.shape[2]
-
-    def copy(source, section, d):
-        block = lax.rem(x - d + SIDE, SIDE)
+    size = outs[0].shape[0]
+
+    def copy(source, n):
+        block = lax.rem(x - n % SIDE + SIDE, SIDE)
         start = pl.multiple_of(block * size, size)
-        return pltpu.make_async_copy(
-            source.at[pl.ds(start, size)], out.at[section, d], sems.at[section, d]
-        )
-
-    for section in range(2):
-        for d in range(SIDE):
-
-            @pl.when(core == section)
-            def _():
-                copy(own, section, d).start()
-
-            @pl.when(core != section)
-            def _():
-                copy(other, section, d).start()
-
-    for section in range(2):
-        for d in range(SIDE):
-            copy(own, section, d).wait()
+        return pltpu.make_async_copy(source.at[pl.ds(start, size)], outs[n], sems.at[n])
+
+    for n in range(2 * SIDE):
+
+        @pl.when(core == n // SIDE)
+        def _():
+            copy(own, n).start()
+
+        @pl.when(core != n // SIDE)
+        def _():
+            copy(other, n).start()
+
+    for n in range(2 * SIDE):
+        copy(own, n).wait()
 
 
 def turn(place, own, other):
     rows, columns = own.shape
-    return pl.pallas_call(
+    blocks = pl.pallas_call(
         turn_kernel,
-        grid_spec=pltpu.PrefetchScalarGridSpec(
-            num_scalar_prefetch=1,
-            grid=(1,),
-            in_specs=[ANY, ANY],
-            out_specs=ANY,
-            scratch_shapes=[pltpu.SemaphoreType.DMA((2, SIDE))],
-        ),
-        out_shape=jax.ShapeDtypeStruct((2, SIDE, rows // SIDE, columns), own.dtype),
+        in_specs=[pl.BlockSpec(memory_space=pltpu.SMEM), ANY, ANY],
+        out_specs=[pl.BlockSpec(memory_space=pltpu.VMEM)] * (2 * SIDE),
+        scratch_shapes=[pltpu.SemaphoreType.DMA((2 * SIDE,))],
+        out_shape=[pltpu.VMEM((rows // SIDE, columns), own.dtype)] * (2 * SIDE),
+        compiler_params=pltpu.CompilerParams(vmem_limit_bytes=40 * 1024 * 1024),
     )(place, own, other)
-
-
-def order_kernel(place, in0, in1, in2, in3, out0, out1, out2, out3, sems):
+    return (blocks[:SIDE], blocks[SIDE:])
+
+
+def order_kernel(place, in0, in1, in2, in3, out0, out1, out2, out3):
     x, y, z = place[2], place[3], place[4]
     blocks = (in0, in1, in2, in3)
     outs = (out0, out1, out2, out3)
     part = in0.shape[1] // SIDE
-
-    def copy(d, e, j):
-        start = pl.multiple_of(lax.rem(y + j, SIDE) * part, part)
-        return pltpu.make_async_copy(
-            blocks[d].at[:, pl.ds(start, part)],
-            outs[e].at[:, pl.ds(j * part, part)],
-            sems.at[e, j],
-        )
-
     for e in range(SIDE):
         for d in range(SIDE):
 
             @pl.when(lax.rem(x - z - e + 2 * SIDE, SIDE) == d)
             def _():
                 for j in range(SIDE):
-                    copy(d, e, j).start()
-
-    for e in range(SIDE):
-        for j in range(SIDE):
-            copy(0, e, j).wait()
+                    start = pl.multiple_of(lax.rem(y + j, SIDE) * part, part)
+                    outs[e][:, pl.ds(j * part, part)] = blocks[d][:, pl.ds(start, part)]
 
 
 def order(place, blocks):
     shape = jax.ShapeDtypeStruct(blocks[0].shape, blocks[0].dtype)
+    whole = pl.BlockSpec(memory_space=pltpu.VMEM)
     return pl.pallas_call(
         order_kernel,
-        grid_spec=pltpu.PrefetchScalarGridSpec(
-            num_scalar_prefetch=1,
-            grid=(1,),
-            in_specs=[ANY] * 4,
-            out_specs=[ANY] * 4,
-            scratch_shapes=[pltpu.SemaphoreType.DMA((SIDE, SIDE))],
-        ),
-        out_shape=[shape] * 4,
+        in_specs=[pl.BlockSpec(memory_space=pltpu.SMEM)] + [whole] * SIDE,
+        out_specs=[whole] * SIDE,
+        out_shape=[shape] * SIDE,
     )(place, *blocks)
 
 
-def line_up_kernel(place, arrived, out, sems):
+def line_up_kernel(place, arrived, out):
     core, z = place[0], place[4]
-    copies = []
     for other in range(2):
         for e in range(SIDE):
             block = lax.rem(core + other, 2) * SIDE + lax.rem(z - e + SIDE, SIDE)
-            copy = pltpu.make_async_copy(
-                arrived.at[block], out.at[other * SIDE + e], sems.at[other, e]
-            )
-            copy.start()
-            copies.append(copy)
-    for copy in copies:
-        copy.wait()
+            out[other * SIDE + e] = arrived[block]
 
 
 def line_up(place, arrived):
+    whole = pl.BlockSpec(memory_space=pltpu.VMEM)
     return pl.pallas_call(
         line_up_kernel,
-        grid_spec=pltpu.PrefetchScalarGridSpec(
-            num_scalar_prefetch=1,
-            grid=(1,),
-            in_specs=[ANY],
-            out_specs=ANY,
-            scratch_shapes=[pltpu.SemaphoreType.DMA((2, SIDE))],
-        ),
+        in_specs=[pl.BlockSpec(memory_space=pltpu.SMEM), whole],
+        out_specs=whole,
         out_shape=jax.ShapeDtypeStruct(arrived.shape, arrived.dtype),
     )(place, arrived)
 
@@ -255,12 +216,7 @@
     columns = merger_weight.shape[1]
     merger = patches.shape[2]
 
-    send_text, send_ups = spread(
-        routing,
-        place,
-        text_embed.reshape(SLOTS, ROWS, columns),
-        upstream.reshape(SLOTS, ROWS, columns),
-    )
+    send_text = spread(routing, place, text_embed.reshape(SLOTS, ROWS, columns))
     arrived_text = lax.all_to_all(send_text, "dp", 0, 0, tiled=True)
     own_weight = llm_weight[0]
     other_weight = lax.ppermute(own_weight, "segment", [(0, 1), (1, 0)])
@@ -271,6 +227,7 @@
     embeds = dot(activated, merger_weight).astype(BF).reshape(MINE, ROWS, columns)
     weights = turn(place, own_weight, other_weight)
     hidden = merge(source, counts, arrived_text, embeds)
+    send_ups = spread(routing, place, upstream.reshape(SLOTS, ROWS, columns))
     arrived_ups = lax.all_to_all(send_ups, "dp", 0, 0, tiled=True)
 
     parts = activated.reshape(MINE * ROWS, 8, merger // 8).transpose(1, 0, 2)
@@ -286,9 +243,9 @@
     rows_of = []
     for section in range(2):
         blocks = [hidden] + [along_x(hidden, d) for d in (1, 2, 3)]
-        preact = dot(blocks[0], weights[section, 0])
+        preact = dot(blocks[0], weights[section][0])
         for d in (1, 3, 2):
-            preact = preact + dot(blocks[d], weights[section, d])
+            preact = preact + dot(blocks[d], weights[section][d])
         saved.append(preact)
         ordered = order(place, blocks)
         tokens = [ordered[0]] + [along_z(ordered[e], e) for e in (1, 2, 3)]
@@ -303,9 +260,9 @@
     for section in (1, 0):
         local = gelu_back(saved[section], cotangent.astype(F32)).astype(BF)
         terms = [
-            along_x(dot_nt(local, weights[section, SIDE - d]).astype(BF), d) for d in (2, 1, 3)
+            along_x(dot_nt(local, weights[section][SIDE - d]).astype(BF), d) for d in (2, 1, 3)
         ]
-        terms.append(dot_nt(local, weights[section, 0]).astype(BF))
+        terms.append(dot_nt(local, weights[section][0]).astype(BF))
         inner = sum(term.astype(F32) for term in terms)
         cotangent = (cotangent.astype(F32) + inner).astype(BF)
         locals_here = [local] + [along_z(local, e) for e in (1, 2, 3)]

time: 879 us -> 242 us (0.28)
  Pallas kernels: 676 us -> 26.5 us
  waiting for transfers between devices: 37.5 us -> 71.9 us
  matrix products: 50.5 us -> 33.7 us
  starting transfers between devices: 91.5 us -> 74.7 us
  local copies, waits for them, and re-layouts: 10.6 us -> 24.5 us
    pallas_call x4, Pallas kernels: 603 us -> 13.6 us  [the longest x1 6.6 us: turn(): pl.pallas_call(turn_kernel, in_specs=[pl.BlockSpec(memory_space=pltpu.SME...]
    pallas_call x1 -> x2, Pallas kernels: 65.6 us -> 5.56 us  [spread(): pl.pallas_call(spread_kernel, grid_spec=pltpu.PrefetchScalarGridSpec(num_...]
    ppermute x15, waiting for transfers between devices: 10.2 us -> 28.2 us  [along_z(): return lax.ppermute(block, 'dp', pairs)]
    unnamed x60 -> x90, local copies, waits for them, and re-layouts: 3.62 us -> 16 us
    ppermute x3, waiting for transfers between devices: 0.01 us -> 10.4 us  [along_y(): return lax.ppermute(block, 'dp', pairs)]
    dot_general x8, matrix products: 21 us -> 11.1 us  [dot_nt(): lax.dot_general(a, b, (((1,), (1,)), ((), ())), preferred_element_type=F32)]
  transfers between devices with their start and end apart: 45 -> 45, of which waited for: 10 -> 13; matrix products, arithmetic and copies ran while one was open for 6% -> 17% of each run, Pallas kernels for 77% -> 11%
where the time goes in v2:
time: 242 us; the launch traced here: 241 us
  starting transfers between devices  74.7 us (31%)
  waiting for transfers between devices  71.9 us (30%)
  matrix products  33.7 us (14%)
  Pallas kernels  26.5 us (11%)
  local copies, waits for them, and re-layouts  24.5 us (10%)
  other arithmetic  7.9 us (3%)
    ppermute x15, waiting for transfers between devices, along_z(): return lax.ppermute(block, 'dp', pairs)  28.2 us
    ppermute x12, starting transfers between devices, along_x(): lax.ppermute(block, 'mp', [(i, (i + distance) % SIDE) for i in range(SIDE)])  19 us
    ppermute x15, starting transfers between devices, along_z(): return lax.ppermute(block, 'dp', pairs)  16.5 us
    unnamed x90, local copies, waits for them, and re-layouts  16 us
    dot_general x9, matrix products, dot(): return jnp.dot(a, b, preferred_element_type=F32)  15.1 us
    ppermute x6, starting transfers between devices, along_y_of(): return lax.ppermute(block, ('segment', 'dp'), pairs)  12.6 us
    all_to_all x1, waiting for transfers between devices, on_device(): arrived_text = lax.all_to_all(send_text, 'dp', 0, 0, tiled=True)  12.1 us
    dot_general x8, matrix products, dot_nt(): lax.dot_general(a, b, (((1,), (1,)), ((), ())), preferred_element_type=F32)  11.1 us
  transfers between devices with their start and end apart: 45, of which 13 were waited for; matrix products, arithmetic and copies ran while one was open for 17% of the time, Pallas kernels for 11%

profile of v2, /device:TPU:0, one launch (start us, length us, event | category | flops | bytes accessed | tf_op | source)
XLA Modules:
  0.0 240.7 jit_solution(15610069270492032538)
XLA Ops:
  1.3 2.8 %shard_map.86 = bf16[16,32,1024]{2,1,0:T(8,128)(2,1)} custom-call(s32[128]{0:T(128)} %routing.3, s32[5]{0:T(128)} %stack.23.place, bf16[8,32,1024]{2,1,0:T(8,128)(2,1)} %bitcast.87), custom_call_target="tpu_custom_call" | custom-call | tf_op jit(solution)/shard_map/pallas_call | solution.py:69
  4.1 8.1 %all-to-all-start = ((bf16[16,32,1024]{2,1,0:T(8,128)(2,1)}), bf16[16,32,1024]{2,1,0:T(8,128)(2,1)S(1)}, u32[]{:S(2)}, u32[]{:S(2)}) async-start(bf16[16,32,1024]{2,1,0:T(8,128)(2,1)} %shard_map.86), calls=%async_computation | async-start | bytes 2097152 | tf_op jit(solution)/shard_map/all_to_all | solution.py:220
  14.7 4.1 %convolution_convert_fusion = bf16[128,1024]{1,0:T(8,128)(2,1)} fusion(bf16[128,2560]{1,0:T(8,128)(2,1)S(1)} %bitcast.76, bf16[2560,1024]{1,0:T(8,128)(2,1)} %param.8), kind=kOutput, calls=%fused_computation.20 | convolution fusion | flops 671219712 | bytes 6160384 | tf_op jit(solution)/shard_map/dot_general | solution.py:18
  18.7 12.1 %all-to-all-done.text = bf16[16,32,1024]{2,1,0:T(8,128)(2,1)S(1)} async-done(((bf16[16,32,1024]{2,1,0:T(8,128)(2,1)}), bf16[16,32,1024]{2,1,0:T(8,128)(2,1)S(1)}, u32[]{:S(2)}, u32[]{:S(2)}) %all-to-all-start) | async-done | bytes 1048608 | tf_op jit(solution)/shard_map/all_to_all | solution.py:220
  30.8 3.5 %all-to-all-start.2 = ((bf16[8,128,320]{1,2,0:T(8,128)(2,1)}), bf16[8,128,320]{1,2,0:T(8,128)(2,1)S(1)}, u32[]{:S(2)}, u32[]{:S(2)}) async-start(bf16[8,128,320]{1,2,0:T(8,128)(2,1)} %copy.10), calls=%async_computation.2 | async-start | bytes 1310720 | tf_op jit(solution)/shard_map/all_to_all | solution.py:237
  35.6 3.7 %shard_map.87 = bf16[4,32,1024]{2,1,0:T(8,128)(2,1)} custom-call(s32[4]{0:T(128)} %and_select_fusion.1.source, s32[4]{0:T(128)} %dynamic_slice.20.counts, bf16[16,32,1024]{2,1,0:T(8,128)(2,1)} %copy-done.17, bf16[4,32,1024]{2,1,0:T(8,128)(2,1)} %bitcast.84), custom_call_target="tpu_custom_call" | custom-call | tf_op jit(solution)/shard_map/pallas_call | solution.py:89
  39.4 1.5 collective-permute-start
  40.8 2.8 %shard_map.89 = bf16[16,32,1024]{2,1,0:T(8,128)(2,1)} custom-call(s32[128]{0:T(128)} %routing.3, s32[5]{0:T(128)} %stack.23.place, bf16[8,32,1024]{2,1,0:T(8,128)(2,1)} %bitcast.88), custom_call_target="tpu_custom_call" | custom-call | tf_op jit(solution)/shard_map/pallas_call | solution.py:69
  43.6 1.7 collective-permute-start.2
  45.4 1.8 collective-permute-start.1
  47.2 6.6 %shard_map.91 = (bf16[1024,1024]{1,0:T(8,128)(2,1)S(1)}, bf16[1024,1024]{1,0:T(8,128)(2,1)S(1)}, bf16[1024,1024]{1,0:T(8,128)(2,1)S(1)}, bf16[1024,1024]{1,0:T(8...) custom-call(s32[5]{0:T(128)} %stack.23.place, ...), custom_call_target="tpu_custom_call" | custom-call | tf_op jit(solution)/shard_map/pallas_call | solution.py:149
  53.8 1.3 copy-done
  59.1 1.4 copy-done.9
  61.8 1.4 copy-done.14
  65.3 4.8 %all-to-all-start.1 = ((bf16[16,32,1024]{2,1,0:T(8,128)(2,1)}), bf16[16,32,1024]{2,1,0:T(8,128)(2,1)S(1)}, u32[]{:S(2)}, u32[]{:S(2)}) async-start(bf16[16,32,1024]{2,1,0:T(8,128)(2,1)} %shard_map.89), calls=%async_computation.1 | async-start | bytes 2097152 | tf_op jit(solution)/shard_map/all_to_all | solution.py:231
  70.9 2.0 fusion.44
  73.0 1.5 fusion.45
  74.7 1.5 add_convert_fusion.2
  77.0 2.3 copy.11.arrived
  79.2 2.1 shard_map.93
  81.4 5.7 %all-to-all-done.1.arrived = bf16[16,32,1024]{2,1,0:T(8,128)(2,1)S(1)} async-done(((bf16[16,32,1024]{2,1,0:T(8,128)(2,1)}), bf16[16,32,1024]{2,1,0:T(8,128)(2,1)S(1)}, u32[]{:S(2)}, u32[]{:S(2)}) %all-to-all-start.1) | async-done | bytes 1048608 | tf_op jit(solution)/shard_map/all_to_all | solution.py:231
  88.1 3.6 %shard_map.90 = bf16[4,32,1024]{2,1,0:T(8,128)(2,1)} custom-call(s32[4]{0:T(128)} %and_select_fusion.1.source, bf16[16,32,1024]{2,1,0:T(8,128)(2,1)} %copy-done.16), custom_call_target="tpu_custom_call" | custom-call | tf_op jit(solution)/shard_map/pallas_call | solution.py:111
  92.9 1.5 collective-permute-start.9
  94.4 2.1 fusion.46
  96.5 3.9 %collective-permute-done.8.in3 = bf16[128,1024]{1,0:T(8,128)(2,1)S(1)} collective-permute-done((bf16[128,1024]{1,0:T(8,128)(2,1)}, bf16[128,1024]{1,0:T(8,128)(2,1)S(1)}, u32[]{:S(2)}, u32[]{:S(2)}) %collective-permute-start.8) | collective-permute-done | bytes 262176 | tf_op jit(solution)/shard_map/ppermute | solution.py:30
  102.6 1.7 fusion.26
  104.4 1.6 convolution_convert_fusion.8
  105.9 1.6 convolution_convert_fusion.7
  107.5 1.6 convolution_convert_fusion.6
  109.1 1.7 collective-permute-start.10
  110.8 3.2 %collective-permute-start.11 = (bf16[128,1024]{1,0:T(8,128)(2,1)}, bf16[128,1024]{1,0:T(8,128)(2,1)}, u32[]{:S(2)}, u32[]{:S(2)}) collective-permute-start(bf16[128,1024]{1,0:T(8,128)(2,1)} %convolution_convert_fusion.7), channel_id=1, source_target_pairs={{0,16},{16,32},{32,48},{48,0},{1,17},{17,33},{33,49},{49,1},{2,18}... | collective-permute-start | bytes 786440 | tf_op jit(solution)/shard_map/ppermute | solution.py:30
  115.0 2.4 %shard_map.88 = (bf16[128,1024]{1,0:T(8,128)(2,1)}, bf16[128,1024]{1,0:T(8,128)(2,1)}, bf16[128,1024]{1,0:T(8,128)(2,1)}, bf16[128,1024]{1,0:T(8,128)(2,1)}) custom-call(s32[5]{0:T(128)} %stack.23.place, bf16[128,1024]{1,0:T(8,128)(2,1)} %bitcast.80, bf16[128,1024]{1,0:T(8,128)(2,1)} %copy-done.23, bf16[128,1024]{1,0:T(8,128)(2,1)} %collective-permute-done.1.in2, ...), custom_call_target="tpu_custom_call" | custom-call | tf_op jit(solution)/shard_map/pallas_call | solution.py:178
  117.6 2.7 %collective-permute-start.25 = (bf16[128,1024]{1,0:T(8,128)(2,1)S(1)}, bf16[128,1024]{1,0:T(8,128)(2,1)}, u32[]{:S(2)}, u32[]{:S(2)}) collective-permute-start(bf16[128,1024]{1,0:T(8,128)(2,1)S(1)} %fusion.26), channel_id=1, source_target_pairs={{0,8},{1,9},{2,10},{3,11},{4,12},{5,13},{6,14},{7,15},{8,0},{9,1},... | collective-permute-start | bytes 786440 | tf_op jit(solution)/shard_map/ppermute | solution.py:37
  120.3 2.4 %shard_map.92 = (bf16[128,1024]{1,0:T(8,128)(2,1)}, bf16[128,1024]{1,0:T(8,128)(2,1)}, bf16[128,1024]{1,0:T(8,128)(2,1)}, bf16[128,1024]{1,0:T(8,128)(2,1)}) custom-call(s32[5]{0:T(128)} %stack.23.place, bf16[128,1024]{1,0:T(8,128)(2,1)} %get-tuple-element.47.in0, bf16[128,1024]{1,0:T(8,128)(2,1)} %copy-done.25, bf16[128,1024]{1,0:T(8,128)(2,1)} %copy-done.27, ...), custom_call_target="tpu_custom_call" | custom-call | tf_op jit(solution)/shard_map/pallas_call | solution.py:178
  123.7 1.5 collective-permute-start.26
  125.8 1.4 collective-permute-start.22
  127.2 3.0 %fusion.19 = (bf16[128,1024]{1,0:T(8,128)(2,1)S(1)}, bf16[128,1024]{1,0:T(8,128)(2,1)S(1)}) fusion(f32[128,1024]{1,0:T(8,128)S(1)} %copy-done.29, bf16[128,1024]{1,0:T(8,128)(2,1)} %collective-permute-done.12, bf16[128,1024]{1,0:T(8,128)(2,1)} %collective-permute-done.11, bf16[128,1024]{1,0:T(8,128)(2,1)} %collective-permute-done.10, ...), kind=kOutput, calls=%fused_computation.51 | convolution fusion | flops 272629760 | bytes 4456448 | tf_op jit(solution)/shard_map/dot_general | solution.py:22
  133.6 2.2 collective-permute-start.3
  135.8 5.8 %collective-permute-done.21 = bf16[128,1024]{1,0:T(8,128)(2,1)S(1)} collective-permute-done((bf16[128,1024]{1,0:T(8,128)(2,1)}, bf16[128,1024]{1,0:T(8,128)(2,1)S(1)}, u32[]{:S(2)}, u32[]{:S(2)}) %collective-permute-start.21) | collective-permute-done | bytes 262176 | tf_op jit(solution)/shard_map/ppermute | solution.py:37
  142.4 2.1 collective-permute-done.22
  144.5 1.9 collective-permute-start.5
  146.4 1.9 collective-permute-start.32
  149.4 2.1 collective-permute-done.3
  152.5 2.7 %collective-permute-start.34 = (bf16[128,1024]{1,0:T(8,128)(2,1)S(1)}, bf16[128,1024]{1,0:T(8,128)(2,1)S(1)}, u32[]{:S(2)}, u32[]{:S(2)}) collective-permute-start(bf16[128,1024]{1,0:T(8,128)(2,1)S(1)} %convolution_convert_fusion.2), channel_id=1, source_target_pairs={{0,48},{16,0},{32,16},{48,32},{1,49},{17,1},{33,17},{49,33},{2,50}... | collective-permute-start | bytes 786440 | tf_op jit(solution)/shard_map/ppermute | solution.py:30
  155.3 1.4 collective-permute-start.28
  156.7 1.4 collective-permute-start.27
  159.7 1.8 collective-permute-start.15
  162.4 11.2 %collective-permute-done.13 = bf16[128,1024]{1,0:T(8,128)(2,1)S(1)} collective-permute-done((bf16[128,1024]{1,0:T(8,128)(2,1)S(1)}, bf16[128,1024]{1,0:T(8,128)(2,1)S(1)}, u32[]{:S(2)}, u32[]{:S(2)}) %collective-permute-start.13) | collective-permute-done | bytes 262176 | tf_op jit(solution)/shard_map/ppermute | solution.py:37
  174.8 2.4 collective-permute-start.37
  177.3 6.6 %collective-permute-done.35 = bf16[128,1024]{1,0:T(8,128)(2,1)S(1)} collective-permute-done((bf16[128,1024]{1,0:T(8,128)(2,1)S(1)}, bf16[128,1024]{1,0:T(8,128)(2,1)S(1)}, u32[]{:S(2)}, u32[]{:S(2)}) %collective-permute-start.35) | collective-permute-done | bytes 262176 | tf_op jit(solution)/shard_map/ppermute | solution.py:37
  186.7 1.3 collective-permute-start.38
  189.3 2.4 %add_convert_fusion = bf16[1024,1024]{1,0:T(8,128)(2,1)S(1)} fusion(f32[1024,1024]{1,0:T(8,128)S(1)} %fusion.50, bf16[512,1024]{1,0:T(8,128)(2,1)S(1)} %constant_dynamic-update-slice_fusion.4, bf16[128,1024]{1,0:T(8,128)(2,1)S(1)} %collective-permute-done.26, bf16[128,1024]{1,0:T(8,128)(2,1)} %collective-permute-done.25, ...), kind=kOutput, calls=%fused_computation | convolution fusion | flops 1080033280 | bytes 8388608 | tf_op jit(solution)/shard_map/dot_general | solution.py:26
  193.3 1.5 collective-permute-start.30
  196.1 1.4 add_convert_fusion.1
  199.5 2.3 collective-permute-start.40
  204.0 1.4 collective-permute-start.31
  205.4 10.4 %collective-permute-done.39 = bf16[80,1024]{1,0:T(8,128)(2,1)S(1)} collective-permute-done((bf16[80,1024]{1,0:T(8,128)(2,1)S(1)}, bf16[80,1024]{1,0:T(8,128)(2,1)S(1)}, u32[]{:S(2)}, u32[]{:S(2)}) %collective-permute-start.39) | collective-permute-done | bytes 163872 | tf_op jit(solution)/shard_map/ppermute | solution.py:44
  215.8 1.9 collective-permute-start.18
  217.7 1.9 collective-permute-start.19
  219.7 5.1 %collective-permute-start.20 = (bf16[256,1024]{1,0:T(8,128)(2,1)}, bf16[256,1024]{1,0:T(8,128)(2,1)}, u32[]{:S(2)}, u32[]{:S(2)}) collective-permute-start(bf16[256,1024]{1,0:T(8,128)(2,1)} %get-tuple-element.37), channel_id=1, source_target_pairs={{0,3},{1,0},{2,1},{3,2},{4,7},{5,4},{6,5},{7,6},{8,11},{9,8},{10,9... | collective-permute-start | bytes 1572872 | tf_op jit(solution)/shard_map/ppermute | solution.py:54
  224.9 1.8 fusion.36
  226.7 7.4 %collective-permute-done.18 = bf16[256,1024]{1,0:T(8,128)(2,1)} collective-permute-done((bf16[256,1024]{1,0:T(8,128)(2,1)}, bf16[256,1024]{1,0:T(8,128)(2,1)}, u32[]{:S(2)}, u32[]{:S(2)}) %collective-permute-start.18) | collective-permute-done | bytes 524320 | tf_op jit(solution)/shard_map/ppermute | solution.py:54
  234.0 2.8 %collective-permute-done.20 = bf16[256,1024]{1,0:T(8,128)(2,1)} collective-permute-done((bf16[256,1024]{1,0:T(8,128)(2,1)}, bf16[256,1024]{1,0:T(8,128)(2,1)}, u32[]{:S(2)}, u32[]{:S(2)}) %collective-permute-start.20) | collective-permute-done | bytes 524320 | tf_op jit(solution)/shard_map/ppermute | solution.py:54
  236.9 3.8 %select_bitcast_fusion = f32[1,256,1024]{2,1,0:T(8,128)} fusion(bf16[256,1024]{1,0:T(8,128)(2,1)} %collective-permute-done.31, bf16[256,1024]{1,0:T(8,128)(2,1)} %collective-permute-done.30, bf16[256,1024]{1,0:T(8,128)(2,1)} %copy-done.30, bf16[256,1024]{1,0:T(8,128)(2,1)} %collective-permute-done.20, bf16[256,1024]{1,0:T(8,128)(2,1)} %collective-permute-done.19, ...), kind=kLoop, calls=%fused_computation.34 | loop fusion | flops 3932160 | bytes 5242881 | tf_op jit(solution)/shard_map/broadcast_in_dim | solution.py:278
  (168 shorter events, 41.3 us)
Async XLA Ops:
  0.6 11.7 %copy-start.28 = (bf16[4,32,2560]{2,1,0:T(8,128)(2,1)S(1)}, bf16[4,32,2560]{2,1,0:T(8,128)(2,1)}, u32[]{:S(2)}) copy-start(bf16[4,32,2560]{2,1,0:T(8,128)(2,1)} %param.7) | copy-start | bytes 1966084
  0.6 46.6 %collective-permute-start.6 = (bf16[4096,1024]{1,0:T(8,128)(2,1)}, bf16[4096,1024]{1,0:T(8,128)(2,1)}, u32[]{:S(2)}, u32[]{:S(2)}) collective-permute-start(bf16[4096,1024]{1,0:T(8,128)(2,1)} %bitcast.74), channel_id=1, source_target_pairs={{0,64},{64,0},{1,65},{65,1},{2,66},{66,2},{3,67},{67,3},{4,68},{68... | collective-permute-start | bytes 25165832 | tf_op jit(solution)/shard_map/ppermute | solution.py:222
  4.1 26.7 %all-to-all-start = ((bf16[16,32,1024]{2,1,0:T(8,128)(2,1)}), bf16[16,32,1024]{2,1,0:T(8,128)(2,1)S(1)}, u32[]{:S(2)}, u32[]{:S(2)}) async-start(bf16[16,32,1024]{2,1,0:T(8,128)(2,1)} %shard_map.86), calls=%async_computation | async-start | bytes 2097152 | tf_op jit(solution)/shard_map/all_to_all | solution.py:220
  14.7 19.7 %copy-start.35 = (s32[128]{0:T(128)S(1)}, s32[128]{0:T(128)}, u32[]{:S(2)}) copy-start(s32[128]{0:T(128)} %routing.3) | copy-start | bytes 1540
  14.7 20.3 %copy-start.41 = (s32[128]{0:T(128)S(1)}, s32[128]{0:T(128)}, u32[]{:S(2)}) copy-start(s32[128]{0:T(128)} %param.9) | copy-start | bytes 1540
  30.8 4.8 %copy-start.17 = (bf16[16,32,1024]{2,1,0:T(8,128)(2,1)}, bf16[16,32,1024]{2,1,0:T(8,128)(2,1)S(1)}, u32[]{:S(2)}) copy-start(bf16[16,32,1024]{2,1,0:T(8,128)(2,1)S(1)} %all-to-all-done.text) | copy-start | bytes 3145732
  30.8 33.7 %all-to-all-start.2 = ((bf16[8,128,320]{1,2,0:T(8,128)(2,1)}), bf16[8,128,320]{1,2,0:T(8,128)(2,1)S(1)}, u32[]{:S(2)}, u32[]{:S(2)}) async-start(bf16[8,128,320]{1,2,0:T(8,128)(2,1)} %copy.10), calls=%async_computation.2 | async-start | bytes 1310720 | tf_op jit(solution)/shard_map/all_to_all | solution.py:237
  39.4 23.9 %collective-permute-start = (bf16[128,1024]{1,0:T(8,128)(2,1)}, bf16[128,1024]{1,0:T(8,128)(2,1)S(1)}, u32[]{:S(2)}, u32[]{:S(2)}) collective-permute-start(bf16[128,1024]{1,0:T(8,128)(2,1)} %bitcast.77), channel_id=1, source_target_pairs={{0,16},{16,32},{32,48},{48,0},{1,17},{17,33},{33,49},{49,1},{2,18}... | collective-permute-start | bytes 786440 | tf_op jit(solution)/shard_map/ppermute | solution.py:30
  43.6 26.5 %collective-permute-start.2 = (bf16[128,1024]{1,0:T(8,128)(2,1)}, bf16[128,1024]{1,0:T(8,128)(2,1)S(1)}, u32[]{:S(2)}, u32[]{:S(2)}) collective-permute-start(bf16[128,1024]{1,0:T(8,128)(2,1)} %bitcast.78), channel_id=1, source_target_pairs={{0,48},{16,0},{32,16},{48,32},{1,49},{17,1},{33,17},{49,33},{2,50}... | collective-permute-start | bytes 786440 | tf_op jit(solution)/shard_map/ppermute | solution.py:30
  45.4 27.6 %collective-permute-start.1 = (bf16[128,1024]{1,0:T(8,128)(2,1)}, bf16[128,1024]{1,0:T(8,128)(2,1)}, u32[]{:S(2)}, u32[]{:S(2)}) collective-permute-start(bf16[128,1024]{1,0:T(8,128)(2,1)} %bitcast.79), channel_id=1, source_target_pairs={{0,32},{16,48},{32,0},{48,16},{1,33},{17,49},{33,1},{49,17},{2,34}... | collective-permute-start | bytes 786440 | tf_op jit(solution)/shard_map/ppermute | solution.py:30
  65.3 21.8 %all-to-all-start.1 = ((bf16[16,32,1024]{2,1,0:T(8,128)(2,1)}), bf16[16,32,1024]{2,1,0:T(8,128)(2,1)S(1)}, u32[]{:S(2)}, u32[]{:S(2)}) async-start(bf16[16,32,1024]{2,1,0:T(8,128)(2,1)} %shard_map.89), calls=%async_computation.1 | async-start | bytes 2097152 | tf_op jit(solution)/shard_map/all_to_all | solution.py:231
  70.1 2.8 %copy-start.3 = (bf16[1024,1024]{1,0:T(8,128)(2,1)S(1)}, bf16[1024,1024]{1,0:T(8,128)(2,1)}, u32[]{:S(2)}) copy-start(bf16[1024,1024]{1,0:T(8,128)(2,1)} %copy-done.2) | copy-start | bytes 6291460
  76.2 18.1 %collective-permute-start.7 = (bf16[128,1024]{1,0:T(8,128)(2,1)}, bf16[128,1024]{1,0:T(8,128)(2,1)S(1)}, u32[]{:S(2)}, u32[]{:S(2)}) collective-permute-start(bf16[128,1024]{1,0:T(8,128)(2,1)} %get-tuple-element.47.in0), channel_id=1, source_target_pairs={{0,16},{16,32},{32,48},{48,0},{1,17},{17,33},{33,49},{49,1},{2,18}... | collective-permute-start | bytes 786440 | tf_op jit(solution)/shard_map/ppermute | solution.py:30
  91.7 8.8 %copy-start.8 = (bf16[1024,1024]{1,0:T(8,128)(2,1)S(1)}, bf16[1024,1024]{1,0:T(8,128)(2,1)}, u32[]{:S(2)}) copy-start(bf16[1024,1024]{1,0:T(8,128)(2,1)} %copy-done.7) | copy-start | bytes 6291460
  91.7 8.8 %collective-permute-start.8 = (bf16[128,1024]{1,0:T(8,128)(2,1)}, bf16[128,1024]{1,0:T(8,128)(2,1)S(1)}, u32[]{:S(2)}, u32[]{:S(2)}) collective-permute-start(bf16[128,1024]{1,0:T(8,128)(2,1)} %get-tuple-element.47.in0), channel_id=1, source_target_pairs={{0,48},{16,0},{32,16},{48,32},{1,49},{17,1},{33,17},{49,33},{2,50}... | collective-permute-start | bytes 786440 | tf_op jit(solution)/shard_map/ppermute | solution.py:30
  92.9 8.1 %collective-permute-start.9 = (bf16[128,1024]{1,0:T(8,128)(2,1)}, bf16[128,1024]{1,0:T(8,128)(2,1)S(1)}, u32[]{:S(2)}, u32[]{:S(2)}) collective-permute-start(bf16[128,1024]{1,0:T(8,128)(2,1)} %get-tuple-element.47.in0), channel_id=1, source_target_pairs={{0,32},{16,48},{32,0},{48,16},{1,33},{17,49},{33,1},{49,17},{2,34}... | collective-permute-start | bytes 786440 | tf_op jit(solution)/shard_map/ppermute | solution.py:30
  94.4 6.6 %copy-start.25 = (bf16[128,1024]{1,0:T(8,128)(2,1)}, bf16[128,1024]{1,0:T(8,128)(2,1)S(1)}, u32[]{:S(2)}) copy-start(bf16[128,1024]{1,0:T(8,128)(2,1)S(1)} %collective-permute-done.7.in1) | copy-start | bytes 786436
  96.5 4.5 %copy-start.10 = (bf16[1024,1024]{1,0:T(8,128)(2,1)S(1)}, bf16[1024,1024]{1,0:T(8,128)(2,1)}, u32[]{:S(2)}) copy-start(bf16[1024,1024]{1,0:T(8,128)(2,1)} %copy-done.9) | copy-start | bytes 6291460
  104.4 3.1 %copy-start.6 = (bf16[1024,1024]{1,0:T(8,128)(2,1)S(1)}, bf16[1024,1024]{1,0:T(8,128)(2,1)}, u32[]{:S(2)}) copy-start(bf16[1024,1024]{1,0:T(8,128)(2,1)} %copy-done.5) | copy-start | bytes 6291460
  105.9 8.3 %copy-start.19 = (bf16[8,128,320]{2,1,0:T(8,128)(2,1)S(1)}, bf16[8,128,320]{2,1,0:T(8,128)(2,1)}, u32[]{:S(2)}) copy-start(bf16[8,128,320]{2,1,0:T(8,128)(2,1)} %shard_map.93) | copy-start | bytes 1966084
  109.1 18.2 %copy-start.29 = (f32[128,1024]{1,0:T(8,128)S(1)}, f32[128,1024]{1,0:T(8,128)}, u32[]{:S(2)}) copy-start(f32[128,1024]{1,0:T(8,128)} %get-tuple-element.48) | copy-start | bytes 1572868
  109.1 18.2 %copy-start.33 = (bf16[4,32,1024]{2,1,0:T(8,128)(2,1)S(1)}, bf16[4,32,1024]{2,1,0:T(8,128)(2,1)}, u32[]{:S(2)}) copy-start(bf16[4,32,1024]{2,1,0:T(8,128)(2,1)} %shard_map.90) | copy-start | bytes 786436
  109.1 14.6 %collective-permute-start.10 = (bf16[128,1024]{1,0:T(8,128)(2,1)}, bf16[128,1024]{1,0:T(8,128)(2,1)}, u32[]{:S(2)}, u32[]{:S(2)}) collective-permute-start(bf16[128,1024]{1,0:T(8,128)(2,1)} %convolution_convert_fusion.8), channel_id=1, source_target_pairs={{0,32},{16,48},{32,0},{48,16},{1,33},{17,49},{33,1},{49,17},{2,34}... | collective-permute-start | bytes 786440 | tf_op jit(solution)/shard_map/ppermute | solution.py:30
  110.8 14.4 %collective-permute-start.11 = (bf16[128,1024]{1,0:T(8,128)(2,1)}, bf16[128,1024]{1,0:T(8,128)(2,1)}, u32[]{:S(2)}, u32[]{:S(2)}) collective-permute-start(bf16[128,1024]{1,0:T(8,128)(2,1)} %convolution_convert_fusion.7), channel_id=1, source_target_pairs={{0,16},{16,32},{32,48},{48,0},{1,17},{17,33},{33,49},{49,1},{2,18}... | collective-permute-start | bytes 786440 | tf_op jit(solution)/shard_map/ppermute | solution.py:30
  114.0 11.8 %collective-permute-start.12 = (bf16[128,1024]{1,0:T(8,128)(2,1)}, bf16[128,1024]{1,0:T(8,128)(2,1)}, u32[]{:S(2)}, u32[]{:S(2)}) collective-permute-start(bf16[128,1024]{1,0:T(8,128)(2,1)} %convolution_convert_fusion.6), channel_id=1, source_target_pairs={{0,48},{16,0},{32,16},{48,32},{1,49},{17,1},{33,17},{49,33},{2,50}... | collective-permute-start | bytes 786440 | tf_op jit(solution)/shard_map/ppermute | solution.py:30
  117.5 16.1 %collective-permute-start.24 = (bf16[128,1024]{1,0:T(8,128)(2,1)S(1)}, bf16[128,1024]{1,0:T(8,128)(2,1)}, u32[]{:S(2)}, u32[]{:S(2)}) collective-permute-start(bf16[128,1024]{1,0:T(8,128)(2,1)S(1)} %fusion.26), channel_id=1, source_target_pairs={{0,4},{1,5},{2,6},{3,7},{4,8},{5,9},{6,10},{7,11},{8,12},{9,13},{1... | collective-permute-start | bytes 786440 | tf_op jit(solution)/shard_map/ppermute | solution.py:37
  117.6 24.0 %collective-permute-start.25 = (bf16[128,1024]{1,0:T(8,128)(2,1)S(1)}, bf16[128,1024]{1,0:T(8,128)(2,1)}, u32[]{:S(2)}, u32[]{:S(2)}) collective-permute-start(bf16[128,1024]{1,0:T(8,128)(2,1)S(1)} %fusion.26), channel_id=1, source_target_pairs={{0,8},{1,9},{2,10},{3,11},{4,12},{5,13},{6,14},{7,15},{8,0},{9,1},... | collective-permute-start | bytes 786440 | tf_op jit(solution)/shard_map/ppermute | solution.py:37
  123.7 22.8 %collective-permute-start.26 = (bf16[128,1024]{1,0:T(8,128)(2,1)S(1)}, bf16[128,1024]{1,0:T(8,128)(2,1)S(1)}, u32[]{:S(2)}, u32[]{:S(2)}) collective-permute-start(bf16[128,1024]{1,0:T(8,128)(2,1)S(1)} %fusion.26), channel_id=1, source_target_pairs={{0,12},{1,13},{2,14},{3,15},{4,0},{5,1},{6,2},{7,3},{8,4},{9,5},{1... | collective-permute-start | bytes 786440 | tf_op jit(solution)/shard_map/ppermute | solution.py:37
  125.2 16.3 %collective-permute-start.21 = (bf16[128,1024]{1,0:T(8,128)(2,1)}, bf16[128,1024]{1,0:T(8,128)(2,1)S(1)}, u32[]{:S(2)}, u32[]{:S(2)}) collective-permute-start(bf16[128,1024]{1,0:T(8,128)(2,1)} %get-tuple-element.31), channel_id=1, source_target_pairs={{0,4},{1,5},{2,6},{3,7},{4,8},{5,9},{6,10},{7,11},{8,12},{9,13},{1... | collective-permute-start | bytes 786440 | tf_op jit(solution)/shard_map/ppermute | solution.py:37
  125.8 18.7 %collective-permute-start.22 = (bf16[128,1024]{1,0:T(8,128)(2,1)}, bf16[128,1024]{1,0:T(8,128)(2,1)S(1)}, u32[]{:S(2)}, u32[]{:S(2)}) collective-permute-start(bf16[128,1024]{1,0:T(8,128)(2,1)} %get-tuple-element.32), channel_id=1, source_target_pairs={{0,8},{1,9},{2,10},{3,11},{4,12},{5,13},{6,14},{7,15},{8,0},{9,1},... | collective-permute-start | bytes 786440 | tf_op jit(solution)/shard_map/ppermute | solution.py:37
  127.2 3.1 %copy-start.4 = (bf16[1024,1024]{1,0:T(8,128)(2,1)S(1)}, bf16[1024,1024]{1,0:T(8,128)(2,1)}, u32[]{:S(2)}) copy-start(bf16[1024,1024]{1,0:T(8,128)(2,1)} %copy-done.2) | copy-start | bytes 6291460
  131.9 9.7 %copy-start.40 = (bf16[128,1024]{1,0:T(8,128)(2,1)S(1)}, bf16[128,1024]{1,0:T(8,128)(2,1)}, u32[]{:S(2)}) copy-start(bf16[128,1024]{1,0:T(8,128)(2,1)} %get-tuple-element.33) | copy-start | bytes 786436
  132.7 8.9 %copy-start.38 = (bf16[128,1024]{1,0:T(8,128)(2,1)S(1)}, bf16[128,1024]{1,0:T(8,128)(2,1)}, u32[]{:S(2)}) copy-start(bf16[128,1024]{1,0:T(8,128)(2,1)} %get-tuple-element.20) | copy-start | bytes 786436
  132.7 11.8 %copy-start.37 = (bf16[128,1024]{1,0:T(8,128)(2,1)S(1)}, bf16[128,1024]{1,0:T(8,128)(2,1)}, u32[]{:S(2)}) copy-start(bf16[128,1024]{1,0:T(8,128)(2,1)} %get-tuple-element.21) | copy-start | bytes 786436
  133.6 24.5 %copy-start.34 = (bf16[128,1024]{1,0:T(8,128)(2,1)S(1)}, bf16[128,1024]{1,0:T(8,128)(2,1)}, u32[]{:S(2)}) copy-start(bf16[128,1024]{1,0:T(8,128)(2,1)} %get-tuple-element.18) | copy-start | bytes 786436
  133.6 18.0 %collective-permute-start.3 = (bf16[128,1024]{1,0:T(8,128)(2,1)S(1)}, bf16[128,1024]{1,0:T(8,128)(2,1)S(1)}, u32[]{:S(2)}, u32[]{:S(2)}) collective-permute-start(bf16[128,1024]{1,0:T(8,128)(2,1)S(1)} %copy-done.39), channel_id=1, source_target_pairs={{0,4},{1,5},{2,6},{3,7},{4,8},{5,9},{6,10},{7,11},{8,12},{9,13},{1... | collective-permute-start | bytes 786440 | tf_op jit(solution)/shard_map/ppermute | solution.py:37
  141.5 11.0 %collective-permute-start.23 = (bf16[128,1024]{1,0:T(8,128)(2,1)S(1)}, bf16[128,1024]{1,0:T(8,128)(2,1)S(1)}, u32[]{:S(2)}, u32[]{:S(2)}) collective-permute-start(bf16[128,1024]{1,0:T(8,128)(2,1)S(1)} %copy-done.40), channel_id=1, source_target_pairs={{0,12},{1,13},{2,14},{3,15},{4,0},{5,1},{6,2},{7,3},{8,4},{9,5},{1... | collective-permute-start | bytes 786440 | tf_op jit(solution)/shard_map/ppermute | solution.py:37
  141.6 13.7 %collective-permute-start.4 = (bf16[128,1024]{1,0:T(8,128)(2,1)S(1)}, bf16[128,1024]{1,0:T(8,128)(2,1)S(1)}, u32[]{:S(2)}, u32[]{:S(2)}) collective-permute-start(bf16[128,1024]{1,0:T(8,128)(2,1)S(1)} %copy-done.38), channel_id=1, source_target_pairs={{0,8},{1,9},{2,10},{3,11},{4,12},{5,13},{6,14},{7,15},{8,0},{9,1},... | collective-permute-start | bytes 786440 | tf_op jit(solution)/shard_map/ppermute | solution.py:37
  144.5 17.0 %copy-start.13 = (bf16[1024,1024]{1,0:T(8,128)(2,1)S(1)}, bf16[1024,1024]{1,0:T(8,128)(2,1)}, u32[]{:S(2)}) copy-start(bf16[1024,1024]{1,0:T(8,128)(2,1)} %copy-done.11) | copy-start | bytes 6291460
  144.5 12.2 %collective-permute-start.5 = (bf16[128,1024]{1,0:T(8,128)(2,1)S(1)}, bf16[128,1024]{1,0:T(8,128)(2,1)S(1)}, u32[]{:S(2)}, u32[]{:S(2)}) collective-permute-start(bf16[128,1024]{1,0:T(8,128)(2,1)S(1)} %copy-done.37), channel_id=1, source_target_pairs={{0,12},{1,13},{2,14},{3,15},{4,0},{5,1},{6,2},{7,3},{8,4},{9,5},{1... | collective-permute-start | bytes 786440 | tf_op jit(solution)/shard_map/ppermute | solution.py:37
  146.4 11.7 %collective-permute-start.32 = (bf16[128,1024]{1,0:T(8,128)(2,1)S(1)}, bf16[128,1024]{1,0:T(8,128)(2,1)S(1)}, u32[]{:S(2)}, u32[]{:S(2)}) collective-permute-start(bf16[128,1024]{1,0:T(8,128)(2,1)S(1)} %convolution_convert_fusion.4), channel_id=1, source_target_pairs={{0,32},{16,48},{32,0},{48,16},{1,33},{17,49},{33,1},{49,17},{2,34}... | collective-permute-start | bytes 786440 | tf_op jit(solution)/shard_map/ppermute | solution.py:30
  151.6 8.0 %collective-permute-start.33 = (bf16[128,1024]{1,0:T(8,128)(2,1)S(1)}, bf16[128,1024]{1,0:T(8,128)(2,1)S(1)}, u32[]{:S(2)}, u32[]{:S(2)}) collective-permute-start(bf16[128,1024]{1,0:T(8,128)(2,1)S(1)} %convolution_convert_fusion.3), channel_id=1, source_target_pairs={{0,16},{16,32},{32,48},{48,0},{1,17},{17,33},{33,49},{49,1},{2,18}... | collective-permute-start | bytes 786440 | tf_op jit(solution)/shard_map/ppermute | solution.py:30
  152.5 7.2 %collective-permute-start.34 = (bf16[128,1024]{1,0:T(8,128)(2,1)S(1)}, bf16[128,1024]{1,0:T(8,128)(2,1)S(1)}, u32[]{:S(2)}, u32[]{:S(2)}) collective-permute-start(bf16[128,1024]{1,0:T(8,128)(2,1)S(1)} %convolution_convert_fusion.2), channel_id=1, source_target_pairs={{0,48},{16,0},{32,16},{48,32},{1,49},{17,1},{33,17},{49,33},{2,50}... | collective-permute-start | bytes 786440 | tf_op jit(solution)/shard_map/ppermute | solution.py:30
  155.3 32.7 %collective-permute-start.28 = (bf16[512,1024]{1,0:T(8,128)(2,1)S(1)}, bf16[512,1024]{1,0:T(8,128)(2,1)S(1)}, u32[]{:S(2)}, u32[]{:S(2)}) collective-permute-start(bf16[512,1024]{1,0:T(8,128)(2,1)S(1)} %pad_maximum_fusion.1), channel_id=1, source_target_pairs={{0,64},{1,65},{2,66},{3,67},{4,68},{5,69},{6,70},{7,71},{8,72},{9,... | collective-permute-start | bytes 3145736 | tf_op jit(solution)/shard_map/ppermute | solution.py:270
  156.7 31.3 %collective-permute-start.27 = (bf16[512,1024]{1,0:T(8,128)(2,1)S(1)}, bf16[512,1024]{1,0:T(8,128)(2,1)S(1)}, u32[]{:S(2)}, u32[]{:S(2)}) collective-permute-start(bf16[512,1024]{1,0:T(8,128)(2,1)S(1)} %constant_dynamic-update-slice_fusion.4), channel_id=1, source_target_pairs={{0,64},{1,65},{2,66},{3,67},{4,68},{5,69},{6,70},{7,71},{8,72},{9,... | collective-permute-start | bytes 3145736 | tf_op jit(solution)/shard_map/ppermute | solution.py:253
  158.1 15.5 %collective-permute-start.13 = (bf16[128,1024]{1,0:T(8,128)(2,1)S(1)}, bf16[128,1024]{1,0:T(8,128)(2,1)S(1)}, u32[]{:S(2)}, u32[]{:S(2)}) collective-permute-start(bf16[128,1024]{1,0:T(8,128)(2,1)S(1)} %get-tuple-element.34), channel_id=1, source_target_pairs={{0,4},{1,5},{2,6},{3,7},{4,8},{5,9},{6,10},{7,11},{8,12},{9,13},{1... | collective-permute-start | bytes 786440 | tf_op jit(solution)/shard_map/ppermute | solution.py:37
  159.6 14.0 %collective-permute-start.14 = (bf16[128,1024]{1,0:T(8,128)(2,1)S(1)}, bf16[128,1024]{1,0:T(8,128)(2,1)S(1)}, u32[]{:S(2)}, u32[]{:S(2)}) collective-permute-start(bf16[128,1024]{1,0:T(8,128)(2,1)S(1)} %get-tuple-element.34), channel_id=1, source_target_pairs={{0,8},{1,9},{2,10},{3,11},{4,12},{5,13},{6,14},{7,15},{8,0},{9,1},... | collective-permute-start | bytes 786440 | tf_op jit(solution)/shard_map/ppermute | solution.py:37
  159.7 15.1 %collective-permute-start.15 = (bf16[128,1024]{1,0:T(8,128)(2,1)S(1)}, bf16[128,1024]{1,0:T(8,128)(2,1)S(1)}, u32[]{:S(2)}, u32[]{:S(2)}) collective-permute-start(bf16[128,1024]{1,0:T(8,128)(2,1)S(1)} %get-tuple-element.34), channel_id=1, source_target_pairs={{0,12},{1,13},{2,14},{3,15},{4,0},{5,1},{6,2},{7,3},{8,4},{9,5},{1... | collective-permute-start | bytes 786440 | tf_op jit(solution)/shard_map/ppermute | solution.py:37
  173.6 10.4 %collective-permute-start.35 = (bf16[128,1024]{1,0:T(8,128)(2,1)S(1)}, bf16[128,1024]{1,0:T(8,128)(2,1)S(1)}, u32[]{:S(2)}, u32[]{:S(2)}) collective-permute-start(bf16[128,1024]{1,0:T(8,128)(2,1)S(1)} %fusion.37), channel_id=1, source_target_pairs={{0,4},{1,5},{2,6},{3,7},{4,8},{5,9},{6,10},{7,11},{8,12},{9,13},{1... | collective-permute-start | bytes 786440 | tf_op jit(solution)/shard_map/ppermute | solution.py:37
  173.6 11.7 %collective-permute-start.36 = (bf16[128,1024]{1,0:T(8,128)(2,1)S(1)}, bf16[128,1024]{1,0:T(8,128)(2,1)S(1)}, u32[]{:S(2)}, u32[]{:S(2)}) collective-permute-start(bf16[128,1024]{1,0:T(8,128)(2,1)S(1)} %fusion.37), channel_id=1, source_target_pairs={{0,8},{1,9},{2,10},{3,11},{4,12},{5,13},{6,14},{7,15},{8,0},{9,1},... | collective-permute-start | bytes 786440 | tf_op jit(solution)/shard_map/ppermute | solution.py:37
  174.8 11.8 %collective-permute-start.37 = (bf16[128,1024]{1,0:T(8,128)(2,1)S(1)}, bf16[128,1024]{1,0:T(8,128)(2,1)S(1)}, u32[]{:S(2)}, u32[]{:S(2)}) collective-permute-start(bf16[128,1024]{1,0:T(8,128)(2,1)S(1)} %fusion.37), channel_id=1, source_target_pairs={{0,12},{1,13},{2,14},{3,15},{4,0},{5,1},{6,2},{7,3},{8,4},{9,5},{1... | collective-permute-start | bytes 786440 | tf_op jit(solution)/shard_map/ppermute | solution.py:37
  184.0 10.8 %collective-permute-start.16 = (bf16[512,1024]{1,0:T(8,128)(2,1)S(1)}, bf16[512,1024]{1,0:T(8,128)(2,1)S(1)}, u32[]{:S(2)}, u32[]{:S(2)}) collective-permute-start(bf16[512,1024]{1,0:T(8,128)(2,1)S(1)} %constant_dynamic-update-slice_fusion), channel_id=1, source_target_pairs={{64,0},{65,1},{66,2},{67,3},{68,4},{69,5},{70,6},{71,7},{72,8},{73... | collective-permute-start | bytes 3145736 | tf_op jit(solution)/shard_map/ppermute | solution.py:253
  185.3 9.5 %collective-permute-start.17 = (bf16[512,1024]{1,0:T(8,128)(2,1)S(1)}, bf16[512,1024]{1,0:T(8,128)(2,1)S(1)}, u32[]{:S(2)}, u32[]{:S(2)}) collective-permute-start(bf16[512,1024]{1,0:T(8,128)(2,1)S(1)} %pad_maximum_fusion), channel_id=1, source_target_pairs={{64,0},{65,1},{66,2},{67,3},{68,4},{69,5},{70,6},{71,7},{72,8},{73... | collective-permute-start | bytes 3145736 | tf_op jit(solution)/shard_map/ppermute | solution.py:270
  186.7 10.9 %collective-permute-start.38 = (bf16[512,1024]{1,0:T(8,128)(2,1)S(1)}, bf16[512,1024]{1,0:T(8,128)(2,1)S(1)}, u32[]{:S(2)}, u32[]{:S(2)}) collective-permute-start(bf16[512,1024]{1,0:T(8,128)(2,1)S(1)} %pad_maximum_fusion.2), channel_id=1, source_target_pairs={{0,64},{64,0},{1,65},{65,1},{2,66},{66,2},{3,67},{67,3},{4,68},{68... | collective-permute-start | bytes 3145736 | tf_op jit(solution)/shard_map/ppermute | solution.py:285
  192.6 11.3 %collective-permute-start.29 = (bf16[256,1024]{1,0:T(8,128)(2,1)S(1)}, bf16[256,1024]{1,0:T(8,128)(2,1)S(1)}, u32[]{:S(2)}, u32[]{:S(2)}) collective-permute-start(bf16[256,1024]{1,0:T(8,128)(2,1)S(1)} %get-tuple-element.39), channel_id=1, source_target_pairs={{64,65},{65,66},{66,67},{67,64},{68,69},{69,70},{70,71},{71,68},{7... | collective-permute-start | bytes 1572872 | tf_op jit(solution)/shard_map/ppermute | solution.py:54
  193.3 33.3 %collective-permute-start.30 = (bf16[256,1024]{1,0:T(8,128)(2,1)}, bf16[256,1024]{1,0:T(8,128)(2,1)}, u32[]{:S(2)}, u32[]{:S(2)}) collective-permute-start(bf16[256,1024]{1,0:T(8,128)(2,1)} %get-tuple-element.41), channel_id=1, source_target_pairs={{64,66},{65,67},{66,64},{67,65},{68,70},{69,71},{70,68},{71,69},{7... | collective-permute-start | bytes 1572872 | tf_op jit(solution)/shard_map/ppermute | solution.py:54
  197.5 5.3 %copy-start.22 = (bf16[1024,1024]{1,0:T(8,128)(2,1)}, bf16[1024,1024]{1,0:T(8,128)(2,1)S(1)}, u32[]{:S(2)}) copy-start(bf16[1024,1024]{1,0:T(8,128)(2,1)S(1)} %add_convert_fusion.1) | copy-start | bytes 6291460
  199.4 16.4 %collective-permute-start.39 = (bf16[80,1024]{1,0:T(8,128)(2,1)S(1)}, bf16[80,1024]{1,0:T(8,128)(2,1)S(1)}, u32[]{:S(2)}, u32[]{:S(2)}) collective-permute-start(bf16[80,1024]{1,0:T(8,128)(2,1)S(1)} %get-tuple-element.44), channel_id=1, source_target_pairs={{0,1},{1,2},{2,3},{3,0},{4,5},{5,6},{6,7},{7,4},{8,9},{9,10},{10,1... | collective-permute-start | bytes 491528 | tf_op jit(solution)/shard_map/ppermute | solution.py:44
  199.5 18.3 %collective-permute-start.40 = (bf16[80,1024]{1,0:T(8,128)(2,1)S(1)}, bf16[80,1024]{1,0:T(8,128)(2,1)}, u32[]{:S(2)}, u32[]{:S(2)}) collective-permute-start(bf16[80,1024]{1,0:T(8,128)(2,1)S(1)} %get-tuple-element.46), channel_id=1, source_target_pairs={{0,2},{1,3},{2,0},{3,1},{4,6},{5,7},{6,4},{7,5},{8,10},{9,11},{10,... | collective-permute-start | bytes 491528 | tf_op jit(solution)/shard_map/ppermute | solution.py:44
  201.7 17.9 %collective-permute-start.41 = (bf16[80,1024]{1,0:T(8,128)(2,1)S(1)}, bf16[80,1024]{1,0:T(8,128)(2,1)}, u32[]{:S(2)}, u32[]{:S(2)}) collective-permute-start(bf16[80,1024]{1,0:T(8,128)(2,1)S(1)} %get-tuple-element.45), channel_id=1, source_target_pairs={{0,3},{1,0},{2,1},{3,2},{4,7},{5,4},{6,5},{7,6},{8,11},{9,8},{10,9... | collective-permute-start | bytes 491528 | tf_op jit(solution)/shard_map/ppermute | solution.py:44
  204.0 22.7 %collective-permute-start.31 = (bf16[256,1024]{1,0:T(8,128)(2,1)S(1)}, bf16[256,1024]{1,0:T(8,128)(2,1)}, u32[]{:S(2)}, u32[]{:S(2)}) collective-permute-start(bf16[256,1024]{1,0:T(8,128)(2,1)S(1)} %get-tuple-element.40), channel_id=1, source_target_pairs={{64,67},{65,64},{66,65},{67,66},{68,71},{69,68},{70,69},{71,70},{7... | collective-permute-start | bytes 1572872 | tf_op jit(solution)/shard_map/ppermute | solution.py:54
  215.8 18.2 %collective-permute-start.18 = (bf16[256,1024]{1,0:T(8,128)(2,1)}, bf16[256,1024]{1,0:T(8,128)(2,1)}, u32[]{:S(2)}, u32[]{:S(2)}) collective-permute-start(bf16[256,1024]{1,0:T(8,128)(2,1)} %get-tuple-element.36), channel_id=1, source_target_pairs={{0,1},{1,2},{2,3},{3,0},{4,5},{5,6},{6,7},{7,4},{8,9},{9,10},{10,1... | collective-permute-start | bytes 1572872 | tf_op jit(solution)/shard_map/ppermute | solution.py:54
  217.7 16.3 %collective-permute-start.19 = (bf16[256,1024]{1,0:T(8,128)(2,1)}, bf16[256,1024]{1,0:T(8,128)(2,1)}, u32[]{:S(2)}, u32[]{:S(2)}) collective-permute-start(bf16[256,1024]{1,0:T(8,128)(2,1)} %get-tuple-element.38), channel_id=1, source_target_pairs={{0,2},{1,3},{2,0},{3,1},{4,6},{5,7},{6,4},{7,5},{8,10},{9,11},{10,... | collective-permute-start | bytes 1572872 | tf_op jit(solution)/shard_map/ppermute | solution.py:54
  219.7 17.2 %collective-permute-start.20 = (bf16[256,1024]{1,0:T(8,128)(2,1)}, bf16[256,1024]{1,0:T(8,128)(2,1)}, u32[]{:S(2)}, u32[]{:S(2)}) collective-permute-start(bf16[256,1024]{1,0:T(8,128)(2,1)} %get-tuple-element.37), channel_id=1, source_target_pairs={{0,3},{1,0},{2,1},{3,2},{4,7},{5,4},{6,5},{7,6},{8,11},{9,8},{10,9... | collective-permute-start | bytes 1572872 | tf_op jit(solution)/shard_map/ppermute | solution.py:54
  (23 other events, 31.5 us)

commit v3 on v2

v3 whole, which is shorter than its diff:
```python
import functools

import jax
import jax.numpy as jnp
from jax import lax
from jax.experimental import pallas as pl
from jax.experimental.pallas import tpu as pltpu
from jax.sharding import PartitionSpec as P

BF = jnp.bfloat16
F32 = jnp.float32
SIDE = 4
SLOTS = 8
ROWS = 32
MINE = 4
ANY = pl.BlockSpec(memory_space=pl.ANY)
WHOLE = pl.BlockSpec(memory_space=pltpu.VMEM)
SCALARS = pl.BlockSpec(memory_space=pltpu.SMEM)
SMALL = pltpu.CompilerParams(vmem_limit_bytes=6 * 1024 * 1024)
Z_GROUPS = [[z * SIDE + y for z in range(SIDE)] for y in range(SIDE)]
Y_GROUPS = [[z * SIDE + y for y in range(SIDE)] for z in range(SIDE)]


def dot(a, b):
    return jnp.dot(a, b, preferred_element_type=F32)


def dot_nt(a, b):
    return lax.dot_general(a, b, (((1,), (1,)), ((), ())), preferred_element_type=F32)


def dot_tn(a, b):
    return lax.dot_general(a, b, (((0,), (0,)), ((), ())), preferred_element_type=F32)


def along_x(block, distance):
    return lax.ppermute(block, "mp", [(i, (i + distance) % SIDE) for i in range(SIDE)])


def along_z(block, distance):
    pairs = [
        (z * SIDE + y, (z + distance) % SIDE * SIDE + y) for z in range(SIDE) for y in range(SIDE)
    ]
    return lax.ppermute(block, "dp", pairs)


def along_y(block, distance):
    pairs = [
        (z * SIDE + y, z * SIDE + (y + distance) % SIDE) for z in range(SIDE) for y in range(SIDE)
    ]
    return lax.ppermute(block, "dp", pairs)


def exchange(blocks, groups):
    return lax.all_to_all(blocks, "dp", 0, 0, tiled=True, axis_index_groups=groups)


def swap(block):
    return lax.ppermute(block, "segment", [(0, 1), (1, 0)])


def after(value, *others):
    return lax.optimization_barrier((value,) + others)[0]


def spread_kernel(routing, place, slots, out):
    core, replica = place[0], place[1]
    for group in range(16):
        slot = jnp.int32(0)
        for j in range(MINE):
            q = routing[(core * 16 + group) * MINE + j]
            slot = jnp.where(lax.shift_right_logical(q, 3) == replica, q & 7, slot)
        out[group] = slots[slot]


def spread(routing, place, slots):
    shape = (16,) + slots.shape[1:]
    return pl.pallas_call(
        spread_kernel,
        in_specs=[SCALARS, SCALARS, WHOLE],
        out_specs=WHOLE,
        out_shape=jax.ShapeDtypeStruct(shape, slots.dtype),
        compiler_params=SMALL,
    )(routing, place, slots)


def merge_kernel(routing, counts, place, arrived, *refs):
    image, out, sems = (refs[0] if len(refs) == 3 else None), refs[-2], refs[-1]
    first = (place[0] * 16 + place[1]) * MINE
    copies = []
    for j in range(MINE):
        replica = lax.shift_right_logical(routing[first + j], 3)
        copy = pltpu.make_async_copy(arrived.at[replica], out.at[j], sems.at[j])
        copy.start()
        copies.append(copy)
    for copy in copies:
        copy.wait()
    if image is not None:
        row = lax.broadcasted_iota(jnp.int32, out.shape[1:], 0)
        for j in range(MINE):
            out[j] = jnp.where(row < counts[first + j], image[j], out[j])


def merge(routing, counts, place, arrived, image=None):
    columns = arrived.shape[2]
    operands = (arrived,) if image is None else (arrived, image)
    return pl.pallas_call(
        merge_kernel,
        in_specs=[SCALARS] * 3 + [ANY] + [WHOLE] * (len(operands) - 1),
        out_specs=WHOLE,
        scratch_shapes=[pltpu.SemaphoreType.DMA((MINE,))],
        out_shape=jax.ShapeDtypeStruct((MINE, ROWS, columns), arrived.dtype),
        compiler_params=SMALL,
    )(routing, counts, place, *operands).reshape(MINE * ROWS, columns)


def turn_kernel(place, own, other, *outs_and_sems):
    outs, sems = outs_and_sems[:-1], outs_and_sems[-1]
    core, x = place[0], place[2]
    size = outs[0].shape[0]

    def copy(source, n):
        block = lax.rem(x - n % SIDE + SIDE, SIDE)
        start = pl.multiple_of(block * size, size)
        return pltpu.make_async_copy(source.at[pl.ds(start, size)], outs[n], sems.at[n])

    for n in range(2 * SIDE):

        @pl.when(core == n // SIDE)
        def _():
            copy(own, n).start()

        @pl.when(core != n // SIDE)
        def _():
            copy(other, n).start()

    for n in range(2 * SIDE):
        copy(own, n).wait()


def turn(place, own, other):
    rows, columns = own.shape
    blocks = pl.pallas_call(
        turn_kernel,
        in_specs=[pl.BlockSpec(memory_space=pltpu.SMEM), ANY, ANY],
        out_specs=[pl.BlockSpec(memory_space=pltpu.VMEM)] * (2 * SIDE),
        scratch_shapes=[pltpu.SemaphoreType.DMA((2 * SIDE,))],
        out_shape=[pltpu.VMEM((rows // SIDE, columns), own.dtype)] * (2 * SIDE),
        compiler_params=pltpu.CompilerParams(vmem_limit_bytes=40 * 1024 * 1024),
    )(place, own, other)
    return (blocks[:SIDE], blocks[SIDE:])


def order_kernel(section, place, in0, in1, in2, in3, out):
    x = place[2]
    blocks = (in0, in1, in2, in3)
    part = in0.shape[1] // SIDE
    for owner in range(SIDE):
        for d in range(SIDE):

            @pl.when(lax.rem(x - d + SIDE, SIDE) == owner)
            def _():
                if section == 0:
                    out[owner] = blocks[d][...]
                else:
                    for y in range(SIDE):
                        out[y, :, pl.ds(owner * part, part)] = blocks[d][:, pl.ds(y * part, part)]


def order(section, place, blocks):
    shape = (SIDE,) + blocks[0].shape
    return pl.pallas_call(
        functools.partial(order_kernel, section),
        in_specs=[SCALARS] + [WHOLE] * SIDE,
        out_specs=WHOLE,
        out_shape=jax.ShapeDtypeStruct(shape, blocks[0].dtype),
        compiler_params=SMALL,
    )(place, *blocks)


def line_up_kernel(place, arrived, out):
    core, z = place[0], place[4]
    for other in range(2):
        for e in range(SIDE):
            block = lax.rem(core + other, 2) * SIDE + lax.rem(z - e + SIDE, SIDE)
            out[other * SIDE + e] = arrived[block]


def line_up(place, arrived):
    return pl.pallas_call(
        line_up_kernel,
        in_specs=[SCALARS, WHOLE],
        out_specs=WHOLE,
        out_shape=jax.ShapeDtypeStruct(arrived.shape, arrived.dtype),
        compiler_params=SMALL,
    )(place, arrived)


def gelu_slope(preact):
    _, pullback = jax.vjp(jax.nn.gelu, preact)
    return pullback(jnp.ones_like(preact))[0]


def on_device(patches, merger_weight, image_counts, routing, text_embed, llm_weight, upstream):
    core = lax.axis_index("segment")
    x = lax.axis_index("mp")
    replica = lax.axis_index("dp")
    z, y = replica // SIDE, replica % SIDE
    place = jnp.stack([core, replica, x, y, z]).astype(jnp.int32)
    group = core * 16 + replica
    columns = merger_weight.shape[1]
    merger = patches.shape[2]
    tokens = MINE * ROWS

    own_weight = llm_weight[0]
    other_weight = swap(own_weight)
    send_text = spread(routing, place, text_embed.reshape(SLOTS, ROWS, columns))
    arrived_text = lax.all_to_all(send_text, "dp", 0, 0, tiled=True)

    activated = jax.nn.gelu(patches.astype(F32)).astype(BF).reshape(tokens, merger)
    embeds = dot(activated, merger_weight).astype(BF).reshape(MINE, ROWS, columns)
    act_parts = activated.reshape(tokens, 8, merger // 8).transpose(1, 0, 2)
    send_ups = spread(routing, place, upstream.reshape(SLOTS, ROWS, columns))
    weights = turn(place, own_weight, other_weight)
    arrived_text, embeds, act_parts, send_ups, weights = lax.optimization_barrier(
        (arrived_text, embeds, act_parts, send_ups, weights)
    )
    hidden = merge(routing, image_counts, place, arrived_text, embeds)

    arrived_ups = lax.all_to_all(after(send_ups, hidden), "dp", 0, 0, tiled=True)
    eights = [
        [c * 16 + zz * SIDE + yy for c in range(2) for zz in range(SIDE)] for yy in range(SIDE)
    ]

    slopes = []
    rows_of = []
    for section in range(2):
        blocks = [hidden] + [along_x(hidden, d) for d in (1, 2, 3)]
        preact = dot(blocks[0], weights[section][0])
        for d in (1, 3, 2):
            preact = preact + dot(blocks[d], weights[section][d])
        if section == 0:
            hidden = (hidden.astype(F32) + jax.nn.gelu(preact)).astype(BF)
        slopes.append(gelu_slope(preact))
        rows_of.append((blocks, preact))

    act_cols = lax.all_to_all(
        after(act_parts, hidden), ("segment", "dp"), 0, 0, tiled=True, axis_index_groups=eights
    )
    act_cols = line_up(place, act_cols).reshape(8 * tokens, merger // 8)
    cotangent = merge(routing, image_counts, place, arrived_ups)
    groups = (Z_GROUPS, Y_GROUPS)
    all_rows = [
        exchange(order(section, place, rows_of[section][0]), groups[section]) for section in (0, 1)
    ]
    all_locals = [None, None]
    for section in (1, 0):
        local = (slopes[section] * cotangent.astype(F32)).astype(BF)
        terms = [
            along_x(dot_nt(local, weights[section][SIDE - d]).astype(BF), d) for d in (2, 1, 3)
        ]
        terms.append(dot_nt(local, weights[section][0]).astype(BF))
        inner = sum(term.astype(F32) for term in terms)
        cotangent = (cotangent.astype(F32) + inner).astype(BF)
        copies = jnp.broadcast_to(local[None], (SIDE,) + local.shape)
        all_locals[section] = exchange(copies, groups[section])

    def my_section(pair):
        first, second = (blocks.reshape(SIDE * tokens, columns) for blocks in pair)
        return (
            jnp.where(core == 0, first, second),
            swap(jnp.where(core == 0, second, first)),
        )

    rows, rows_swapped = my_section(all_rows)
    local, local_swapped = my_section(all_locals)
    part = dot_tn(rows, local) + dot_tn(rows_swapped, local_swapped)
    part = part.astype(BF).reshape(SIDE, -1, columns)
    sums = [[c * 16 + n for n in g] for c, gs in ((0, Y_GROUPS), (1, Z_GROUPS)) for g in gs]
    part = lax.all_to_all(part, ("segment", "dp"), 0, 0, tiled=True, axis_index_groups=sums)
    llm_grad = jnp.sum(part.astype(F32), axis=0)[None]

    counts = lax.dynamic_slice_in_dim(image_counts, group * MINE, MINE)
    image_rows = (jnp.arange(ROWS)[None] < counts[:, None]).reshape(tokens)
    image_grad = jnp.where(image_rows[:, None], cotangent, jnp.zeros((), BF))
    grads = [image_grad] + [along_z(image_grad, e) for e in (1, 2, 3)]
    grads = jnp.concatenate(grads, axis=0)
    grads_swapped = swap(grads)
    half = grads.shape[0]
    part = dot_tn(act_cols[:half], grads) + dot_tn(act_cols[half:], grads_swapped)
    part = part.astype(BF).reshape(SIDE, -1, columns)

    def toward(j):
        return lax.dynamic_index_in_dim(part, (y + j) % SIDE, 0, keepdims=False)

    merger_grad = toward(0).astype(F32)
    for j in (1, 2, 3):
        merger_grad = merger_grad + along_y(toward(j), j).astype(F32)
    return (llm_grad, merger_grad)


def solution(mesh):
    return jax.shard_map(
        on_device,
        mesh=mesh,
        in_specs=(
            P(("segment", "dp"), None, None),
            P(None, "mp"),
            P(),
            P(),
            P(None, "dp", "mp"),
            P("segment", None, "mp"),
            P(None, "dp", "mp"),
        ),
        out_specs=(P("segment", "dp", "mp"), P(("segment", "dp"), "mp")),
        check_vma=False,
    )
```

time: 242 us -> 205 us (0.85)
  waiting for transfers between devices: 71.9 us -> 33.3 us
  matrix products: 33.7 us -> 49.3 us
  Pallas kernels: 26.5 us -> 17.1 us
  starting transfers between devices: 74.7 us -> 70.8 us
    all_to_all x2 -> x7, starting transfers between devices: 8.34 us -> 32.4 us  [the longest x4 17.4 us: exchange(): lax.all_to_all(blocks, 'dp', 0, 0, tiled=True, axis_index_groups=groups)]
    ppermute x12 -> x4, starting transfers between devices: 19.3 us -> 0.1 us  [swap(): return lax.ppermute(block, 'segment', [(0, 1), (1, 0)])]
    ppermute x15 -> x3, waiting for transfers between devices: 28.2 us -> 9.85 us  [along_z(): return lax.ppermute(block, 'dp', pairs)]
    ppermute x15 -> x3, starting transfers between devices: 16.5 us -> 3.24 us  [along_z(): return lax.ppermute(block, 'dp', pairs)]
    all_to_all x1, waiting for transfers between devices: 12.1 us -> 0.01 us  [on_device(): arrived_text = lax.all_to_all(send_text, 'dp', 0, 0, tiled=True)]
    ppermute x12 -> x4, waiting for transfers between devices: 10.2 us -> 0.01 us  [swap(): return lax.ppermute(block, 'segment', [(0, 1), (1, 0)])]
    pallas_call x7, Pallas kernels: 19.9 us -> 10.4 us  [the longest x2 4.59 us: order(): pl.pallas_call(functools.partial(order_kernel, section), in_specs=[SCALAR...]
    dot_general x8, matrix products: 11.1 us -> 19.2 us  [dot_nt(): lax.dot_general(a, b, (((1,), (1,)), ((), ())), preferred_element_type=F32)]
  transfers between devices with their start and end apart: 45 -> 30, of which waited for: 13 -> 8; matrix products, arithmetic and copies ran while one was open for 17% -> 33% of each run, Pallas kernels for 11% -> 8%
where the time goes in v3:
time: 205 us; the launch traced here: 204 us
  starting transfers between devices  70.8 us (35%)
  matrix products  49.3 us (24%)
  waiting for transfers between devices  33.3 us (16%)
  local copies, waits for them, and re-layouts  23.6 us (12%)
  Pallas kernels  17.1 us (8%)
  other arithmetic  8.36 us (4%)
    ppermute x12, starting transfers between devices, along_x(): lax.ppermute(block, 'mp', [(i, (i + distance) % SIDE) for i in range(SIDE)])  20.7 us
    dot_general x9, matrix products, dot(): return jnp.dot(a, b, preferred_element_type=F32)  19.8 us
    dot_general x8, matrix products, dot_nt(): lax.dot_general(a, b, (((1,), (1,)), ((), ())), preferred_element_type=F32)  19.2 us
    all_to_all x4, starting transfers between devices, exchange(): lax.all_to_all(blocks, 'dp', 0, 0, tiled=True, axis_index_groups=groups)  17.4 us
    unnamed x70, local copies, waits for them, and re-layouts  13.1 us
    ppermute x3, waiting for transfers between devices, along_y(): return lax.ppermute(block, 'dp', pairs)  11.2 us
    dot_general x4, matrix products, dot_tn(): lax.dot_general(a, b, (((0,), (0,)), ((), ())), preferred_element_type=F32)  10.3 us
    all_to_all x4, waiting for transfers between devices, exchange(): lax.all_to_all(blocks, 'dp', 0, 0, tiled=True, axis_index_groups=groups)  10.2 us
  transfers between devices with their start and end apart: 30, of which 8 were waited for; matrix products, arithmetic and copies ran while one was open for 33% of the time, Pallas kernels for 8%

profile of v3, /device:TPU:0, one launch (start us, length us, event | category | flops | bytes accessed | tf_op | source)
XLA Modules:
  0.0 203.6 jit_solution(8126552084677819523)
XLA Ops:
  2.5 1.6 shard_map.86
  4.2 8.3 %all-to-all-start = ((bf16[16,32,1024]{2,1,0:T(8,128)(2,1)}), bf16[16,32,1024]{2,1,0:T(8,128)(2,1)S(1)}, u32[]{:S(2)}, u32[]{:S(2)}) async-start(bf16[16,32,1024]{2,1,0:T(8,128)(2,1)} %shard_map.86), calls=%async_computation | async-start | bytes 2097152 | tf_op jit(solution)/shard_map/all_to_all | solution.py:218
  12.5 1.6 shard_map.87
  14.5 1.5 reshape_reshape.3
  16.1 4.0 %convolution_convert_fusion = bf16[128,1024]{1,0:T(8,128)(2,1)} fusion(bf16[128,2560]{1,0:T(8,128)(2,1)S(1)} %bitcast.88, bf16[2560,1024]{1,0:T(8,128)(2,1)} %param.8), kind=kOutput, calls=%fused_computation.21 | convolution fusion | flops 671219712 | bytes 6160384 | tf_op jit(solution)/shard_map/dot_general | solution.py:25
  20.1 6.7 %shard_map.88 = (bf16[1024,1024]{1,0:T(8,128)(2,1)S(1)}, bf16[1024,1024]{1,0:T(8,128)(2,1)S(1)}, bf16[1024,1024]{1,0:T(8,128)(2,1)S(1)}, bf16[1024,1024]{1,0:T(8...) custom-call(s32[5]{0:T(128)} %copy-done.19, ...), custom_call_target="tpu_custom_call" | custom-call | tf_op jit(solution)/shard_map/pallas_call | solution.py:143
  26.9 1.3 copy-done
  30.8 1.3 copy-done.6
  32.2 1.4 copy-done.9
  34.9 1.4 copy-done.14
  38.3 1.6 collective-permute-start.1
  39.8 2.7 %collective-permute-start.2 = (bf16[128,1024]{1,0:T(8,128)(2,1)S(1)}, bf16[128,1024]{1,0:T(8,128)(2,1)}, u32[]{:S(2)}, u32[]{:S(2)}) collective-permute-start(bf16[128,1024]{1,0:T(8,128)(2,1)S(1)} %bitcast.77), channel_id=1, source_target_pairs={{0,32},{16,48},{32,0},{48,16},{1,33},{17,49},{33,1},{49,17},{2,34}... | collective-permute-start | bytes 786440 | tf_op jit(solution)/shard_map/ppermute | solution.py:37
  42.6 1.4 collective-permute-start.3
  44.0 7.2 %all-to-all-start.3 = ((bf16[16,32,1024]{2,1,0:T(8,128)(2,1)}), bf16[16,32,1024]{2,1,0:T(8,128)(2,1)S(1)}, u32[]{:S(2)}, u32[]{:S(2)}) async-start(bf16[16,32,1024]{2,1,0:T(8,128)(2,1)} %shard_map.87), calls=%async_computation.3 | async-start | bytes 2097152 | tf_op jit(solution)/shard_map/all_to_all | solution.py:230
  51.2 2.2 %fusion.37 = f32[128,1024]{1,0:T(8,128)S(1)} fusion(bf16[128,1024]{1,0:T(8,128)(2,1)S(1)} %bitcast.79, bf16[1024,1024]{1,0:T(8,128)(2,1)} %copy-done.4), kind=kOutput, calls=%fused_computation.73 | convolution fusion | flops 268435456 | bytes 2883584 | tf_op jit(solution)/shard_map/dot_general | solution.py:25
  53.4 1.5 convolution_add_fusion.4
  55.1 1.4 fusion.38
  56.5 2.4 %add_convert_fusion = (bf16[128,1024]{1,0:T(8,128)(2,1)}, f32[128,1024]{1,0:T(8,128)}) fusion(bf16[4,32,1024]{2,1,0:T(8,128)(2,1)S(1)} %shard_map.89, f32[128,1024]{1,0:T(8,128)S(1)} %fusion.38, f32[128,1024]{1,0:T(8,128)S(1)} %convolution_add_fusion.4, bf16[128,1024]{1,0:T(8,128)(2,1)} %collective-permute-done.3.in3, ...), kind=kOutput, calls=%fused_computation.63 | convolution fusion | flops 270139392 | bytes 4456448 | tf_op jit(solution)/shard_map/dot_general | solution.py:25
  60.8 1.6 collective-permute-start.6
  62.3 2.2 %shard_map.90 = bf16[4,128,1024]{2,1,0:T(8,128)(2,1)} custom-call(s32[5]{0:T(128)S(1)} %copy-done.20, bf16[128,1024]{1,0:T(8,128)(2,1)S(1)} %bitcast.80, bf16[128,1024]{1,0:T(8,128)(2,1)} %collective-permute-done.1.in1, bf16[128,1024]{1,0:T(8,128)(2,1)} %collective-permute-done.2.in2, bf16[128,1024]{1,0:T(8,128)(2,1)} %collective-permute-done.3.in3), custom_call_target="tpu_custom_call" | custom-call | tf_op jit(solution)/shard_map/pallas_call | solution.py:172
  64.6 2.2 %fusion.39 = f32[128,1024]{1,0:T(8,128)} fusion(bf16[128,1024]{1,0:T(8,128)(2,1)} %get-tuple-element.53.in0, bf16[1024,1024]{1,0:T(8,128)(2,1)S(1)} %copy-done.15), kind=kOutput, calls=%fused_computation.75 | convolution fusion | flops 268435456 | bytes 2883584 | tf_op jit(solution)/shard_map/dot_general | solution.py:25
  67.8 4.3 %all-to-all-start.1 = ((bf16[4,128,1024]{2,1,0:T(8,128)(2,1)}), bf16[4,128,1024]{2,1,0:T(8,128)(2,1)}, u32[]{:S(2)}, u32[]{:S(2)}) async-start(bf16[4,128,1024]{2,1,0:T(8,128)(2,1)} %shard_map.90), calls=%async_computation.1 | async-start | bytes 2097152 | tf_op jit(solution)/shard_map/all_to_all | solution.py:55
  73.0 2.1 %fusion.40 = f32[128,1024]{1,0:T(8,128)S(1)} fusion(bf16[128,1024]{1,0:T(8,128)(2,1)} %collective-permute-done.5.in2, bf16[1024,1024]{1,0:T(8,128)(2,1)} %copy-done.3), kind=kOutput, calls=%fused_computation.76 | convolution fusion | flops 268435456 | bytes 2883584 | tf_op jit(solution)/shard_map/dot_general | solution.py:25
  75.2 2.4 %shard_map.91 = bf16[4,128,1024]{2,1,0:T(8,128)(2,1)} custom-call(s32[5]{0:T(128)S(1)} %copy-done.20, bf16[128,1024]{1,0:T(8,128)(2,1)} %get-tuple-element.53.in0, bf16[128,1024]{1,0:T(8,128)(2,1)} %collective-permute-done.4.in1, bf16[128,1024]{1,0:T(8,128)(2,1)} %collective-permute-done.5.in2, bf16[128,1024]{1,0:T(8,128)(2,1)} %collective-permute-done.6.in3), custom_call_target="tpu_custom_call" | custom-call | tf_op jit(solution)/shard_map/pallas_call | solution.py:172
  77.5 1.5 convolution_add_fusion.2
  80.0 2.4 %fusion.18 = bf16[128,1024]{1,0:T(8,128)(2,1)} fusion(bf16[128,1024]{1,0:T(8,128)(2,1)S(1)} %bitcast.84, f32[128,1024]{1,0:T(8,128)S(1)} %fusion.40, f32[128,1024]{1,0:T(8,128)S(1)} %convolution_add_fusion.2, bf16[128,1024]{1,0:T(8,128)(2,1)} %collective-permute-done.6.in3, bf16[1024,1024]{1,0:T(8,128)(2,1)S(1)} %copy-done.13), kind=kOutput, calls=%fused_computation.49 | convolution fusion | flops 271319040 | bytes 3932160 | tf_op jit(solution)/shard_map/dot_general | solution.py:25
  82.4 2.7 %all-to-all-done.1 = bf16[4,128,1024]{2,1,0:T(8,128)(2,1)} async-done(((bf16[4,128,1024]{2,1,0:T(8,128)(2,1)}), bf16[4,128,1024]{2,1,0:T(8,128)(2,1)}, u32[]{:S(2)}, u32[]{:S(2)}) %all-to-all-start.1) | async-done | bytes 1048608 | tf_op jit(solution)/shard_map/all_to_all | solution.py:55
  85.1 4.0 %all-to-all-start.2 = ((bf16[4,128,1024]{2,1,0:T(8,128)(2,1)}), bf16[4,128,1024]{2,1,0:T(8,128)(2,1)S(1)}, u32[]{:S(2)}, u32[]{:S(2)}) async-start(bf16[4,128,1024]{2,1,0:T(8,128)(2,1)} %shard_map.91), calls=%async_computation.2 | async-start | bytes 2097152 | tf_op jit(solution)/shard_map/all_to_all | solution.py:55
  89.1 3.3 %convolution_convert_fusion.8 = bf16[128,1024]{1,0:T(8,128)(2,1)} fusion(bf16[128,1024]{1,0:T(8,128)(2,1)} %fusion.18, bf16[1024,1024]{1,0:T(8,128)(2,1)} %copy-done.3), kind=kOutput, calls=%fused_computation.31 | convolution fusion | flops 268566528 | bytes 2621440 | tf_op jit(solution)/shard_map/dot_general | solution.py:29
  92.4 3.1 %convolution_convert_fusion.7 = bf16[128,1024]{1,0:T(8,128)(2,1)} fusion(bf16[128,1024]{1,0:T(8,128)(2,1)S(1)} %copy-done.26, bf16[1024,1024]{1,0:T(8,128)(2,1)} %copy-done.12), kind=kOutput, calls=%fused_computation.30 | convolution fusion | flops 268566528 | bytes 2621440 | tf_op jit(solution)/shard_map/dot_general | solution.py:29
  95.6 1.5 convolution_convert_fusion.6
  97.1 2.6 %collective-permute-start.7 = (bf16[128,1024]{1,0:T(8,128)(2,1)}, bf16[128,1024]{1,0:T(8,128)(2,1)}, u32[]{:S(2)}, u32[]{:S(2)}) collective-permute-start(bf16[128,1024]{1,0:T(8,128)(2,1)} %convolution_convert_fusion.8), channel_id=1, source_target_pairs={{0,32},{16,48},{32,0},{48,16},{1,33},{17,49},{33,1},{49,17},{2,34}... | collective-permute-start | bytes 786440 | tf_op jit(solution)/shard_map/ppermute | solution.py:37
  99.7 3.2 %collective-permute-start.9 = (bf16[128,1024]{1,0:T(8,128)(2,1)}, bf16[128,1024]{1,0:T(8,128)(2,1)}, u32[]{:S(2)}, u32[]{:S(2)}) collective-permute-start(bf16[128,1024]{1,0:T(8,128)(2,1)} %convolution_convert_fusion.6), channel_id=1, source_target_pairs={{0,48},{16,0},{32,16},{48,32},{1,49},{17,1},{33,17},{49,33},{2,50}... | collective-permute-start | bytes 786440 | tf_op jit(solution)/shard_map/ppermute | solution.py:37
  103.0 2.0 %broadcast_in_dim.30 = bf16[4,128,1024]{2,1,0:T(8,128)(2,1)} broadcast(bf16[128,1024]{1,0:T(8,128)(2,1)} %fusion.18), dimensions={1,2} | broadcast | bytes 1310720 | tf_op jit(solution)/shard_map/broadcast_in_dim | solution.py:265
  105.1 4.8 %all-to-all-start.5 = ((bf16[4,128,1024]{2,1,0:T(8,128)(2,1)}), bf16[4,128,1024]{2,1,0:T(8,128)(2,1)}, u32[]{:S(2)}, u32[]{:S(2)}) async-start(bf16[4,128,1024]{2,1,0:T(8,128)(2,1)} %broadcast_in_dim.30), calls=%async_computation.5 | async-start | bytes 2097152 | tf_op jit(solution)/shard_map/all_to_all | solution.py:55
  110.1 3.9 %fusion.16 = (bf16[128,1024]{1,0:T(8,128)(2,1)S(1)}, bf16[128,1024]{1,0:T(8,128)(2,1)}) fusion(f32[128,1024]{1,0:T(8,128)} %get-tuple-element.54, bf16[128,1024]{1,0:T(8,128)(2,1)} %collective-permute-done.9, bf16[128,1024]{1,0:T(8,128)(2,1)} %collective-permute-done.8, bf16[128,1024]{1,0:T(8,128)(2,1)} %collective-permute-done.7, ...), kind=kOutput, calls=%fused_computation.47 | convolution fusion | flops 272498688 | bytes 4456448 | tf_op jit(solution)/shard_map/dot_general | solution.py:29
  114.0 1.5 convolution_convert_fusion.4
  115.5 2.4 %collective-permute-start.12 = (bf16[128,1024]{1,0:T(8,128)(2,1)}, bf16[128,1024]{1,0:T(8,128)(2,1)}, u32[]{:S(2)}, u32[]{:S(2)}) collective-permute-start(bf16[128,1024]{1,0:T(8,128)(2,1)} %convolution_convert_fusion.4), channel_id=1, source_target_pairs={{0,32},{16,48},{32,0},{48,16},{1,33},{17,49},{33,1},{49,17},{2,34}... | collective-permute-start | bytes 786440 | tf_op jit(solution)/shard_map/ppermute | solution.py:37
  117.9 2.9 %all-to-all-done.5 = bf16[4,128,1024]{2,1,0:T(8,128)(2,1)} async-done(((bf16[4,128,1024]{2,1,0:T(8,128)(2,1)}), bf16[4,128,1024]{2,1,0:T(8,128)(2,1)}, u32[]{:S(2)}, u32[]{:S(2)}) %all-to-all-start.5) | async-done | bytes 1048608 | tf_op jit(solution)/shard_map/all_to_all | solution.py:55
  120.9 2.0 %broadcast_in_dim.14 = bf16[4,128,1024]{2,1,0:T(8,128)(2,1)} broadcast(bf16[128,1024]{1,0:T(8,128)(2,1)} %copy-done.24), dimensions={1,2} | broadcast | bytes 1310720 | tf_op jit(solution)/shard_map/broadcast_in_dim | solution.py:265
  122.9 4.4 %all-to-all-start.4 = ((bf16[4,128,1024]{2,1,0:T(8,128)(2,1)}), bf16[4,128,1024]{2,1,0:T(8,128)(2,1)}, u32[]{:S(2)}, u32[]{:S(2)}) async-start(bf16[4,128,1024]{2,1,0:T(8,128)(2,1)} %broadcast_in_dim.14), calls=%async_computation.4 | async-start | bytes 2097152 | tf_op jit(solution)/shard_map/all_to_all | solution.py:55
  127.3 1.5 convolution_convert_fusion.3
  129.7 1.6 convolution_convert_fusion.2
  131.3 2.4 %collective-permute-start.14 = (bf16[128,1024]{1,0:T(8,128)(2,1)}, bf16[128,1024]{1,0:T(8,128)(2,1)}, u32[]{:S(2)}, u32[]{:S(2)}) collective-permute-start(bf16[128,1024]{1,0:T(8,128)(2,1)} %convolution_convert_fusion.2), channel_id=1, source_target_pairs={{0,48},{16,0},{32,16},{48,32},{1,49},{17,1},{33,17},{49,33},{2,50}... | collective-permute-start | bytes 786440 | tf_op jit(solution)/shard_map/ppermute | solution.py:37
  134.8 4.6 %all-to-all-done.4 = bf16[4,128,1024]{2,1,0:T(8,128)(2,1)} async-done(((bf16[4,128,1024]{2,1,0:T(8,128)(2,1)}), bf16[4,128,1024]{2,1,0:T(8,128)(2,1)}, u32[]{:S(2)}, u32[]{:S(2)}) %all-to-all-start.4) | async-done | bytes 1048608 | tf_op jit(solution)/shard_map/all_to_all | solution.py:55
  139.4 2.4 %broadcast_select_fusion.1 = bf16[4,128,1024]{2,1,0:T(8,128)(2,1)} fusion(bf16[4,128,1024]{2,1,0:T(8,128)(2,1)} %all-to-all-done.5, bf16[4,128,1024]{2,1,0:T(8,128)(2,1)} %all-to-all-done.4, pred[]{:T(512)S(6)} %eq.12), kind=kLoop, calls=%fused_computation.38 | loop fusion | flops 524288 | bytes 3145729 | tf_op jit(solution)/shard_map/jit(_where)/select_n | solution.py:272
  141.8 2.7 %fusion.34 = bf16[128,1024]{1,0:T(8,128)(2,1)} fusion(bf16[128,1024]{1,0:T(8,128)(2,1)} %collective-permute-done.14, bf16[128,1024]{1,0:T(8,128)(2,1)} %collective-permute-done.13, bf16[128,1024]{1,0:T(8,128)(2,1)} %collective-permute-done.12, bf16[128,1024]{1,0:T(8,128)(2,1)S(1)} %copy-done.34, pred[128]{0:T(512)(128)(4,1)S(1)} %lt.63, ...), kind=kOutput, calls=%fused_computation.67 | convolution fusion | flops 270008320 | bytes 3670144 | tf_op jit(solution)/shard_map/dot_general | solution.py:29
  145.0 2.1 %collective-permute-start.16 = (bf16[128,1024]{1,0:T(8,128)(2,1)}, bf16[128,1024]{1,0:T(8,128)(2,1)S(1)}, u32[]{:S(2)}, u32[]{:S(2)}) collective-permute-start(bf16[128,1024]{1,0:T(8,128)(2,1)} %fusion.34), channel_id=1, source_target_pairs={{0,8},{1,9},{2,10},{3,11},{4,12},{5,13},{6,14},{7,15},{8,0},{9,1},... | collective-permute-start | bytes 786440 | tf_op jit(solution)/shard_map/ppermute | solution.py:44
  147.7 2.4 %copy.13 = bf16[8,128,320]{1,2,0:T(8,128)(2,1)} copy(bf16[8,128,320]{2,0,1:T(8,128)(2,1)} %bitcast.89) | data formatting | bytes 1310720 | tf_op jit(solution)/shard_map/optimization_barrier | solution.py:63
  150.1 4.2 %all-to-all-start.7 = ((bf16[8,128,320]{1,2,0:T(8,128)(2,1)}), bf16[8,128,320]{1,2,0:T(8,128)(2,1)S(1)}, u32[]{:S(2)}, u32[]{:S(2)}) async-start(bf16[8,128,320]{1,2,0:T(8,128)(2,1)} %copy.13), calls=%async_computation.7 | async-start | bytes 1310720 | tf_op jit(solution)/shard_map/all_to_all | solution.py:247
  154.3 9.8 %collective-permute-done.15 = bf16[128,1024]{1,0:T(8,128)(2,1)S(1)} collective-permute-done((bf16[128,1024]{1,0:T(8,128)(2,1)}, bf16[128,1024]{1,0:T(8,128)(2,1)S(1)}, u32[]{:S(2)}, u32[]{:S(2)}) %collective-permute-start.15) | collective-permute-done | bytes 262176 | tf_op jit(solution)/shard_map/ppermute | solution.py:44
  164.1 2.2 %pad_maximum_fusion = bf16[512,1024]{1,0:T(8,128)(2,1)} fusion(bf16[128,1024]{1,0:T(8,128)(2,1)S(1)} %collective-permute-done.17, bf16[128,1024]{1,0:T(8,128)(2,1)S(1)} %collective-permute-done.16, bf16[128,1024]{1,0:T(8,128)(2,1)S(1)} %collective-permute-done.15, bf16[128,1024]{1,0:T(8,128)(2,1)} %fusion.34), kind=kLoop, calls=%fused_computation.32 | loop fusion | flops 4194304 | bytes 2097152 | tf_op jit(solution)/shard_map/concatenate | solution.py:287
  166.4 2.8 %fusion.12 = f32[1024,1024,1]{1,0,2:T(8,128)S(1)} fusion(bf16[4,128,1024]{2,1,0:T(8,128)(2,1)} %all-to-all-done.4, bf16[4,128,1024]{2,1,0:T(8,128)(2,1)} %all-to-all-done.5, bf16[4,128,1024]{2,1,0:T(8,128)(2,1)} %all-to-all-done.1, bf16[4,128,1024]{2,1,0:T(8,128)(2,1)S(1)} %all-to-all-done.2, pred[]{:T(512)S(6)} %eq.12), kind=kOutput, calls=%fused_computation.33 | convolution fusion | flops 1074790400 | bytes 8388609 | tf_op jit(solution)/shard_map/dot_general | solution.py:33
  169.2 4.2 %fusion = bf16[1024,1024]{1,0:T(8,128)(2,1)} fusion(f32[1024,1024,1]{1,0,2:T(8,128)S(1)} %fusion.12, bf16[512,1024]{1,0:T(8,128)(2,1)} %collective-permute-done.10, bf16[512,1024]{1,0:T(8,128)(2,1)} %collective-permute-done.11), kind=kOutput, calls=%fused_computation.1 | convolution fusion | flops 1075838976 | bytes 8388608 | tf_op jit(solution)/shard_map/dot_general | solution.py:33
  174.3 3.6 %all-to-all-start.6 = ((bf16[4,256,1024]{2,1,0:T(8,128)(2,1)}), bf16[4,256,1024]{2,1,0:T(8,128)(2,1)S(1)}, u32[]{:S(2)}, u32[]{:S(2)}) async-start(bf16[4,256,1024]{2,1,0:T(8,128)(2,1)} %bitcast.87), calls=%async_computation.6 | async-start | bytes 4194304 | tf_op jit(solution)/shard_map/all_to_all | solution.py:280
  178.0 1.4 copy.14.arrived
  180.2 1.8 fusion.41
  182.0 1.5 fusion.1
  184.2 1.9 collective-permute-start.19
  186.2 2.7 %collective-permute-start.20 = (bf16[80,1024]{1,0:T(8,128)(2,1)}, bf16[80,1024]{1,0:T(8,128)(2,1)S(1)}, u32[]{:S(2)}, u32[]{:S(2)}) collective-permute-start(bf16[80,1024]{1,0:T(8,128)(2,1)} %get-tuple-element.52), channel_id=1, source_target_pairs={{0,2},{1,3},{2,0},{3,1},{4,6},{5,7},{6,4},{7,5},{8,10},{9,11},{10,... | collective-permute-start | bytes 491528 | tf_op jit(solution)/shard_map/ppermute | solution.py:51
  188.9 1.5 collective-permute-start.21
  190.3 9.1 %collective-permute-done.19 = bf16[80,1024]{1,0:T(8,128)(2,1)S(1)} collective-permute-done((bf16[80,1024]{1,0:T(8,128)(2,1)}, bf16[80,1024]{1,0:T(8,128)(2,1)S(1)}, u32[]{:S(2)}, u32[]{:S(2)}) %collective-permute-start.19) | collective-permute-done | bytes 163872 | tf_op jit(solution)/shard_map/ppermute | solution.py:51
  199.4 2.1 %collective-permute-done.20 = bf16[80,1024]{1,0:T(8,128)(2,1)S(1)} collective-permute-done((bf16[80,1024]{1,0:T(8,128)(2,1)}, bf16[80,1024]{1,0:T(8,128)(2,1)S(1)}, u32[]{:S(2)}, u32[]{:S(2)}) %collective-permute-start.20) | collective-permute-done | bytes 163872 | tf_op jit(solution)/shard_map/ppermute | solution.py:51
  202.3 1.3 convert_reduce_fusion
  (112 shorter events, 19.7 us)
Async XLA Ops:
  0.6 19.5 %collective-permute-start = (bf16[4096,1024]{1,0:T(8,128)(2,1)}, bf16[4096,1024]{1,0:T(8,128)(2,1)}, u32[]{:S(2)}, u32[]{:S(2)}) collective-permute-start(bf16[4096,1024]{1,0:T(8,128)(2,1)} %bitcast.85), channel_id=1, source_target_pairs={{0,64},{64,0},{1,65},{65,1},{2,66},{66,2},{3,67},{67,3},{4,68},{68... | collective-permute-start | bytes 25165832 | tf_op jit(solution)/shard_map/ppermute | solution.py:59
  0.8 13.3 %copy-start.19 = (s32[5]{0:T(128)}, s32[5]{0:T(128)S(1)}, u32[]{:S(2)}) copy-start(s32[5]{0:T(128)S(1)} %stack.23.place) | copy-start | bytes 64
  0.8 1.0 copy-start.17
  2.5 9.9 %copy-start.18 = (bf16[2,128,1024]{2,1,0:T(8,128)(2,1)S(1)}, bf16[2,128,1024]{2,1,0:T(8,128)(2,1)}, u32[]{:S(2)}) copy-start(bf16[2,128,1024]{2,1,0:T(8,128)(2,1)} %param.13) | copy-start | bytes 1572868
  4.2 9.9 %copy-start.29 = (bf16[4,32,2560]{2,1,0:T(8,128)(2,1)S(1)}, bf16[4,32,2560]{2,1,0:T(8,128)(2,1)}, u32[]{:S(2)}) copy-start(bf16[4,32,2560]{2,1,0:T(8,128)(2,1)} %param.7) | copy-start | bytes 1966084
  4.2 32.1 %all-to-all-start = ((bf16[16,32,1024]{2,1,0:T(8,128)(2,1)}), bf16[16,32,1024]{2,1,0:T(8,128)(2,1)S(1)}, u32[]{:S(2)}, u32[]{:S(2)}) async-start(bf16[16,32,1024]{2,1,0:T(8,128)(2,1)} %shard_map.86), calls=%async_computation | async-start | bytes 2097152 | tf_op jit(solution)/shard_map/all_to_all | solution.py:218
  20.1 16.2 %copy-start.20 = (s32[5]{0:T(128)S(1)}, s32[5]{0:T(128)}, u32[]{:S(2)}) copy-start(s32[5]{0:T(128)} %copy-done.19) | copy-start | bytes 64
  20.1 16.2 %copy-start.22 = (s32[128]{0:T(128)S(1)}, s32[128]{0:T(128)}, u32[]{:S(2)}) copy-start(s32[128]{0:T(128)} %routing.7) | copy-start | bytes 1540
  20.1 16.2 %copy-start.23 = (s32[128]{0:T(128)S(1)}, s32[128]{0:T(128)}, u32[]{:S(2)}) copy-start(s32[128]{0:T(128)} %counts.3) | copy-start | bytes 1540
  26.9 1.3 copy-start
  28.2 1.3 copy-start.3
  29.5 1.3 copy-start.4
  30.8 1.3 copy-start.6
  32.2 1.4 copy-start.9
  33.6 1.3 copy-start.12
  34.9 1.4 copy-start.14
  36.3 1.0 copy-start.16
  38.3 15.2 %collective-permute-start.1 = (bf16[128,1024]{1,0:T(8,128)(2,1)S(1)}, bf16[128,1024]{1,0:T(8,128)(2,1)}, u32[]{:S(2)}, u32[]{:S(2)}) collective-permute-start(bf16[128,1024]{1,0:T(8,128)(2,1)S(1)} %bitcast.76), channel_id=1, source_target_pairs={{0,16},{16,32},{32,48},{48,0},{1,17},{17,33},{33,49},{49,1},{2,18}... | collective-permute-start | bytes 786440 | tf_op jit(solution)/shard_map/ppermute | solution.py:37
  39.8 15.2 %collective-permute-start.2 = (bf16[128,1024]{1,0:T(8,128)(2,1)S(1)}, bf16[128,1024]{1,0:T(8,128)(2,1)}, u32[]{:S(2)}, u32[]{:S(2)}) collective-permute-start(bf16[128,1024]{1,0:T(8,128)(2,1)S(1)} %bitcast.77), channel_id=1, source_target_pairs={{0,32},{16,48},{32,0},{48,16},{1,33},{17,49},{33,1},{49,17},{2,34}... | collective-permute-start | bytes 786440 | tf_op jit(solution)/shard_map/ppermute | solution.py:37
  42.6 13.9 %collective-permute-start.3 = (bf16[128,1024]{1,0:T(8,128)(2,1)S(1)}, bf16[128,1024]{1,0:T(8,128)(2,1)}, u32[]{:S(2)}, u32[]{:S(2)}) collective-permute-start(bf16[128,1024]{1,0:T(8,128)(2,1)S(1)} %bitcast.78), channel_id=1, source_target_pairs={{0,48},{16,0},{32,16},{48,32},{1,49},{17,1},{33,17},{49,33},{2,50}... | collective-permute-start | bytes 786440 | tf_op jit(solution)/shard_map/ppermute | solution.py:37
  44.0 23.8 %all-to-all-start.3 = ((bf16[16,32,1024]{2,1,0:T(8,128)(2,1)}), bf16[16,32,1024]{2,1,0:T(8,128)(2,1)S(1)}, u32[]{:S(2)}, u32[]{:S(2)}) async-start(bf16[16,32,1024]{2,1,0:T(8,128)(2,1)} %shard_map.87), calls=%async_computation.3 | async-start | bytes 2097152 | tf_op jit(solution)/shard_map/all_to_all | solution.py:230
  51.2 2.2 %copy-start.7 = (bf16[1024,1024]{1,0:T(8,128)(2,1)S(1)}, bf16[1024,1024]{1,0:T(8,128)(2,1)}, u32[]{:S(2)}) copy-start(bf16[1024,1024]{1,0:T(8,128)(2,1)} %copy-done.6) | copy-start | bytes 6291460
  53.4 1.7 copy-start.1
  58.9 5.7 %copy-start.15 = (bf16[1024,1024]{1,0:T(8,128)(2,1)S(1)}, bf16[1024,1024]{1,0:T(8,128)(2,1)}, u32[]{:S(2)}) copy-start(bf16[1024,1024]{1,0:T(8,128)(2,1)} %copy-done.14) | copy-start | bytes 6291460
  58.9 16.3 %collective-permute-start.4 = (bf16[128,1024]{1,0:T(8,128)(2,1)}, bf16[128,1024]{1,0:T(8,128)(2,1)}, u32[]{:S(2)}, u32[]{:S(2)}) collective-permute-start(bf16[128,1024]{1,0:T(8,128)(2,1)} %get-tuple-element.53.in0), channel_id=1, source_target_pairs={{0,16},{16,32},{32,48},{48,0},{1,17},{17,33},{33,49},{49,1},{2,18}... | collective-permute-start | bytes 786440 | tf_op jit(solution)/shard_map/ppermute | solution.py:37
  59.5 13.5 %collective-permute-start.5 = (bf16[128,1024]{1,0:T(8,128)(2,1)}, bf16[128,1024]{1,0:T(8,128)(2,1)}, u32[]{:S(2)}, u32[]{:S(2)}) collective-permute-start(bf16[128,1024]{1,0:T(8,128)(2,1)} %get-tuple-element.53.in0), channel_id=1, source_target_pairs={{0,32},{16,48},{32,0},{48,16},{1,33},{17,49},{33,1},{49,17},{2,34}... | collective-permute-start | bytes 786440 | tf_op jit(solution)/shard_map/ppermute | solution.py:37
  60.8 14.4 %collective-permute-start.6 = (bf16[128,1024]{1,0:T(8,128)(2,1)}, bf16[128,1024]{1,0:T(8,128)(2,1)}, u32[]{:S(2)}, u32[]{:S(2)}) collective-permute-start(bf16[128,1024]{1,0:T(8,128)(2,1)} %get-tuple-element.53.in0), channel_id=1, source_target_pairs={{0,48},{16,0},{32,16},{48,32},{1,49},{17,1},{33,17},{49,33},{2,50}... | collective-permute-start | bytes 786440 | tf_op jit(solution)/shard_map/ppermute | solution.py:37
  67.8 17.3 %all-to-all-start.1 = ((bf16[4,128,1024]{2,1,0:T(8,128)(2,1)}), bf16[4,128,1024]{2,1,0:T(8,128)(2,1)}, u32[]{:S(2)}, u32[]{:S(2)}) async-start(bf16[4,128,1024]{2,1,0:T(8,128)(2,1)} %shard_map.90), calls=%async_computation.1 | async-start | bytes 2097152 | tf_op jit(solution)/shard_map/all_to_all | solution.py:55
  72.1 5.4 %copy-start.10 = (bf16[1024,1024]{1,0:T(8,128)(2,1)S(1)}, bf16[1024,1024]{1,0:T(8,128)(2,1)}, u32[]{:S(2)}) copy-start(bf16[1024,1024]{1,0:T(8,128)(2,1)} %copy-done.9) | copy-start | bytes 6291460
  72.1 5.4 %copy-start.28 = (f32[128,1024]{1,0:T(8,128)S(1)}, f32[128,1024]{1,0:T(8,128)}, u32[]{:S(2)}) copy-start(f32[128,1024]{1,0:T(8,128)} %fusion.39) | copy-start | bytes 1572868
  77.5 2.5 %copy-start.13 = (bf16[1024,1024]{1,0:T(8,128)(2,1)S(1)}, bf16[1024,1024]{1,0:T(8,128)(2,1)}, u32[]{:S(2)}) copy-start(bf16[1024,1024]{1,0:T(8,128)(2,1)} %copy-done.12) | copy-start | bytes 6291460
  85.1 17.9 %all-to-all-start.2 = ((bf16[4,128,1024]{2,1,0:T(8,128)(2,1)}), bf16[4,128,1024]{2,1,0:T(8,128)(2,1)S(1)}, u32[]{:S(2)}, u32[]{:S(2)}) async-start(bf16[4,128,1024]{2,1,0:T(8,128)(2,1)} %shard_map.91), calls=%async_computation.2 | async-start | bytes 2097152 | tf_op jit(solution)/shard_map/all_to_all | solution.py:55
  89.1 3.4 %copy-start.26 = (bf16[128,1024]{1,0:T(8,128)(2,1)S(1)}, bf16[128,1024]{1,0:T(8,128)(2,1)}, u32[]{:S(2)}) copy-start(bf16[128,1024]{1,0:T(8,128)(2,1)} %fusion.18) | copy-start | bytes 786436
  89.1 6.5 %copy-start.11 = (bf16[1024,1024]{1,0:T(8,128)(2,1)S(1)}, bf16[1024,1024]{1,0:T(8,128)(2,1)}, u32[]{:S(2)}) copy-start(bf16[1024,1024]{1,0:T(8,128)(2,1)} %copy-done.9) | copy-start | bytes 6291460
  97.1 12.9 %collective-permute-start.7 = (bf16[128,1024]{1,0:T(8,128)(2,1)}, bf16[128,1024]{1,0:T(8,128)(2,1)}, u32[]{:S(2)}, u32[]{:S(2)}) collective-permute-start(bf16[128,1024]{1,0:T(8,128)(2,1)} %convolution_convert_fusion.8), channel_id=1, source_target_pairs={{0,32},{16,48},{32,0},{48,16},{1,33},{17,49},{33,1},{49,17},{2,34}... | collective-permute-start | bytes 786440 | tf_op jit(solution)/shard_map/ppermute | solution.py:37
  99.7 10.3 %collective-permute-start.8 = (bf16[128,1024]{1,0:T(8,128)(2,1)}, bf16[128,1024]{1,0:T(8,128)(2,1)}, u32[]{:S(2)}, u32[]{:S(2)}) collective-permute-start(bf16[128,1024]{1,0:T(8,128)(2,1)} %convolution_convert_fusion.7), channel_id=1, source_target_pairs={{0,16},{16,32},{32,48},{48,0},{1,17},{17,33},{33,49},{49,1},{2,18}... | collective-permute-start | bytes 786440 | tf_op jit(solution)/shard_map/ppermute | solution.py:37
  99.7 10.3 %collective-permute-start.9 = (bf16[128,1024]{1,0:T(8,128)(2,1)}, bf16[128,1024]{1,0:T(8,128)(2,1)}, u32[]{:S(2)}, u32[]{:S(2)}) collective-permute-start(bf16[128,1024]{1,0:T(8,128)(2,1)} %convolution_convert_fusion.6), channel_id=1, source_target_pairs={{0,48},{16,0},{32,16},{48,32},{1,49},{17,1},{33,17},{49,33},{2,50}... | collective-permute-start | bytes 786440 | tf_op jit(solution)/shard_map/ppermute | solution.py:37
  105.1 15.8 %all-to-all-start.5 = ((bf16[4,128,1024]{2,1,0:T(8,128)(2,1)}), bf16[4,128,1024]{2,1,0:T(8,128)(2,1)}, u32[]{:S(2)}, u32[]{:S(2)}) async-start(bf16[4,128,1024]{2,1,0:T(8,128)(2,1)} %broadcast_in_dim.30), calls=%async_computation.5 | async-start | bytes 2097152 | tf_op jit(solution)/shard_map/all_to_all | solution.py:55
  110.0 4.0 %copy-start.2 = (bf16[1024,1024]{1,0:T(8,128)(2,1)S(1)}, bf16[1024,1024]{1,0:T(8,128)(2,1)}, u32[]{:S(2)}) copy-start(bf16[1024,1024]{1,0:T(8,128)(2,1)} %copy-done) | copy-start | bytes 6291460
  114.0 1.5 copy-start.24
  115.5 26.2 %collective-permute-start.12 = (bf16[128,1024]{1,0:T(8,128)(2,1)}, bf16[128,1024]{1,0:T(8,128)(2,1)}, u32[]{:S(2)}, u32[]{:S(2)}) collective-permute-start(bf16[128,1024]{1,0:T(8,128)(2,1)} %convolution_convert_fusion.4), channel_id=1, source_target_pairs={{0,32},{16,48},{32,0},{48,16},{1,33},{17,49},{33,1},{49,17},{2,34}... | collective-permute-start | bytes 786440 | tf_op jit(solution)/shard_map/ppermute | solution.py:37
  117.9 9.4 %copy-start.25 = (bf16[128,1024]{1,0:T(8,128)(2,1)S(1)}, bf16[128,1024]{1,0:T(8,128)(2,1)}, u32[]{:S(2)}) copy-start(bf16[128,1024]{1,0:T(8,128)(2,1)} %copy-done.24) | copy-start | bytes 786436
  122.9 16.5 %all-to-all-start.4 = ((bf16[4,128,1024]{2,1,0:T(8,128)(2,1)}), bf16[4,128,1024]{2,1,0:T(8,128)(2,1)}, u32[]{:S(2)}, u32[]{:S(2)}) async-start(bf16[4,128,1024]{2,1,0:T(8,128)(2,1)} %broadcast_in_dim.14), calls=%async_computation.4 | async-start | bytes 2097152 | tf_op jit(solution)/shard_map/all_to_all | solution.py:55
  127.3 2.4 %copy-start.8 = (bf16[1024,1024]{1,0:T(8,128)(2,1)S(1)}, bf16[1024,1024]{1,0:T(8,128)(2,1)}, u32[]{:S(2)}) copy-start(bf16[1024,1024]{1,0:T(8,128)(2,1)} %copy-done.6) | copy-start | bytes 6291460
  128.9 12.9 %collective-permute-start.13 = (bf16[128,1024]{1,0:T(8,128)(2,1)}, bf16[128,1024]{1,0:T(8,128)(2,1)}, u32[]{:S(2)}, u32[]{:S(2)}) collective-permute-start(bf16[128,1024]{1,0:T(8,128)(2,1)} %convolution_convert_fusion.3), channel_id=1, source_target_pairs={{0,16},{16,32},{32,48},{48,0},{1,17},{17,33},{33,49},{49,1},{2,18}... | collective-permute-start | bytes 786440 | tf_op jit(solution)/shard_map/ppermute | solution.py:37
  131.3 10.5 %collective-permute-start.14 = (bf16[128,1024]{1,0:T(8,128)(2,1)}, bf16[128,1024]{1,0:T(8,128)(2,1)}, u32[]{:S(2)}, u32[]{:S(2)}) collective-permute-start(bf16[128,1024]{1,0:T(8,128)(2,1)} %convolution_convert_fusion.2), channel_id=1, source_target_pairs={{0,48},{16,0},{32,16},{48,32},{1,49},{17,1},{33,17},{49,33},{2,50}... | collective-permute-start | bytes 786440 | tf_op jit(solution)/shard_map/ppermute | solution.py:37
  134.8 7.0 %copy-start.5 = (bf16[1024,1024]{1,0:T(8,128)(2,1)S(1)}, bf16[1024,1024]{1,0:T(8,128)(2,1)}, u32[]{:S(2)}) copy-start(bf16[1024,1024]{1,0:T(8,128)(2,1)} %copy-done.4) | copy-start | bytes 6291460
  134.8 34.5 %collective-permute-start.10 = (bf16[512,1024]{1,0:T(8,128)(2,1)}, bf16[512,1024]{1,0:T(8,128)(2,1)}, u32[]{:S(2)}, u32[]{:S(2)}) collective-permute-start(bf16[512,1024]{1,0:T(8,128)(2,1)} %bitcast.15), channel_id=1, source_target_pairs={{0,64},{64,0},{1,65},{65,1},{2,66},{66,2},{3,67},{67,3},{4,68},{68... | collective-permute-start | bytes 3145736 | tf_op jit(solution)/shard_map/ppermute | solution.py:59
  139.4 2.4 %copy-start.34 = (bf16[128,1024]{1,0:T(8,128)(2,1)S(1)}, bf16[128,1024]{1,0:T(8,128)(2,1)}, u32[]{:S(2)}) copy-start(bf16[128,1024]{1,0:T(8,128)(2,1)} %get-tuple-element.47) | copy-start | bytes 786436
  141.7 27.5 %collective-permute-start.11 = (bf16[512,1024]{1,0:T(8,128)(2,1)}, bf16[512,1024]{1,0:T(8,128)(2,1)}, u32[]{:S(2)}, u32[]{:S(2)}) collective-permute-start(bf16[512,1024]{1,0:T(8,128)(2,1)} %bitcast.16), channel_id=1, source_target_pairs={{0,64},{64,0},{1,65},{65,1},{2,66},{66,2},{3,67},{67,3},{4,68},{68... | collective-permute-start | bytes 3145736 | tf_op jit(solution)/shard_map/ppermute | solution.py:59
  144.5 19.7 %collective-permute-start.15 = (bf16[128,1024]{1,0:T(8,128)(2,1)}, bf16[128,1024]{1,0:T(8,128)(2,1)S(1)}, u32[]{:S(2)}, u32[]{:S(2)}) collective-permute-start(bf16[128,1024]{1,0:T(8,128)(2,1)} %fusion.34), channel_id=1, source_target_pairs={{0,4},{1,5},{2,6},{3,7},{4,8},{5,9},{6,10},{7,11},{8,12},{9,13},{1... | collective-permute-start | bytes 786440 | tf_op jit(solution)/shard_map/ppermute | solution.py:44
  145.0 19.1 %collective-permute-start.16 = (bf16[128,1024]{1,0:T(8,128)(2,1)}, bf16[128,1024]{1,0:T(8,128)(2,1)S(1)}, u32[]{:S(2)}, u32[]{:S(2)}) collective-permute-start(bf16[128,1024]{1,0:T(8,128)(2,1)} %fusion.34), channel_id=1, source_target_pairs={{0,8},{1,9},{2,10},{3,11},{4,12},{5,13},{6,14},{7,15},{8,0},{9,1},... | collective-permute-start | bytes 786440 | tf_op jit(solution)/shard_map/ppermute | solution.py:44
  147.1 17.0 %collective-permute-start.17 = (bf16[128,1024]{1,0:T(8,128)(2,1)}, bf16[128,1024]{1,0:T(8,128)(2,1)S(1)}, u32[]{:S(2)}, u32[]{:S(2)}) collective-permute-start(bf16[128,1024]{1,0:T(8,128)(2,1)} %fusion.34), channel_id=1, source_target_pairs={{0,12},{1,13},{2,14},{3,15},{4,0},{5,1},{6,2},{7,3},{8,4},{9,5},{1... | collective-permute-start | bytes 786440 | tf_op jit(solution)/shard_map/ppermute | solution.py:44
  150.1 23.4 %all-to-all-start.7 = ((bf16[8,128,320]{1,2,0:T(8,128)(2,1)}), bf16[8,128,320]{1,2,0:T(8,128)(2,1)S(1)}, u32[]{:S(2)}, u32[]{:S(2)}) async-start(bf16[8,128,320]{1,2,0:T(8,128)(2,1)} %copy.13), calls=%async_computation.7 | async-start | bytes 1310720 | tf_op jit(solution)/shard_map/all_to_all | solution.py:247
  164.1 5.1 %copy-start.30 = (bf16[128,1024]{1,0:T(8,128)(2,1)}, bf16[128,1024]{1,0:T(8,128)(2,1)S(1)}, u32[]{:S(2)}) copy-start(bf16[128,1024]{1,0:T(8,128)(2,1)S(1)} %collective-permute-done.16) | copy-start | bytes 786436
  164.1 5.1 %copy-start.32 = (bf16[128,1024]{1,0:T(8,128)(2,1)}, bf16[128,1024]{1,0:T(8,128)(2,1)S(1)}, u32[]{:S(2)}) copy-start(bf16[128,1024]{1,0:T(8,128)(2,1)S(1)} %collective-permute-done.17) | copy-start | bytes 786436
  166.4 13.8 %collective-permute-start.18 = (bf16[512,1024]{1,0:T(8,128)(2,1)}, bf16[512,1024]{1,0:T(8,128)(2,1)}, u32[]{:S(2)}, u32[]{:S(2)}) collective-permute-start(bf16[512,1024]{1,0:T(8,128)(2,1)} %pad_maximum_fusion), channel_id=1, source_target_pairs={{0,64},{64,0},{1,65},{65,1},{2,66},{66,2},{3,67},{67,3},{4,68},{68... | collective-permute-start | bytes 3145736 | tf_op jit(solution)/shard_map/ppermute | solution.py:59
  173.5 0.8 copy-start.27
  174.3 28.0 %all-to-all-start.6 = ((bf16[4,256,1024]{2,1,0:T(8,128)(2,1)}), bf16[4,256,1024]{2,1,0:T(8,128)(2,1)S(1)}, u32[]{:S(2)}, u32[]{:S(2)}) async-start(bf16[4,256,1024]{2,1,0:T(8,128)(2,1)} %bitcast.87), calls=%async_computation.6 | async-start | bytes 4194304 | tf_op jit(solution)/shard_map/all_to_all | solution.py:280
  180.1 1.9 copy-start.31
  180.1 1.9 copy-start.33
  184.2 15.1 %collective-permute-start.19 = (bf16[80,1024]{1,0:T(8,128)(2,1)}, bf16[80,1024]{1,0:T(8,128)(2,1)S(1)}, u32[]{:S(2)}, u32[]{:S(2)}) collective-permute-start(bf16[80,1024]{1,0:T(8,128)(2,1)} %get-tuple-element.50), channel_id=1, source_target_pairs={{0,1},{1,2},{2,3},{3,0},{4,5},{5,6},{6,7},{7,4},{8,9},{9,10},{10,1... | collective-permute-start | bytes 491528 | tf_op jit(solution)/shard_map/ppermute | solution.py:51
  186.2 15.3 %collective-permute-start.20 = (bf16[80,1024]{1,0:T(8,128)(2,1)}, bf16[80,1024]{1,0:T(8,128)(2,1)S(1)}, u32[]{:S(2)}, u32[]{:S(2)}) collective-permute-start(bf16[80,1024]{1,0:T(8,128)(2,1)} %get-tuple-element.52), channel_id=1, source_target_pairs={{0,2},{1,3},{2,0},{3,1},{4,6},{5,7},{6,4},{7,5},{8,10},{9,11},{10,... | collective-permute-start | bytes 491528 | tf_op jit(solution)/shard_map/ppermute | solution.py:51
  188.9 12.6 %collective-permute-start.21 = (bf16[80,1024]{1,0:T(8,128)(2,1)S(1)}, bf16[80,1024]{1,0:T(8,128)(2,1)S(1)}, u32[]{:S(2)}, u32[]{:S(2)}) collective-permute-start(bf16[80,1024]{1,0:T(8,128)(2,1)S(1)} %get-tuple-element.51), channel_id=1, source_target_pairs={{0,3},{1,0},{2,1},{3,2},{4,7},{5,4},{6,5},{7,6},{8,11},{9,8},{10,9... | collective-permute-start | bytes 491528 | tf_op jit(solution)/shard_map/ppermute | solution.py:51
  (1 other events, 0.7 us)

commit v4 on v3

--- a/solution.py
+++ b/solution.py
@@ -13,6 +13,7 @@
 SLOTS = 8
 ROWS = 32
 MINE = 4
+FETCH_ORDER = (0, 1, 3, 2)
 ANY = pl.BlockSpec(memory_space=pl.ANY)
 WHOLE = pl.BlockSpec(memory_space=pltpu.VMEM)
 SCALARS = pl.BlockSpec(memory_space=pltpu.SMEM)
@@ -114,41 +115,183 @@
     )(routing, counts, place, *operands).reshape(MINE * ROWS, columns)
 
 
-def turn_kernel(place, own, other, *outs_and_sems):
-    outs, sems = outs_and_sems[:-1], outs_and_sems[-1]
+def gelu_parts(x):
+    scale = 0.7978845608028654
+    t = jnp.tanh(scale * (x + 0.044715 * (x * x * x)))
+    cdf = 0.5 * (1.0 + t)
+    slope = cdf + 0.5 * x * (1.0 - t * t) * (scale * (1.0 + 3 * 0.044715 * (x * x)))
+    return x * cdf, slope
+
+
+def fetch_weights(section, place, own, other, held, sems):
     core, x = place[0], place[2]
+    size = held.shape[1]
+
+    def copy(source, d):
+        start = pl.multiple_of(lax.rem(x - d + SIDE, SIDE) * size, size)
+        return pltpu.make_async_copy(source.at[pl.ds(start, size)], held.at[d], sems.at[d])
+
+    for d in FETCH_ORDER:
+
+        @pl.when(core == section)
+        def _():
+            copy(own, d).start()
+
+        @pl.when(core != section)
+        def _():
+            copy(other, d).start()
+
+    return lambda d: copy(own, d).wait()
+
+
+def forward_product(wait, held, blocks):
+    total = None
+    for d in FETCH_ORDER:
+        wait(d)
+        product = dot(blocks[d][...], held[d])
+        total = product if total is None else total + product
+    return total
+
+
+def forward_kernel(place, own, other, b0, b1, b2, b3, hidden, slope, held, sems):
+    wait = fetch_weights(0, place, own, other, held, sems)
+    activation, slope[...] = gelu_parts(forward_product(wait, held, (b0, b1, b2, b3)))
+    hidden[...] = (b0[...].astype(F32) + activation).astype(BF)
+
+
+def send_terms(local, copies, held, terms, wait=None):
+    for n in range(SIDE):
+        copies[n] = local
+    for d in (2, 1, 3, 0):
+        block = (SIDE - d) % SIDE
+        if wait is not None:
+            wait(block)
+        terms[d][...] = dot_nt(local, held[block]).astype(BF)
+
+
+def middle_kernel(
+    place, own, other, b0, b1, b2, b3, upstream, copies, t0, t1, t2, t3, held, sems
+):
+    wait = fetch_weights(1, place, own, other, held, sems)
+    _, slope = gelu_parts(forward_product(wait, held, (b0, b1, b2, b3)))
+    local = (slope * upstream[...].astype(F32)).astype(BF)
+    send_terms(local, copies, held, (t0, t1, t2, t3))
+
+
+def summed(cotangent, terms):
+    total = terms[0][...].astype(F32)
+    for term in terms[1:]:
+        total = total + term[...].astype(F32)
+    return (cotangent[...].astype(F32) + total).astype(BF)
+
+
+def backward_kernel(
+    place, own, other, r0, r1, r2, r3, upstream, slope, cotangent, copies, t0, t1, t2, t3, held, sems
+):
+    wait = fetch_weights(0, place, own, other, held, sems)
+    now = summed(upstream, (r0, r1, r2, r3))
+    cotangent[...] = now
+    local = (slope[...] * now.astype(F32)).astype(BF)
+    send_terms(local, copies, held, (t0, t1, t2, t3), wait)
+
+
+def last_kernel(counts, place, r0, r1, r2, r3, cotangent, out):
+    now = summed(cotangent, (r0, r1, r2, r3))
+    first = (place[0] * 16 + place[1]) * MINE
+    row = lax.broadcasted_iota(jnp.int32, (ROWS, now.shape[1]), 0)
+    for j in range(MINE):
+        rows = pl.ds(j * ROWS, ROWS)
+        held = now[j * ROWS : (j + 1) * ROWS]
+        out[rows] = jnp.where(row < counts[first + j], held, jnp.zeros_like(held))
+
+
+def step(kernel, place, own, other, operands, outs):
+    rows, columns = own.shape
+    return pl.pallas_call(
+        kernel,
+        in_specs=[SCALARS, ANY, ANY] + [WHOLE] * len(operands),
+        out_specs=[WHOLE] * len(outs),
+        out_shape=outs,
+        scratch_shapes=[
+            pltpu.VMEM((SIDE, rows // SIDE, columns), own.dtype),
+            pltpu.SemaphoreType.DMA((SIDE,)),
+        ],
+        compiler_params=pltpu.CompilerParams(vmem_limit_bytes=24 * 1024 * 1024),
+    )(place, own, other, *operands)
+
+
+def weight_grad_kernel(place, *refs):
+    operands, out, held, sems = refs[:8], refs[8], refs[9], refs[10]
+    for section in range(2):
+
+        @pl.when(place[0] == section)
+        def _():
+            for n in range(4):
+                pltpu.make_async_copy(operands[section * 4 + n], held.at[n], sems.at[n]).start()
+
+    for n in range(4):
+        pltpu.make_async_copy(operands[n], held.at[n], sems.at[n]).wait()
+    size = held.shape[1] * held.shape[2]
+    rows, rows_far, local, local_far = (held[n].reshape(size, held.shape[3]) for n in range(4))
+    total = dot_tn(rows, local) + dot_tn(rows_far, local_far)
+    out[...] = total.astype(BF).reshape(out.shape)
+
+
+def weight_grad(place, operands):
+    shape = operands[0].shape
+    columns = shape[2]
+    return pl.pallas_call(
+        weight_grad_kernel,
+        in_specs=[SCALARS] + [ANY] * 8,
+        out_specs=WHOLE,
+        out_shape=jax.ShapeDtypeStruct((SIDE, columns // SIDE, columns), BF),
+        scratch_shapes=[pltpu.VMEM((4,) + shape, BF), pltpu.SemaphoreType.DMA((4,))],
+        compiler_params=pltpu.CompilerParams(vmem_limit_bytes=24 * 1024 * 1024),
+    )(place, *operands)
+
+
+def merger_kernel(place, act, *refs):
+    grads, outs, held = refs[:8], refs[8:12], refs[12]
+    total = None
+    for n in range(8):
+        product = dot_tn(act[n], grads[n][...])
+        total = product if total is None else total + product
+    held[...] = total
     size = outs[0].shape[0]
-
-    def copy(source, n):
-        block = lax.rem(x - n % SIDE + SIDE, SIDE)
-        start = pl.multiple_of(block * size, size)
-        return pltpu.make_async_copy(source.at[pl.ds(start, size)], outs[n], sems.at[n])
-
-    for n in range(2 * SIDE):
-
-        @pl.when(core == n // SIDE)
-        def _():
-            copy(own, n).start()
-
-        @pl.when(core != n // SIDE)
-        def _():
-            copy(other, n).start()
-
-    for n in range(2 * SIDE):
-        copy(own, n).wait()
-
-
-def turn(place, own, other):
-    rows, columns = own.shape
-    blocks = pl.pallas_call(
-        turn_kernel,
-        in_specs=[pl.BlockSpec(memory_space=pltpu.SMEM), ANY, ANY],
-        out_specs=[pl.BlockSpec(memory_space=pltpu.VMEM)] * (2 * SIDE),
-        scratch_shapes=[pltpu.SemaphoreType.DMA((2 * SIDE,))],
-        out_shape=[pltpu.VMEM((rows // SIDE, columns), own.dtype)] * (2 * SIDE),
-        compiler_params=pltpu.CompilerParams(vmem_limit_bytes=40 * 1024 * 1024),
-    )(place, own, other)
-    return (blocks[:SIDE], blocks[SIDE:])
+    for j in range(SIDE):
+        start = pl.multiple_of(lax.rem(place[3] + j, SIDE) * size, size)
+        outs[j][...] = held[pl.ds(start, size)].astype(BF)
+
+
+def merger_parts(place, act, grads):
+    columns = grads[0].shape[1]
+    rows = act.shape[2]
+    shape = jax.ShapeDtypeStruct((rows // SIDE, columns), BF)
+    return pl.pallas_call(
+        merger_kernel,
+        in_specs=[SCALARS] + [WHOLE] * 9,
+        out_specs=[WHOLE] * SIDE,
+        out_shape=[shape] * SIDE,
+        scratch_shapes=[pltpu.VMEM((rows, columns), F32)],
+        compiler_params=pltpu.CompilerParams(vmem_limit_bytes=16 * 1024 * 1024),
+    )(place, act, *grads)
+
+
+def split_kernel(activated, out):
+    size = out.shape[2]
+    for n in range(8):
+        out[n] = activated[:, n * size : (n + 1) * size]
+
+
+def split(activated):
+    rows, columns = activated.shape
+    return pl.pallas_call(
+        split_kernel,
+        in_specs=[WHOLE],
+        out_specs=WHOLE,
+        out_shape=jax.ShapeDtypeStruct((8, rows, columns // 8), activated.dtype),
+        compiler_params=SMALL,
+    )(activated)
 
 
 def order_kernel(section, place, in0, in1, in2, in3, out):
@@ -196,106 +339,93 @@
     )(place, arrived)
 
 
-def gelu_slope(preact):
-    _, pullback = jax.vjp(jax.nn.gelu, preact)
-    return pullback(jnp.ones_like(preact))[0]
-
-
 def on_device(patches, merger_weight, image_counts, routing, text_embed, llm_weight, upstream):
     core = lax.axis_index("segment")
     x = lax.axis_index("mp")
     replica = lax.axis_index("dp")
     z, y = replica // SIDE, replica % SIDE
     place = jnp.stack([core, replica, x, y, z]).astype(jnp.int32)
-    group = core * 16 + replica
     columns = merger_weight.shape[1]
     merger = patches.shape[2]
     tokens = MINE * ROWS
-
-    own_weight = llm_weight[0]
-    other_weight = swap(own_weight)
+    block = jax.ShapeDtypeStruct((tokens, columns), BF)
+    block4 = jax.ShapeDtypeStruct((SIDE, tokens, columns), BF)
+    groups = (Z_GROUPS, Y_GROUPS)
+
+    own = llm_weight[0]
+    other = swap(own)
     send_text = spread(routing, place, text_embed.reshape(SLOTS, ROWS, columns))
     arrived_text = lax.all_to_all(send_text, "dp", 0, 0, tiled=True)
-
     activated = jax.nn.gelu(patches.astype(F32)).astype(BF).reshape(tokens, merger)
     embeds = dot(activated, merger_weight).astype(BF).reshape(MINE, ROWS, columns)
-    act_parts = activated.reshape(tokens, 8, merger // 8).transpose(1, 0, 2)
+    act_parts = split(activated)
     send_ups = spread(routing, place, upstream.reshape(SLOTS, ROWS, columns))
-    weights = turn(place, own_weight, other_weight)
-    arrived_text, embeds, act_parts, send_ups, weights = lax.optimization_barrier(
-        (arrived_text, embeds, act_parts, send_ups, weights)
-    )
-    hidden = merge(routing, image_counts, place, arrived_text, embeds)
-
-    arrived_ups = lax.all_to_all(after(send_ups, hidden), "dp", 0, 0, tiled=True)
+    arrived_text, embeds, act_parts, send_ups, other = lax.optimization_barrier(
+        (arrived_text, embeds, act_parts, send_ups, other)
+    )
+    start = merge(routing, image_counts, place, arrived_text, embeds)
+
+    arrived_ups = lax.all_to_all(after(send_ups, start), "dp", 0, 0, tiled=True)
+    blocks0 = [start] + [along_x(start, d) for d in (1, 2, 3)]
+    hidden, slope = step(
+        forward_kernel, place, own, other, blocks0, [block, jax.ShapeDtypeStruct(block.shape, F32)]
+    )
+    blocks1 = [hidden] + [along_x(hidden, d) for d in (1, 2, 3)]
+    rows0 = exchange(order(0, place, blocks0), Z_GROUPS)
+    top = merge(routing, image_counts, place, arrived_ups)
     eights = [
         [c * 16 + zz * SIDE + yy for c in range(2) for zz in range(SIDE)] for yy in range(SIDE)
     ]
-
-    slopes = []
-    rows_of = []
-    for section in range(2):
-        blocks = [hidden] + [along_x(hidden, d) for d in (1, 2, 3)]
-        preact = dot(blocks[0], weights[section][0])
-        for d in (1, 3, 2):
-            preact = preact + dot(blocks[d], weights[section][d])
-        if section == 0:
-            hidden = (hidden.astype(F32) + jax.nn.gelu(preact)).astype(BF)
-        slopes.append(gelu_slope(preact))
-        rows_of.append((blocks, preact))
-
     act_cols = lax.all_to_all(
         after(act_parts, hidden), ("segment", "dp"), 0, 0, tiled=True, axis_index_groups=eights
     )
-    act_cols = line_up(place, act_cols).reshape(8 * tokens, merger // 8)
-    cotangent = merge(routing, image_counts, place, arrived_ups)
-    groups = (Z_GROUPS, Y_GROUPS)
-    all_rows = [
-        exchange(order(section, place, rows_of[section][0]), groups[section]) for section in (0, 1)
-    ]
-    all_locals = [None, None]
-    for section in (1, 0):
-        local = (slopes[section] * cotangent.astype(F32)).astype(BF)
-        terms = [
-            along_x(dot_nt(local, weights[section][SIDE - d]).astype(BF), d) for d in (2, 1, 3)
-        ]
-        terms.append(dot_nt(local, weights[section][0]).astype(BF))
-        inner = sum(term.astype(F32) for term in terms)
-        cotangent = (cotangent.astype(F32) + inner).astype(BF)
-        copies = jnp.broadcast_to(local[None], (SIDE,) + local.shape)
-        all_locals[section] = exchange(copies, groups[section])
-
-    def my_section(pair):
-        first, second = (blocks.reshape(SIDE * tokens, columns) for blocks in pair)
-        return (
-            jnp.where(core == 0, first, second),
-            swap(jnp.where(core == 0, second, first)),
-        )
-
-    rows, rows_swapped = my_section(all_rows)
-    local, local_swapped = my_section(all_locals)
-    part = dot_tn(rows, local) + dot_tn(rows_swapped, local_swapped)
-    part = part.astype(BF).reshape(SIDE, -1, columns)
+
+    local1, *terms = step(
+        middle_kernel, place, own, other, blocks1 + [top], [block4] + [block] * SIDE
+    )
+    terms = [terms[0]] + [along_x(terms[d], d) for d in (1, 2, 3)]
+    rows1 = exchange(order(1, place, blocks1), Y_GROUPS)
+    local1 = exchange(local1, Y_GROUPS)
+
+    cotangent, local0, *terms = step(
+        backward_kernel,
+        place,
+        own,
+        other,
+        terms + [top, slope],
+        [block, block4] + [block] * SIDE,
+    )
+    terms = [terms[0]] + [along_x(terms[d], d) for d in (1, 2, 3)]
+    local0 = exchange(local0, Z_GROUPS)
+    to_first, to_second = [(1, 0)], [(0, 1)]
+    operands = []
+    for mine, pairs in (
+        (rows0, to_first),
+        (local0, to_first),
+        (rows1, to_second),
+        (local1, to_second),
+    ):
+        operands.append((mine, lax.ppermute(mine, "segment", pairs)))
+    part = weight_grad(
+        place, operands[0] + operands[1] + operands[2] + operands[3]
+    )
     sums = [[c * 16 + n for n in g] for c, gs in ((0, Y_GROUPS), (1, Z_GROUPS)) for g in gs]
     part = lax.all_to_all(part, ("segment", "dp"), 0, 0, tiled=True, axis_index_groups=sums)
     llm_grad = jnp.sum(part.astype(F32), axis=0)[None]
 
-    counts = lax.dynamic_slice_in_dim(image_counts, group * MINE, MINE)
-    image_rows = (jnp.arange(ROWS)[None] < counts[:, None]).reshape(tokens)
-    image_grad = jnp.where(image_rows[:, None], cotangent, jnp.zeros((), BF))
-    grads = [image_grad] + [along_z(image_grad, e) for e in (1, 2, 3)]
-    grads = jnp.concatenate(grads, axis=0)
-    grads_swapped = swap(grads)
-    half = grads.shape[0]
-    part = dot_tn(act_cols[:half], grads) + dot_tn(act_cols[half:], grads_swapped)
-    part = part.astype(BF).reshape(SIDE, -1, columns)
-
-    def toward(j):
-        return lax.dynamic_index_in_dim(part, (y + j) % SIDE, 0, keepdims=False)
-
-    merger_grad = toward(0).astype(F32)
+    grad = pl.pallas_call(
+        last_kernel,
+        in_specs=[SCALARS, SCALARS] + [WHOLE] * 5,
+        out_specs=WHOLE,
+        out_shape=block,
+        compiler_params=SMALL,
+    )(image_counts, place, *terms, cotangent)
+    act_cols = line_up(place, act_cols)
+    grads = [grad] + [along_z(grad, e) for e in (1, 2, 3)]
+    parts = merger_parts(place, act_cols, grads + [swap(g) for g in grads])
+    merger_grad = parts[0].astype(F32)
     for j in (1, 2, 3):
-        merger_grad = merger_grad + along_y(toward(j), j).astype(F32)
+        merger_grad = merger_grad + along_y(parts[j], j).astype(F32)
     return (llm_grad, merger_grad)
 
 

time: 205 us -> 243 us (1.19)
  waiting for transfers between devices: 33.3 us -> 92.5 us
  matrix products: 49.3 us -> 3.35 us
  Pallas kernels: 17.1 us -> 33.7 us
  local copies, waits for them, and re-layouts: 23.6 us -> 32.3 us
  other arithmetic: 8.36 us -> 4.31 us
  starting transfers between devices: 70.8 us -> 74.2 us
    ppermute x12, waiting for transfers between devices: 0.92 us -> 48.8 us  [along_x(): lax.ppermute(block, 'mp', [(i, (i + distance) % SIDE) for i in range(SIDE)])]
    dot_general x12 -> x0, matrix products: 29.6 us -> none  [the longest x8 19.2 us: dot_nt(): lax.dot_general(a, b, (((1,), (1,)), ((), ())), preferred_element_type=F32)]
    pallas_call x1 -> x7, Pallas kernels: 6.73 us -> 24.5 us  [the longest x3 15.2 us: step(): pl.pallas_call(kernel, in_specs=[SCALARS, ANY, ANY] + [WHOLE] * len(opera...]
    dot_general x9 -> x1, matrix products: 19.8 us -> 3.35 us  [dot(): return jnp.dot(a, b, preferred_element_type=F32)]
    unnamed x70 -> x78, local copies, waits for them, and re-layouts: 13.1 us -> 28.5 us
    all_to_all x1, waiting for transfers between devices: 0.01 us -> 12 us  [on_device(): arrived_text = lax.all_to_all(send_text, 'dp', 0, 0, tiled=True)]
    ppermute x0 -> x4, starting transfers between devices: none -> 9.87 us  [on_device(): operands.append((mine, lax.ppermute(mine, 'segment', pairs)))]
    ppermute x12, starting transfers between devices: 20.7 us -> 15.1 us  [along_x(): lax.ppermute(block, 'mp', [(i, (i + distance) % SIDE) for i in range(SIDE)])]
  transfers between devices with their start and end apart: 30 -> 35, of which waited for: 8 -> 17; matrix products, arithmetic and copies ran while one was open for 33% -> 3% of each run, Pallas kernels for 8% -> 14%
where the time goes in v4:
time: 243 us; the launch traced here: 241 us
  waiting for transfers between devices  92.5 us (38%)
  starting transfers between devices  74.2 us (31%)
  Pallas kernels  33.7 us (14%)
  local copies, waits for them, and re-layouts  32.3 us (13%)
  other arithmetic  4.31 us (2%)
  matrix products  3.35 us (1%)
    ppermute x12, waiting for transfers between devices, along_x(): lax.ppermute(block, 'mp', [(i, (i + distance) % SIDE) for i in range(SIDE)])  48.8 us
    unnamed x78, local copies, waits for them, and re-layouts  28.5 us
    all_to_all x4, starting transfers between devices, exchange(): lax.all_to_all(blocks, 'dp', 0, 0, tiled=True, axis_index_groups=groups)  17.9 us
    pallas_call x3, Pallas kernels, step(): pl.pallas_call(kernel, in_specs=[SCALARS, ANY, ANY] + [WHOLE] * len(opera...  15.2 us
    ppermute x12, starting transfers between devices, along_x(): lax.ppermute(block, 'mp', [(i, (i + distance) % SIDE) for i in range(SIDE)])  15.1 us
    ppermute x3, waiting for transfers between devices, along_z(): return lax.ppermute(block, 'dp', pairs)  13.3 us
    all_to_all x1, waiting for transfers between devices, on_device(): arrived_text = lax.all_to_all(send_text, 'dp', 0, 0, tiled=True)  12 us
    ppermute x4, starting transfers between devices, on_device(): operands.append((mine, lax.ppermute(mine, 'segment', pairs)))  9.87 us
  transfers between devices with their start and end apart: 35, of which 17 were waited for; matrix products, arithmetic and copies ran while one was open for 3% of the time, Pallas kernels for 14%

profile of v4, /device:TPU:0, one launch (start us, length us, event | category | flops | bytes accessed | tf_op | source)
XLA Modules:
  0.0 241.3 jit_solution(16897921234187363061)
XLA Ops:
  0.8 1.0 copy-done.18
  2.5 1.6 shard_map.86
  4.2 8.3 %all-to-all-start = ((bf16[16,32,1024]{2,1,0:T(8,128)(2,1)}), bf16[16,32,1024]{2,1,0:T(8,128)(2,1)S(1)}, u32[]{:S(2)}, u32[]{:S(2)}) async-start(bf16[16,32,1024]{2,1,0:T(8,128)(2,1)} %shard_map.86), calls=%async_computation | async-start | bytes 2097152 | tf_op jit(solution)/shard_map/all_to_all | solution.py:358
  13.1 0.9 copy-done.3
  14.0 1.6 shard_map.88
  15.7 3.3 %convolution_convert_fusion = bf16[128,1024]{1,0:T(8,128)(2,1)S(1)} fusion(bf16[128,2560]{1,0:T(8,128)(2,1)S(1)} %bitcast.20, bf16[2560,1024]{1,0:T(8,128)(2,1)} %param.8), kind=kOutput, calls=%fused_computation.11 | convolution fusion | flops 671219712 | bytes 6160384 | tf_op jit(solution)/shard_map/dot_general | solution.py:26
  19.0 12.0 %all-to-all-done.arrived = bf16[16,32,1024]{2,1,0:T(8,128)(2,1)S(1)} async-done(((bf16[16,32,1024]{2,1,0:T(8,128)(2,1)}), bf16[16,32,1024]{2,1,0:T(8,128)(2,1)S(1)}, u32[]{:S(2)}, u32[]{:S(2)}) %all-to-all-start) | async-done | bytes 1048608 | tf_op jit(solution)/shard_map/all_to_all | solution.py:358
  31.0 1.0 shard_map.89
  32.0 3.7 %all-to-all-start.2 = ((bf16[16,32,1024]{2,1,0:T(8,128)(2,1)}), bf16[16,32,1024]{2,1,0:T(8,128)(2,1)S(1)}, u32[]{:S(2)}, u32[]{:S(2)}) async-start(bf16[16,32,1024]{2,1,0:T(8,128)(2,1)} %shard_map.88), calls=%async_computation.2 | async-start | bytes 2097152 | tf_op jit(solution)/shard_map/all_to_all | solution.py:368
  35.7 2.8 %collective-permute-start.3 = (bf16[128,1024]{1,0:T(8,128)(2,1)S(1)}, bf16[128,1024]{1,0:T(8,128)(2,1)S(1)}, u32[]{:S(2)}, u32[]{:S(2)}) collective-permute-start(bf16[128,1024]{1,0:T(8,128)(2,1)S(1)} %bitcast.21), channel_id=1, source_target_pairs={{0,48},{16,0},{32,16},{48,32},{1,49},{17,1},{33,17},{49,33},{2,50}... | collective-permute-start | bytes 786440 | tf_op jit(solution)/shard_map/ppermute | solution.py:38
  39.3 0.9 collective-permute-start.1
  40.2 8.9 %collective-permute-done.3.in3.b3 = bf16[128,1024]{1,0:T(8,128)(2,1)S(1)} collective-permute-done((bf16[128,1024]{1,0:T(8,128)(2,1)S(1)}, bf16[128,1024]{1,0:T(8,128)(2,1)S(1)}, u32[]{:S(2)}, u32[]{:S(2)}) %collective-permute-start.3) | collective-permute-done | bytes 262176 | tf_op jit(solution)/shard_map/ppermute | solution.py:38
  49.3 3.5 %collective-permute-done.1.in1.b1 = bf16[128,1024]{1,0:T(8,128)(2,1)S(1)} collective-permute-done((bf16[128,1024]{1,0:T(8,128)(2,1)S(1)}, bf16[128,1024]{1,0:T(8,128)(2,1)S(1)}, u32[]{:S(2)}, u32[]{:S(2)}) %collective-permute-start.1) | collective-permute-done | bytes 262176 | tf_op jit(solution)/shard_map/ppermute | solution.py:38
  52.7 1.7 shard_map.90
  55.1 4.4 %all-to-all-start.1 = ((bf16[4,128,1024]{2,1,0:T(8,128)(2,1)}), bf16[4,128,1024]{2,1,0:T(8,128)(2,1)S(1)}, u32[]{:S(2)}, u32[]{:S(2)}) async-start(bf16[4,128,1024]{2,1,0:T(8,128)(2,1)} %shard_map.90), calls=%async_computation.1 | async-start | bytes 2097152 | tf_op jit(solution)/shard_map/all_to_all | solution.py:56
  59.5 3.4 %copy-done = bf16[1,4096,1024]{2,1,0:T(8,128)(2,1)S(1)} copy-done((bf16[1,4096,1024]{2,1,0:T(8,128)(2,1)S(1)}, bf16[1,4096,1024]{2,1,0:T(8,128)(2,1)}, u32[]{:S(2)}) %copy-start) | copy-done | bytes 8388632
  62.8 0.9 copy-done.5
  63.8 3.0 %shard_map.91 = (bf16[128,1024]{1,0:T(8,128)(2,1)S(1)}, f32[128,1024]{1,0:T(8,128)S(1)}) custom-call(s32[5]{0:T(128)S(1)} %stack.23.place, bf16[4096,1024]{1,0:T(8,128)(2,1)S(1)} %bitcast.16, bf16[4096,1024]{1,0:T(8,128)(2,1)} %collective-permute-done.other, bf16[128,1024]{1,0:T(8,128)(2,1)S(1)} %bitcast.25, ...), custom_call_target="tpu_custom_call" | custom-call | tf_op jit(solution)/shard_map/pallas_call | solution.py:210
  69.0 0.8 collective-permute-start.5
  69.9 6.5 %collective-permute-done.7.b3.in3 = bf16[128,1024]{1,0:T(8,128)(2,1)S(1)} collective-permute-done((bf16[128,1024]{1,0:T(8,128)(2,1)S(1)}, bf16[128,1024]{1,0:T(8,128)(2,1)S(1)}, u32[]{:S(2)}, u32[]{:S(2)}) %collective-permute-start.7) | collective-permute-done | bytes 262176 | tf_op jit(solution)/shard_map/ppermute | solution.py:38
  76.3 2.6 %collective-permute-done.6.b2.in2 = bf16[128,1024]{1,0:T(8,128)(2,1)S(1)} collective-permute-done((bf16[128,1024]{1,0:T(8,128)(2,1)S(1)}, bf16[128,1024]{1,0:T(8,128)(2,1)S(1)}, u32[]{:S(2)}, u32[]{:S(2)}) %collective-permute-start.6) | collective-permute-done | bytes 262176 | tf_op jit(solution)/shard_map/ppermute | solution.py:38
  79.0 5.5 %collective-permute-done.5.b1.in1 = bf16[128,1024]{1,0:T(8,128)(2,1)S(1)} collective-permute-done((bf16[128,1024]{1,0:T(8,128)(2,1)S(1)}, bf16[128,1024]{1,0:T(8,128)(2,1)S(1)}, u32[]{:S(2)}, u32[]{:S(2)}) %collective-permute-start.5) | collective-permute-done | bytes 262176 | tf_op jit(solution)/shard_map/ppermute | solution.py:38
  84.4 1.7 shard_map.95
  88.9 4.2 %all-to-all-start.4 = ((bf16[4,128,1024]{2,1,0:T(8,128)(2,1)}), bf16[4,128,1024]{2,1,0:T(8,128)(2,1)S(1)}, u32[]{:S(2)}, u32[]{:S(2)}) async-start(bf16[4,128,1024]{2,1,0:T(8,128)(2,1)} %shard_map.95), calls=%async_computation.4 | async-start | bytes 2097152 | tf_op jit(solution)/shard_map/all_to_all | solution.py:56
  93.2 1.0 shard_map.92
  94.4 3.4 %copy-done.1 = bf16[1,4096,1024]{2,1,0:T(8,128)(2,1)S(1)} copy-done((bf16[1,4096,1024]{2,1,0:T(8,128)(2,1)S(1)}, bf16[1,4096,1024]{2,1,0:T(8,128)(2,1)}, u32[]{:S(2)}) %copy-start.1) | copy-done | bytes 8388632
  97.7 7.5 %shard_map.93 = (bf16[4,128,1024]{2,1,0:T(8,128)(2,1)S(1)}, bf16[128,1024]{1,0:T(8,128)(2,1)S(1)}, bf16[128,1024]{1,0:T(8,128)(2,1)S(1)}, bf16[128,1024]{1,0:T(8,128)(2,1)S(1)}, bf16[128,1024]{1,0:T(8,128)(2,1)S(1)}) custom-call(s32[5]{0:T(128)S(1)} %stack.23.place, bf16[4096,1024]{1,0:T(8,128)(2,1)S(1)} %bitcast.17, ...), custom_call_target="tpu_custom_call" | custom-call | tf_op jit(solution)/shard_map/pallas_call | solution.py:210
  105.2 1.0 copy-done.6
  109.1 4.8 %all-to-all-start.5 = ((bf16[4,128,1024]{2,1,0:T(8,128)(2,1)}), bf16[4,128,1024]{2,1,0:T(8,128)(2,1)S(1)}, u32[]{:S(2)}, u32[]{:S(2)}) async-start(bf16[4,128,1024]{2,1,0:T(8,128)(2,1)} %copy-done.6), calls=%async_computation.5 | async-start | bytes 2097152 | tf_op jit(solution)/shard_map/all_to_all | solution.py:56
  113.9 2.1 collective-permute-start.9
  116.0 1.3 collective-permute-start.10
  117.3 9.4 %collective-permute-done.8.r1 = bf16[128,1024]{1,0:T(8,128)(2,1)S(1)} collective-permute-done((bf16[128,1024]{1,0:T(8,128)(2,1)}, bf16[128,1024]{1,0:T(8,128)(2,1)S(1)}, u32[]{:S(2)}, u32[]{:S(2)}) %collective-permute-start.8) | collective-permute-done | bytes 262176 | tf_op jit(solution)/shard_map/ppermute | solution.py:38
  127.3 3.4 %copy-done.2 = bf16[1,4096,1024]{2,1,0:T(8,128)(2,1)S(1)} copy-done((bf16[1,4096,1024]{2,1,0:T(8,128)(2,1)S(1)}, bf16[1,4096,1024]{2,1,0:T(8,128)(2,1)}, u32[]{:S(2)}) %copy-start.2) | copy-done | bytes 8388632
  130.6 1.0 copy-done.17
  131.7 0.9 copy-done.21
  132.6 4.7 %shard_map.94 = (bf16[128,1024]{1,0:T(8,128)(2,1)S(1)}, bf16[4,128,1024]{2,1,0:T(8,128)(2,1)S(1)}, bf16[128,1024]{1,0:T(8,128)(2,1)S(1)}, bf16[128,1024]{1,0:T(8...) custom-call(s32[5]{0:T(128)S(1)} %stack.23.place, bf16[4096,1024]{1,0:T(8,128)(2,1)S(1)} %bitcast.18, ...), custom_call_target="tpu_custom_call" | custom-call | tf_op jit(solution)/shard_map/pallas_call | solution.py:210
  137.4 1.0 copy-done.7
  141.8 4.5 %all-to-all-start.3 = ((bf16[4,128,1024]{2,1,0:T(8,128)(2,1)}), bf16[4,128,1024]{2,1,0:T(8,128)(2,1)}, u32[]{:S(2)}, u32[]{:S(2)}) async-start(bf16[4,128,1024]{2,1,0:T(8,128)(2,1)} %copy-done.7), calls=%async_computation.3 | async-start | bytes 2097152 | tf_op jit(solution)/shard_map/all_to_all | solution.py:56
  146.4 1.3 collective-permute-start.4
  147.7 5.0 %collective-permute-start.12 = (bf16[4,128,1024]{2,1,0:T(8,128)(2,1)S(1)}, bf16[4,128,1024]{2,1,0:T(8,128)(2,1)}, u32[]{:S(2)}, u32[]{:S(2)}) collective-permute-start(bf16[4,128,1024]{2,1,0:T(8,128)(2,1)S(1)} %all-to-all-done.4.refs_4_), channel_id=1, source_target_pairs={{0,64},{1,65},{2,66},{3,67},{4,68},{5,69},{6,70},{7,71},{8,72},{9,... | collective-permute-start | bytes 3145736 | tf_op jit(solution)/shard_map/ppermute | solution.py:408
  152.6 2.3 collective-permute-start.13
  155.0 7.0 %all-to-all-done.3.refs_2_ = bf16[4,128,1024]{2,1,0:T(8,128)(2,1)} async-done(((bf16[4,128,1024]{2,1,0:T(8,128)(2,1)}), bf16[4,128,1024]{2,1,0:T(8,128)(2,1)}, u32[]{:S(2)}, u32[]{:S(2)}) %all-to-all-start.3) | async-done | bytes 1048608 | tf_op jit(solution)/shard_map/all_to_all | solution.py:56
  161.9 1.3 collective-permute-start.11
  163.2 2.2 copy.9
  165.5 4.2 %all-to-all-start.7 = ((bf16[8,128,320]{1,2,0:T(8,128)(2,1)}), bf16[8,128,320]{1,2,0:T(8,128)(2,1)}, u32[]{:S(2)}, u32[]{:S(2)}) async-start(bf16[8,128,320]{1,2,0:T(8,128)(2,1)} %copy.9), calls=%async_computation.7 | async-start | bytes 1310720 | tf_op jit(solution)/shard_map/all_to_all | solution.py:379
  169.7 6.2 %shard_map.96 = bf16[4,256,1024]{2,1,0:T(8,128)(2,1)} custom-call(s32[5]{0:T(128)S(1)} %stack.23.place, bf16[4,128,1024]{2,1,0:T(8,128)(2,1)S(1)} %all-to-all-done.1.refs_0_, bf16[4,128,1024]{2,1,0:T(8,128)(2,1)} %collective-permute-done.4.refs_1_, bf16[4,128,1024]{2,1,0:T(8,128)(2,1)} %all-to-all-done.3.refs_2_, ...), custom_call_target="tpu_custom_call" | custom-call | tf_op jit(solution)/shard_map/pallas_call | solution.py:243
  175.9 4.9 %all-to-all-done.7 = bf16[8,128,320]{1,2,0:T(8,128)(2,1)} async-done(((bf16[8,128,320]{1,2,0:T(8,128)(2,1)}), bf16[8,128,320]{1,2,0:T(8,128)(2,1)}, u32[]{:S(2)}, u32[]{:S(2)}) %all-to-all-start.7) | async-done | bytes 655392 | tf_op jit(solution)/shard_map/all_to_all | solution.py:379
  180.9 4.4 %all-to-all-start.6 = ((bf16[4,256,1024]{2,1,0:T(8,128)(2,1)}), bf16[4,256,1024]{2,1,0:T(8,128)(2,1)}, u32[]{:S(2)}, u32[]{:S(2)}) async-start(bf16[4,256,1024]{2,1,0:T(8,128)(2,1)} %shard_map.96), calls=%async_computation.6 | async-start | bytes 4194304 | tf_op jit(solution)/shard_map/all_to_all | solution.py:413
  185.3 1.0 collective-permute-start.14
  186.4 3.9 %collective-permute-start.15 = (bf16[128,1024]{1,0:T(8,128)(2,1)S(1)}, bf16[128,1024]{1,0:T(8,128)(2,1)S(1)}, u32[]{:S(2)}, u32[]{:S(2)}) collective-permute-start(bf16[128,1024]{1,0:T(8,128)(2,1)S(1)} %copy-done.32), channel_id=1, source_target_pairs={{0,32},{16,48},{32,0},{48,16},{1,33},{17,49},{33,1},{49,17},{2,34}... | collective-permute-start | bytes 786440 | tf_op jit(solution)/shard_map/ppermute | solution.py:38
  190.3 4.9 %collective-permute-done.14.r1 = bf16[128,1024]{1,0:T(8,128)(2,1)S(1)} collective-permute-done((bf16[128,1024]{1,0:T(8,128)(2,1)S(1)}, bf16[128,1024]{1,0:T(8,128)(2,1)S(1)}, u32[]{:S(2)}, u32[]{:S(2)}) %collective-permute-start.14) | collective-permute-done | bytes 262176 | tf_op jit(solution)/shard_map/ppermute | solution.py:38
  195.1 6.8 %collective-permute-done.15.r2 = bf16[128,1024]{1,0:T(8,128)(2,1)S(1)} collective-permute-done((bf16[128,1024]{1,0:T(8,128)(2,1)S(1)}, bf16[128,1024]{1,0:T(8,128)(2,1)S(1)}, u32[]{:S(2)}, u32[]{:S(2)}) %collective-permute-start.15) | collective-permute-done | bytes 262176 | tf_op jit(solution)/shard_map/ppermute | solution.py:38
  202.7 2.9 %collective-permute-start.19 = (bf16[128,1024]{1,0:T(8,128)(2,1)S(1)}, bf16[128,1024]{1,0:T(8,128)(2,1)S(1)}, u32[]{:S(2)}, u32[]{:S(2)}) collective-permute-start(bf16[128,1024]{1,0:T(8,128)(2,1)S(1)} %shard_map.98.refs_0_), channel_id=1, source_target_pairs={{0,12},{1,13},{2,14},{3,15},{4,0},{5,1},{6,2},{7,3},{8,4},{9,5},{1... | collective-permute-start | bytes 786440 | tf_op jit(solution)/shard_map/ppermute | solution.py:45
  205.6 0.9 collective-permute-start.18
  206.5 10.1 %collective-permute-done.19.refs_3_ = bf16[128,1024]{1,0:T(8,128)(2,1)S(1)} collective-permute-done((bf16[128,1024]{1,0:T(8,128)(2,1)S(1)}, bf16[128,1024]{1,0:T(8,128)(2,1)S(1)}, u32[]{:S(2)}, u32[]{:S(2)}) %collective-permute-start.19) | collective-permute-done | bytes 262176 | tf_op jit(solution)/shard_map/ppermute | solution.py:45
  217.2 3.2 %collective-permute-done.17.refs_1_ = bf16[128,1024]{1,0:T(8,128)(2,1)S(1)} collective-permute-done((bf16[128,1024]{1,0:T(8,128)(2,1)S(1)}, bf16[128,1024]{1,0:T(8,128)(2,1)S(1)}, u32[]{:S(2)}, u32[]{:S(2)}) %collective-permute-start.17) | collective-permute-done | bytes 262176 | tf_op jit(solution)/shard_map/ppermute | solution.py:45
  220.3 1.4 copy.10.arrived
  222.5 2.2 shard_map.99
  224.6 2.0 collective-permute-start.24
  226.7 2.7 %collective-permute-start.25 = (bf16[80,1024]{1,0:T(8,128)(2,1)S(1)}, bf16[80,1024]{1,0:T(8,128)(2,1)S(1)}, u32[]{:S(2)}, u32[]{:S(2)}) collective-permute-start(bf16[80,1024]{1,0:T(8,128)(2,1)S(1)} %get-tuple-element.48), channel_id=1, source_target_pairs={{0,2},{1,3},{2,0},{3,1},{4,6},{5,7},{6,4},{7,5},{8,10},{9,11},{10,... | collective-permute-start | bytes 491528 | tf_op jit(solution)/shard_map/ppermute | solution.py:52
  229.4 1.5 collective-permute-start.26
  230.9 1.9 collective-permute-done.24
  232.8 4.7 %collective-permute-done.25 = bf16[80,1024]{1,0:T(8,128)(2,1)S(1)} collective-permute-done((bf16[80,1024]{1,0:T(8,128)(2,1)S(1)}, bf16[80,1024]{1,0:T(8,128)(2,1)S(1)}, u32[]{:S(2)}, u32[]{:S(2)}) %collective-permute-start.25) | collective-permute-done | bytes 163872 | tf_op jit(solution)/shard_map/ppermute | solution.py:52
  238.3 3.0 %convert_reduce_fusion = f32[256,1024]{1,0:T(8,128)} fusion(bf16[4,256,1024]{2,1,0:T(8,128)(2,1)} %all-to-all-done.6), kind=kLoop, calls=%fused_computation | loop fusion | flops 1835008 | bytes 3145728 | tf_op jit(solution)/shard_map/reduce_sum | solution.py:414
  (105 shorter events, 18.2 us)
Async XLA Ops:
  0.6 30.4 %collective-permute-start = (bf16[4096,1024]{1,0:T(8,128)(2,1)}, bf16[4096,1024]{1,0:T(8,128)(2,1)}, u32[]{:S(2)}, u32[]{:S(2)}) collective-permute-start(bf16[4096,1024]{1,0:T(8,128)(2,1)} %bitcast.15), channel_id=1, source_target_pairs={{0,64},{64,0},{1,65},{65,1},{2,66},{66,2},{3,67},{67,3},{4,68},{68... | collective-permute-start | bytes 25165832 | tf_op jit(solution)/shard_map/ppermute | solution.py:60
  0.8 1.0 copy-start.18
  4.2 8.3 %copy-start.38 = (bf16[4,32,2560]{2,1,0:T(8,128)(2,1)S(1)}, bf16[4,32,2560]{2,1,0:T(8,128)(2,1)}, u32[]{:S(2)}) copy-start(bf16[4,32,2560]{2,1,0:T(8,128)(2,1)} %param.7) | copy-start | bytes 1966084
  4.2 26.8 %all-to-all-start = ((bf16[16,32,1024]{2,1,0:T(8,128)(2,1)}), bf16[16,32,1024]{2,1,0:T(8,128)(2,1)S(1)}, u32[]{:S(2)}, u32[]{:S(2)}) async-start(bf16[16,32,1024]{2,1,0:T(8,128)(2,1)} %shard_map.86), calls=%async_computation | async-start | bytes 2097152 | tf_op jit(solution)/shard_map/all_to_all | solution.py:358
  12.4 1.6 copy-start.19
  12.5 1.6 copy-start.27
  13.1 0.9 copy-start.3
  15.7 15.3 %copy-start.28 = (s32[128]{0:T(128)S(1)}, s32[128]{0:T(128)}, u32[]{:S(2)}) copy-start(s32[128]{0:T(128)} %counts.5) | copy-start | bytes 1540
  32.0 23.1 %all-to-all-start.2 = ((bf16[16,32,1024]{2,1,0:T(8,128)(2,1)}), bf16[16,32,1024]{2,1,0:T(8,128)(2,1)S(1)}, u32[]{:S(2)}, u32[]{:S(2)}) async-start(bf16[16,32,1024]{2,1,0:T(8,128)(2,1)} %shard_map.88), calls=%async_computation.2 | async-start | bytes 2097152 | tf_op jit(solution)/shard_map/all_to_all | solution.py:368
  35.7 13.4 %collective-permute-start.3 = (bf16[128,1024]{1,0:T(8,128)(2,1)S(1)}, bf16[128,1024]{1,0:T(8,128)(2,1)S(1)}, u32[]{:S(2)}, u32[]{:S(2)}) collective-permute-start(bf16[128,1024]{1,0:T(8,128)(2,1)S(1)} %bitcast.21), channel_id=1, source_target_pairs={{0,48},{16,0},{32,16},{48,32},{1,49},{17,1},{33,17},{49,33},{2,50}... | collective-permute-start | bytes 786440 | tf_op jit(solution)/shard_map/ppermute | solution.py:38
  38.5 10.8 %collective-permute-start.2 = (bf16[128,1024]{1,0:T(8,128)(2,1)S(1)}, bf16[128,1024]{1,0:T(8,128)(2,1)S(1)}, u32[]{:S(2)}, u32[]{:S(2)}) collective-permute-start(bf16[128,1024]{1,0:T(8,128)(2,1)S(1)} %bitcast.22), channel_id=1, source_target_pairs={{0,32},{16,48},{32,0},{48,16},{1,33},{17,49},{33,1},{49,17},{2,34}... | collective-permute-start | bytes 786440 | tf_op jit(solution)/shard_map/ppermute | solution.py:38
  39.3 13.4 %collective-permute-start.1 = (bf16[128,1024]{1,0:T(8,128)(2,1)S(1)}, bf16[128,1024]{1,0:T(8,128)(2,1)S(1)}, u32[]{:S(2)}, u32[]{:S(2)}) collective-permute-start(bf16[128,1024]{1,0:T(8,128)(2,1)S(1)} %bitcast.23), channel_id=1, source_target_pairs={{0,16},{16,32},{32,48},{48,0},{1,17},{17,33},{33,49},{49,1},{2,18}... | collective-permute-start | bytes 786440 | tf_op jit(solution)/shard_map/ppermute | solution.py:38
  54.4 0.7 copy-start.4
  55.1 33.8 %all-to-all-start.1 = ((bf16[4,128,1024]{2,1,0:T(8,128)(2,1)}), bf16[4,128,1024]{2,1,0:T(8,128)(2,1)S(1)}, u32[]{:S(2)}, u32[]{:S(2)}) async-start(bf16[4,128,1024]{2,1,0:T(8,128)(2,1)} %shard_map.90), calls=%async_computation.1 | async-start | bytes 2097152 | tf_op jit(solution)/shard_map/all_to_all | solution.py:56
  59.5 3.4 %copy-start = (bf16[1,4096,1024]{2,1,0:T(8,128)(2,1)S(1)}, bf16[1,4096,1024]{2,1,0:T(8,128)(2,1)}, u32[]{:S(2)}) copy-start(bf16[1,4096,1024]{2,1,0:T(8,128)(2,1)} %param.12) | copy-start | bytes 25165828
  62.8 0.9 copy-start.5
  66.8 0.8 copy-start.16
  67.6 8.7 %collective-permute-start.7 = (bf16[128,1024]{1,0:T(8,128)(2,1)S(1)}, bf16[128,1024]{1,0:T(8,128)(2,1)S(1)}, u32[]{:S(2)}, u32[]{:S(2)}) collective-permute-start(bf16[128,1024]{1,0:T(8,128)(2,1)S(1)} %get-tuple-element.29.b0.in0), channel_id=1, source_target_pairs={{0,48},{16,0},{32,16},{48,32},{1,49},{17,1},{33,17},{49,33},{2,50}... | collective-permute-start | bytes 786440 | tf_op jit(solution)/shard_map/ppermute | solution.py:38
  68.2 10.7 %collective-permute-start.6 = (bf16[128,1024]{1,0:T(8,128)(2,1)S(1)}, bf16[128,1024]{1,0:T(8,128)(2,1)S(1)}, u32[]{:S(2)}, u32[]{:S(2)}) collective-permute-start(bf16[128,1024]{1,0:T(8,128)(2,1)S(1)} %get-tuple-element.29.b0.in0), channel_id=1, source_target_pairs={{0,32},{16,48},{32,0},{48,16},{1,33},{17,49},{33,1},{49,17},{2,34}... | collective-permute-start | bytes 786440 | tf_op jit(solution)/shard_map/ppermute | solution.py:38
  69.0 15.4 %collective-permute-start.5 = (bf16[128,1024]{1,0:T(8,128)(2,1)S(1)}, bf16[128,1024]{1,0:T(8,128)(2,1)S(1)}, u32[]{:S(2)}, u32[]{:S(2)}) collective-permute-start(bf16[128,1024]{1,0:T(8,128)(2,1)S(1)} %get-tuple-element.29.b0.in0), channel_id=1, source_target_pairs={{0,16},{16,32},{32,48},{48,0},{1,17},{17,33},{33,49},{49,1},{2,18}... | collective-permute-start | bytes 786440 | tf_op jit(solution)/shard_map/ppermute | solution.py:38
  87.5 0.7 copy-start.12
  88.9 20.1 %all-to-all-start.4 = ((bf16[4,128,1024]{2,1,0:T(8,128)(2,1)}), bf16[4,128,1024]{2,1,0:T(8,128)(2,1)S(1)}, u32[]{:S(2)}, u32[]{:S(2)}) async-start(bf16[4,128,1024]{2,1,0:T(8,128)(2,1)} %shard_map.95), calls=%async_computation.4 | async-start | bytes 2097152 | tf_op jit(solution)/shard_map/all_to_all | solution.py:56
  93.2 1.0 copy-start.9
  93.2 1.0 copy-start.11
  93.2 1.1 copy-start.13
  93.2 1.2 copy-start.15
  94.4 3.4 %copy-start.1 = (bf16[1,4096,1024]{2,1,0:T(8,128)(2,1)S(1)}, bf16[1,4096,1024]{2,1,0:T(8,128)(2,1)}, u32[]{:S(2)}) copy-start(bf16[1,4096,1024]{2,1,0:T(8,128)(2,1)} %param.12) | copy-start | bytes 25165828
  105.2 1.0 copy-start.6
  106.9 0.7 copy-start.35
  107.6 0.7 copy-start.36
  109.1 32.8 %all-to-all-start.5 = ((bf16[4,128,1024]{2,1,0:T(8,128)(2,1)}), bf16[4,128,1024]{2,1,0:T(8,128)(2,1)S(1)}, u32[]{:S(2)}, u32[]{:S(2)}) async-start(bf16[4,128,1024]{2,1,0:T(8,128)(2,1)} %copy-done.6), calls=%async_computation.5 | async-start | bytes 2097152 | tf_op jit(solution)/shard_map/all_to_all | solution.py:56
  113.9 12.8 %collective-permute-start.8 = (bf16[128,1024]{1,0:T(8,128)(2,1)}, bf16[128,1024]{1,0:T(8,128)(2,1)S(1)}, u32[]{:S(2)}, u32[]{:S(2)}) collective-permute-start(bf16[128,1024]{1,0:T(8,128)(2,1)} %copy-done.37), channel_id=1, source_target_pairs={{0,16},{16,32},{32,48},{48,0},{1,17},{17,33},{33,49},{49,1},{2,18}... | collective-permute-start | bytes 786440 | tf_op jit(solution)/shard_map/ppermute | solution.py:38
  113.9 12.8 %collective-permute-start.9 = (bf16[128,1024]{1,0:T(8,128)(2,1)}, bf16[128,1024]{1,0:T(8,128)(2,1)S(1)}, u32[]{:S(2)}, u32[]{:S(2)}) collective-permute-start(bf16[128,1024]{1,0:T(8,128)(2,1)} %copy-done.36), channel_id=1, source_target_pairs={{0,32},{16,48},{32,0},{48,16},{1,33},{17,49},{33,1},{49,17},{2,34}... | collective-permute-start | bytes 786440 | tf_op jit(solution)/shard_map/ppermute | solution.py:38
  116.0 11.3 %collective-permute-start.10 = (bf16[128,1024]{1,0:T(8,128)(2,1)}, bf16[128,1024]{1,0:T(8,128)(2,1)S(1)}, u32[]{:S(2)}, u32[]{:S(2)}) collective-permute-start(bf16[128,1024]{1,0:T(8,128)(2,1)} %copy-done.35), channel_id=1, source_target_pairs={{0,48},{16,0},{32,16},{48,32},{1,49},{17,1},{33,17},{49,33},{2,50}... | collective-permute-start | bytes 786440 | tf_op jit(solution)/shard_map/ppermute | solution.py:38
  127.3 3.4 %copy-start.2 = (bf16[1,4096,1024]{2,1,0:T(8,128)(2,1)S(1)}, bf16[1,4096,1024]{2,1,0:T(8,128)(2,1)}, u32[]{:S(2)}) copy-start(bf16[1,4096,1024]{2,1,0:T(8,128)(2,1)} %param.12) | copy-start | bytes 25165828
  130.6 1.0 copy-start.17
  131.7 0.9 copy-start.21
  137.4 1.0 copy-start.7
  138.3 0.7 copy-start.22
  141.8 20.1 %all-to-all-start.3 = ((bf16[4,128,1024]{2,1,0:T(8,128)(2,1)}), bf16[4,128,1024]{2,1,0:T(8,128)(2,1)}, u32[]{:S(2)}, u32[]{:S(2)}) async-start(bf16[4,128,1024]{2,1,0:T(8,128)(2,1)} %copy-done.7), calls=%async_computation.3 | async-start | bytes 2097152 | tf_op jit(solution)/shard_map/all_to_all | solution.py:56
  146.4 23.3 %collective-permute-start.4 = (bf16[4,128,1024]{2,1,0:T(8,128)(2,1)S(1)}, bf16[4,128,1024]{2,1,0:T(8,128)(2,1)}, u32[]{:S(2)}, u32[]{:S(2)}) collective-permute-start(bf16[4,128,1024]{2,1,0:T(8,128)(2,1)S(1)} %all-to-all-done.1.refs_0_), channel_id=1, source_target_pairs={{64,0},{65,1},{66,2},{67,3},{68,4},{69,5},{70,6},{71,7},{72,8},{73... | collective-permute-start | bytes 3145736 | tf_op jit(solution)/shard_map/ppermute | solution.py:408
  147.7 22.0 %collective-permute-start.12 = (bf16[4,128,1024]{2,1,0:T(8,128)(2,1)S(1)}, bf16[4,128,1024]{2,1,0:T(8,128)(2,1)}, u32[]{:S(2)}, u32[]{:S(2)}) collective-permute-start(bf16[4,128,1024]{2,1,0:T(8,128)(2,1)S(1)} %all-to-all-done.4.refs_4_), channel_id=1, source_target_pairs={{0,64},{1,65},{2,66},{3,67},{4,68},{5,69},{6,70},{7,71},{8,72},{9,... | collective-permute-start | bytes 3145736 | tf_op jit(solution)/shard_map/ppermute | solution.py:408
  152.6 17.0 %collective-permute-start.13 = (bf16[4,128,1024]{2,1,0:T(8,128)(2,1)S(1)}, bf16[4,128,1024]{2,1,0:T(8,128)(2,1)}, u32[]{:S(2)}, u32[]{:S(2)}) collective-permute-start(bf16[4,128,1024]{2,1,0:T(8,128)(2,1)S(1)} %all-to-all-done.5.refs_6_), channel_id=1, source_target_pairs={{0,64},{1,65},{2,66},{3,67},{4,68},{5,69},{6,70},{7,71},{8,72},{9,... | collective-permute-start | bytes 3145736 | tf_op jit(solution)/shard_map/ppermute | solution.py:408
  161.9 7.8 %collective-permute-start.11 = (bf16[4,128,1024]{2,1,0:T(8,128)(2,1)}, bf16[4,128,1024]{2,1,0:T(8,128)(2,1)}, u32[]{:S(2)}, u32[]{:S(2)}) collective-permute-start(bf16[4,128,1024]{2,1,0:T(8,128)(2,1)} %all-to-all-done.3.refs_2_), channel_id=1, source_target_pairs={{64,0},{65,1},{66,2},{67,3},{68,4},{69,5},{70,6},{71,7},{72,8},{73... | collective-permute-start | bytes 3145736 | tf_op jit(solution)/shard_map/ppermute | solution.py:408
  165.5 15.4 %all-to-all-start.7 = ((bf16[8,128,320]{1,2,0:T(8,128)(2,1)}), bf16[8,128,320]{1,2,0:T(8,128)(2,1)}, u32[]{:S(2)}, u32[]{:S(2)}) async-start(bf16[8,128,320]{1,2,0:T(8,128)(2,1)} %copy.9), calls=%async_computation.7 | async-start | bytes 1310720 | tf_op jit(solution)/shard_map/all_to_all | solution.py:379
  175.9 9.4 %copy-start.34 = (bf16[128,1024]{1,0:T(8,128)(2,1)S(1)}, bf16[128,1024]{1,0:T(8,128)(2,1)}, u32[]{:S(2)}) copy-start(bf16[128,1024]{1,0:T(8,128)(2,1)} %copy-done.33) | copy-start | bytes 786436
  175.9 10.5 %copy-start.32 = (bf16[128,1024]{1,0:T(8,128)(2,1)S(1)}, bf16[128,1024]{1,0:T(8,128)(2,1)}, u32[]{:S(2)}) copy-start(bf16[128,1024]{1,0:T(8,128)(2,1)} %copy-done.31) | copy-start | bytes 786436
  175.9 14.3 %copy-start.30 = (bf16[128,1024]{1,0:T(8,128)(2,1)S(1)}, bf16[128,1024]{1,0:T(8,128)(2,1)}, u32[]{:S(2)}) copy-start(bf16[128,1024]{1,0:T(8,128)(2,1)} %copy-done.29) | copy-start | bytes 786436
  175.9 26.0 %copy-start.23 = (bf16[128,1024]{1,0:T(8,128)(2,1)S(1)}, bf16[128,1024]{1,0:T(8,128)(2,1)}, u32[]{:S(2)}) copy-start(bf16[128,1024]{1,0:T(8,128)(2,1)} %copy-done.22) | copy-start | bytes 786436
  175.9 26.0 %copy-start.25 = (bf16[128,1024]{1,0:T(8,128)(2,1)S(1)}, bf16[128,1024]{1,0:T(8,128)(2,1)}, u32[]{:S(2)}) copy-start(bf16[128,1024]{1,0:T(8,128)(2,1)} %copy-done.24) | copy-start | bytes 786436
  180.9 57.4 %all-to-all-start.6 = ((bf16[4,256,1024]{2,1,0:T(8,128)(2,1)}), bf16[4,256,1024]{2,1,0:T(8,128)(2,1)}, u32[]{:S(2)}, u32[]{:S(2)}) async-start(bf16[4,256,1024]{2,1,0:T(8,128)(2,1)} %shard_map.96), calls=%async_computation.6 | async-start | bytes 4194304 | tf_op jit(solution)/shard_map/all_to_all | solution.py:413
  185.3 9.8 %collective-permute-start.14 = (bf16[128,1024]{1,0:T(8,128)(2,1)S(1)}, bf16[128,1024]{1,0:T(8,128)(2,1)S(1)}, u32[]{:S(2)}, u32[]{:S(2)}) collective-permute-start(bf16[128,1024]{1,0:T(8,128)(2,1)S(1)} %copy-done.34), channel_id=1, source_target_pairs={{0,16},{16,32},{32,48},{48,0},{1,17},{17,33},{33,49},{49,1},{2,18}... | collective-permute-start | bytes 786440 | tf_op jit(solution)/shard_map/ppermute | solution.py:38
  186.4 15.6 %collective-permute-start.15 = (bf16[128,1024]{1,0:T(8,128)(2,1)S(1)}, bf16[128,1024]{1,0:T(8,128)(2,1)S(1)}, u32[]{:S(2)}, u32[]{:S(2)}) collective-permute-start(bf16[128,1024]{1,0:T(8,128)(2,1)S(1)} %copy-done.32), channel_id=1, source_target_pairs={{0,32},{16,48},{32,0},{48,16},{1,33},{17,49},{33,1},{49,17},{2,34}... | collective-permute-start | bytes 786440 | tf_op jit(solution)/shard_map/ppermute | solution.py:38
  190.3 11.7 %collective-permute-start.16 = (bf16[128,1024]{1,0:T(8,128)(2,1)S(1)}, bf16[128,1024]{1,0:T(8,128)(2,1)S(1)}, u32[]{:S(2)}, u32[]{:S(2)}) collective-permute-start(bf16[128,1024]{1,0:T(8,128)(2,1)S(1)} %copy-done.30), channel_id=1, source_target_pairs={{0,48},{16,0},{32,16},{48,32},{1,49},{17,1},{33,17},{49,33},{2,50}... | collective-permute-start | bytes 786440 | tf_op jit(solution)/shard_map/ppermute | solution.py:38
  202.7 14.0 %collective-permute-start.19 = (bf16[128,1024]{1,0:T(8,128)(2,1)S(1)}, bf16[128,1024]{1,0:T(8,128)(2,1)S(1)}, u32[]{:S(2)}, u32[]{:S(2)}) collective-permute-start(bf16[128,1024]{1,0:T(8,128)(2,1)S(1)} %shard_map.98.refs_0_), channel_id=1, source_target_pairs={{0,12},{1,13},{2,14},{3,15},{4,0},{5,1},{6,2},{7,3},{8,4},{9,5},{1... | collective-permute-start | bytes 786440 | tf_op jit(solution)/shard_map/ppermute | solution.py:45
  205.6 11.1 %collective-permute-start.18 = (bf16[128,1024]{1,0:T(8,128)(2,1)S(1)}, bf16[128,1024]{1,0:T(8,128)(2,1)S(1)}, u32[]{:S(2)}, u32[]{:S(2)}) collective-permute-start(bf16[128,1024]{1,0:T(8,128)(2,1)S(1)} %shard_map.98.refs_0_), channel_id=1, source_target_pairs={{0,8},{1,9},{2,10},{3,11},{4,12},{5,13},{6,14},{7,15},{8,0},{9,1},... | collective-permute-start | bytes 786440 | tf_op jit(solution)/shard_map/ppermute | solution.py:45
  206.4 13.9 %collective-permute-start.17 = (bf16[128,1024]{1,0:T(8,128)(2,1)S(1)}, bf16[128,1024]{1,0:T(8,128)(2,1)S(1)}, u32[]{:S(2)}, u32[]{:S(2)}) collective-permute-start(bf16[128,1024]{1,0:T(8,128)(2,1)S(1)} %shard_map.98.refs_0_), channel_id=1, source_target_pairs={{0,4},{1,5},{2,6},{3,7},{4,8},{5,9},{6,10},{7,11},{8,12},{9,13},{1... | collective-permute-start | bytes 786440 | tf_op jit(solution)/shard_map/ppermute | solution.py:45
  206.5 15.9 %collective-permute-start.20 = (bf16[128,1024]{1,0:T(8,128)(2,1)S(1)}, bf16[128,1024]{1,0:T(8,128)(2,1)S(1)}, u32[]{:S(2)}, u32[]{:S(2)}) collective-permute-start(bf16[128,1024]{1,0:T(8,128)(2,1)S(1)} %shard_map.98.refs_0_), channel_id=1, source_target_pairs={{0,64},{64,0},{1,65},{65,1},{2,66},{66,2},{3,67},{67,3},{4,68},{68... | collective-permute-start | bytes 786440 | tf_op jit(solution)/shard_map/ppermute | solution.py:60
  216.7 5.8 %collective-permute-start.23 = (bf16[128,1024]{1,0:T(8,128)(2,1)S(1)}, bf16[128,1024]{1,0:T(8,128)(2,1)S(1)}, u32[]{:S(2)}, u32[]{:S(2)}) collective-permute-start(bf16[128,1024]{1,0:T(8,128)(2,1)S(1)} %collective-permute-done.19.refs_3_), channel_id=1, source_target_pairs={{0,64},{64,0},{1,65},{65,1},{2,66},{66,2},{3,67},{67,3},{4,68},{68... | collective-permute-start | bytes 786440 | tf_op jit(solution)/shard_map/ppermute | solution.py:60
  216.7 5.8 %collective-permute-start.22 = (bf16[128,1024]{1,0:T(8,128)(2,1)S(1)}, bf16[128,1024]{1,0:T(8,128)(2,1)S(1)}, u32[]{:S(2)}, u32[]{:S(2)}) collective-permute-start(bf16[128,1024]{1,0:T(8,128)(2,1)S(1)} %collective-permute-done.18.refs_2_), channel_id=1, source_target_pairs={{0,64},{64,0},{1,65},{65,1},{2,66},{66,2},{3,67},{67,3},{4,68},{68... | collective-permute-start | bytes 786440 | tf_op jit(solution)/shard_map/ppermute | solution.py:60
  220.3 2.1 collective-permute-start.21
  224.6 8.1 %collective-permute-start.24 = (bf16[80,1024]{1,0:T(8,128)(2,1)S(1)}, bf16[80,1024]{1,0:T(8,128)(2,1)S(1)}, u32[]{:S(2)}, u32[]{:S(2)}) collective-permute-start(bf16[80,1024]{1,0:T(8,128)(2,1)S(1)} %get-tuple-element.47), channel_id=1, source_target_pairs={{0,1},{1,2},{2,3},{3,0},{4,5},{5,6},{6,7},{7,4},{8,9},{9,10},{10,1... | collective-permute-start | bytes 491528 | tf_op jit(solution)/shard_map/ppermute | solution.py:52
  226.7 10.8 %collective-permute-start.25 = (bf16[80,1024]{1,0:T(8,128)(2,1)S(1)}, bf16[80,1024]{1,0:T(8,128)(2,1)S(1)}, u32[]{:S(2)}, u32[]{:S(2)}) collective-permute-start(bf16[80,1024]{1,0:T(8,128)(2,1)S(1)} %get-tuple-element.48), channel_id=1, source_target_pairs={{0,2},{1,3},{2,0},{3,1},{4,6},{5,7},{6,4},{7,5},{8,10},{9,11},{10,... | collective-permute-start | bytes 491528 | tf_op jit(solution)/shard_map/ppermute | solution.py:52
  229.4 8.1 %collective-permute-start.26 = (bf16[80,1024]{1,0:T(8,128)(2,1)S(1)}, bf16[80,1024]{1,0:T(8,128)(2,1)S(1)}, u32[]{:S(2)}, u32[]{:S(2)}) collective-permute-start(bf16[80,1024]{1,0:T(8,128)(2,1)S(1)} %get-tuple-element.49), channel_id=1, source_target_pairs={{0,3},{1,0},{2,1},{3,2},{4,7},{5,4},{6,5},{7,6},{8,11},{9,8},{10,9... | collective-permute-start | bytes 491528 | tf_op jit(solution)/shard_map/ppermute | solution.py:52
  (10 other events, 7.0 us)

commit v5 on v4

--- a/solution.py
+++ b/solution.py
@@ -17,7 +17,7 @@
 ANY = pl.BlockSpec(memory_space=pl.ANY)
 WHOLE = pl.BlockSpec(memory_space=pltpu.VMEM)
 SCALARS = pl.BlockSpec(memory_space=pltpu.SMEM)
-SMALL = pltpu.CompilerParams(vmem_limit_bytes=6 * 1024 * 1024)
+LIMIT = pltpu.CompilerParams(vmem_limit_bytes=60 * 1024 * 1024)
 Z_GROUPS = [[z * SIDE + y for z in range(SIDE)] for y in range(SIDE)]
 Y_GROUPS = [[z * SIDE + y for y in range(SIDE)] for z in range(SIDE)]
 
@@ -81,7 +81,7 @@
         in_specs=[SCALARS, SCALARS, WHOLE],
         out_specs=WHOLE,
         out_shape=jax.ShapeDtypeStruct(shape, slots.dtype),
-        compiler_params=SMALL,
+        compiler_params=LIMIT,
     )(routing, place, slots)
 
 
@@ -111,7 +111,7 @@
         out_specs=WHOLE,
         scratch_shapes=[pltpu.SemaphoreType.DMA((MINE,))],
         out_shape=jax.ShapeDtypeStruct((MINE, ROWS, columns), arrived.dtype),
-        compiler_params=SMALL,
+        compiler_params=LIMIT,
     )(routing, counts, place, *operands).reshape(MINE * ROWS, columns)
 
 
@@ -159,9 +159,7 @@
     hidden[...] = (b0[...].astype(F32) + activation).astype(BF)
 
 
-def send_terms(local, copies, held, terms, wait=None):
-    for n in range(SIDE):
-        copies[n] = local
+def send_terms(local, held, terms, wait=None):
     for d in (2, 1, 3, 0):
         block = (SIDE - d) % SIDE
         if wait is not None:
@@ -170,12 +168,13 @@
 
 
 def middle_kernel(
-    place, own, other, b0, b1, b2, b3, upstream, copies, t0, t1, t2, t3, held, sems
+    place, own, other, b0, b1, b2, b3, upstream, out, t0, t1, t2, t3, held, sems
 ):
     wait = fetch_weights(1, place, own, other, held, sems)
     _, slope = gelu_parts(forward_product(wait, held, (b0, b1, b2, b3)))
     local = (slope * upstream[...].astype(F32)).astype(BF)
-    send_terms(local, copies, held, (t0, t1, t2, t3))
+    out[...] = local
+    send_terms(local, held, (t0, t1, t2, t3))
 
 
 def summed(cotangent, terms):
@@ -186,13 +185,14 @@
 
 
 def backward_kernel(
-    place, own, other, r0, r1, r2, r3, upstream, slope, cotangent, copies, t0, t1, t2, t3, held, sems
+    place, own, other, r0, r1, r2, r3, upstream, slope, cotangent, out, t0, t1, t2, t3, held, sems
 ):
     wait = fetch_weights(0, place, own, other, held, sems)
     now = summed(upstream, (r0, r1, r2, r3))
     cotangent[...] = now
     local = (slope[...] * now.astype(F32)).astype(BF)
-    send_terms(local, copies, held, (t0, t1, t2, t3), wait)
+    out[...] = local
+    send_terms(local, held, (t0, t1, t2, t3), wait)
 
 
 def last_kernel(counts, place, r0, r1, r2, r3, cotangent, out):
@@ -216,46 +216,64 @@
             pltpu.VMEM((SIDE, rows // SIDE, columns), own.dtype),
             pltpu.SemaphoreType.DMA((SIDE,)),
         ],
-        compiler_params=pltpu.CompilerParams(vmem_limit_bytes=24 * 1024 * 1024),
+        compiler_params=LIMIT,
     )(place, own, other, *operands)
 
 
-def weight_grad_kernel(place, *refs):
-    operands, out, held, sems = refs[:8], refs[8], refs[9], refs[10]
-    for section in range(2):
-
-        @pl.when(place[0] == section)
-        def _():
-            for n in range(4):
-                pltpu.make_async_copy(operands[section * 4 + n], held.at[n], sems.at[n]).start()
-
-    for n in range(4):
-        pltpu.make_async_copy(operands[n], held.at[n], sems.at[n]).wait()
-    size = held.shape[1] * held.shape[2]
-    rows, rows_far, local, local_far = (held[n].reshape(size, held.shape[3]) for n in range(4))
-    total = dot_tn(rows, local) + dot_tn(rows_far, local_far)
+def weight_grad_kernel(place, rows0, rows0_far, both1, both1_far, *refs):
+    locals0, out, rows, local, sems = refs[:8], refs[8], refs[9], refs[10], refs[11]
+    z = place[4]
+    count = rows0.shape[1]
+
+    def copy(source, to, n, which):
+        return pltpu.make_async_copy(source, to.at[n], sems.at[which, n])
+
+    @pl.when(place[0] == 0)
+    def _():
+        for far, source in enumerate((rows0, rows0_far)):
+            for e in range(SIDE):
+                n = far * SIDE + e
+                copy(source.at[lax.rem(z - e + SIDE, SIDE)], rows, n, 0).start()
+                copy(locals0[n], local, n, 1).start()
+
+    @pl.when(place[0] == 1)
+    def _():
+        for far, source in enumerate((both1, both1_far)):
+            for e in range(SIDE):
+                n = far * SIDE + e
+                copy(source.at[e, pl.ds(0, count)], rows, n, 0).start()
+                copy(source.at[e, pl.ds(count, count)], local, n, 1).start()
+
+    for n in range(2 * SIDE):
+        copy(rows0.at[0], rows, n, 0).wait()
+        copy(rows0.at[0], local, n, 1).wait()
+    columns = out.shape[2]
+    total = dot_tn(rows[...].reshape(-1, columns), local[...].reshape(-1, columns))
     out[...] = total.astype(BF).reshape(out.shape)
 
 
-def weight_grad(place, operands):
-    shape = operands[0].shape
-    columns = shape[2]
+def weight_grad(place, rows0, rows0_far, both1, both1_far, locals0):
+    _, count, columns = rows0.shape
+    held = pltpu.VMEM((2 * SIDE, count, columns), BF)
     return pl.pallas_call(
         weight_grad_kernel,
-        in_specs=[SCALARS] + [ANY] * 8,
+        in_specs=[SCALARS] + [ANY] * 12,
         out_specs=WHOLE,
         out_shape=jax.ShapeDtypeStruct((SIDE, columns // SIDE, columns), BF),
-        scratch_shapes=[pltpu.VMEM((4,) + shape, BF), pltpu.SemaphoreType.DMA((4,))],
-        compiler_params=pltpu.CompilerParams(vmem_limit_bytes=24 * 1024 * 1024),
-    )(place, *operands)
+        scratch_shapes=[held, held, pltpu.SemaphoreType.DMA((2, 2 * SIDE))],
+        compiler_params=LIMIT,
+    )(place, rows0, rows0_far, both1, both1_far, *locals0)
 
 
 def merger_kernel(place, act, *refs):
     grads, outs, held = refs[:8], refs[8:12], refs[12]
+    core, z = place[0], place[4]
     total = None
-    for n in range(8):
-        product = dot_tn(act[n], grads[n][...])
-        total = product if total is None else total + product
+    for far in range(2):
+        for e in range(SIDE):
+            n = lax.rem(core + far, 2) * SIDE + lax.rem(z - e + SIDE, SIDE)
+            product = dot(act[n], grads[far * SIDE + e][...])
+            total = product if total is None else total + product
     held[...] = total
     size = outs[0].shape[0]
     for j in range(SIDE):
@@ -265,7 +283,7 @@
 
 def merger_parts(place, act, grads):
     columns = grads[0].shape[1]
-    rows = act.shape[2]
+    rows = act.shape[1]
     shape = jax.ShapeDtypeStruct((rows // SIDE, columns), BF)
     return pl.pallas_call(
         merger_kernel,
@@ -273,31 +291,16 @@
         out_specs=[WHOLE] * SIDE,
         out_shape=[shape] * SIDE,
         scratch_shapes=[pltpu.VMEM((rows, columns), F32)],
-        compiler_params=pltpu.CompilerParams(vmem_limit_bytes=16 * 1024 * 1024),
+        compiler_params=LIMIT,
     )(place, act, *grads)
 
 
-def split_kernel(activated, out):
-    size = out.shape[2]
-    for n in range(8):
-        out[n] = activated[:, n * size : (n + 1) * size]
-
-
-def split(activated):
-    rows, columns = activated.shape
-    return pl.pallas_call(
-        split_kernel,
-        in_specs=[WHOLE],
-        out_specs=WHOLE,
-        out_shape=jax.ShapeDtypeStruct((8, rows, columns // 8), activated.dtype),
-        compiler_params=SMALL,
-    )(activated)
-
-
-def order_kernel(section, place, in0, in1, in2, in3, out):
+def order_kernel(section, place, in0, in1, in2, in3, *refs):
+    out = refs[-1]
     x = place[2]
     blocks = (in0, in1, in2, in3)
-    part = in0.shape[1] // SIDE
+    rows, columns = in0.shape
+    part = columns // SIDE
     for owner in range(SIDE):
         for d in range(SIDE):
 
@@ -307,36 +310,24 @@
                     out[owner] = blocks[d][...]
                 else:
                     for y in range(SIDE):
-                        out[y, :, pl.ds(owner * part, part)] = blocks[d][:, pl.ds(y * part, part)]
-
-
-def order(section, place, blocks):
-    shape = (SIDE,) + blocks[0].shape
+                        out[y, pl.ds(0, rows), pl.ds(owner * part, part)] = blocks[d][
+                            :, pl.ds(y * part, part)
+                        ]
+
+    if section == 1:
+        for y in range(SIDE):
+            out[y, pl.ds(rows, rows)] = refs[0][...]
+
+
+def order(section, place, operands):
+    rows, columns = operands[0].shape
     return pl.pallas_call(
         functools.partial(order_kernel, section),
-        in_specs=[SCALARS] + [WHOLE] * SIDE,
+        in_specs=[SCALARS] + [WHOLE] * len(operands),
         out_specs=WHOLE,
-        out_shape=jax.ShapeDtypeStruct(shape, blocks[0].dtype),
-        compiler_params=SMALL,
-    )(place, *blocks)
-
-
-def line_up_kernel(place, arrived, out):
-    core, z = place[0], place[4]
-    for other in range(2):
-        for e in range(SIDE):
-            block = lax.rem(core + other, 2) * SIDE + lax.rem(z - e + SIDE, SIDE)
-            out[other * SIDE + e] = arrived[block]
-
-
-def line_up(place, arrived):
-    return pl.pallas_call(
-        line_up_kernel,
-        in_specs=[SCALARS, WHOLE],
-        out_specs=WHOLE,
-        out_shape=jax.ShapeDtypeStruct(arrived.shape, arrived.dtype),
-        compiler_params=SMALL,
-    )(place, arrived)
+        out_shape=jax.ShapeDtypeStruct((SIDE, rows * (section + 1), columns), BF),
+        compiler_params=LIMIT,
+    )(place, *operands)
 
 
 def on_device(patches, merger_weight, image_counts, routing, text_embed, llm_weight, upstream):
@@ -349,8 +340,6 @@
     merger = patches.shape[2]
     tokens = MINE * ROWS
     block = jax.ShapeDtypeStruct((tokens, columns), BF)
-    block4 = jax.ShapeDtypeStruct((SIDE, tokens, columns), BF)
-    groups = (Z_GROUPS, Y_GROUPS)
 
     own = llm_weight[0]
     other = swap(own)
@@ -358,57 +347,45 @@
     arrived_text = lax.all_to_all(send_text, "dp", 0, 0, tiled=True)
     activated = jax.nn.gelu(patches.astype(F32)).astype(BF).reshape(tokens, merger)
     embeds = dot(activated, merger_weight).astype(BF).reshape(MINE, ROWS, columns)
-    act_parts = split(activated)
+    act_parts = activated.T.reshape(8, merger // 8, tokens)
     send_ups = spread(routing, place, upstream.reshape(SLOTS, ROWS, columns))
-    arrived_text, embeds, act_parts, send_ups, other = lax.optimization_barrier(
-        (arrived_text, embeds, act_parts, send_ups, other)
+    arrived_ups = lax.all_to_all(after(send_ups, embeds), "dp", 0, 0, tiled=True)
+    arrived_text, embeds, act_parts, other = lax.optimization_barrier(
+        (arrived_text, embeds, act_parts, other)
     )
     start = merge(routing, image_counts, place, arrived_text, embeds)
 
-    arrived_ups = lax.all_to_all(after(send_ups, start), "dp", 0, 0, tiled=True)
     blocks0 = [start] + [along_x(start, d) for d in (1, 2, 3)]
-    hidden, slope = step(
-        forward_kernel, place, own, other, blocks0, [block, jax.ShapeDtypeStruct(block.shape, F32)]
-    )
-    blocks1 = [hidden] + [along_x(hidden, d) for d in (1, 2, 3)]
-    rows0 = exchange(order(0, place, blocks0), Z_GROUPS)
-    top = merge(routing, image_counts, place, arrived_ups)
     eights = [
         [c * 16 + zz * SIDE + yy for c in range(2) for zz in range(SIDE)] for yy in range(SIDE)
     ]
     act_cols = lax.all_to_all(
-        after(act_parts, hidden), ("segment", "dp"), 0, 0, tiled=True, axis_index_groups=eights
-    )
+        after(act_parts, blocks0[1]), ("segment", "dp"), 0, 0, tiled=True, axis_index_groups=eights
+    )
+    hidden, slope = step(
+        forward_kernel, place, own, other, blocks0, [block, jax.ShapeDtypeStruct(block.shape, F32)]
+    )
+    blocks1 = [hidden] + [along_x(hidden, d) for d in (1, 2, 3)]
+    rows0 = exchange(after(order(0, place, blocks0), blocks1[1]), Z_GROUPS)
+    top = merge(routing, image_counts, place, arrived_ups)
 
     local1, *terms = step(
-        middle_kernel, place, own, other, blocks1 + [top], [block4] + [block] * SIDE
+        middle_kernel, place, own, other, blocks1 + [top], [block] + [block] * SIDE
     )
     terms = [terms[0]] + [along_x(terms[d], d) for d in (1, 2, 3)]
-    rows1 = exchange(order(1, place, blocks1), Y_GROUPS)
-    local1 = exchange(local1, Y_GROUPS)
+    both1 = order(1, place, blocks1 + [local1])
+    both1 = exchange(after(both1, terms[1]), Y_GROUPS)
 
     cotangent, local0, *terms = step(
-        backward_kernel,
-        place,
-        own,
-        other,
-        terms + [top, slope],
-        [block, block4] + [block] * SIDE,
+        backward_kernel, place, own, other, terms + [top, slope], [block] * (2 + SIDE)
     )
     terms = [terms[0]] + [along_x(terms[d], d) for d in (1, 2, 3)]
-    local0 = exchange(local0, Z_GROUPS)
     to_first, to_second = [(1, 0)], [(0, 1)]
-    operands = []
-    for mine, pairs in (
-        (rows0, to_first),
-        (local0, to_first),
-        (rows1, to_second),
-        (local1, to_second),
-    ):
-        operands.append((mine, lax.ppermute(mine, "segment", pairs)))
-    part = weight_grad(
-        place, operands[0] + operands[1] + operands[2] + operands[3]
-    )
+    rows0_far = lax.ppermute(rows0, "segment", to_first)
+    both1_far = lax.ppermute(both1, "segment", to_second)
+    locals0 = [local0] + [along_z(local0, e) for e in (1, 2, 3)]
+    locals0 += [lax.ppermute(value, "segment", to_first) for value in locals0]
+    part = weight_grad(place, rows0, rows0_far, both1, both1_far, locals0)
     sums = [[c * 16 + n for n in g] for c, gs in ((0, Y_GROUPS), (1, Z_GROUPS)) for g in gs]
     part = lax.all_to_all(part, ("segment", "dp"), 0, 0, tiled=True, axis_index_groups=sums)
     llm_grad = jnp.sum(part.astype(F32), axis=0)[None]
@@ -418,9 +395,8 @@
         in_specs=[SCALARS, SCALARS] + [WHOLE] * 5,
         out_specs=WHOLE,
         out_shape=block,
-        compiler_params=SMALL,
+        compiler_params=LIMIT,
     )(image_counts, place, *terms, cotangent)
-    act_cols = line_up(place, act_cols)
     grads = [grad] + [along_z(grad, e) for e in (1, 2, 3)]
     parts = merger_parts(place, act_cols, grads + [swap(g) for g in grads])
     merger_grad = parts[0].astype(F32)

time: 243 us -> 255 us (1.049)
  blocking collectives: 0 us -> 28.3 us
  local copies, waits for them, and re-layouts: 32.3 us -> 8.04 us
  Pallas kernels: 33.7 us -> 51.7 us
  waiting for transfers between devices: 92.5 us -> 87.2 us
  starting transfers between devices: 74.2 us -> 69.7 us
    all_to_all x0 -> x1, blocking collectives: none -> 28.3 us  [exchange(): lax.all_to_all(blocks, 'dp', 0, 0, tiled=True, axis_index_groups=groups)]
    unnamed x78 -> x66, local copies, waits for them, and re-layouts: 28.5 us -> 6.29 us
    ppermute x12, waiting for transfers between devices: 48.8 us -> 32.5 us  [along_x(): lax.ppermute(block, 'mp', [(i, (i + distance) % SIDE) for i in range(SIDE)])]
    all_to_all x4 -> x1, starting transfers between devices: 17.9 us -> 4.07 us  [exchange(): lax.all_to_all(blocks, 'dp', 0, 0, tiled=True, axis_index_groups=groups)]
    ppermute x3 -> x6, waiting for transfers between devices: 13.3 us -> 24.4 us  [along_z(): return lax.ppermute(block, 'dp', pairs)]
    pallas_call x3, Pallas kernels: 15.2 us -> 24.3 us  [step(): pl.pallas_call(kernel, in_specs=[SCALARS, ANY, ANY] + [WHOLE] * len(opera...]
    ppermute x3 -> x6, starting transfers between devices: 3.85 us -> 11.2 us  [along_z(): return lax.ppermute(block, 'dp', pairs)]
    ppermute x12, starting transfers between devices: 15.1 us -> 20.5 us  [along_x(): lax.ppermute(block, 'mp', [(i, (i + distance) % SIDE) for i in range(SIDE)])]
  transfers between devices with their start and end apart: 35 -> 37, of which waited for: 17 -> 20; matrix products, arithmetic and copies ran while one was open for 3% -> 3% of each run, Pallas kernels for 14% -> 17%
where the time goes in v5:
time: 255 us; the launch traced here: 254 us
  waiting for transfers between devices  87.2 us (34%)
  starting transfers between devices  69.7 us (27%)
  Pallas kernels  51.7 us (20%)
  blocking collectives  28.3 us (11%)
  local copies, waits for them, and re-layouts  8.04 us (3%)
  matrix products  4.04 us (2%)
  other arithmetic  3.51 us (1%)
    ppermute x12, waiting for transfers between devices, along_x(): lax.ppermute(block, 'mp', [(i, (i + distance) % SIDE) for i in range(SIDE)])  32.5 us
    all_to_all x1, blocking collectives, exchange(): lax.all_to_all(blocks, 'dp', 0, 0, tiled=True, axis_index_groups=groups)  28.3 us
    ppermute x6, waiting for transfers between devices, along_z(): return lax.ppermute(block, 'dp', pairs)  24.4 us
    pallas_call x3, Pallas kernels, step(): pl.pallas_call(kernel, in_specs=[SCALARS, ANY, ANY] + [WHOLE] * len(opera...  24.3 us
    ppermute x12, starting transfers between devices, along_x(): lax.ppermute(block, 'mp', [(i, (i + distance) % SIDE) for i in range(SIDE)])  20.5 us
    all_to_all x1, waiting for transfers between devices, on_device(): arrived_text = lax.all_to_all(send_text, 'dp', 0, 0, tiled=True)  11.8 us
    ppermute x6, starting transfers between devices, along_z(): return lax.ppermute(block, 'dp', pairs)  11.2 us
    ppermute x3, waiting for transfers between devices, along_y(): return lax.ppermute(block, 'dp', pairs)  8.56 us
  transfers between devices with their start and end apart: 37, of which 20 were waited for; matrix products, arithmetic and copies ran while one was open for 3% of the time, Pallas kernels for 17%

profile of v5, /device:TPU:0, one launch (start us, length us, event | category | flops | bytes accessed | tf_op | source)
XLA Modules:
  0.0 253.5 jit_solution(13794662915841472595)
XLA Ops:
  1.4 2.1 shard_map.86
  3.6 8.1 %all-to-all-start = ((bf16[16,32,1024]{2,1,0:T(8,128)(2,1)}), bf16[16,32,1024]{2,1,0:T(8,128)(2,1)S(1)}, u32[]{:S(2)}, u32[]{:S(2)}) async-start(bf16[16,32,1024]{2,1,0:T(8,128)(2,1)} %shard_map.86), calls=%async_computation | async-start | bytes 2097152 | tf_op jit(solution)/shard_map/all_to_all | solution.py:347
  11.7 2.2 shard_map.90
  14.4 4.0 %convolution_convert_fusion = bf16[128,1024]{1,0:T(8,128)(2,1)} fusion(bf16[128,2560]{1,0:T(8,128)(2,1)S(1)} %bitcast.22, bf16[2560,1024]{1,0:T(8,128)(2,1)} %param.8), kind=kOutput, calls=%fused_computation.11 | convolution fusion | flops 671219712 | bytes 6160384 | tf_op jit(solution)/shard_map/dot_general | solution.py:26
  18.4 11.8 %all-to-all-done.arrived = bf16[16,32,1024]{2,1,0:T(8,128)(2,1)S(1)} async-done(((bf16[16,32,1024]{2,1,0:T(8,128)(2,1)}), bf16[16,32,1024]{2,1,0:T(8,128)(2,1)S(1)}, u32[]{:S(2)}, u32[]{:S(2)}) %all-to-all-start) | async-done | bytes 1048608 | tf_op jit(solution)/shard_map/all_to_all | solution.py:347
  30.3 3.7 %all-to-all-start.2 = ((bf16[16,32,1024]{2,1,0:T(8,128)(2,1)}), bf16[16,32,1024]{2,1,0:T(8,128)(2,1)S(1)}, u32[]{:S(2)}, u32[]{:S(2)}) async-start(bf16[16,32,1024]{2,1,0:T(8,128)(2,1)} %shard_map.90), calls=%async_computation.2 | async-start | bytes 2097152 | tf_op jit(solution)/shard_map/all_to_all | solution.py:352
  33.9 1.1 copy.9
  35.0 2.7 %shard_map.87 = bf16[4,32,1024]{2,1,0:T(8,128)(2,1)} custom-call(s32[128]{0:T(128)} %routing.7, s32[128]{0:T(128)} %counts.5, s32[5]{0:T(128)} %stack.23.place, bf16[16,32,1024]{2,1,0:T(8,128)(2,1)} %copy-done.2, bf16[4,32,1024]{2,1,0:T(8,128)(2,1)} %bitcast.33), custom_call_target="tpu_custom_call" | custom-call | tf_op jit(solution)/shard_map/pallas_call | solution.py:108
  37.7 1.6 collective-permute-start.1
  39.2 2.7 %collective-permute-start.2 = (bf16[128,1024]{1,0:T(8,128)(2,1)}, bf16[128,1024]{1,0:T(8,128)(2,1)S(1)}, u32[]{:S(2)}, u32[]{:S(2)}) collective-permute-start(bf16[128,1024]{1,0:T(8,128)(2,1)} %bitcast.26), channel_id=1, source_target_pairs={{0,32},{16,48},{32,0},{48,16},{1,33},{17,49},{33,1},{49,17},{2,34}... | collective-permute-start | bytes 786440 | tf_op jit(solution)/shard_map/ppermute | solution.py:38
  42.0 1.4 collective-permute-start.3
  43.4 4.0 %collective-permute-done.1.in1.b1 = bf16[128,1024]{1,0:T(8,128)(2,1)S(1)} collective-permute-done((bf16[128,1024]{1,0:T(8,128)(2,1)}, bf16[128,1024]{1,0:T(8,128)(2,1)S(1)}, u32[]{:S(2)}, u32[]{:S(2)}) %collective-permute-start.1) | collective-permute-done | bytes 262176 | tf_op jit(solution)/shard_map/ppermute | solution.py:38
  47.4 5.7 %collective-permute-done.2.in2.b2 = bf16[128,1024]{1,0:T(8,128)(2,1)S(1)} collective-permute-done((bf16[128,1024]{1,0:T(8,128)(2,1)}, bf16[128,1024]{1,0:T(8,128)(2,1)S(1)}, u32[]{:S(2)}, u32[]{:S(2)}) %collective-permute-start.2) | collective-permute-done | bytes 262176 | tf_op jit(solution)/shard_map/ppermute | solution.py:38
  54.6 6.3 %shard_map.89 = (bf16[128,1024]{1,0:T(8,128)(2,1)}, f32[128,1024]{1,0:T(8,128)}) custom-call(s32[5]{0:T(128)} %stack.23.place, bf16[4096,1024]{1,0:T(8,128)(2,1)} %bitcast.19, bf16[4096,1024]{1,0:T(8,128)(2,1)} %collective-permute-done.other, bf16[128,1024]{1,0:T(8,128)(2,1)} %bitcast.28, bf16[128,1024]{1,0:T(8,128)(2,1)} %copy-done.4, ...), custom_call_target="tpu_custom_call" | custom-call | tf_op jit(solution)/shard_map/pallas_call | solution.py:210
  60.9 0.7 collective-permute-start.4
  61.6 2.4 collective-permute-start.6
  64.0 1.6 collective-permute-start.7
  65.6 1.0 copy-done.1
  66.6 2.3 shard_map.91
  69.1 6.7 %collective-permute-done.6.b2.in2 = bf16[128,1024]{1,0:T(8,128)(2,1)S(1)} collective-permute-done((bf16[128,1024]{1,0:T(8,128)(2,1)}, bf16[128,1024]{1,0:T(8,128)(2,1)S(1)}, u32[]{:S(2)}, u32[]{:S(2)}) %collective-permute-start.6) | collective-permute-done | bytes 262176 | tf_op jit(solution)/shard_map/ppermute | solution.py:38
  76.5 9.0 %shard_map.92 = (bf16[128,1024]{1,0:T(8,128)(2,1)}, bf16[128,1024]{1,0:T(8,128)(2,1)}, bf16[128,1024]{1,0:T(8,128)(2,1)}, bf16[128,1024]{1,0:T(8,128)(2,1)}, bf16[128,1024]{1,0:T(8,128)(2,1)}) custom-call(s32[5]{0:T(128)} %stack.23.place, bf16[4096,1024]{1,0:T(8,128)(2,1)} %bitcast.20, bf16[4096,1024]{1,0:T(8,128)(2,1)} %collective-permute-done.other, ...), custom_call_target="tpu_custom_call" | custom-call | tf_op jit(solution)/shard_map/pallas_call | solution.py:210
  85.5 0.8 collective-permute-start.8
  86.3 2.8 %shard_map.93 = bf16[4,256,1024]{2,1,0:T(8,128)(2,1)} custom-call(s32[5]{0:T(128)} %stack.23.place, bf16[128,1024]{1,0:T(8,128)(2,1)} %get-tuple-element.30.b0.in0, bf16[128,1024]{1,0:T(8,128)(2,1)} %copy-done.7, bf16[128,1024]{1,0:T(8,128)(2,1)} %copy-done.8, bf16[128,1024]{1,0:T(8,128)(2,1)} %copy-done.9, bf16[128,1024]{1,0:T(8,128)(2,1)} %get-tuple-element.33.refs_0_), custom_call_target="tpu_custom_call" | custom-call | tf_op jit(solution)/shard_map/pallas_call | solution.py:324
  89.1 4.9 %collective-permute-done.8.r1 = bf16[128,1024]{1,0:T(8,128)(2,1)S(1)} collective-permute-done((bf16[128,1024]{1,0:T(8,128)(2,1)}, bf16[128,1024]{1,0:T(8,128)(2,1)S(1)}, u32[]{:S(2)}, u32[]{:S(2)}) %collective-permute-start.8) | collective-permute-done | bytes 262176 | tf_op jit(solution)/shard_map/ppermute | solution.py:38
  94.0 28.3 %all_to_all.30.both1 = bf16[4,256,1024]{2,1,0:T(8,128)(2,1)S(1)} all-to-all(bf16[4,256,1024]{2,1,0:T(8,128)(2,1)} %shard_map.93), channel_id=1, replica_groups={{0,1,2,3},{4,5,6,7},{8,9,10,11},{12,13,14,15},{16,17,18,19},{20,21,22,2..., dimensions={0} | all-to-all | bytes 4194304 | tf_op jit(solution)/shard_map/all_to_all | solution.py:56
  122.3 2.7 %collective-permute-start.9 = (bf16[4,256,1024]{2,1,0:T(8,128)(2,1)S(1)}, bf16[4,256,1024]{2,1,0:T(8,128)(2,1)}, u32[]{:S(2)}, u32[]{:S(2)}) collective-permute-start(bf16[4,256,1024]{2,1,0:T(8,128)(2,1)S(1)} %all_to_all.30.both1), channel_id=1, source_target_pairs={{0,64},{1,65},{2,66},{3,67},{4,68},{5,69},{6,70},{7,71},{8,72},{9,... | collective-permute-start | bytes 6291464 | tf_op jit(solution)/shard_map/ppermute | solution.py:385
  125.1 2.3 shard_map.88
  127.4 4.1 %all-to-all-start.1 = ((bf16[4,128,1024]{2,1,0:T(8,128)(2,1)}), bf16[4,128,1024]{2,1,0:T(8,128)(2,1)S(1)}, u32[]{:S(2)}, u32[]{:S(2)}) async-start(bf16[4,128,1024]{2,1,0:T(8,128)(2,1)} %shard_map.88), calls=%async_computation.1 | async-start | bytes 2097152 | tf_op jit(solution)/shard_map/all_to_all | solution.py:56
  131.4 1.8 collective-permute-start.10
  133.2 2.7 %collective-permute-start.11 = (bf16[128,1024]{1,0:T(8,128)(2,1)}, bf16[128,1024]{1,0:T(8,128)(2,1)}, u32[]{:S(2)}, u32[]{:S(2)}) collective-permute-start(bf16[128,1024]{1,0:T(8,128)(2,1)} %get-tuple-element.38), channel_id=1, source_target_pairs={{0,48},{16,0},{32,16},{48,32},{1,49},{17,1},{33,17},{49,33},{2,50}... | collective-permute-start | bytes 786440 | tf_op jit(solution)/shard_map/ppermute | solution.py:38
  135.9 6.4 %all-to-all-done.1.rows0 = bf16[4,128,1024]{2,1,0:T(8,128)(2,1)S(1)} async-done(((bf16[4,128,1024]{2,1,0:T(8,128)(2,1)}), bf16[4,128,1024]{2,1,0:T(8,128)(2,1)S(1)}, u32[]{:S(2)}, u32[]{:S(2)}) %all-to-all-start.1) | async-done | bytes 1048608 | tf_op jit(solution)/shard_map/all_to_all | solution.py:56
  142.3 1.3 collective-permute-start.5
  144.3 9.0 %shard_map.94 = (bf16[128,1024]{1,0:T(8,128)(2,1)}, bf16[128,1024]{1,0:T(8,128)(2,1)}, bf16[128,1024]{1,0:T(8,128)(2,1)}, bf16[128,1024]{1,0:T(8,128)(2,1)}, bf1...) custom-call(s32[5]{0:T(128)} %stack.23.place, bf16[4096,1024]{1,0:T(8,128)(2,1)} %bitcast.21, ...), custom_call_target="tpu_custom_call" | custom-call | tf_op jit(solution)/shard_map/pallas_call | solution.py:210
  153.9 5.4 %all-to-all-start.5 = ((bf16[8,320,128]{2,1,0:T(8,128)(2,1)}), bf16[8,320,128]{2,1,0:T(8,128)(2,1)}, u32[]{:S(2)}, u32[]{:S(2)}) async-start(bf16[8,320,128]{2,1,0:T(8,128)(2,1)} %bitcast.24), calls=%async_computation.5 | async-start | bytes 1310720 | tf_op jit(solution)/shard_map/all_to_all | solution.py:362
  159.3 3.5 %collective-permute-start.13 = (bf16[128,1024]{1,0:T(8,128)(2,1)S(1)}, bf16[128,1024]{1,0:T(8,128)(2,1)S(1)}, u32[]{:S(2)}, u32[]{:S(2)}) collective-permute-start(bf16[128,1024]{1,0:T(8,128)(2,1)S(1)} %copy-done.23), channel_id=1, source_target_pairs={{0,8},{1,9},{2,10},{3,11},{4,12},{5,13},{6,14},{7,15},{8,0},{9,1},... | collective-permute-start | bytes 786440 | tf_op jit(solution)/shard_map/ppermute | solution.py:45
  162.8 1.2 collective-permute-start.14
  164.0 1.3 collective-permute-start.15
  165.3 11.4 %collective-permute-done.13.refs_2_ = bf16[128,1024]{1,0:T(8,128)(2,1)S(1)} collective-permute-done((bf16[128,1024]{1,0:T(8,128)(2,1)S(1)}, bf16[128,1024]{1,0:T(8,128)(2,1)S(1)}, u32[]{:S(2)}, u32[]{:S(2)}) %collective-permute-start.13) | collective-permute-done | bytes 262176 | tf_op jit(solution)/shard_map/ppermute | solution.py:45
  176.7 1.3 collective-permute-start.16
  178.0 2.8 %collective-permute-done.14.refs_3_ = bf16[128,1024]{1,0:T(8,128)(2,1)S(1)} collective-permute-done((bf16[128,1024]{1,0:T(8,128)(2,1)S(1)}, bf16[128,1024]{1,0:T(8,128)(2,1)S(1)}, u32[]{:S(2)}, u32[]{:S(2)}) %collective-permute-start.14) | collective-permute-done | bytes 262176 | tf_op jit(solution)/shard_map/ppermute | solution.py:45
  180.8 1.3 collective-permute-start.17
  182.1 1.3 collective-permute-start.18
  183.5 0.8 collective-permute-done.17.refs_6_
  184.3 1.3 collective-permute-done.18.refs_7_
  186.3 6.6 %shard_map.95 = bf16[4,256,1024]{2,1,0:T(8,128)(2,1)} custom-call(s32[5]{0:T(128)} %stack.23.place, bf16[4,128,1024]{2,1,0:T(8,128)(2,1)} %copy-done.3, bf16[4,128,1024]{2,1,0:T(8,128)(2,1)} %collective-permute-done.5.rows0_far, bf16[4,256,1024]{2,1,0:T(8,128)(2,1)} %copy-done, bf16[4,256,1024]{2,1,0:T(8,128)(2,1)} %collective-permute-done.9.both1_far, ...), custom_call_target="tpu_custom_call" | custom-call | tf_op jit(solution)/shard_map/pallas_call | solution.py:258
  193.0 3.8 %all-to-all-start.4 = ((bf16[4,256,1024]{2,1,0:T(8,128)(2,1)}), bf16[4,256,1024]{2,1,0:T(8,128)(2,1)S(1)}, u32[]{:S(2)}, u32[]{:S(2)}) async-start(bf16[4,256,1024]{2,1,0:T(8,128)(2,1)} %shard_map.95), calls=%async_computation.4 | async-start | bytes 4194304 | tf_op jit(solution)/shard_map/all_to_all | solution.py:390
  196.7 2.1 collective-permute-start.19
  198.8 1.6 collective-permute-start.20
  200.4 1.1 collective-permute-start.21
  201.6 5.2 %collective-permute-done.19.r1 = bf16[128,1024]{1,0:T(8,128)(2,1)S(1)} collective-permute-done((bf16[128,1024]{1,0:T(8,128)(2,1)S(1)}, bf16[128,1024]{1,0:T(8,128)(2,1)S(1)}, u32[]{:S(2)}, u32[]{:S(2)}) %collective-permute-start.19) | collective-permute-done | bytes 262176 | tf_op jit(solution)/shard_map/ppermute | solution.py:38
  206.8 5.6 %collective-permute-done.20.r2 = bf16[128,1024]{1,0:T(8,128)(2,1)S(1)} collective-permute-done((bf16[128,1024]{1,0:T(8,128)(2,1)S(1)}, bf16[128,1024]{1,0:T(8,128)(2,1)S(1)}, u32[]{:S(2)}, u32[]{:S(2)}) %collective-permute-start.20) | collective-permute-done | bytes 262176 | tf_op jit(solution)/shard_map/ppermute | solution.py:38
  213.3 2.2 shard_map.96.refs_0_
  215.5 1.7 collective-permute-start.22
  217.2 2.2 collective-permute-start.23
  219.4 2.0 collective-permute-start.24
  221.3 3.4 %collective-permute-done.22.refs_1_ = bf16[128,1024]{1,0:T(8,128)(2,1)S(1)} collective-permute-done((bf16[128,1024]{1,0:T(8,128)(2,1)}, bf16[128,1024]{1,0:T(8,128)(2,1)S(1)}, u32[]{:S(2)}, u32[]{:S(2)}) %collective-permute-start.22) | collective-permute-done | bytes 262176 | tf_op jit(solution)/shard_map/ppermute | solution.py:45
  224.7 6.8 %collective-permute-done.23.refs_2_ = bf16[128,1024]{1,0:T(8,128)(2,1)S(1)} collective-permute-done((bf16[128,1024]{1,0:T(8,128)(2,1)}, bf16[128,1024]{1,0:T(8,128)(2,1)S(1)}, u32[]{:S(2)}, u32[]{:S(2)}) %collective-permute-start.23) | collective-permute-done | bytes 262176 | tf_op jit(solution)/shard_map/ppermute | solution.py:45
  232.0 1.0 collective-permute-done.27.refs_6_
  234.5 4.2 %shard_map.97 = (bf16[80,1024]{1,0:T(8,128)(2,1)}, bf16[80,1024]{1,0:T(8,128)(2,1)}, bf16[80,1024]{1,0:T(8,128)(2,1)}, bf16[80,1024]{1,0:T(8,128)(2,1)}) custom-call(s32[5]{0:T(128)} %stack.23.place, bf16[8,320,128]{2,1,0:T(8,128)(2,1)} %all-to-all-done.5.act, bf16[128,1024]{1,0:T(8,128)(2,1)} %shard_map.96.refs_0_, bf16[128,1024]{1,0:T(8,128)(2,1)} %copy-done.13, ...), custom_call_target="tpu_custom_call" | custom-call | tf_op jit(solution)/shard_map/pallas_call | solution.py:288
  238.8 1.8 collective-permute-start.30
  240.6 1.3 collective-permute-start.31
  241.9 7.9 %collective-permute-done.29 = bf16[80,1024]{1,0:T(8,128)(2,1)S(1)} collective-permute-done((bf16[80,1024]{1,0:T(8,128)(2,1)}, bf16[80,1024]{1,0:T(8,128)(2,1)S(1)}, u32[]{:S(2)}, u32[]{:S(2)}) %collective-permute-start.29) | collective-permute-done | bytes 163872 | tf_op jit(solution)/shard_map/ppermute | solution.py:52
  250.4 1.7 convert_add_fusion.1
  252.2 1.3 convert_reduce_fusion
  (95 shorter events, 9.2 us)
Async XLA Ops:
  0.6 34.4 %collective-permute-start = (bf16[4096,1024]{1,0:T(8,128)(2,1)}, bf16[4096,1024]{1,0:T(8,128)(2,1)}, u32[]{:S(2)}, u32[]{:S(2)}) collective-permute-start(bf16[4096,1024]{1,0:T(8,128)(2,1)} %bitcast.18), channel_id=1, source_target_pairs={{0,64},{64,0},{1,65},{65,1},{2,66},{66,2},{3,67},{67,3},{4,68},{68... | collective-permute-start | bytes 25165832 | tf_op jit(solution)/shard_map/ppermute | solution.py:60
  3.6 26.7 %all-to-all-start = ((bf16[16,32,1024]{2,1,0:T(8,128)(2,1)}), bf16[16,32,1024]{2,1,0:T(8,128)(2,1)S(1)}, u32[]{:S(2)}, u32[]{:S(2)}) async-start(bf16[16,32,1024]{2,1,0:T(8,128)(2,1)} %shard_map.86), calls=%async_computation | async-start | bytes 2097152 | tf_op jit(solution)/shard_map/all_to_all | solution.py:347
  11.7 2.2 copy-start.10
  30.3 4.7 %copy-start.2 = (bf16[16,32,1024]{2,1,0:T(8,128)(2,1)}, bf16[16,32,1024]{2,1,0:T(8,128)(2,1)S(1)}, u32[]{:S(2)}) copy-start(bf16[16,32,1024]{2,1,0:T(8,128)(2,1)S(1)} %all-to-all-done.arrived) | copy-start | bytes 3145732
  30.3 35.3 %all-to-all-start.2 = ((bf16[16,32,1024]{2,1,0:T(8,128)(2,1)}), bf16[16,32,1024]{2,1,0:T(8,128)(2,1)S(1)}, u32[]{:S(2)}, u32[]{:S(2)}) async-start(bf16[16,32,1024]{2,1,0:T(8,128)(2,1)} %shard_map.90), calls=%async_computation.2 | async-start | bytes 2097152 | tf_op jit(solution)/shard_map/all_to_all | solution.py:352
  37.7 9.7 %collective-permute-start.1 = (bf16[128,1024]{1,0:T(8,128)(2,1)}, bf16[128,1024]{1,0:T(8,128)(2,1)S(1)}, u32[]{:S(2)}, u32[]{:S(2)}) collective-permute-start(bf16[128,1024]{1,0:T(8,128)(2,1)} %bitcast.25), channel_id=1, source_target_pairs={{0,16},{16,32},{32,48},{48,0},{1,17},{17,33},{33,49},{49,1},{2,18}... | collective-permute-start | bytes 786440 | tf_op jit(solution)/shard_map/ppermute | solution.py:38
  39.2 13.9 %collective-permute-start.2 = (bf16[128,1024]{1,0:T(8,128)(2,1)}, bf16[128,1024]{1,0:T(8,128)(2,1)S(1)}, u32[]{:S(2)}, u32[]{:S(2)}) collective-permute-start(bf16[128,1024]{1,0:T(8,128)(2,1)} %bitcast.26), channel_id=1, source_target_pairs={{0,32},{16,48},{32,0},{48,16},{1,33},{17,49},{33,1},{49,17},{2,34}... | collective-permute-start | bytes 786440 | tf_op jit(solution)/shard_map/ppermute | solution.py:38
  42.0 11.2 %collective-permute-start.3 = (bf16[128,1024]{1,0:T(8,128)(2,1)}, bf16[128,1024]{1,0:T(8,128)(2,1)S(1)}, u32[]{:S(2)}, u32[]{:S(2)}) collective-permute-start(bf16[128,1024]{1,0:T(8,128)(2,1)} %bitcast.27), channel_id=1, source_target_pairs={{0,48},{16,0},{32,16},{48,32},{1,49},{17,1},{33,17},{49,33},{2,50}... | collective-permute-start | bytes 786440 | tf_op jit(solution)/shard_map/ppermute | solution.py:38
  47.4 5.8 %copy-start.4 = (bf16[128,1024]{1,0:T(8,128)(2,1)}, bf16[128,1024]{1,0:T(8,128)(2,1)S(1)}, u32[]{:S(2)}) copy-start(bf16[128,1024]{1,0:T(8,128)(2,1)S(1)} %collective-permute-done.1.in1.b1) | copy-start | bytes 786436
  53.9 0.7 copy-start.6
  60.9 8.2 %collective-permute-start.4 = (bf16[128,1024]{1,0:T(8,128)(2,1)}, bf16[128,1024]{1,0:T(8,128)(2,1)S(1)}, u32[]{:S(2)}, u32[]{:S(2)}) collective-permute-start(bf16[128,1024]{1,0:T(8,128)(2,1)} %get-tuple-element.30.b0.in0), channel_id=1, source_target_pairs={{0,16},{16,32},{32,48},{48,0},{1,17},{17,33},{33,49},{49,1},{2,18}... | collective-permute-start | bytes 786440 | tf_op jit(solution)/shard_map/ppermute | solution.py:38
  61.6 14.1 %collective-permute-start.6 = (bf16[128,1024]{1,0:T(8,128)(2,1)}, bf16[128,1024]{1,0:T(8,128)(2,1)S(1)}, u32[]{:S(2)}, u32[]{:S(2)}) collective-permute-start(bf16[128,1024]{1,0:T(8,128)(2,1)} %get-tuple-element.30.b0.in0), channel_id=1, source_target_pairs={{0,32},{16,48},{32,0},{48,16},{1,33},{17,49},{33,1},{49,17},{2,34}... | collective-permute-start | bytes 786440 | tf_op jit(solution)/shard_map/ppermute | solution.py:38
  64.0 11.7 %collective-permute-start.7 = (bf16[128,1024]{1,0:T(8,128)(2,1)}, bf16[128,1024]{1,0:T(8,128)(2,1)S(1)}, u32[]{:S(2)}, u32[]{:S(2)}) collective-permute-start(bf16[128,1024]{1,0:T(8,128)(2,1)} %get-tuple-element.30.b0.in0), channel_id=1, source_target_pairs={{0,48},{16,0},{32,16},{48,32},{1,49},{17,1},{33,17},{49,33},{2,50}... | collective-permute-start | bytes 786440 | tf_op jit(solution)/shard_map/ppermute | solution.py:38
  65.6 1.0 copy-start.1
  69.1 6.7 %copy-start.7 = (bf16[128,1024]{1,0:T(8,128)(2,1)}, bf16[128,1024]{1,0:T(8,128)(2,1)S(1)}, u32[]{:S(2)}) copy-start(bf16[128,1024]{1,0:T(8,128)(2,1)S(1)} %collective-permute-done.4.b1.in1) | copy-start | bytes 786436
  75.7 0.7 copy-start.8
  75.7 0.8 copy-start.9
  85.5 8.5 %collective-permute-start.8 = (bf16[128,1024]{1,0:T(8,128)(2,1)}, bf16[128,1024]{1,0:T(8,128)(2,1)S(1)}, u32[]{:S(2)}, u32[]{:S(2)}) collective-permute-start(bf16[128,1024]{1,0:T(8,128)(2,1)} %get-tuple-element.34), channel_id=1, source_target_pairs={{0,16},{16,32},{32,48},{48,0},{1,17},{17,33},{33,49},{49,1},{2,18}... | collective-permute-start | bytes 786440 | tf_op jit(solution)/shard_map/ppermute | solution.py:38
  94.0 28.3 %copy-start.11 = (bf16[128,1024]{1,0:T(8,128)(2,1)}, bf16[128,1024]{1,0:T(8,128)(2,1)S(1)}, u32[]{:S(2)}) copy-start(bf16[128,1024]{1,0:T(8,128)(2,1)S(1)} %collective-permute-done.8.r1) | copy-start | bytes 786436
  122.3 5.1 %copy-start = (bf16[4,256,1024]{2,1,0:T(8,128)(2,1)}, bf16[4,256,1024]{2,1,0:T(8,128)(2,1)S(1)}, u32[]{:S(2)}) copy-start(bf16[4,256,1024]{2,1,0:T(8,128)(2,1)S(1)} %all_to_all.30.both1) | copy-start | bytes 6291460
  122.3 63.3 %collective-permute-start.9 = (bf16[4,256,1024]{2,1,0:T(8,128)(2,1)S(1)}, bf16[4,256,1024]{2,1,0:T(8,128)(2,1)}, u32[]{:S(2)}, u32[]{:S(2)}) collective-permute-start(bf16[4,256,1024]{2,1,0:T(8,128)(2,1)S(1)} %all_to_all.30.both1), channel_id=1, source_target_pairs={{0,64},{1,65},{2,66},{3,67},{4,68},{5,69},{6,70},{7,71},{8,72},{9,... | collective-permute-start | bytes 6291464 | tf_op jit(solution)/shard_map/ppermute | solution.py:385
  127.4 15.0 %all-to-all-start.1 = ((bf16[4,128,1024]{2,1,0:T(8,128)(2,1)}), bf16[4,128,1024]{2,1,0:T(8,128)(2,1)S(1)}, u32[]{:S(2)}, u32[]{:S(2)}) async-start(bf16[4,128,1024]{2,1,0:T(8,128)(2,1)} %shard_map.88), calls=%async_computation.1 | async-start | bytes 2097152 | tf_op jit(solution)/shard_map/all_to_all | solution.py:56
  131.4 12.2 %collective-permute-start.10 = (bf16[128,1024]{1,0:T(8,128)(2,1)}, bf16[128,1024]{1,0:T(8,128)(2,1)S(1)}, u32[]{:S(2)}, u32[]{:S(2)}) collective-permute-start(bf16[128,1024]{1,0:T(8,128)(2,1)} %get-tuple-element.37), channel_id=1, source_target_pairs={{0,32},{16,48},{32,0},{48,16},{1,33},{17,49},{33,1},{49,17},{2,34}... | collective-permute-start | bytes 786440 | tf_op jit(solution)/shard_map/ppermute | solution.py:38
  133.2 10.4 %collective-permute-start.11 = (bf16[128,1024]{1,0:T(8,128)(2,1)}, bf16[128,1024]{1,0:T(8,128)(2,1)}, u32[]{:S(2)}, u32[]{:S(2)}) collective-permute-start(bf16[128,1024]{1,0:T(8,128)(2,1)} %get-tuple-element.38), channel_id=1, source_target_pairs={{0,48},{16,0},{32,16},{48,32},{1,49},{17,1},{33,17},{49,33},{2,50}... | collective-permute-start | bytes 786440 | tf_op jit(solution)/shard_map/ppermute | solution.py:38
  142.3 11.0 %copy-start.3 = (bf16[4,128,1024]{2,1,0:T(8,128)(2,1)}, bf16[4,128,1024]{2,1,0:T(8,128)(2,1)S(1)}, u32[]{:S(2)}) copy-start(bf16[4,128,1024]{2,1,0:T(8,128)(2,1)S(1)} %all-to-all-done.1.rows0) | copy-start | bytes 3145732
  142.3 43.3 %collective-permute-start.5 = (bf16[4,128,1024]{2,1,0:T(8,128)(2,1)S(1)}, bf16[4,128,1024]{2,1,0:T(8,128)(2,1)}, u32[]{:S(2)}, u32[]{:S(2)}) collective-permute-start(bf16[4,128,1024]{2,1,0:T(8,128)(2,1)S(1)} %all-to-all-done.1.rows0), channel_id=1, source_target_pairs={{64,0},{65,1},{66,2},{67,3},{68,4},{69,5},{70,6},{71,7},{72,8},{73... | collective-permute-start | bytes 3145736 | tf_op jit(solution)/shard_map/ppermute | solution.py:384
  153.3 6.0 %copy-start.23 = (bf16[128,1024]{1,0:T(8,128)(2,1)S(1)}, bf16[128,1024]{1,0:T(8,128)(2,1)}, u32[]{:S(2)}) copy-start(bf16[128,1024]{1,0:T(8,128)(2,1)} %get-tuple-element.40.refs_0_) | copy-start | bytes 786436
  153.3 10.7 %collective-permute-start.12 = (bf16[128,1024]{1,0:T(8,128)(2,1)}, bf16[128,1024]{1,0:T(8,128)(2,1)}, u32[]{:S(2)}, u32[]{:S(2)}) collective-permute-start(bf16[128,1024]{1,0:T(8,128)(2,1)} %get-tuple-element.40.refs_0_), channel_id=1, source_target_pairs={{0,4},{1,5},{2,6},{3,7},{4,8},{5,9},{6,10},{7,11},{8,12},{9,13},{1... | collective-permute-start | bytes 786440 | tf_op jit(solution)/shard_map/ppermute | solution.py:45
  153.9 39.0 %all-to-all-start.5 = ((bf16[8,320,128]{2,1,0:T(8,128)(2,1)}), bf16[8,320,128]{2,1,0:T(8,128)(2,1)}, u32[]{:S(2)}, u32[]{:S(2)}) async-start(bf16[8,320,128]{2,1,0:T(8,128)(2,1)} %bitcast.24), calls=%async_computation.5 | async-start | bytes 1310720 | tf_op jit(solution)/shard_map/all_to_all | solution.py:362
  159.3 17.4 %collective-permute-start.13 = (bf16[128,1024]{1,0:T(8,128)(2,1)S(1)}, bf16[128,1024]{1,0:T(8,128)(2,1)S(1)}, u32[]{:S(2)}, u32[]{:S(2)}) collective-permute-start(bf16[128,1024]{1,0:T(8,128)(2,1)S(1)} %copy-done.23), channel_id=1, source_target_pairs={{0,8},{1,9},{2,10},{3,11},{4,12},{5,13},{6,14},{7,15},{8,0},{9,1},... | collective-permute-start | bytes 786440 | tf_op jit(solution)/shard_map/ppermute | solution.py:45
  162.8 18.0 %collective-permute-start.14 = (bf16[128,1024]{1,0:T(8,128)(2,1)S(1)}, bf16[128,1024]{1,0:T(8,128)(2,1)S(1)}, u32[]{:S(2)}, u32[]{:S(2)}) collective-permute-start(bf16[128,1024]{1,0:T(8,128)(2,1)S(1)} %copy-done.23), channel_id=1, source_target_pairs={{0,12},{1,13},{2,14},{3,15},{4,0},{5,1},{6,2},{7,3},{8,4},{9,5},{1... | collective-permute-start | bytes 786440 | tf_op jit(solution)/shard_map/ppermute | solution.py:45
  164.0 18.1 %collective-permute-start.15 = (bf16[128,1024]{1,0:T(8,128)(2,1)S(1)}, bf16[128,1024]{1,0:T(8,128)(2,1)S(1)}, u32[]{:S(2)}, u32[]{:S(2)}) collective-permute-start(bf16[128,1024]{1,0:T(8,128)(2,1)S(1)} %copy-done.23), channel_id=1, source_target_pairs={{64,0},{65,1},{66,2},{67,3},{68,4},{69,5},{70,6},{71,7},{72,8},{73... | collective-permute-start | bytes 786440 | tf_op jit(solution)/shard_map/ppermute | solution.py:387
  176.7 8.9 %copy-start.24 = (bf16[128,1024]{1,0:T(8,128)(2,1)}, bf16[128,1024]{1,0:T(8,128)(2,1)S(1)}, u32[]{:S(2)}) copy-start(bf16[128,1024]{1,0:T(8,128)(2,1)S(1)} %collective-permute-done.13.refs_2_) | copy-start | bytes 786436
  176.7 6.7 %collective-permute-start.16 = (bf16[128,1024]{1,0:T(8,128)(2,1)}, bf16[128,1024]{1,0:T(8,128)(2,1)S(1)}, u32[]{:S(2)}, u32[]{:S(2)}) collective-permute-start(bf16[128,1024]{1,0:T(8,128)(2,1)} %collective-permute-done.12.refs_1_), channel_id=1, source_target_pairs={{64,0},{65,1},{66,2},{67,3},{68,4},{69,5},{70,6},{71,7},{72,8},{73... | collective-permute-start | bytes 786440 | tf_op jit(solution)/shard_map/ppermute | solution.py:387
  180.8 4.8 %copy-start.25 = (bf16[128,1024]{1,0:T(8,128)(2,1)}, bf16[128,1024]{1,0:T(8,128)(2,1)S(1)}, u32[]{:S(2)}) copy-start(bf16[128,1024]{1,0:T(8,128)(2,1)S(1)} %collective-permute-done.14.refs_3_) | copy-start | bytes 786436
  180.8 3.4 %collective-permute-start.17 = (bf16[128,1024]{1,0:T(8,128)(2,1)S(1)}, bf16[128,1024]{1,0:T(8,128)(2,1)S(1)}, u32[]{:S(2)}, u32[]{:S(2)}) collective-permute-start(bf16[128,1024]{1,0:T(8,128)(2,1)S(1)} %collective-permute-done.13.refs_2_), channel_id=1, source_target_pairs={{64,0},{65,1},{66,2},{67,3},{68,4},{69,5},{70,6},{71,7},{72,8},{73... | collective-permute-start | bytes 786440 | tf_op jit(solution)/shard_map/ppermute | solution.py:387
  182.1 3.5 %copy-start.26 = (bf16[128,1024]{1,0:T(8,128)(2,1)}, bf16[128,1024]{1,0:T(8,128)(2,1)S(1)}, u32[]{:S(2)}) copy-start(bf16[128,1024]{1,0:T(8,128)(2,1)S(1)} %collective-permute-done.15.refs_4_) | copy-start | bytes 786436
  182.1 3.4 %collective-permute-start.18 = (bf16[128,1024]{1,0:T(8,128)(2,1)S(1)}, bf16[128,1024]{1,0:T(8,128)(2,1)S(1)}, u32[]{:S(2)}, u32[]{:S(2)}) collective-permute-start(bf16[128,1024]{1,0:T(8,128)(2,1)S(1)} %collective-permute-done.14.refs_3_), channel_id=1, source_target_pairs={{64,0},{65,1},{66,2},{67,3},{68,4},{69,5},{70,6},{71,7},{72,8},{73... | collective-permute-start | bytes 786440 | tf_op jit(solution)/shard_map/ppermute | solution.py:387
  183.5 2.1 copy-start.27
  184.3 1.4 copy-start.28
  192.9 3.8 %copy-start.32 = (bf16[128,1024]{1,0:T(8,128)(2,1)S(1)}, bf16[128,1024]{1,0:T(8,128)(2,1)}, u32[]{:S(2)}) copy-start(bf16[128,1024]{1,0:T(8,128)(2,1)} %get-tuple-element.44) | copy-start | bytes 786436
  192.9 5.9 %copy-start.31 = (bf16[128,1024]{1,0:T(8,128)(2,1)S(1)}, bf16[128,1024]{1,0:T(8,128)(2,1)}, u32[]{:S(2)}) copy-start(bf16[128,1024]{1,0:T(8,128)(2,1)} %get-tuple-element.45) | copy-start | bytes 786436
  192.9 7.5 %copy-start.30 = (bf16[128,1024]{1,0:T(8,128)(2,1)S(1)}, bf16[128,1024]{1,0:T(8,128)(2,1)}, u32[]{:S(2)}) copy-start(bf16[128,1024]{1,0:T(8,128)(2,1)} %get-tuple-element.46) | copy-start | bytes 786436
  193.0 59.2 %all-to-all-start.4 = ((bf16[4,256,1024]{2,1,0:T(8,128)(2,1)}), bf16[4,256,1024]{2,1,0:T(8,128)(2,1)S(1)}, u32[]{:S(2)}, u32[]{:S(2)}) async-start(bf16[4,256,1024]{2,1,0:T(8,128)(2,1)} %shard_map.95), calls=%async_computation.4 | async-start | bytes 4194304 | tf_op jit(solution)/shard_map/all_to_all | solution.py:390
  196.7 10.0 %collective-permute-start.19 = (bf16[128,1024]{1,0:T(8,128)(2,1)S(1)}, bf16[128,1024]{1,0:T(8,128)(2,1)S(1)}, u32[]{:S(2)}, u32[]{:S(2)}) collective-permute-start(bf16[128,1024]{1,0:T(8,128)(2,1)S(1)} %copy-done.32), channel_id=1, source_target_pairs={{0,16},{16,32},{32,48},{48,0},{1,17},{17,33},{33,49},{49,1},{2,18}... | collective-permute-start | bytes 786440 | tf_op jit(solution)/shard_map/ppermute | solution.py:38
  198.8 13.6 %collective-permute-start.20 = (bf16[128,1024]{1,0:T(8,128)(2,1)S(1)}, bf16[128,1024]{1,0:T(8,128)(2,1)S(1)}, u32[]{:S(2)}, u32[]{:S(2)}) collective-permute-start(bf16[128,1024]{1,0:T(8,128)(2,1)S(1)} %copy-done.31), channel_id=1, source_target_pairs={{0,32},{16,48},{32,0},{48,16},{1,33},{17,49},{33,1},{49,17},{2,34}... | collective-permute-start | bytes 786440 | tf_op jit(solution)/shard_map/ppermute | solution.py:38
  200.4 12.2 %collective-permute-start.21 = (bf16[128,1024]{1,0:T(8,128)(2,1)S(1)}, bf16[128,1024]{1,0:T(8,128)(2,1)S(1)}, u32[]{:S(2)}, u32[]{:S(2)}) collective-permute-start(bf16[128,1024]{1,0:T(8,128)(2,1)S(1)} %copy-done.30), channel_id=1, source_target_pairs={{0,48},{16,0},{32,16},{48,32},{1,49},{17,1},{33,17},{49,33},{2,50}... | collective-permute-start | bytes 786440 | tf_op jit(solution)/shard_map/ppermute | solution.py:38
  206.8 5.9 %copy-start.20 = (bf16[128,1024]{1,0:T(8,128)(2,1)}, bf16[128,1024]{1,0:T(8,128)(2,1)S(1)}, u32[]{:S(2)}) copy-start(bf16[128,1024]{1,0:T(8,128)(2,1)S(1)} %collective-permute-done.19.r1) | copy-start | bytes 786436
  215.5 9.2 %collective-permute-start.22 = (bf16[128,1024]{1,0:T(8,128)(2,1)}, bf16[128,1024]{1,0:T(8,128)(2,1)S(1)}, u32[]{:S(2)}, u32[]{:S(2)}) collective-permute-start(bf16[128,1024]{1,0:T(8,128)(2,1)} %shard_map.96.refs_0_), channel_id=1, source_target_pairs={{0,4},{1,5},{2,6},{3,7},{4,8},{5,9},{6,10},{7,11},{8,12},{9,13},{1... | collective-permute-start | bytes 786440 | tf_op jit(solution)/shard_map/ppermute | solution.py:45
  217.2 14.3 %collective-permute-start.23 = (bf16[128,1024]{1,0:T(8,128)(2,1)}, bf16[128,1024]{1,0:T(8,128)(2,1)S(1)}, u32[]{:S(2)}, u32[]{:S(2)}) collective-permute-start(bf16[128,1024]{1,0:T(8,128)(2,1)} %shard_map.96.refs_0_), channel_id=1, source_target_pairs={{0,8},{1,9},{2,10},{3,11},{4,12},{5,13},{6,14},{7,15},{8,0},{9,1},... | collective-permute-start | bytes 786440 | tf_op jit(solution)/shard_map/ppermute | solution.py:45
  219.4 12.1 %collective-permute-start.24 = (bf16[128,1024]{1,0:T(8,128)(2,1)}, bf16[128,1024]{1,0:T(8,128)(2,1)S(1)}, u32[]{:S(2)}, u32[]{:S(2)}) collective-permute-start(bf16[128,1024]{1,0:T(8,128)(2,1)} %shard_map.96.refs_0_), channel_id=1, source_target_pairs={{0,12},{1,13},{2,14},{3,15},{4,0},{5,1},{6,2},{7,3},{8,4},{9,5},{1... | collective-permute-start | bytes 786440 | tf_op jit(solution)/shard_map/ppermute | solution.py:45
  221.3 10.7 %collective-permute-start.25 = (bf16[128,1024]{1,0:T(8,128)(2,1)}, bf16[128,1024]{1,0:T(8,128)(2,1)S(1)}, u32[]{:S(2)}, u32[]{:S(2)}) collective-permute-start(bf16[128,1024]{1,0:T(8,128)(2,1)} %shard_map.96.refs_0_), channel_id=1, source_target_pairs={{0,64},{64,0},{1,65},{65,1},{2,66},{66,2},{3,67},{67,3},{4,68},{68... | collective-permute-start | bytes 786440 | tf_op jit(solution)/shard_map/ppermute | solution.py:60
  224.7 8.7 %copy-start.13 = (bf16[128,1024]{1,0:T(8,128)(2,1)}, bf16[128,1024]{1,0:T(8,128)(2,1)S(1)}, u32[]{:S(2)}) copy-start(bf16[128,1024]{1,0:T(8,128)(2,1)S(1)} %collective-permute-done.22.refs_1_) | copy-start | bytes 786436
  224.7 7.3 %collective-permute-start.26 = (bf16[128,1024]{1,0:T(8,128)(2,1)S(1)}, bf16[128,1024]{1,0:T(8,128)(2,1)S(1)}, u32[]{:S(2)}, u32[]{:S(2)}) collective-permute-start(bf16[128,1024]{1,0:T(8,128)(2,1)S(1)} %collective-permute-done.22.refs_1_), channel_id=1, source_target_pairs={{0,64},{64,0},{1,65},{65,1},{2,66},{66,2},{3,67},{67,3},{4,68},{68... | collective-permute-start | bytes 786440 | tf_op jit(solution)/shard_map/ppermute | solution.py:60
  231.5 1.9 copy-start.14
  231.5 1.5 collective-permute-start.27
  231.5 1.9 copy-start.15
  231.5 1.9 collective-permute-start.28
  232.0 1.4 copy-start.16
  232.0 1.4 copy-start.17
  233.0 0.7 copy-start.18
  238.6 11.2 %collective-permute-start.29 = (bf16[80,1024]{1,0:T(8,128)(2,1)}, bf16[80,1024]{1,0:T(8,128)(2,1)S(1)}, u32[]{:S(2)}, u32[]{:S(2)}) collective-permute-start(bf16[80,1024]{1,0:T(8,128)(2,1)} %get-tuple-element.49), channel_id=1, source_target_pairs={{0,1},{1,2},{2,3},{3,0},{4,5},{5,6},{6,7},{7,4},{8,9},{9,10},{10,1... | collective-permute-start | bytes 491528 | tf_op jit(solution)/shard_map/ppermute | solution.py:52
  238.8 11.0 %collective-permute-start.30 = (bf16[80,1024]{1,0:T(8,128)(2,1)}, bf16[80,1024]{1,0:T(8,128)(2,1)S(1)}, u32[]{:S(2)}, u32[]{:S(2)}) collective-permute-start(bf16[80,1024]{1,0:T(8,128)(2,1)} %get-tuple-element.50), channel_id=1, source_target_pairs={{0,2},{1,3},{2,0},{3,1},{4,6},{5,7},{6,4},{7,5},{8,10},{9,11},{10,... | collective-permute-start | bytes 491528 | tf_op jit(solution)/shard_map/ppermute | solution.py:52
  240.6 9.8 %collective-permute-start.31 = (bf16[80,1024]{1,0:T(8,128)(2,1)}, bf16[80,1024]{1,0:T(8,128)(2,1)S(1)}, u32[]{:S(2)}, u32[]{:S(2)}) collective-permute-start(bf16[80,1024]{1,0:T(8,128)(2,1)} %get-tuple-element.51), channel_id=1, source_target_pairs={{0,3},{1,0},{2,1},{3,2},{4,7},{5,4},{6,5},{7,6},{8,11},{9,8},{10,9... | collective-permute-start | bytes 491528 | tf_op jit(solution)/shard_map/ppermute | solution.py:52
  (6 other events, 4.2 us)

commit v6 on v5

v6 whole, which is shorter than its diff:
```python
import functools

import jax
import jax.numpy as jnp
from jax import lax
from jax.experimental import pallas as pl
from jax.experimental.pallas import tpu as pltpu
from jax.sharding import PartitionSpec as P

BF = jnp.bfloat16
F32 = jnp.float32
SIDE = 4
SLOTS = 8
ROWS = 32
MINE = 4
FETCH_ORDER = (0, 1, 3, 2)
ANY = pl.BlockSpec(memory_space=pl.ANY)
WHOLE = pl.BlockSpec(memory_space=pltpu.VMEM)
SCALARS = pl.BlockSpec(memory_space=pltpu.SMEM)
SMALL = pltpu.CompilerParams(vmem_limit_bytes=8 * 1024 * 1024)
ORDER = pltpu.CompilerParams(vmem_limit_bytes=12 * 1024 * 1024)
LIMIT = pltpu.CompilerParams(vmem_limit_bytes=60 * 1024 * 1024)
Z_GROUPS = [[z * SIDE + y for z in range(SIDE)] for y in range(SIDE)]
Y_GROUPS = [[z * SIDE + y for y in range(SIDE)] for z in range(SIDE)]


def dot(a, b):
    return jnp.dot(a, b, preferred_element_type=F32)


def dot_nt(a, b):
    return lax.dot_general(a, b, (((1,), (1,)), ((), ())), preferred_element_type=F32)


def dot_tn(a, b):
    return lax.dot_general(a, b, (((0,), (0,)), ((), ())), preferred_element_type=F32)


def along_x(block, distance):
    return lax.ppermute(block, "mp", [(i, (i + distance) % SIDE) for i in range(SIDE)])


def along_z(block, distance):
    pairs = [
        (z * SIDE + y, (z + distance) % SIDE * SIDE + y) for z in range(SIDE) for y in range(SIDE)
    ]
    return lax.ppermute(block, "dp", pairs)


def along_y(block, distance):
    pairs = [
        (z * SIDE + y, z * SIDE + (y + distance) % SIDE) for z in range(SIDE) for y in range(SIDE)
    ]
    return lax.ppermute(block, "dp", pairs)


def along_mine(block, distance):
    pairs = []
    for z in range(SIDE):
        for y in range(SIDE):
            here = z * SIDE + y
            pairs.append((here, (z + distance) % SIDE * SIDE + y))
            pairs.append((16 + here, 16 + z * SIDE + (y + distance) % SIDE))
    return lax.ppermute(block, ("segment", "dp"), pairs)


def swap(block):
    return lax.ppermute(block, "segment", [(0, 1), (1, 0)])


def after(value, *others):
    return lax.optimization_barrier((value,) + others)[0]


def spread_kernel(routing, place, slots, out):
    core, replica = place[0], place[1]
    for group in range(16):
        slot = jnp.int32(0)
        for j in range(MINE):
            q = routing[(core * 16 + group) * MINE + j]
            slot = jnp.where(lax.shift_right_logical(q, 3) == replica, q & 7, slot)
        out[group] = slots[slot]


def spread(routing, place, slots):
    shape = (16,) + slots.shape[1:]
    return pl.pallas_call(
        spread_kernel,
        in_specs=[SCALARS, SCALARS, WHOLE],
        out_specs=WHOLE,
        out_shape=jax.ShapeDtypeStruct(shape, slots.dtype),
        compiler_params=LIMIT,
    )(routing, place, slots)


def merge_kernel(routing, counts, place, arrived, image, out, sems):
    first = (place[0] * 16 + place[1]) * MINE
    copies = []
    for j in range(MINE):
        replica = lax.shift_right_logical(routing[first + j], 3)
        copy = pltpu.make_async_copy(arrived.at[replica], out.at[j], sems.at[j])
        copy.start()
        copies.append(copy)
    row = lax.broadcasted_iota(jnp.int32, out.shape[1:], 0)
    for j in range(MINE):
        copies[j].wait()
        out[j] = jnp.where(row < counts[first + j], image[j], out[j])


def merge(routing, counts, place, arrived, image):
    columns = arrived.shape[2]
    return pl.pallas_call(
        merge_kernel,
        in_specs=[SCALARS] * 3 + [ANY, WHOLE],
        out_specs=WHOLE,
        scratch_shapes=[pltpu.SemaphoreType.DMA((MINE,))],
        out_shape=jax.ShapeDtypeStruct((MINE, ROWS, columns), arrived.dtype),
        compiler_params=LIMIT,
    )(routing, counts, place, arrived, image).reshape(MINE * ROWS, columns)


def pick_kernel(routing, place, arrived, out, sems):
    first = (place[0] * 16 + place[1]) * MINE
    copies = []
    for j in range(MINE):
        replica = lax.shift_right_logical(routing[first + j], 3)
        copy = pltpu.make_async_copy(arrived.at[replica], out.at[j], sems.at[j])
        copy.start()
        copies.append(copy)
    for copy in copies:
        copy.wait()


def pick(routing, place, arrived):
    columns = arrived.shape[2]
    return pl.pallas_call(
        pick_kernel,
        in_specs=[SCALARS] * 2 + [ANY],
        out_specs=WHOLE,
        scratch_shapes=[pltpu.SemaphoreType.DMA((MINE,))],
        out_shape=jax.ShapeDtypeStruct((MINE, ROWS, columns), arrived.dtype),
        compiler_params=SMALL,
    )(routing, place, arrived).reshape(MINE * ROWS, columns)


def gelu_parts(x):
    scale = 0.7978845608028654
    t = jnp.tanh(scale * (x + 0.044715 * (x * x * x)))
    cdf = 0.5 * (1.0 + t)
    slope = cdf + 0.5 * x * (1.0 - t * t) * (scale * (1.0 + 3 * 0.044715 * (x * x)))
    return x * cdf, slope


def fetch_weights(section, place, own, other, held, sems):
    core, x = place[0], place[2]
    size = held.shape[1]

    def copy(source, d):
        start = pl.multiple_of(lax.rem(x - d + SIDE, SIDE) * size, size)
        return pltpu.make_async_copy(source.at[pl.ds(start, size)], held.at[d], sems.at[d])

    for d in FETCH_ORDER:

        @pl.when(core == section)
        def _():
            copy(own, d).start()

        @pl.when(core != section)
        def _():
            copy(other, d).start()

    return lambda d: copy(own, d).wait()


def forward_product(wait, held, blocks):
    total = None
    for d in FETCH_ORDER:
        wait(d)
        product = dot(blocks[d][...], held[d][...])
        total = product if total is None else total + product
    return total


def send_terms(local, held, put, first, wait=None):
    for d in (2, 1, 3, 0):
        block = (SIDE - d) % SIDE
        if wait is not None:
            wait(block)
        put(first + d, dot_nt(local, held[block][...]).astype(BF))


def forward_body(wait, held, blocks, put):
    activation, slope = gelu_parts(forward_product(wait, held, blocks))
    put(0, (blocks[0][...].astype(F32) + activation).astype(BF))
    put(1, slope)


def middle_body(wait, held, operands, put):
    _, slope = gelu_parts(forward_product(wait, held, operands[:SIDE]))
    local = (slope * operands[SIDE][...].astype(F32)).astype(BF)
    put(0, local)
    send_terms(local, held, put, 1)


def summed(cotangent, terms):
    total = terms[0][...].astype(F32)
    for term in terms[1:]:
        total = total + term[...].astype(F32)
    return (cotangent[...].astype(F32) + total).astype(BF)


def backward_body(wait, held, operands, put):
    upstream, slope, local1, place = operands[SIDE:]
    now = summed(upstream, operands[:SIDE])
    put(0, now)
    local = (slope[...] * now.astype(F32)).astype(BF)
    first = place[0] == 0
    put(1, jnp.where(first, local, local1[...]))
    put(2, jnp.where(first, local1[...], local))
    send_terms(local, held, put, 3, wait)


def step_kernel(body, section, count, outs, place, own, other, *refs):
    sources, targets = refs[:count], refs[count : count + outs]
    operands = refs[count + outs : 2 * count + outs]
    results = refs[2 * count + outs : 2 * (count + outs)]
    held, weight_sems, in_sems, out_sems = refs[2 * (count + outs) :]
    copies = [
        pltpu.make_async_copy(sources[n], operands[n], in_sems.at[n]) for n in range(count)
    ]
    for copy in copies:
        copy.start()
    wait = fetch_weights(section, place, own, other, held, weight_sems)
    for copy in copies:
        copy.wait()
    out_copies = []

    def put(n, value):
        results[n][...] = value
        copy = pltpu.make_async_copy(results[n], targets[n], out_sems.at[n])
        copy.start()
        out_copies.append(copy)

    body(wait, held, operands, put)
    for copy in out_copies:
        copy.wait()


def step(body, section, place, own, other, operands, outs):
    rows, columns = own.shape
    count = len(operands)
    return pl.pallas_call(
        functools.partial(step_kernel, body, section, count, len(outs)),
        in_specs=[SCALARS] + [ANY] * (2 + count),
        out_specs=[ANY] * len(outs),
        out_shape=outs,
        scratch_shapes=[
            *(pltpu.VMEM(value.shape, value.dtype) for value in list(operands) + list(outs)),
            pltpu.VMEM((SIDE, rows // SIDE, columns), own.dtype),
            pltpu.SemaphoreType.DMA((SIDE,)),
            pltpu.SemaphoreType.DMA((count,)),
            pltpu.SemaphoreType.DMA((len(outs),)),
        ],
        compiler_params=LIMIT,
    )(place, own, other, *operands)


def turn_kernel(place, own, other, *outs_and_sems):
    outs, sems = outs_and_sems[:-1], outs_and_sems[-1]
    core, x = place[0], place[2]
    size = outs[0].shape[0]

    def copy(source, n):
        block = lax.rem(x - n % SIDE + SIDE, SIDE)
        start = pl.multiple_of(block * size, size)
        return pltpu.make_async_copy(source.at[pl.ds(start, size)], outs[n], sems.at[n])

    for n in range(2 * SIDE):

        @pl.when(core == n // SIDE)
        def _():
            copy(own, n).start()

        @pl.when(core != n // SIDE)
        def _():
            copy(other, n).start()

    for n in range(2 * SIDE):
        copy(own, n).wait()


def turn(place, own, other):
    rows, columns = own.shape
    blocks = pl.pallas_call(
        turn_kernel,
        in_specs=[pl.BlockSpec(memory_space=pltpu.SMEM), ANY, ANY],
        out_specs=[pl.BlockSpec(memory_space=pltpu.VMEM)] * (2 * SIDE),
        scratch_shapes=[pltpu.SemaphoreType.DMA((2 * SIDE,))],
        out_shape=[pltpu.VMEM((rows // SIDE, columns), own.dtype)] * (2 * SIDE),
        compiler_params=SMALL,
    )(place, own, other)
    return (blocks[:SIDE], blocks[SIDE:])


def held_kernel(body, count, outs, *refs):
    weights, operands, results = refs[:SIDE], refs[SIDE : SIDE + count], refs[SIDE + count :]

    def put(n, value):
        results[n][...] = value

    body(lambda d: None, weights, operands, put)


def held_step(body, weights, operands, outs):
    count = len(operands)
    return pl.pallas_call(
        functools.partial(held_kernel, body, count, len(outs)),
        in_specs=[
            SCALARS if value.dtype == jnp.int32 else WHOLE for value in list(weights) + operands
        ],
        out_specs=[WHOLE] * len(outs),
        out_shape=outs,
        compiler_params=pltpu.CompilerParams(vmem_limit_bytes=16 * 1024 * 1024),
    )(*weights, *operands)


def last_kernel(counts, place, r0, r1, r2, r3, cotangent, out):
    now = summed(cotangent, (r0, r1, r2, r3))
    first = (place[0] * 16 + place[1]) * MINE
    row = lax.broadcasted_iota(jnp.int32, (ROWS, now.shape[1]), 0)
    for j in range(MINE):
        rows = pl.ds(j * ROWS, ROWS)
        held = now[j * ROWS : (j + 1) * ROWS]
        out[rows] = jnp.where(row < counts[first + j], held, jnp.zeros_like(held))


def weight_grad_kernel(*refs):
    rows, local, out = refs[:SIDE], refs[SIDE : 2 * SIDE], refs[2 * SIDE]
    total = None
    for n in range(SIDE):
        product = dot_tn(rows[n][...], local[n][...])
        total = product if total is None else total + product
    out[...] = total.astype(BF).reshape(out.shape)


def weight_grad(rows, local):
    columns = local[0].shape[1]
    return pl.pallas_call(
        weight_grad_kernel,
        in_specs=[WHOLE] * (2 * SIDE),
        out_specs=WHOLE,
        out_shape=jax.ShapeDtypeStruct((SIDE, columns // SIDE, columns), BF),
        compiler_params=LIMIT,
    )(*rows, *local)


def merger_kernel(place, act, *refs):
    grads, outs, held = refs[:8], refs[8:12], refs[12]
    core, z = place[0], place[4]
    total = None
    for far in range(2):
        for e in range(SIDE):
            n = lax.rem(core + far, 2) * SIDE + lax.rem(z - e + SIDE, SIDE)
            product = dot(act[n], grads[far * SIDE + e][...])
            total = product if total is None else total + product
    held[...] = total
    size = outs[0].shape[0]
    for j in range(SIDE):
        start = pl.multiple_of(lax.rem(place[3] + j, SIDE) * size, size)
        outs[j][...] = held[pl.ds(start, size)].astype(BF)


def merger_parts(place, act, grads):
    columns = grads[0].shape[1]
    rows = act.shape[1]
    shape = jax.ShapeDtypeStruct((rows // SIDE, columns), BF)
    return pl.pallas_call(
        merger_kernel,
        in_specs=[SCALARS] + [WHOLE] * 9,
        out_specs=[WHOLE] * SIDE,
        out_shape=[shape] * SIDE,
        scratch_shapes=[pltpu.VMEM((rows, columns), F32)],
        compiler_params=LIMIT,
    )(place, act, *grads)


def order_kernel(place, *refs):
    blocks, keep, give = refs[: 2 * SIDE], refs[2 * SIDE], refs[2 * SIDE + 1]
    core, x, y, z = place[0], place[2], place[3], place[4]
    part = blocks[0].shape[1] // SIDE

    def write(section, out):
        for d in range(SIDE):
            block = blocks[section * SIDE + d]
            if section == 0:
                out[lax.rem(x - d - z + 2 * SIDE, SIDE)] = block[...]
            else:
                to = pl.ds(pl.multiple_of(lax.rem(x - d + SIDE, SIDE) * part, part), part)
                for e in range(SIDE):
                    of = pl.ds(pl.multiple_of(lax.rem(y + e, SIDE) * part, part), part)
                    out[e, :, to] = block[:, of]

    @pl.when(core == 0)
    def _():
        write(0, keep)
        write(1, give)

    @pl.when(core == 1)
    def _():
        write(1, keep)
        write(0, give)


def order(place, blocks):
    shape = jax.ShapeDtypeStruct((SIDE,) + blocks[0].shape, BF)
    return pl.pallas_call(
        order_kernel,
        in_specs=[SCALARS] + [WHOLE] * (2 * SIDE),
        out_specs=[WHOLE] * 2,
        out_shape=[shape] * 2,
        compiler_params=ORDER,
    )(place, *blocks)


def pair_kernel(keep, far, *outs):
    rows = keep.shape[1]
    for n, out in enumerate(outs):
        out[pl.ds(0, rows)] = keep[n]
        out[pl.ds(rows, rows)] = far[n]


def pair(keep, far):
    count, rows, columns = keep.shape
    return pl.pallas_call(
        pair_kernel,
        in_specs=[WHOLE] * 2,
        out_specs=[WHOLE] * count,
        out_shape=[jax.ShapeDtypeStruct((2 * rows, columns), BF)] * count,
        compiler_params=ORDER,
    )(keep, far)


def on_device(patches, merger_weight, image_counts, routing, text_embed, llm_weight, upstream):
    core = lax.axis_index("segment")
    x = lax.axis_index("mp")
    replica = lax.axis_index("dp")
    z, y = replica // SIDE, replica % SIDE
    place = jnp.stack([core, replica, x, y, z]).astype(jnp.int32)
    columns = merger_weight.shape[1]
    merger = patches.shape[2]
    tokens = MINE * ROWS
    block = jax.ShapeDtypeStruct((tokens, columns), BF)

    own = llm_weight[0]
    other = swap(own)
    send_text = spread(routing, place, text_embed.reshape(SLOTS, ROWS, columns))
    arrived_text = lax.all_to_all(send_text, "dp", 0, 0, tiled=True)
    activated = jax.nn.gelu(patches.astype(F32)).astype(BF).reshape(tokens, merger)
    embeds = dot(activated, merger_weight).astype(BF).reshape(MINE, ROWS, columns)
    send_ups = spread(routing, place, upstream.reshape(SLOTS, ROWS, columns))
    act_parts = activated.T.reshape(8, merger // 8, tokens)
    arrived_text, embeds, act_parts, send_ups, other = lax.optimization_barrier(
        (arrived_text, embeds, act_parts, send_ups, other)
    )
    start = merge(routing, image_counts, place, arrived_text, embeds)

    blocks0 = [start] + [along_x(start, d) for d in (1, 2, 3)]
    arrived_ups = lax.all_to_all(after(send_ups, start), "dp", 0, 0, tiled=True)
    hidden, slope = step(
        forward_body, 0, place, own, other, blocks0, [block, jax.ShapeDtypeStruct(block.shape, F32)]
    )

    blocks1 = [hidden] + [along_x(hidden, d) for d in (1, 2, 3)]
    top = pick(routing, place, arrived_ups)
    weights = turn(place, own, after(other, top))
    local1, *terms = held_step(middle_body, weights[1], blocks1 + [top], [block] * 5)

    terms = [terms[0]] + [along_x(terms[d], d) for d in (1, 2, 3)]
    keep, give = order(place, [after(blocks0[0], local1)] + blocks0[1:] + blocks1)
    rows = pair(keep, swap(give))
    rows = [rows[0]] + [along_mine(rows[e], e) for e in (1, 2, 3)]
    cotangent, keep, give, *sends = held_step(
        backward_body, weights[0], terms + [top, slope, local1, place], [block] * 7
    )

    ends = [sends[0]] + [along_x(sends[d], d) for d in (1, 2, 3)]
    local = pair(keep[None], swap(give)[None])[0]
    local = [local] + [along_mine(local, e) for e in (1, 2, 3)]
    eights = [
        [c * 16 + zz * SIDE + yy for c in range(2) for zz in range(SIDE)] for yy in range(SIDE)
    ]
    act_cols = lax.all_to_all(
        after(act_parts, cotangent), ("segment", "dp"), 0, 0, tiled=True, axis_index_groups=eights
    )
    grad = pl.pallas_call(
        last_kernel,
        in_specs=[SCALARS, SCALARS] + [WHOLE] * 5,
        out_specs=WHOLE,
        out_shape=block,
        compiler_params=SMALL,
    )(image_counts, place, *ends, after(cotangent, *rows[1:], *local[1:]))
    going = grad
    grads = [grad] + [along_z(going, e) for e in (1, 2, 3)]

    part = weight_grad([after(rows[0], grad)] + rows[1:], local)
    sums = [[c * 16 + n for n in g] for c, gs in ((0, Y_GROUPS), (1, Z_GROUPS)) for g in gs]
    part = lax.all_to_all(part, ("segment", "dp"), 0, 0, tiled=True, axis_index_groups=sums)
    llm_grad = jnp.sum(part.astype(F32), axis=0)[None]

    parts = merger_parts(place, act_cols, grads + [swap(g) for g in grads])
    merger_grad = parts[0].astype(F32)
    for j in (1, 2, 3):
        merger_grad = merger_grad + along_y(parts[j], j).astype(F32)
    return (llm_grad, merger_grad)


def solution(mesh):
    return jax.shard_map(
        on_device,
        mesh=mesh,
        in_specs=(
            P(("segment", "dp"), None, None),
            P(None, "mp"),
            P(),
            P(),
            P(None, "dp", "mp"),
            P("segment", None, "mp"),
            P(None, "dp", "mp"),
        ),
        out_specs=(P("segment", "dp", "mp"), P(("segment", "dp"), "mp")),
        check_vma=False,
    )
```

time: 255 us -> 193 us (0.76)
  blocking collectives: 28.3 us -> 0 us
  waiting for transfers between devices: 87.2 us -> 70 us
  Pallas kernels: 51.7 us -> 39.1 us
  starting transfers between devices: 69.7 us -> 64.3 us
    all_to_all x1 -> x0, blocking collectives: 28.3 us -> none  [exchange(): lax.all_to_all(blocks, 'dp', 0, 0, tiled=True, axis_index_groups=groups)]
    ppermute x6 -> x3, waiting for transfers between devices: 24.4 us -> 12.5 us  [along_z(): return lax.ppermute(block, 'dp', pairs)]
    pallas_call x8 -> x10, Pallas kernels: 41 us -> 29.9 us  [the longest x2 7.65 us: held_step(): pl.pallas_call(functools.partial(held_kernel, body, count, len(outs)), in...]
    ppermute x6, waiting for transfers between devices: 2.13 us -> 13.1 us  [along_mine(): return lax.ppermute(block, ('segment', 'dp'), pairs)]
    ppermute x12, waiting for transfers between devices: 32.5 us -> 22.1 us  [along_x(): lax.ppermute(block, 'mp', [(i, (i + distance) % SIDE) for i in range(SIDE)])]
    all_to_all x3 -> x2, waiting for transfers between devices: 6.39 us -> 0.01 us  [the longest x1 0.01 us: on_device(): arrived_ups = lax.all_to_all(after(send_ups, start), 'dp', 0, 0, tiled=True)]
    ppermute x6 -> x3, starting transfers between devices: 11.2 us -> 5.5 us  [along_z(): return lax.ppermute(block, 'dp', pairs)]
    all_to_all x3 -> x2, starting transfers between devices: 13.1 us -> 7.99 us  [the longest x1 4.2 us: on_device(): lax.all_to_all(after(act_parts, cotangent), ('segment', 'dp'), 0, 0, tile...]
  transfers between devices with their start and end apart: 37 -> 35, of which waited for: 20 -> 18; matrix products, arithmetic and copies ran while one was open for 3% -> 4% of each run, Pallas kernels for 17% -> 16%
where the time goes in v6:
time: 193 us; the launch traced here: 191 us
  waiting for transfers between devices  70 us (36%)
  starting transfers between devices  64.3 us (33%)
  Pallas kernels  39.1 us (20%)
  local copies, waits for them, and re-layouts  9.3 us (5%)
  matrix products  4.04 us (2%)
  other arithmetic  3.52 us (2%)
    ppermute x12, waiting for transfers between devices, along_x(): lax.ppermute(block, 'mp', [(i, (i + distance) % SIDE) for i in range(SIDE)])  22.1 us
    ppermute x12, starting transfers between devices, along_x(): lax.ppermute(block, 'mp', [(i, (i + distance) % SIDE) for i in range(SIDE)])  20.8 us
    ppermute x6, waiting for transfers between devices, along_mine(): return lax.ppermute(block, ('segment', 'dp'), pairs)  13.1 us
    ppermute x3, waiting for transfers between devices, along_z(): return lax.ppermute(block, 'dp', pairs)  12.5 us
    all_to_all x1, waiting for transfers between devices, on_device(): arrived_text = lax.all_to_all(send_text, 'dp', 0, 0, tiled=True)  10.8 us
    ppermute x6, starting transfers between devices, along_mine(): return lax.ppermute(block, ('segment', 'dp'), pairs)  10.8 us
    ppermute x3, waiting for transfers between devices, along_y(): return lax.ppermute(block, 'dp', pairs)  8.45 us
    all_to_all x1, starting transfers between devices, on_device(): arrived_text = lax.all_to_all(send_text, 'dp', 0, 0, tiled=True)  8.13 us
  transfers between devices with their start and end apart: 35, of which 18 were waited for; matrix products, arithmetic and copies ran while one was open for 4% of the time, Pallas kernels for 16%

profile of v6, /device:TPU:0, one launch (start us, length us, event | category | flops | bytes accessed | tf_op | source)
XLA Modules:
  0.0 191.4 jit_solution(10500762717905292772)
XLA Ops:
  0.8 0.6 stack.23.place.refs_11_
  1.4 2.1 %shard_map.86 = bf16[16,32,1024]{2,1,0:T(8,128)(2,1)} custom-call(s32[128]{0:T(128)} %routing.7, s32[5]{0:T(128)} %stack.23.place.refs_11_, bf16[8,32,1024]{2,1,0:T(8,128)(2,1)} %bitcast.37), custom_call_target="tpu_custom_call" | custom-call | tf_op jit(solution)/shard_map/pallas_call | solution.py:87
  3.5 8.1 %all-to-all-start = ((bf16[16,32,1024]{2,1,0:T(8,128)(2,1)}), bf16[16,32,1024]{2,1,0:T(8,128)(2,1)S(1)}, u32[]{:S(2)}, u32[]{:S(2)}) async-start(bf16[16,32,1024]{2,1,0:T(8,128)(2,1)} %shard_map.86), calls=%async_computation | async-start | bytes 2097152 | tf_op jit(solution)/shard_map/all_to_all | solution.py:457
  12.1 1.1 copy.9
  13.2 2.1 %shard_map.87 = bf16[16,32,1024]{2,1,0:T(8,128)(2,1)} custom-call(s32[128]{0:T(128)} %routing.7, s32[5]{0:T(128)} %stack.23.place.refs_11_, bf16[8,32,1024]{2,1,0:T(8,128)(2,1)} %bitcast.38), custom_call_target="tpu_custom_call" | custom-call | tf_op jit(solution)/shard_map/pallas_call | solution.py:87
  15.4 4.0 %convolution_convert_fusion = bf16[128,1024]{1,0:T(8,128)(2,1)} fusion(bf16[128,2560]{1,0:T(8,128)(2,1)S(1)} %bitcast.33, bf16[2560,1024]{1,0:T(8,128)(2,1)} %param.8), kind=kOutput, calls=%fused_computation.11 | convolution fusion | flops 671219712 | bytes 6160384 | tf_op jit(solution)/shard_map/dot_general | solution.py:28
  19.4 10.8 %all-to-all-done.arrived = bf16[16,32,1024]{2,1,0:T(8,128)(2,1)S(1)} async-done(((bf16[16,32,1024]{2,1,0:T(8,128)(2,1)}), bf16[16,32,1024]{2,1,0:T(8,128)(2,1)S(1)}, u32[]{:S(2)}, u32[]{:S(2)}) %all-to-all-start) | async-done | bytes 1048608 | tf_op jit(solution)/shard_map/all_to_all | solution.py:457
  30.2 1.0 copy-done.17
  31.2 2.7 %shard_map.88 = bf16[4,32,1024]{2,1,0:T(8,128)(2,1)} custom-call(s32[128]{0:T(128)} %routing.7, s32[128]{0:T(128)} %counts.3, s32[5]{0:T(128)} %stack.23.place.refs_11_, bf16[16,32,1024]{2,1,0:T(8,128)(2,1)} %copy-done.17, bf16[4,32,1024]{2,1,0:T(8,128)(2,1)} %bitcast.36), custom_call_target="tpu_custom_call" | custom-call | tf_op jit(solution)/shard_map/pallas_call | solution.py:112
  33.9 3.8 %all-to-all-start.1 = ((bf16[16,32,1024]{2,1,0:T(8,128)(2,1)}), bf16[16,32,1024]{2,1,0:T(8,128)(2,1)S(1)}, u32[]{:S(2)}, u32[]{:S(2)}) async-start(bf16[16,32,1024]{2,1,0:T(8,128)(2,1)} %shard_map.87), calls=%async_computation.1 | async-start | bytes 2097152 | tf_op jit(solution)/shard_map/all_to_all | solution.py:468
  37.7 1.6 collective-permute-start.1
  39.3 2.7 %collective-permute-start.2 = (bf16[128,1024]{1,0:T(8,128)(2,1)S(1)}, bf16[128,1024]{1,0:T(8,128)(2,1)S(1)}, u32[]{:S(2)}, u32[]{:S(2)}) collective-permute-start(bf16[128,1024]{1,0:T(8,128)(2,1)S(1)} %bitcast.25), channel_id=1, source_target_pairs={{0,32},{16,48},{32,0},{48,16},{1,33},{17,49},{33,1},{49,17},{2,34}... | collective-permute-start | bytes 786440 | tf_op jit(solution)/shard_map/ppermute | solution.py:40
  42.0 1.4 collective-permute-start.3
  43.4 3.8 %collective-permute-done.1.refs_1_ = bf16[128,1024]{1,0:T(8,128)(2,1)S(1)} collective-permute-done((bf16[128,1024]{1,0:T(8,128)(2,1)S(1)}, bf16[128,1024]{1,0:T(8,128)(2,1)S(1)}, u32[]{:S(2)}, u32[]{:S(2)}) %collective-permute-start.1) | collective-permute-done | bytes 262176 | tf_op jit(solution)/shard_map/ppermute | solution.py:40
  47.3 5.7 %collective-permute-done.2.refs_2_ = bf16[128,1024]{1,0:T(8,128)(2,1)S(1)} collective-permute-done((bf16[128,1024]{1,0:T(8,128)(2,1)S(1)}, bf16[128,1024]{1,0:T(8,128)(2,1)S(1)}, u32[]{:S(2)}, u32[]{:S(2)}) %collective-permute-start.2) | collective-permute-done | bytes 262176 | tf_op jit(solution)/shard_map/ppermute | solution.py:40
  53.0 0.7 copy-done.6
  53.7 0.7 copy-done.8
  54.4 7.1 %shard_map.91 = (bf16[128,1024]{1,0:T(8,128)(2,1)}, f32[128,1024]{1,0:T(8,128)}) custom-call(s32[5]{0:T(128)} %stack.23.place.refs_11_, bf16[4096,1024]{1,0:T(8,128)(2,1)} %bitcast.21, bf16[4096,1024]{1,0:T(8,128)(2,1)} %collective-permute-done.other, bf16[128,1024]{1,0:T(8,128)(2,1)} %bitcast.23, bf16[128,1024]{1,0:T(8,128)(2,1)} %copy-done.4, ...), custom_call_target="tpu_custom_call" | custom-call | tf_op jit(solution)/shard_map/pallas_call | solution.py:252
  61.5 0.7 collective-permute-start.4
  62.2 2.4 %collective-permute-start.5 = (bf16[128,1024]{1,0:T(8,128)(2,1)}, bf16[128,1024]{1,0:T(8,128)(2,1)S(1)}, u32[]{:S(2)}, u32[]{:S(2)}) collective-permute-start(bf16[128,1024]{1,0:T(8,128)(2,1)} %get-tuple-element.55.refs_4_), channel_id=1, source_target_pairs={{0,32},{16,48},{32,0},{48,16},{1,33},{17,49},{33,1},{49,17},{2,34}... | collective-permute-start | bytes 786440 | tf_op jit(solution)/shard_map/ppermute | solution.py:40
  64.6 1.6 collective-permute-start.6
  66.2 0.9 shard_map.89
  67.1 3.4 %copy-done = bf16[1,4096,1024]{2,1,0:T(8,128)(2,1)S(1)} copy-done((bf16[1,4096,1024]{2,1,0:T(8,128)(2,1)S(1)}, bf16[1,4096,1024]{2,1,0:T(8,128)(2,1)}, u32[]{:S(2)}) %copy-start) | copy-done | bytes 8388632
  70.5 4.7 %shard_map.90 = (bf16[1024,1024]{1,0:T(8,128)(2,1)S(1)}, bf16[1024,1024]{1,0:T(8,128)(2,1)S(1)}, bf16[1024,1024]{1,0:T(8,128)(2,1)S(1)}, bf16[1024,1024]{1,0:T(8...) custom-call(s32[5]{0:T(128)S(1)} %copy-done.14, ...), custom_call_target="tpu_custom_call" | custom-call | tf_op jit(solution)/shard_map/pallas_call | solution.py:294
  75.7 4.2 %shard_map.92 = (bf16[128,1024]{1,0:T(8,128)(2,1)S(1)}, bf16[128,1024]{1,0:T(8,128)(2,1)S(1)}, bf16[128,1024]{1,0:T(8,128)(2,1)S(1)}, bf16[128,1024]{1,0:T(8,128)(2,1)S(1)}, bf16[128,1024]{1,0:T(8,128)(2,1)S(1)}) custom-call(bf16[1024,1024]{1,0:T(8,128)(2,1)S(1)} %get-tuple-element.51.refs_0_, bf16[1024,1024]{1,0:T(8,128)(2,1)S(1)} %get-tuple-element.52.refs_1_, ...), custom_call_target="tpu_custom_call" | custom-call | tf_op jit(solution)/shard_map/pallas_call | solution.py:316
  80.0 0.8 shard_map.93
  80.9 0.8 collective-permute-start.8
  81.8 2.8 %collective-permute-start.9 = (bf16[128,1024]{1,0:T(8,128)(2,1)S(1)}, bf16[128,1024]{1,0:T(8,128)(2,1)S(1)}, u32[]{:S(2)}, u32[]{:S(2)}) collective-permute-start(bf16[128,1024]{1,0:T(8,128)(2,1)S(1)} %get-tuple-element.67), channel_id=1, source_target_pairs={{0,32},{16,48},{32,0},{48,16},{1,33},{17,49},{33,1},{49,17},{2,34}... | collective-permute-start | bytes 786440 | tf_op jit(solution)/shard_map/ppermute | solution.py:40
  85.1 5.9 %collective-permute-done.8.refs_5_ = bf16[128,1024]{1,0:T(8,128)(2,1)S(1)} collective-permute-done((bf16[128,1024]{1,0:T(8,128)(2,1)S(1)}, bf16[128,1024]{1,0:T(8,128)(2,1)S(1)}, u32[]{:S(2)}, u32[]{:S(2)}) %collective-permute-start.8) | collective-permute-done | bytes 262176 | tf_op jit(solution)/shard_map/ppermute | solution.py:40
  90.9 5.9 %collective-permute-done.9.refs_6_ = bf16[128,1024]{1,0:T(8,128)(2,1)S(1)} collective-permute-done((bf16[128,1024]{1,0:T(8,128)(2,1)S(1)}, bf16[128,1024]{1,0:T(8,128)(2,1)S(1)}, u32[]{:S(2)}, u32[]{:S(2)}) %collective-permute-start.9) | collective-permute-done | bytes 262176 | tf_op jit(solution)/shard_map/ppermute | solution.py:40
  97.1 3.4 %shard_map.95 = (bf16[128,1024]{1,0:T(8,128)(2,1)S(1)}, bf16[128,1024]{1,0:T(8,128)(2,1)S(1)}, bf16[128,1024]{1,0:T(8,128)(2,1)S(1)}, bf16[128,1024]{1,0:T(8,128...) custom-call(bf16[1024,1024]{1,0:T(8,128)(2,1)S(1)} %get-tuple-element.61.ref, ...), custom_call_target="tpu_custom_call" | custom-call | tf_op jit(solution)/shard_map/pallas_call | solution.py:316
  100.6 1.5 collective-permute-done.17
  102.2 1.5 collective-permute-start.18
  103.7 2.6 %collective-permute-start.19 = (bf16[256,1024]{1,0:T(8,128)(2,1)S(1)}, bf16[256,1024]{1,0:T(8,128)(2,1)}, u32[]{:S(2)}, u32[]{:S(2)}) collective-permute-start(bf16[256,1024]{1,0:T(8,128)(2,1)S(1)} %shard_map.96.refs_4_), channel_id=1, source_target_pairs={{0,8},{64,66},{1,9},{65,67},{2,10},{66,64},{3,11},{67,65},{4,12},{... | collective-permute-start | bytes 1572872 | tf_op jit(solution)/shard_map/ppermute | solution.py:64
  106.3 1.5 collective-permute-start.20
  108.0 0.8 copy-done.12
  109.3 4.2 %all-to-all-start.3 = ((bf16[8,320,128]{2,1,0:T(8,128)(2,1)}), bf16[8,320,128]{2,1,0:T(8,128)(2,1)}, u32[]{:S(2)}, u32[]{:S(2)}) async-start(bf16[8,320,128]{2,1,0:T(8,128)(2,1)} %bitcast.34), calls=%async_computation.3 | async-start | bytes 1310720 | tf_op jit(solution)/shard_map/all_to_all | solution.py:492
  113.5 3.4 %collective-permute-start.15 = (bf16[256,1024]{1,0:T(8,128)(2,1)S(1)}, bf16[256,1024]{1,0:T(8,128)(2,1)S(1)}, u32[]{:S(2)}, u32[]{:S(2)}) collective-permute-start(bf16[256,1024]{1,0:T(8,128)(2,1)S(1)} %get-tuple-element.76), channel_id=1, source_target_pairs={{0,8},{64,66},{1,9},{65,67},{2,10},{66,64},{3,11},{67,65},{4,12},{... | collective-permute-start | bytes 1572872 | tf_op jit(solution)/shard_map/ppermute | solution.py:64
  116.9 1.2 collective-permute-start.16
  118.1 2.2 %collective-permute-done.19.refs_6_ = bf16[256,1024]{1,0:T(8,128)(2,1)} collective-permute-done((bf16[256,1024]{1,0:T(8,128)(2,1)S(1)}, bf16[256,1024]{1,0:T(8,128)(2,1)}, u32[]{:S(2)}, u32[]{:S(2)}) %collective-permute-start.19) | collective-permute-done | bytes 524320 | tf_op jit(solution)/shard_map/ppermute | solution.py:64
  120.3 1.0 collective-permute-start.11
  121.7 2.6 %collective-permute-start.12 = (bf16[128,1024]{1,0:T(8,128)(2,1)S(1)}, bf16[128,1024]{1,0:T(8,128)(2,1)S(1)}, u32[]{:S(2)}, u32[]{:S(2)}) collective-permute-start(bf16[128,1024]{1,0:T(8,128)(2,1)S(1)} %get-tuple-element.72), channel_id=1, source_target_pairs={{0,32},{16,48},{32,0},{48,16},{1,33},{17,49},{33,1},{49,17},{2,34}... | collective-permute-start | bytes 786440 | tf_op jit(solution)/shard_map/ppermute | solution.py:40
  124.4 4.0 %collective-permute-done.14.refs_1_ = bf16[256,1024]{1,0:T(8,128)(2,1)} collective-permute-done((bf16[256,1024]{1,0:T(8,128)(2,1)S(1)}, bf16[256,1024]{1,0:T(8,128)(2,1)}, u32[]{:S(2)}, u32[]{:S(2)}) %collective-permute-start.14) | collective-permute-done | bytes 524320 | tf_op jit(solution)/shard_map/ppermute | solution.py:64
  128.3 2.6 %collective-permute-start.13 = (bf16[128,1024]{1,0:T(8,128)(2,1)S(1)}, bf16[128,1024]{1,0:T(8,128)(2,1)S(1)}, u32[]{:S(2)}, u32[]{:S(2)}) collective-permute-start(bf16[128,1024]{1,0:T(8,128)(2,1)S(1)} %get-tuple-element.73), channel_id=1, source_target_pairs={{0,48},{16,0},{32,16},{48,32},{1,49},{17,1},{33,17},{49,33},{2,50}... | collective-permute-start | bytes 786440 | tf_op jit(solution)/shard_map/ppermute | solution.py:40
  131.0 6.5 %collective-permute-done.15.refs_2_ = bf16[256,1024]{1,0:T(8,128)(2,1)S(1)} collective-permute-done((bf16[256,1024]{1,0:T(8,128)(2,1)S(1)}, bf16[256,1024]{1,0:T(8,128)(2,1)S(1)}, u32[]{:S(2)}, u32[]{:S(2)}) %collective-permute-start.15) | collective-permute-done | bytes 524320 | tf_op jit(solution)/shard_map/ppermute | solution.py:64
  137.5 0.8 copy-done.20
  138.3 0.7 shard_map.97.refs_0_
  139.0 6.0 %shard_map.98 = bf16[4,256,1024]{2,1,0:T(8,128)(2,1)} custom-call(bf16[256,1024]{1,0:T(8,128)(2,1)} %copy-done.12, bf16[256,1024]{1,0:T(8,128)(2,1)} %collective-permute-done.14.refs_1_, bf16[256,1024]{1,0:T(8,128)(2,1)} %copy-done.19, bf16[256,1024]{1,0:T(8,128)(2,1)} %copy-done.20, bf16[256,1024]{1,0:T(8,128)(2,1)} %copy-done.3, ...), custom_call_target="tpu_custom_call" | custom-call | tf_op jit(solution)/shard_map/pallas_call | solution.py:348
  145.0 4.3 %all-to-all-start.2 = ((bf16[4,256,1024]{2,1,0:T(8,128)(2,1)}), bf16[4,256,1024]{2,1,0:T(8,128)(2,1)S(1)}, u32[]{:S(2)}, u32[]{:S(2)}) async-start(bf16[4,256,1024]{2,1,0:T(8,128)(2,1)} %shard_map.98), calls=%async_computation.2 | async-start | bytes 4194304 | tf_op jit(solution)/shard_map/all_to_all | solution.py:507
  149.3 1.9 collective-permute-start.21
  151.2 2.1 %collective-permute-start.22 = (bf16[128,1024]{1,0:T(8,128)(2,1)S(1)}, bf16[128,1024]{1,0:T(8,128)(2,1)S(1)}, u32[]{:S(2)}, u32[]{:S(2)}) collective-permute-start(bf16[128,1024]{1,0:T(8,128)(2,1)S(1)} %shard_map.97.refs_0_), channel_id=1, source_target_pairs={{0,8},{1,9},{2,10},{3,11},{4,12},{5,13},{6,14},{7,15},{8,0},{9,1},... | collective-permute-start | bytes 786440 | tf_op jit(solution)/shard_map/ppermute | solution.py:47
  153.3 1.5 collective-permute-start.23
  154.8 12.4 %collective-permute-done.21.refs_1_ = bf16[128,1024]{1,0:T(8,128)(2,1)S(1)} collective-permute-done((bf16[128,1024]{1,0:T(8,128)(2,1)S(1)}, bf16[128,1024]{1,0:T(8,128)(2,1)S(1)}, u32[]{:S(2)}, u32[]{:S(2)}) %collective-permute-start.21) | collective-permute-done | bytes 262176 | tf_op jit(solution)/shard_map/ppermute | solution.py:47
  167.3 3.0 %collective-permute-start.26 = (bf16[128,1024]{1,0:T(8,128)(2,1)S(1)}, bf16[128,1024]{1,0:T(8,128)(2,1)S(1)}, u32[]{:S(2)}, u32[]{:S(2)}) collective-permute-start(bf16[128,1024]{1,0:T(8,128)(2,1)S(1)} %collective-permute-done.22.refs_2_), channel_id=1, source_target_pairs={{0,64},{64,0},{1,65},{65,1},{2,66},{66,2},{3,67},{67,3},{4,68},{68... | collective-permute-start | bytes 786440 | tf_op jit(solution)/shard_map/ppermute | solution.py:68
  170.3 1.0 collective-permute-done.26.refs_6_
  172.1 4.2 %shard_map.99 = (bf16[80,1024]{1,0:T(8,128)(2,1)}, bf16[80,1024]{1,0:T(8,128)(2,1)}, bf16[80,1024]{1,0:T(8,128)(2,1)}, bf16[80,1024]{1,0:T(8,128)(2,1)}) custom-call(s32[5]{0:T(128)} %stack.23.place.refs_11_, bf16[8,320,128]{2,1,0:T(8,128)(2,1)} %all-to-all-done.3.act, bf16[128,1024]{1,0:T(8,128)(2,1)} %copy-done.11, bf16[128,1024]{1,0:T(8,128)(2,1)} %copy-done.21, ...), custom_call_target="tpu_custom_call" | custom-call | tf_op jit(solution)/shard_map/pallas_call | solution.py:377
  176.3 0.6 collective-permute-start.30
  176.9 2.1 %collective-permute-start.29 = (bf16[80,1024]{1,0:T(8,128)(2,1)}, bf16[80,1024]{1,0:T(8,128)(2,1)S(1)}, u32[]{:S(2)}, u32[]{:S(2)}) collective-permute-start(bf16[80,1024]{1,0:T(8,128)(2,1)} %get-tuple-element.86), channel_id=1, source_target_pairs={{0,2},{1,3},{2,0},{3,1},{4,6},{5,7},{6,4},{7,5},{8,10},{9,11},{10,... | collective-permute-start | bytes 491528 | tf_op jit(solution)/shard_map/ppermute | solution.py:54
  179.0 0.8 collective-permute-start.28
  179.8 3.7 %collective-permute-done.30 = bf16[80,1024]{1,0:T(8,128)(2,1)S(1)} collective-permute-done((bf16[80,1024]{1,0:T(8,128)(2,1)}, bf16[80,1024]{1,0:T(8,128)(2,1)S(1)}, u32[]{:S(2)}, u32[]{:S(2)}) %collective-permute-start.30) | collective-permute-done | bytes 163872 | tf_op jit(solution)/shard_map/ppermute | solution.py:54
  183.5 2.1 %collective-permute-done.29 = bf16[80,1024]{1,0:T(8,128)(2,1)S(1)} collective-permute-done((bf16[80,1024]{1,0:T(8,128)(2,1)}, bf16[80,1024]{1,0:T(8,128)(2,1)S(1)}, u32[]{:S(2)}, u32[]{:S(2)}) %collective-permute-start.29) | collective-permute-done | bytes 163872 | tf_op jit(solution)/shard_map/ppermute | solution.py:54
  185.6 2.6 %collective-permute-done.28 = bf16[80,1024]{1,0:T(8,128)(2,1)S(1)} collective-permute-done((bf16[80,1024]{1,0:T(8,128)(2,1)}, bf16[80,1024]{1,0:T(8,128)(2,1)S(1)}, u32[]{:S(2)}, u32[]{:S(2)}) %collective-permute-start.28) | collective-permute-done | bytes 163872 | tf_op jit(solution)/shard_map/ppermute | solution.py:54
  188.3 1.7 convert_add_fusion.1
  190.0 1.3 convert_reduce_fusion
  (80 shorter events, 4.0 us)
Async XLA Ops:
  0.6 11.0 %copy-start.18 = (bf16[4,32,2560]{2,1,0:T(8,128)(2,1)S(1)}, bf16[4,32,2560]{2,1,0:T(8,128)(2,1)}, u32[]{:S(2)}) copy-start(bf16[4,32,2560]{2,1,0:T(8,128)(2,1)} %param.7) | copy-start | bytes 1966084
  0.6 29.6 %collective-permute-start = (bf16[4096,1024]{1,0:T(8,128)(2,1)}, bf16[4096,1024]{1,0:T(8,128)(2,1)}, u32[]{:S(2)}, u32[]{:S(2)}) collective-permute-start(bf16[4096,1024]{1,0:T(8,128)(2,1)} %bitcast.20), channel_id=1, source_target_pairs={{0,64},{64,0},{1,65},{65,1},{2,66},{66,2},{3,67},{67,3},{4,68},{68... | collective-permute-start | bytes 25165832 | tf_op jit(solution)/shard_map/ppermute | solution.py:68
  3.5 26.7 %all-to-all-start = ((bf16[16,32,1024]{2,1,0:T(8,128)(2,1)}), bf16[16,32,1024]{2,1,0:T(8,128)(2,1)S(1)}, u32[]{:S(2)}, u32[]{:S(2)}) async-start(bf16[16,32,1024]{2,1,0:T(8,128)(2,1)} %shard_map.86), calls=%async_computation | async-start | bytes 2097152 | tf_op jit(solution)/shard_map/all_to_all | solution.py:457
  30.2 1.0 copy-start.17
  33.9 3.8 %copy-start.1 = (bf16[4,32,1024]{2,1,0:T(8,128)(2,1)S(1)}, bf16[4,32,1024]{2,1,0:T(8,128)(2,1)}, u32[]{:S(2)}) copy-start(bf16[4,32,1024]{2,1,0:T(8,128)(2,1)} %shard_map.88) | copy-start | bytes 786436
  33.9 32.3 %all-to-all-start.1 = ((bf16[16,32,1024]{2,1,0:T(8,128)(2,1)}), bf16[16,32,1024]{2,1,0:T(8,128)(2,1)S(1)}, u32[]{:S(2)}, u32[]{:S(2)}) async-start(bf16[16,32,1024]{2,1,0:T(8,128)(2,1)} %shard_map.87), calls=%async_computation.1 | async-start | bytes 2097152 | tf_op jit(solution)/shard_map/all_to_all | solution.py:468
  37.7 28.5 %copy-start.14 = (s32[5]{0:T(128)S(1)}, s32[5]{0:T(128)}, u32[]{:S(2)}) copy-start(s32[5]{0:T(128)} %stack.23.place.refs_11_) | copy-start | bytes 64
  37.7 28.5 %copy-start.15 = (s32[128]{0:T(128)S(1)}, s32[128]{0:T(128)}, u32[]{:S(2)}) copy-start(s32[128]{0:T(128)} %routing.7) | copy-start | bytes 1540
  37.7 9.5 %collective-permute-start.1 = (bf16[128,1024]{1,0:T(8,128)(2,1)S(1)}, bf16[128,1024]{1,0:T(8,128)(2,1)S(1)}, u32[]{:S(2)}, u32[]{:S(2)}) collective-permute-start(bf16[128,1024]{1,0:T(8,128)(2,1)S(1)} %bitcast.24), channel_id=1, source_target_pairs={{0,16},{16,32},{32,48},{48,0},{1,17},{17,33},{33,49},{49,1},{2,18}... | collective-permute-start | bytes 786440 | tf_op jit(solution)/shard_map/ppermute | solution.py:40
  39.3 13.7 %collective-permute-start.2 = (bf16[128,1024]{1,0:T(8,128)(2,1)S(1)}, bf16[128,1024]{1,0:T(8,128)(2,1)S(1)}, u32[]{:S(2)}, u32[]{:S(2)}) collective-permute-start(bf16[128,1024]{1,0:T(8,128)(2,1)S(1)} %bitcast.25), channel_id=1, source_target_pairs={{0,32},{16,48},{32,0},{48,16},{1,33},{17,49},{33,1},{49,17},{2,34}... | collective-permute-start | bytes 786440 | tf_op jit(solution)/shard_map/ppermute | solution.py:40
  42.0 11.0 %collective-permute-start.3 = (bf16[128,1024]{1,0:T(8,128)(2,1)S(1)}, bf16[128,1024]{1,0:T(8,128)(2,1)S(1)}, u32[]{:S(2)}, u32[]{:S(2)}) collective-permute-start(bf16[128,1024]{1,0:T(8,128)(2,1)S(1)} %bitcast.26), channel_id=1, source_target_pairs={{0,48},{16,0},{32,16},{48,32},{1,49},{17,1},{33,17},{49,33},{2,50}... | collective-permute-start | bytes 786440 | tf_op jit(solution)/shard_map/ppermute | solution.py:40
  47.2 5.8 %copy-start.4 = (bf16[128,1024]{1,0:T(8,128)(2,1)}, bf16[128,1024]{1,0:T(8,128)(2,1)S(1)}, u32[]{:S(2)}) copy-start(bf16[128,1024]{1,0:T(8,128)(2,1)S(1)} %collective-permute-done.1.refs_1_) | copy-start | bytes 786436
  53.0 0.7 copy-start.6
  53.7 0.7 copy-start.8
  61.5 13.7 %collective-permute-start.4 = (bf16[128,1024]{1,0:T(8,128)(2,1)}, bf16[128,1024]{1,0:T(8,128)(2,1)S(1)}, u32[]{:S(2)}, u32[]{:S(2)}) collective-permute-start(bf16[128,1024]{1,0:T(8,128)(2,1)} %get-tuple-element.55.refs_4_), channel_id=1, source_target_pairs={{0,16},{16,32},{32,48},{48,0},{1,17},{17,33},{33,49},{49,1},{2,18}... | collective-permute-start | bytes 786440 | tf_op jit(solution)/shard_map/ppermute | solution.py:40
  62.2 13.5 %collective-permute-start.5 = (bf16[128,1024]{1,0:T(8,128)(2,1)}, bf16[128,1024]{1,0:T(8,128)(2,1)S(1)}, u32[]{:S(2)}, u32[]{:S(2)}) collective-permute-start(bf16[128,1024]{1,0:T(8,128)(2,1)} %get-tuple-element.55.refs_4_), channel_id=1, source_target_pairs={{0,32},{16,48},{32,0},{48,16},{1,33},{17,49},{33,1},{49,17},{2,34}... | collective-permute-start | bytes 786440 | tf_op jit(solution)/shard_map/ppermute | solution.py:40
  64.6 11.1 %collective-permute-start.6 = (bf16[128,1024]{1,0:T(8,128)(2,1)}, bf16[128,1024]{1,0:T(8,128)(2,1)S(1)}, u32[]{:S(2)}, u32[]{:S(2)}) collective-permute-start(bf16[128,1024]{1,0:T(8,128)(2,1)} %get-tuple-element.55.refs_4_), channel_id=1, source_target_pairs={{0,48},{16,0},{32,16},{48,32},{1,49},{17,1},{33,17},{49,33},{2,50}... | collective-permute-start | bytes 786440 | tf_op jit(solution)/shard_map/ppermute | solution.py:40
  67.1 3.4 %copy-start = (bf16[1,4096,1024]{2,1,0:T(8,128)(2,1)S(1)}, bf16[1,4096,1024]{2,1,0:T(8,128)(2,1)}, u32[]{:S(2)}) copy-start(bf16[1,4096,1024]{2,1,0:T(8,128)(2,1)} %param.12) | copy-start | bytes 25165828
  70.5 5.2 %copy-start.10 = (bf16[128,1024]{1,0:T(8,128)(2,1)S(1)}, bf16[128,1024]{1,0:T(8,128)(2,1)}, u32[]{:S(2)}) copy-start(bf16[128,1024]{1,0:T(8,128)(2,1)} %get-tuple-element.55.refs_4_) | copy-start | bytes 786436
  75.7 4.3 %copy-start.2 = (bf16[4,32,1024]{2,1,0:T(8,128)(2,1)S(1)}, bf16[4,32,1024]{2,1,0:T(8,128)(2,1)}, u32[]{:S(2)}) copy-start(bf16[4,32,1024]{2,1,0:T(8,128)(2,1)} %shard_map.88) | copy-start | bytes 786436
  75.7 4.3 %copy-start.5 = (bf16[128,1024]{1,0:T(8,128)(2,1)S(1)}, bf16[128,1024]{1,0:T(8,128)(2,1)}, u32[]{:S(2)}) copy-start(bf16[128,1024]{1,0:T(8,128)(2,1)} %copy-done.4) | copy-start | bytes 786436
  75.7 4.3 %copy-start.7 = (bf16[128,1024]{1,0:T(8,128)(2,1)S(1)}, bf16[128,1024]{1,0:T(8,128)(2,1)}, u32[]{:S(2)}) copy-start(bf16[128,1024]{1,0:T(8,128)(2,1)} %copy-done.6) | copy-start | bytes 786436
  75.7 4.3 %copy-start.9 = (bf16[128,1024]{1,0:T(8,128)(2,1)S(1)}, bf16[128,1024]{1,0:T(8,128)(2,1)}, u32[]{:S(2)}) copy-start(bf16[128,1024]{1,0:T(8,128)(2,1)} %copy-done.8) | copy-start | bytes 786436
  80.0 17.1 %copy-start.13 = (f32[128,1024]{1,0:T(8,128)S(1)}, f32[128,1024]{1,0:T(8,128)}, u32[]{:S(2)}) copy-start(f32[128,1024]{1,0:T(8,128)} %get-tuple-element.69.refs_9_) | copy-start | bytes 1572868
  80.8 27.0 %collective-permute-start.7 = (bf16[4,128,1024]{2,1,0:T(8,128)(2,1)S(1)}, bf16[4,128,1024]{2,1,0:T(8,128)(2,1)S(1)}, u32[]{:S(2)}, u32[]{:S(2)}) collective-permute-start(bf16[4,128,1024]{2,1,0:T(8,128)(2,1)S(1)} %get-tuple-element.59), channel_id=1, source_target_pairs={{0,64},{64,0},{1,65},{65,1},{2,66},{66,2},{3,67},{67,3},{4,68},{68... | collective-permute-start | bytes 3145736 | tf_op jit(solution)/shard_map/ppermute | solution.py:68
  80.9 10.0 %collective-permute-start.8 = (bf16[128,1024]{1,0:T(8,128)(2,1)S(1)}, bf16[128,1024]{1,0:T(8,128)(2,1)S(1)}, u32[]{:S(2)}, u32[]{:S(2)}) collective-permute-start(bf16[128,1024]{1,0:T(8,128)(2,1)S(1)} %get-tuple-element.66), channel_id=1, source_target_pairs={{0,16},{16,32},{32,48},{48,0},{1,17},{17,33},{33,49},{49,1},{2,18}... | collective-permute-start | bytes 786440 | tf_op jit(solution)/shard_map/ppermute | solution.py:40
  81.8 15.1 %collective-permute-start.9 = (bf16[128,1024]{1,0:T(8,128)(2,1)S(1)}, bf16[128,1024]{1,0:T(8,128)(2,1)S(1)}, u32[]{:S(2)}, u32[]{:S(2)}) collective-permute-start(bf16[128,1024]{1,0:T(8,128)(2,1)S(1)} %get-tuple-element.67), channel_id=1, source_target_pairs={{0,32},{16,48},{32,0},{48,16},{1,33},{17,49},{33,1},{49,17},{2,34}... | collective-permute-start | bytes 786440 | tf_op jit(solution)/shard_map/ppermute | solution.py:40
  84.6 12.5 %collective-permute-start.10 = (bf16[128,1024]{1,0:T(8,128)(2,1)S(1)}, bf16[128,1024]{1,0:T(8,128)(2,1)S(1)}, u32[]{:S(2)}, u32[]{:S(2)}) collective-permute-start(bf16[128,1024]{1,0:T(8,128)(2,1)S(1)} %get-tuple-element.68), channel_id=1, source_target_pairs={{0,48},{16,0},{32,16},{48,32},{1,49},{17,1},{33,17},{49,33},{2,50}... | collective-permute-start | bytes 786440 | tf_op jit(solution)/shard_map/ppermute | solution.py:40
  100.5 1.6 collective-permute-start.17
  102.1 36.2 %copy-start.16 = (s32[128]{0:T(128)S(1)}, s32[128]{0:T(128)}, u32[]{:S(2)}) copy-start(s32[128]{0:T(128)} %counts.3) | copy-start | bytes 1540
  102.2 36.9 %copy-start.3 = (bf16[256,1024]{1,0:T(8,128)(2,1)}, bf16[256,1024]{1,0:T(8,128)(2,1)S(1)}, u32[]{:S(2)}) copy-start(bf16[256,1024]{1,0:T(8,128)(2,1)S(1)} %shard_map.96.refs_4_) | copy-start | bytes 1572868
  102.2 14.7 %collective-permute-start.18 = (bf16[256,1024]{1,0:T(8,128)(2,1)S(1)}, bf16[256,1024]{1,0:T(8,128)(2,1)}, u32[]{:S(2)}, u32[]{:S(2)}) collective-permute-start(bf16[256,1024]{1,0:T(8,128)(2,1)S(1)} %shard_map.96.refs_4_), channel_id=1, source_target_pairs={{0,4},{64,65},{1,5},{65,66},{2,6},{66,67},{3,7},{67,64},{4,8},{68,... | collective-permute-start | bytes 1572872 | tf_op jit(solution)/shard_map/ppermute | solution.py:64
  103.7 16.6 %collective-permute-start.19 = (bf16[256,1024]{1,0:T(8,128)(2,1)S(1)}, bf16[256,1024]{1,0:T(8,128)(2,1)}, u32[]{:S(2)}, u32[]{:S(2)}) collective-permute-start(bf16[256,1024]{1,0:T(8,128)(2,1)S(1)} %shard_map.96.refs_4_), channel_id=1, source_target_pairs={{0,8},{64,66},{1,9},{65,67},{2,10},{66,64},{3,11},{67,65},{4,12},{... | collective-permute-start | bytes 1572872 | tf_op jit(solution)/shard_map/ppermute | solution.py:64
  106.3 15.4 %collective-permute-start.20 = (bf16[256,1024]{1,0:T(8,128)(2,1)S(1)}, bf16[256,1024]{1,0:T(8,128)(2,1)}, u32[]{:S(2)}, u32[]{:S(2)}) collective-permute-start(bf16[256,1024]{1,0:T(8,128)(2,1)S(1)} %shard_map.96.refs_4_), channel_id=1, source_target_pairs={{0,12},{64,67},{1,13},{65,64},{2,14},{66,65},{3,15},{67,66},{4,0},... | collective-permute-start | bytes 1572872 | tf_op jit(solution)/shard_map/ppermute | solution.py:64
  108.0 0.8 copy-start.12
  108.8 19.6 %collective-permute-start.14 = (bf16[256,1024]{1,0:T(8,128)(2,1)S(1)}, bf16[256,1024]{1,0:T(8,128)(2,1)}, u32[]{:S(2)}, u32[]{:S(2)}) collective-permute-start(bf16[256,1024]{1,0:T(8,128)(2,1)S(1)} %get-tuple-element.75), channel_id=1, source_target_pairs={{0,4},{64,65},{1,5},{65,66},{2,6},{66,67},{3,7},{67,64},{4,8},{68,... | collective-permute-start | bytes 1572872 | tf_op jit(solution)/shard_map/ppermute | solution.py:64
  109.3 35.7 %all-to-all-start.3 = ((bf16[8,320,128]{2,1,0:T(8,128)(2,1)}), bf16[8,320,128]{2,1,0:T(8,128)(2,1)}, u32[]{:S(2)}, u32[]{:S(2)}) async-start(bf16[8,320,128]{2,1,0:T(8,128)(2,1)} %bitcast.34), calls=%async_computation.3 | async-start | bytes 1310720 | tf_op jit(solution)/shard_map/all_to_all | solution.py:492
  113.5 23.9 %collective-permute-start.15 = (bf16[256,1024]{1,0:T(8,128)(2,1)S(1)}, bf16[256,1024]{1,0:T(8,128)(2,1)S(1)}, u32[]{:S(2)}, u32[]{:S(2)}) collective-permute-start(bf16[256,1024]{1,0:T(8,128)(2,1)S(1)} %get-tuple-element.76), channel_id=1, source_target_pairs={{0,8},{64,66},{1,9},{65,67},{2,10},{66,64},{3,11},{67,65},{4,12},{... | collective-permute-start | bytes 1572872 | tf_op jit(solution)/shard_map/ppermute | solution.py:64
  116.9 20.5 %collective-permute-start.16 = (bf16[256,1024]{1,0:T(8,128)(2,1)S(1)}, bf16[256,1024]{1,0:T(8,128)(2,1)S(1)}, u32[]{:S(2)}, u32[]{:S(2)}) collective-permute-start(bf16[256,1024]{1,0:T(8,128)(2,1)S(1)} %get-tuple-element.77), channel_id=1, source_target_pairs={{0,12},{64,67},{1,13},{65,64},{2,14},{66,65},{3,15},{67,66},{4,0},... | collective-permute-start | bytes 1572872 | tf_op jit(solution)/shard_map/ppermute | solution.py:64
  120.3 17.2 %collective-permute-start.11 = (bf16[128,1024]{1,0:T(8,128)(2,1)S(1)}, bf16[128,1024]{1,0:T(8,128)(2,1)S(1)}, u32[]{:S(2)}, u32[]{:S(2)}) collective-permute-start(bf16[128,1024]{1,0:T(8,128)(2,1)S(1)} %get-tuple-element.71), channel_id=1, source_target_pairs={{0,16},{16,32},{32,48},{48,0},{1,17},{17,33},{33,49},{49,1},{2,18}... | collective-permute-start | bytes 786440 | tf_op jit(solution)/shard_map/ppermute | solution.py:40
  121.7 15.7 %collective-permute-start.12 = (bf16[128,1024]{1,0:T(8,128)(2,1)S(1)}, bf16[128,1024]{1,0:T(8,128)(2,1)S(1)}, u32[]{:S(2)}, u32[]{:S(2)}) collective-permute-start(bf16[128,1024]{1,0:T(8,128)(2,1)S(1)} %get-tuple-element.72), channel_id=1, source_target_pairs={{0,32},{16,48},{32,0},{48,16},{1,33},{17,49},{33,1},{49,17},{2,34}... | collective-permute-start | bytes 786440 | tf_op jit(solution)/shard_map/ppermute | solution.py:40
  128.3 9.1 %collective-permute-start.13 = (bf16[128,1024]{1,0:T(8,128)(2,1)S(1)}, bf16[128,1024]{1,0:T(8,128)(2,1)S(1)}, u32[]{:S(2)}, u32[]{:S(2)}) collective-permute-start(bf16[128,1024]{1,0:T(8,128)(2,1)S(1)} %get-tuple-element.73), channel_id=1, source_target_pairs={{0,48},{16,0},{32,16},{48,32},{1,49},{17,1},{33,17},{49,33},{2,50}... | collective-permute-start | bytes 786440 | tf_op jit(solution)/shard_map/ppermute | solution.py:40
  137.4 1.6 copy-start.19
  137.5 0.8 copy-start.20
  139.0 15.8 %copy-start.11 = (bf16[128,1024]{1,0:T(8,128)(2,1)}, bf16[128,1024]{1,0:T(8,128)(2,1)S(1)}, u32[]{:S(2)}) copy-start(bf16[128,1024]{1,0:T(8,128)(2,1)S(1)} %shard_map.97.refs_0_) | copy-start | bytes 786436
  145.0 45.0 %all-to-all-start.2 = ((bf16[4,256,1024]{2,1,0:T(8,128)(2,1)}), bf16[4,256,1024]{2,1,0:T(8,128)(2,1)S(1)}, u32[]{:S(2)}, u32[]{:S(2)}) async-start(bf16[4,256,1024]{2,1,0:T(8,128)(2,1)} %shard_map.98), calls=%async_computation.2 | async-start | bytes 4194304 | tf_op jit(solution)/shard_map/all_to_all | solution.py:507
  149.3 18.0 %collective-permute-start.21 = (bf16[128,1024]{1,0:T(8,128)(2,1)S(1)}, bf16[128,1024]{1,0:T(8,128)(2,1)S(1)}, u32[]{:S(2)}, u32[]{:S(2)}) collective-permute-start(bf16[128,1024]{1,0:T(8,128)(2,1)S(1)} %shard_map.97.refs_0_), channel_id=1, source_target_pairs={{0,4},{1,5},{2,6},{3,7},{4,8},{5,9},{6,10},{7,11},{8,12},{9,13},{1... | collective-permute-start | bytes 786440 | tf_op jit(solution)/shard_map/ppermute | solution.py:47
  151.2 16.1 %collective-permute-start.22 = (bf16[128,1024]{1,0:T(8,128)(2,1)S(1)}, bf16[128,1024]{1,0:T(8,128)(2,1)S(1)}, u32[]{:S(2)}, u32[]{:S(2)}) collective-permute-start(bf16[128,1024]{1,0:T(8,128)(2,1)S(1)} %shard_map.97.refs_0_), channel_id=1, source_target_pairs={{0,8},{1,9},{2,10},{3,11},{4,12},{5,13},{6,14},{7,15},{8,0},{9,1},... | collective-permute-start | bytes 786440 | tf_op jit(solution)/shard_map/ppermute | solution.py:47
  153.3 16.9 %collective-permute-start.23 = (bf16[128,1024]{1,0:T(8,128)(2,1)S(1)}, bf16[128,1024]{1,0:T(8,128)(2,1)S(1)}, u32[]{:S(2)}, u32[]{:S(2)}) collective-permute-start(bf16[128,1024]{1,0:T(8,128)(2,1)S(1)} %shard_map.97.refs_0_), channel_id=1, source_target_pairs={{0,12},{1,13},{2,14},{3,15},{4,0},{5,1},{6,2},{7,3},{8,4},{9,5},{1... | collective-permute-start | bytes 786440 | tf_op jit(solution)/shard_map/ppermute | solution.py:47
  154.8 15.5 %collective-permute-start.24 = (bf16[128,1024]{1,0:T(8,128)(2,1)S(1)}, bf16[128,1024]{1,0:T(8,128)(2,1)S(1)}, u32[]{:S(2)}, u32[]{:S(2)}) collective-permute-start(bf16[128,1024]{1,0:T(8,128)(2,1)S(1)} %shard_map.97.refs_0_), channel_id=1, source_target_pairs={{0,64},{64,0},{1,65},{65,1},{2,66},{66,2},{3,67},{67,3},{4,68},{68... | collective-permute-start | bytes 786440 | tf_op jit(solution)/shard_map/ppermute | solution.py:68
  167.3 4.6 %copy-start.21 = (bf16[128,1024]{1,0:T(8,128)(2,1)}, bf16[128,1024]{1,0:T(8,128)(2,1)S(1)}, u32[]{:S(2)}) copy-start(bf16[128,1024]{1,0:T(8,128)(2,1)S(1)} %collective-permute-done.21.refs_1_) | copy-start | bytes 786436
  167.3 3.1 %collective-permute-start.25 = (bf16[128,1024]{1,0:T(8,128)(2,1)S(1)}, bf16[128,1024]{1,0:T(8,128)(2,1)S(1)}, u32[]{:S(2)}, u32[]{:S(2)}) collective-permute-start(bf16[128,1024]{1,0:T(8,128)(2,1)S(1)} %collective-permute-done.21.refs_1_), channel_id=1, source_target_pairs={{0,64},{64,0},{1,65},{65,1},{2,66},{66,2},{3,67},{67,3},{4,68},{68... | collective-permute-start | bytes 786440 | tf_op jit(solution)/shard_map/ppermute | solution.py:68
  167.3 4.6 %copy-start.22 = (bf16[128,1024]{1,0:T(8,128)(2,1)}, bf16[128,1024]{1,0:T(8,128)(2,1)S(1)}, u32[]{:S(2)}) copy-start(bf16[128,1024]{1,0:T(8,128)(2,1)S(1)} %collective-permute-done.22.refs_2_) | copy-start | bytes 786436
  167.3 4.1 %collective-permute-start.26 = (bf16[128,1024]{1,0:T(8,128)(2,1)S(1)}, bf16[128,1024]{1,0:T(8,128)(2,1)S(1)}, u32[]{:S(2)}, u32[]{:S(2)}) collective-permute-start(bf16[128,1024]{1,0:T(8,128)(2,1)S(1)} %collective-permute-done.22.refs_2_), channel_id=1, source_target_pairs={{0,64},{64,0},{1,65},{65,1},{2,66},{66,2},{3,67},{67,3},{4,68},{68... | collective-permute-start | bytes 786440 | tf_op jit(solution)/shard_map/ppermute | solution.py:68
  170.2 1.7 copy-start.23
  170.2 1.7 collective-permute-start.27
  170.3 1.6 copy-start.24
  170.3 1.6 copy-start.25
  171.4 0.7 copy-start.26
  176.3 7.2 %collective-permute-start.30 = (bf16[80,1024]{1,0:T(8,128)(2,1)}, bf16[80,1024]{1,0:T(8,128)(2,1)S(1)}, u32[]{:S(2)}, u32[]{:S(2)}) collective-permute-start(bf16[80,1024]{1,0:T(8,128)(2,1)} %get-tuple-element.87), channel_id=1, source_target_pairs={{0,3},{1,0},{2,1},{3,2},{4,7},{5,4},{6,5},{7,6},{8,11},{9,8},{10,9... | collective-permute-start | bytes 491528 | tf_op jit(solution)/shard_map/ppermute | solution.py:54
  176.9 8.8 %collective-permute-start.29 = (bf16[80,1024]{1,0:T(8,128)(2,1)}, bf16[80,1024]{1,0:T(8,128)(2,1)S(1)}, u32[]{:S(2)}, u32[]{:S(2)}) collective-permute-start(bf16[80,1024]{1,0:T(8,128)(2,1)} %get-tuple-element.86), channel_id=1, source_target_pairs={{0,2},{1,3},{2,0},{3,1},{4,6},{5,7},{6,4},{7,5},{8,10},{9,11},{10,... | collective-permute-start | bytes 491528 | tf_op jit(solution)/shard_map/ppermute | solution.py:54
  179.0 9.3 %collective-permute-start.28 = (bf16[80,1024]{1,0:T(8,128)(2,1)}, bf16[80,1024]{1,0:T(8,128)(2,1)S(1)}, u32[]{:S(2)}, u32[]{:S(2)}) collective-permute-start(bf16[80,1024]{1,0:T(8,128)(2,1)} %get-tuple-element.85), channel_id=1, source_target_pairs={{0,1},{1,2},{2,3},{3,0},{4,5},{5,6},{6,7},{7,4},{8,9},{9,10},{10,1... | collective-permute-start | bytes 491528 | tf_op jit(solution)/shard_map/ppermute | solution.py:54

commit v7 on v6

--- a/solution.py
+++ b/solution.py
@@ -64,6 +64,16 @@
     return lax.ppermute(block, ("segment", "dp"), pairs)
 
 
+def along_other(block, distance):
+    pairs = []
+    for z in range(SIDE):
+        for y in range(SIDE):
+            here = z * SIDE + y
+            pairs.append((here, z * SIDE + (y + distance) % SIDE))
+            pairs.append((16 + here, 16 + (z + distance) % SIDE * SIDE + y))
+    return lax.ppermute(block, ("segment", "dp"), pairs)
+
+
 def swap(block):
     return lax.ppermute(block, "segment", [(0, 1), (1, 0)])
 
@@ -334,54 +344,93 @@
         out[rows] = jnp.where(row < counts[first + j], held, jnp.zeros_like(held))
 
 
-def weight_grad_kernel(*refs):
-    rows, local, out = refs[:SIDE], refs[SIDE : 2 * SIDE], refs[2 * SIDE]
+def weight_grad_kernel(place, *refs):
+    rows, local, outs, held = refs[:4], refs[4:8], refs[8:12], refs[12]
+    there = jnp.where(place[0] == 0, place[3], place[4])
     total = None
     for n in range(SIDE):
         product = dot_tn(rows[n][...], local[n][...])
         total = product if total is None else total + product
-    out[...] = total.astype(BF).reshape(out.shape)
-
-
-def weight_grad(rows, local):
-    columns = local[0].shape[1]
-    return pl.pallas_call(
-        weight_grad_kernel,
-        in_specs=[WHOLE] * (2 * SIDE),
-        out_specs=WHOLE,
-        out_shape=jax.ShapeDtypeStruct((SIDE, columns // SIDE, columns), BF),
-        compiler_params=LIMIT,
-    )(*rows, *local)
-
-
-def merger_kernel(place, act, *refs):
-    grads, outs, held = refs[:8], refs[8:12], refs[12]
-    core, z = place[0], place[4]
-    total = None
-    for far in range(2):
-        for e in range(SIDE):
-            n = lax.rem(core + far, 2) * SIDE + lax.rem(z - e + SIDE, SIDE)
-            product = dot(act[n], grads[far * SIDE + e][...])
-            total = product if total is None else total + product
     held[...] = total
     size = outs[0].shape[0]
     for j in range(SIDE):
-        start = pl.multiple_of(lax.rem(place[3] + j, SIDE) * size, size)
+        start = pl.multiple_of(lax.rem(there + j, SIDE) * size, size)
         outs[j][...] = held[pl.ds(start, size)].astype(BF)
 
 
-def merger_parts(place, act, grads):
+def weight_grad(place, rows, local):
+    columns = local[0].shape[1]
+    shape = jax.ShapeDtypeStruct((columns // SIDE, columns), BF)
+    return pl.pallas_call(
+        weight_grad_kernel,
+        in_specs=[SCALARS] + [WHOLE] * (2 * SIDE),
+        out_specs=[WHOLE] * SIDE,
+        out_shape=[shape] * SIDE,
+        scratch_shapes=[pltpu.VMEM((columns, columns), F32)],
+        compiler_params=LIMIT,
+    )(place, *rows, *local)
+
+
+def columns_kernel(place, activated, far, *outs):
+    core, y, z = place[0], place[3], place[4]
+    half, tokens = far.shape
+    rows = half // SIDE
+    part = rows // SIDE
+
+    def put(out, to, start):
+        out[to, :tokens] = activated[pl.ds(pl.multiple_of(core * half + start, part), to.size)]
+        out[to, tokens:] = far[pl.ds(pl.multiple_of(start, part), to.size)]
+
+    @pl.when(core == 0)
+    def _():
+        for e, out in enumerate(outs):
+            put(out, pl.ds(0, rows), lax.rem(z + e, SIDE) * rows)
+
+    @pl.when(core == 1)
+    def _():
+        for e, out in enumerate(outs):
+            for m in range(SIDE):
+                put(out, pl.ds(m * part, part), m * rows + lax.rem(y + e, SIDE) * part)
+
+
+def columns_out(place, activated, far):
+    half, tokens = far.shape
+    shape = jax.ShapeDtypeStruct((half // SIDE, 2 * tokens), BF)
+    return pl.pallas_call(
+        columns_kernel,
+        in_specs=[SCALARS] + [WHOLE] * 2,
+        out_specs=[WHOLE] * SIDE,
+        out_shape=[shape] * SIDE,
+        compiler_params=ORDER,
+    )(place, activated, far)
+
+
+def merger_kernel(place, *refs):
+    acts, grads, outs, held = refs[:4], refs[4:8], refs[8:12], refs[12]
+    there = jnp.where(place[0] == 0, place[3], place[4])
+    total = None
+    for n in range(SIDE):
+        product = dot(acts[n][...], grads[n][...])
+        total = product if total is None else total + product
+    held[...] = total
+    size = outs[0].shape[0]
+    for j in range(SIDE):
+        start = pl.multiple_of(lax.rem(there + j, SIDE) * size, size)
+        outs[j][...] = held[pl.ds(start, size)].astype(BF)
+
+
+def merger_parts(place, acts, grads):
     columns = grads[0].shape[1]
-    rows = act.shape[1]
+    rows = acts[0].shape[0]
     shape = jax.ShapeDtypeStruct((rows // SIDE, columns), BF)
     return pl.pallas_call(
         merger_kernel,
-        in_specs=[SCALARS] + [WHOLE] * 9,
+        in_specs=[SCALARS] + [WHOLE] * (2 * SIDE),
         out_specs=[WHOLE] * SIDE,
         out_shape=[shape] * SIDE,
         scratch_shapes=[pltpu.VMEM((rows, columns), F32)],
         compiler_params=LIMIT,
-    )(place, act, *grads)
+    )(place, *acts, *grads)
 
 
 def order_kernel(place, *refs):
@@ -422,17 +471,34 @@
     )(place, *blocks)
 
 
-def pair_kernel(keep, far, *outs):
+def pair_kernel(keep, far, out):
+    rows = keep.shape[-2]
+    out[..., pl.ds(0, rows), :] = keep[...]
+    out[..., pl.ds(rows, rows), :] = far[...]
+
+
+def pair(keep, far):
+    shape = keep.shape[:-2] + (2 * keep.shape[-2], keep.shape[-1])
+    return pl.pallas_call(
+        pair_kernel,
+        in_specs=[WHOLE] * 2,
+        out_specs=WHOLE,
+        out_shape=jax.ShapeDtypeStruct(shape, BF),
+        compiler_params=ORDER,
+    )(keep, far)
+
+
+def pairs_kernel(keep, far, *outs):
     rows = keep.shape[1]
     for n, out in enumerate(outs):
         out[pl.ds(0, rows)] = keep[n]
         out[pl.ds(rows, rows)] = far[n]
 
 
-def pair(keep, far):
+def pairs(keep, far):
     count, rows, columns = keep.shape
     return pl.pallas_call(
-        pair_kernel,
+        pairs_kernel,
         in_specs=[WHOLE] * 2,
         out_specs=[WHOLE] * count,
         out_shape=[jax.ShapeDtypeStruct((2 * rows, columns), BF)] * count,
@@ -458,9 +524,15 @@
     activated = jax.nn.gelu(patches.astype(F32)).astype(BF).reshape(tokens, merger)
     embeds = dot(activated, merger_weight).astype(BF).reshape(MINE, ROWS, columns)
     send_ups = spread(routing, place, upstream.reshape(SLOTS, ROWS, columns))
-    act_parts = activated.T.reshape(8, merger // 8, tokens)
-    arrived_text, embeds, act_parts, send_ups, other = lax.optimization_barrier(
-        (arrived_text, embeds, act_parts, send_ups, other)
+    act_columns = activated.T
+    act_far = swap(
+        lax.dynamic_slice_in_dim(act_columns, (1 - core) * (merger // 2), merger // 2)
+    )
+    acts = columns_out(place, act_columns, act_far)
+    acts = [acts[0]] + [along_mine(acts[e], e) for e in (1, 2, 3)]
+    mine = [[c * 16 + n for n in g] for c, gs in ((0, Z_GROUPS), (1, Y_GROUPS)) for g in gs]
+    arrived_text, embeds, acts, send_ups, other = lax.optimization_barrier(
+        (arrived_text, embeds, acts, send_ups, other)
     )
     start = merge(routing, image_counts, place, arrived_text, embeds)
 
@@ -477,40 +549,36 @@
 
     terms = [terms[0]] + [along_x(terms[d], d) for d in (1, 2, 3)]
     keep, give = order(place, [after(blocks0[0], local1)] + blocks0[1:] + blocks1)
-    rows = pair(keep, swap(give))
+    rows = pairs(keep, swap(give))
     rows = [rows[0]] + [along_mine(rows[e], e) for e in (1, 2, 3)]
     cotangent, keep, give, *sends = held_step(
-        backward_body, weights[0], terms + [top, slope, local1, place], [block] * 7
+        backward_body, weights[0], terms + [after(top, rows[0]), slope, local1, place], [block] * 7
     )
 
     ends = [sends[0]] + [along_x(sends[d], d) for d in (1, 2, 3)]
-    local = pair(keep[None], swap(give)[None])[0]
+    local = pair(keep, swap(give))
     local = [local] + [along_mine(local, e) for e in (1, 2, 3)]
-    eights = [
-        [c * 16 + zz * SIDE + yy for c in range(2) for zz in range(SIDE)] for yy in range(SIDE)
-    ]
-    act_cols = lax.all_to_all(
-        after(act_parts, cotangent), ("segment", "dp"), 0, 0, tiled=True, axis_index_groups=eights
-    )
     grad = pl.pallas_call(
         last_kernel,
         in_specs=[SCALARS, SCALARS] + [WHOLE] * 5,
         out_specs=WHOLE,
         out_shape=block,
         compiler_params=SMALL,
-    )(image_counts, place, *ends, after(cotangent, *rows[1:], *local[1:]))
+    )(image_counts, place, *ends, after(cotangent, *rows[1:]))
+    grad = pair(grad, swap(grad))
     going = grad
-    grads = [grad] + [along_z(going, e) for e in (1, 2, 3)]
-
-    part = weight_grad([after(rows[0], grad)] + rows[1:], local)
-    sums = [[c * 16 + n for n in g] for c, gs in ((0, Y_GROUPS), (1, Z_GROUPS)) for g in gs]
-    part = lax.all_to_all(part, ("segment", "dp"), 0, 0, tiled=True, axis_index_groups=sums)
-    llm_grad = jnp.sum(part.astype(F32), axis=0)[None]
-
-    parts = merger_parts(place, act_cols, grads + [swap(g) for g in grads])
+    grads = [grad] + [along_mine(going, e) for e in (1, 2, 3)]
+
+    parts = weight_grad(place, [after(rows[0], grad)] + rows[1:], local)
+    llm_grad = parts[0].astype(F32)
+    for j in (1, 2, 3):
+        llm_grad = llm_grad + along_other(parts[j], j).astype(F32)
+    llm_grad = llm_grad[None]
+
+    parts = merger_parts(place, [acts[0]] + acts[1:], grads)
     merger_grad = parts[0].astype(F32)
     for j in (1, 2, 3):
-        merger_grad = merger_grad + along_y(parts[j], j).astype(F32)
+        merger_grad = merger_grad + along_other(parts[j], j).astype(F32)
     return (llm_grad, merger_grad)
 
 

time: 193 us -> 173 us (0.90)
  waiting for transfers between devices: 70 us -> 52.8 us
    ppermute x6, waiting for transfers between devices: 20.9 us -> 6.37 us  [along_other(): return lax.ppermute(block, ('segment', 'dp'), pairs)]
    all_to_all x1, waiting for transfers between devices: 10.8 us -> 0.01 us  [on_device(): arrived_text = lax.all_to_all(send_text, 'dp', 0, 0, tiled=True)]
    ppermute x6 -> x12, starting transfers between devices: 10.8 us -> 21.2 us  [along_mine(): return lax.ppermute(block, ('segment', 'dp'), pairs)]
    all_to_all x2 -> x0, starting transfers between devices: 8.48 us -> none  [the longest x1 4.28 us: on_device(): lax.all_to_all(part, ('segment', 'dp'), 0, 0, tiled=True, axis_index_grou...]
    ppermute x12, waiting for transfers between devices: 22.1 us -> 29.8 us  [along_x(): lax.ppermute(block, 'mp', [(i, (i + distance) % SIDE) for i in range(SIDE)])]
    ppermute x7 -> x5, starting transfers between devices: 3.31 us -> 0.53 us  [swap(): return lax.ppermute(block, 'segment', [(0, 1), (1, 0)])]
    unnamed x54 -> x62, local copies, waits for them, and re-layouts: 7.58 us -> 8.14 us
    pallas_call x4 -> x6, Pallas kernels: 10.3 us -> 10.8 us  [the longest x1 6.37 us: weight_grad(): pl.pallas_call(weight_grad_kernel, in_specs=[SCALARS] + [WHOLE] * (2 * SI...]
  transfers between devices with their start and end apart: 35 -> 37, of which waited for: 18 -> 16; matrix products, arithmetic and copies ran while one was open for 4% -> 4% of each run, Pallas kernels for 16% -> 19%
where the time goes in v7:
time: 173 us; the launch traced here: 172 us
  starting transfers between devices  62.7 us (36%)
  waiting for transfers between devices  52.8 us (31%)
  Pallas kernels  39.8 us (23%)
  local copies, waits for them, and re-layouts  9.08 us (5%)
  matrix products  4.04 us (2%)
  other arithmetic  2.56 us (1%)
    ppermute x12, waiting for transfers between devices, along_x(): lax.ppermute(block, 'mp', [(i, (i + distance) % SIDE) for i in range(SIDE)])  29.8 us
    ppermute x12, starting transfers between devices, along_mine(): return lax.ppermute(block, ('segment', 'dp'), pairs)  21.2 us
    ppermute x12, starting transfers between devices, along_x(): lax.ppermute(block, 'mp', [(i, (i + distance) % SIDE) for i in range(SIDE)])  19 us
    ppermute x12, waiting for transfers between devices, along_mine(): return lax.ppermute(block, ('segment', 'dp'), pairs)  13.3 us
    ppermute x6, starting transfers between devices, along_other(): return lax.ppermute(block, ('segment', 'dp'), pairs)  8.48 us
    unnamed x62, local copies, waits for them, and re-layouts  8.14 us
    all_to_all x1, starting transfers between devices, on_device(): arrived_text = lax.all_to_all(send_text, 'dp', 0, 0, tiled=True)  8.13 us
    pallas_call x2, Pallas kernels, held_step(): pl.pallas_call(functools.partial(held_kernel, body, count, len(outs)), in...  7.64 us
  transfers between devices with their start and end apart: 37, of which 16 were waited for; matrix products, arithmetic and copies ran while one was open for 4% of the time, Pallas kernels for 19%

profile of v7, /device:TPU:0, one launch (start us, length us, event | category | flops | bytes accessed | tf_op | source)
XLA Modules:
  0.0 172.1 jit_solution(3094678847165658688)
XLA Ops:
  1.4 2.1 %shard_map.86 = bf16[16,32,1024]{2,1,0:T(8,128)(2,1)} custom-call(s32[128]{0:T(128)} %routing.7, s32[5]{0:T(128)} %stack.23.place.refs_11_, bf16[8,32,1024]{2,1,0:T(8,128)(2,1)} %bitcast.33), custom_call_target="tpu_custom_call" | custom-call | tf_op jit(solution)/shard_map/pallas_call | solution.py:97
  3.5 8.1 %all-to-all-start = ((bf16[16,32,1024]{2,1,0:T(8,128)(2,1)}), bf16[16,32,1024]{2,1,0:T(8,128)(2,1)S(1)}, u32[]{:S(2)}, u32[]{:S(2)}) async-start(bf16[16,32,1024]{2,1,0:T(8,128)(2,1)} %shard_map.86), calls=%async_computation | async-start | bytes 2097152 | tf_op jit(solution)/shard_map/all_to_all | solution.py:523
  12.8 1.6 collective-permute-done.far
  15.7 2.0 %collective-permute-start.1 = (bf16[320,256]{1,0:T(8,128)(2,1)S(1)}, bf16[320,256]{1,0:T(8,128)(2,1)S(1)}, u32[]{:S(2)}, u32[]{:S(2)}) collective-permute-start(bf16[320,256]{1,0:T(8,128)(2,1)S(1)} %get-tuple-element.57), channel_id=1, source_target_pairs={{0,4},{64,65},{1,5},{65,66},{2,6},{66,67},{3,7},{67,64},{4,8},{68,... | collective-permute-start | bytes 491528 | tf_op jit(solution)/shard_map/ppermute | solution.py:64
  17.7 3.6 %collective-permute-start.2 = (bf16[320,256]{1,0:T(8,128)(2,1)S(1)}, bf16[320,256]{1,0:T(8,128)(2,1)S(1)}, u32[]{:S(2)}, u32[]{:S(2)}) collective-permute-start(bf16[320,256]{1,0:T(8,128)(2,1)S(1)} %get-tuple-element.58), channel_id=1, source_target_pairs={{0,8},{64,66},{1,9},{65,67},{2,10},{66,64},{3,11},{67,65},{4,12},{... | collective-permute-start | bytes 491528 | tf_op jit(solution)/shard_map/ppermute | solution.py:64
  21.3 1.0 collective-permute-start.3
  22.3 4.0 %convolution_convert_fusion = bf16[128,1024]{1,0:T(8,128)(2,1)} fusion(bf16[128,2560]{1,0:T(8,128)(2,1)S(1)} %bitcast.31, bf16[2560,1024]{1,0:T(8,128)(2,1)} %param.8), kind=kOutput, calls=%fused_computation.10 | convolution fusion | flops 671219712 | bytes 6160384 | tf_op jit(solution)/shard_map/dot_general | solution.py:28
  26.3 2.1 %shard_map.88 = bf16[16,32,1024]{2,1,0:T(8,128)(2,1)} custom-call(s32[128]{0:T(128)} %routing.7, s32[5]{0:T(128)} %stack.23.place.refs_11_, bf16[8,32,1024]{2,1,0:T(8,128)(2,1)} %bitcast.34), custom_call_target="tpu_custom_call" | custom-call | tf_op jit(solution)/shard_map/pallas_call | solution.py:97
  28.5 2.9 %collective-permute-done.2.refs_2_ = bf16[320,256]{1,0:T(8,128)(2,1)S(1)} collective-permute-done((bf16[320,256]{1,0:T(8,128)(2,1)S(1)}, bf16[320,256]{1,0:T(8,128)(2,1)S(1)}, u32[]{:S(2)}, u32[]{:S(2)}) %collective-permute-start.2) | collective-permute-done | bytes 163872 | tf_op jit(solution)/shard_map/ppermute | solution.py:64
  31.4 1.0 copy-done.19
  32.3 2.7 %shard_map.89 = bf16[4,32,1024]{2,1,0:T(8,128)(2,1)} custom-call(s32[128]{0:T(128)} %routing.7, s32[128]{0:T(128)} %counts.3, s32[5]{0:T(128)} %stack.23.place.refs_11_, bf16[16,32,1024]{2,1,0:T(8,128)(2,1)} %copy-done.19, bf16[4,32,1024]{2,1,0:T(8,128)(2,1)} %bitcast.32), custom_call_target="tpu_custom_call" | custom-call | tf_op jit(solution)/shard_map/pallas_call | solution.py:122
  35.0 5.2 %all-to-all-start.1 = ((bf16[16,32,1024]{2,1,0:T(8,128)(2,1)}), bf16[16,32,1024]{2,1,0:T(8,128)(2,1)S(1)}, u32[]{:S(2)}, u32[]{:S(2)}) async-start(bf16[16,32,1024]{2,1,0:T(8,128)(2,1)} %shard_map.88), calls=%async_computation.1 | async-start | bytes 2097152 | tf_op jit(solution)/shard_map/all_to_all | solution.py:540
  40.3 1.6 collective-permute-start.5
  41.9 2.7 %collective-permute-start.6 = (bf16[128,1024]{1,0:T(8,128)(2,1)S(1)}, bf16[128,1024]{1,0:T(8,128)(2,1)S(1)}, u32[]{:S(2)}, u32[]{:S(2)}) collective-permute-start(bf16[128,1024]{1,0:T(8,128)(2,1)S(1)} %bitcast.25), channel_id=1, source_target_pairs={{0,32},{16,48},{32,0},{48,16},{1,33},{17,49},{33,1},{49,17},{2,34}... | collective-permute-start | bytes 786440 | tf_op jit(solution)/shard_map/ppermute | solution.py:40
  44.6 1.4 collective-permute-start.7
  46.0 3.8 %collective-permute-done.5.refs_1_ = bf16[128,1024]{1,0:T(8,128)(2,1)S(1)} collective-permute-done((bf16[128,1024]{1,0:T(8,128)(2,1)S(1)}, bf16[128,1024]{1,0:T(8,128)(2,1)S(1)}, u32[]{:S(2)}, u32[]{:S(2)}) %collective-permute-start.5) | collective-permute-done | bytes 262176 | tf_op jit(solution)/shard_map/ppermute | solution.py:40
  49.8 6.5 %collective-permute-done.6.refs_2_ = bf16[128,1024]{1,0:T(8,128)(2,1)S(1)} collective-permute-done((bf16[128,1024]{1,0:T(8,128)(2,1)S(1)}, bf16[128,1024]{1,0:T(8,128)(2,1)S(1)}, u32[]{:S(2)}, u32[]{:S(2)}) %collective-permute-start.6) | collective-permute-done | bytes 262176 | tf_op jit(solution)/shard_map/ppermute | solution.py:40
  56.3 0.7 copy-done.7
  57.0 0.7 copy-done.9
  57.7 7.1 %shard_map.92 = (bf16[128,1024]{1,0:T(8,128)(2,1)}, f32[128,1024]{1,0:T(8,128)}) custom-call(s32[5]{0:T(128)} %stack.23.place.refs_11_, bf16[4096,1024]{1,0:T(8,128)(2,1)} %bitcast.20, bf16[4096,1024]{1,0:T(8,128)(2,1)} %collective-permute-done.4.other, bf16[128,1024]{1,0:T(8,128)(2,1)} %bitcast.23, bf16[128,1024]{1,0:T(8,128)(2,1)} %copy-done.5, ...), custom_call_target="tpu_custom_call" | custom-call | tf_op jit(solution)/shard_map/pallas_call | solution.py:262
  65.6 2.4 %collective-permute-start.9 = (bf16[128,1024]{1,0:T(8,128)(2,1)}, bf16[128,1024]{1,0:T(8,128)(2,1)S(1)}, u32[]{:S(2)}, u32[]{:S(2)}) collective-permute-start(bf16[128,1024]{1,0:T(8,128)(2,1)} %get-tuple-element.70.refs_4_), channel_id=1, source_target_pairs={{0,32},{16,48},{32,0},{48,16},{1,33},{17,49},{33,1},{49,17},{2,34}... | collective-permute-start | bytes 786440 | tf_op jit(solution)/shard_map/ppermute | solution.py:40
  67.9 1.6 collective-permute-start.10
  69.5 0.9 shard_map.90
  70.5 3.4 %copy-done = bf16[1,4096,1024]{2,1,0:T(8,128)(2,1)S(1)} copy-done((bf16[1,4096,1024]{2,1,0:T(8,128)(2,1)S(1)}, bf16[1,4096,1024]{2,1,0:T(8,128)(2,1)}, u32[]{:S(2)}) %copy-start) | copy-done | bytes 8388632
  73.9 4.7 %shard_map.91 = (bf16[1024,1024]{1,0:T(8,128)(2,1)S(1)}, bf16[1024,1024]{1,0:T(8,128)(2,1)S(1)}, bf16[1024,1024]{1,0:T(8,128)(2,1)S(1)}, bf16[1024,1024]{1,0:T(8...) custom-call(s32[5]{0:T(128)S(1)} %copy-done.16, ...), custom_call_target="tpu_custom_call" | custom-call | tf_op jit(solution)/shard_map/pallas_call | solution.py:304
  78.6 0.8 collective-permute-done.9.refs_6_
  79.4 4.2 %shard_map.93 = (bf16[128,1024]{1,0:T(8,128)(2,1)S(1)}, bf16[128,1024]{1,0:T(8,128)(2,1)S(1)}, bf16[128,1024]{1,0:T(8,128)(2,1)S(1)}, bf16[128,1024]{1,0:T(8,128)(2,1)S(1)}, bf16[128,1024]{1,0:T(8,128)(2,1)S(1)}) custom-call(bf16[1024,1024]{1,0:T(8,128)(2,1)S(1)} %get-tuple-element.66.refs_0_, bf16[1024,1024]{1,0:T(8,128)(2,1)S(1)} %get-tuple-element.67.refs_1_, ...), custom_call_target="tpu_custom_call" | custom-call | tf_op jit(solution)/shard_map/pallas_call | solution.py:326
  83.7 0.9 shard_map.94
  84.8 1.0 collective-permute-start.12
  85.7 1.7 collective-permute-done.11.far
  87.6 0.8 copy-done.12
  88.4 1.6 collective-permute-start.18
  90.0 1.3 collective-permute-start.13
  91.3 2.0 %collective-permute-start.14 = (bf16[128,1024]{1,0:T(8,128)(2,1)S(1)}, bf16[128,1024]{1,0:T(8,128)(2,1)S(1)}, u32[]{:S(2)}, u32[]{:S(2)}) collective-permute-start(bf16[128,1024]{1,0:T(8,128)(2,1)S(1)} %get-tuple-element.83), channel_id=1, source_target_pairs={{0,48},{16,0},{32,16},{48,32},{1,49},{17,1},{33,17},{49,33},{2,50}... | collective-permute-start | bytes 786440 | tf_op jit(solution)/shard_map/ppermute | solution.py:40
  93.3 2.7 %collective-permute-start.19 = (bf16[256,1024]{1,0:T(8,128)(2,1)S(1)}, bf16[256,1024]{1,0:T(8,128)(2,1)S(1)}, u32[]{:S(2)}, u32[]{:S(2)}) collective-permute-start(bf16[256,1024]{1,0:T(8,128)(2,1)S(1)} %get-tuple-element.92), channel_id=1, source_target_pairs={{0,8},{64,66},{1,9},{65,67},{2,10},{66,64},{3,11},{67,65},{4,12},{... | collective-permute-start | bytes 1572872 | tf_op jit(solution)/shard_map/ppermute | solution.py:64
  96.0 1.6 collective-permute-start.20
  97.6 3.4 %collective-permute-done.13.refs_6_ = bf16[128,1024]{1,0:T(8,128)(2,1)S(1)} collective-permute-done((bf16[128,1024]{1,0:T(8,128)(2,1)S(1)}, bf16[128,1024]{1,0:T(8,128)(2,1)S(1)}, u32[]{:S(2)}, u32[]{:S(2)}) %collective-permute-start.13) | collective-permute-done | bytes 262176 | tf_op jit(solution)/shard_map/ppermute | solution.py:40
  101.1 3.7 %collective-permute-done.14.refs_7_ = bf16[128,1024]{1,0:T(8,128)(2,1)S(1)} collective-permute-done((bf16[128,1024]{1,0:T(8,128)(2,1)S(1)}, bf16[128,1024]{1,0:T(8,128)(2,1)S(1)}, u32[]{:S(2)}, u32[]{:S(2)}) %collective-permute-start.14) | collective-permute-done | bytes 262176 | tf_op jit(solution)/shard_map/ppermute | solution.py:40
  104.8 3.4 %shard_map.96 = (bf16[128,1024]{1,0:T(8,128)(2,1)S(1)}, bf16[128,1024]{1,0:T(8,128)(2,1)S(1)}, bf16[128,1024]{1,0:T(8,128)(2,1)S(1)}, bf16[128,1024]{1,0:T(8,128...) custom-call(bf16[1024,1024]{1,0:T(8,128)(2,1)S(1)} %get-tuple-element.76.ref, ...), custom_call_target="tpu_custom_call" | custom-call | tf_op jit(solution)/shard_map/pallas_call | solution.py:326
  108.2 1.1 collective-permute-start.15
  109.3 3.0 %collective-permute-start.16 = (bf16[128,1024]{1,0:T(8,128)(2,1)S(1)}, bf16[128,1024]{1,0:T(8,128)(2,1)S(1)}, u32[]{:S(2)}, u32[]{:S(2)}) collective-permute-start(bf16[128,1024]{1,0:T(8,128)(2,1)S(1)} %get-tuple-element.88), channel_id=1, source_target_pairs={{0,32},{16,48},{32,0},{48,16},{1,33},{17,49},{33,1},{49,17},{2,34}... | collective-permute-start | bytes 786440 | tf_op jit(solution)/shard_map/ppermute | solution.py:40
  112.6 4.8 %collective-permute-done.15.r1 = bf16[128,1024]{1,0:T(8,128)(2,1)S(1)} collective-permute-done((bf16[128,1024]{1,0:T(8,128)(2,1)S(1)}, bf16[128,1024]{1,0:T(8,128)(2,1)S(1)}, u32[]{:S(2)}, u32[]{:S(2)}) %collective-permute-start.15) | collective-permute-done | bytes 262176 | tf_op jit(solution)/shard_map/ppermute | solution.py:40
  117.4 6.8 %collective-permute-done.16.r2 = bf16[128,1024]{1,0:T(8,128)(2,1)S(1)} collective-permute-done((bf16[128,1024]{1,0:T(8,128)(2,1)S(1)}, bf16[128,1024]{1,0:T(8,128)(2,1)S(1)}, u32[]{:S(2)}, u32[]{:S(2)}) %collective-permute-start.16) | collective-permute-done | bytes 262176 | tf_op jit(solution)/shard_map/ppermute | solution.py:40
  124.2 0.7 shard_map.97.keep
  125.1 1.5 collective-permute-start.23
  126.6 2.7 %collective-permute-start.24 = (bf16[256,1024]{1,0:T(8,128)(2,1)S(1)}, bf16[256,1024]{1,0:T(8,128)(2,1)S(1)}, u32[]{:S(2)}, u32[]{:S(2)}) collective-permute-start(bf16[256,1024]{1,0:T(8,128)(2,1)S(1)} %shard_map.99.refs_4_), channel_id=1, source_target_pairs={{0,8},{64,66},{1,9},{65,67},{2,10},{66,64},{3,11},{67,65},{4,12},{... | collective-permute-start | bytes 1572872 | tf_op jit(solution)/shard_map/ppermute | solution.py:64
  129.3 1.4 collective-permute-start.25
  131.5 0.9 collective-permute-start.30
  132.3 3.2 %collective-permute-done.23.refs_5_ = bf16[256,1024]{1,0:T(8,128)(2,1)S(1)} collective-permute-done((bf16[256,1024]{1,0:T(8,128)(2,1)S(1)}, bf16[256,1024]{1,0:T(8,128)(2,1)S(1)}, u32[]{:S(2)}, u32[]{:S(2)}) %collective-permute-start.23) | collective-permute-done | bytes 524320 | tf_op jit(solution)/shard_map/ppermute | solution.py:64
  135.5 1.5 collective-permute-start.31
  137.0 5.2 %collective-permute-done.24.refs_6_ = bf16[256,1024]{1,0:T(8,128)(2,1)S(1)} collective-permute-done((bf16[256,1024]{1,0:T(8,128)(2,1)S(1)}, bf16[256,1024]{1,0:T(8,128)(2,1)S(1)}, u32[]{:S(2)}, u32[]{:S(2)}) %collective-permute-start.24) | collective-permute-done | bytes 524320 | tf_op jit(solution)/shard_map/ppermute | solution.py:64
  142.3 0.8 copy-done.25
  143.0 6.4 %shard_map.100 = (bf16[256,1024]{1,0:T(8,128)(2,1)}, bf16[256,1024]{1,0:T(8,128)(2,1)}, bf16[256,1024]{1,0:T(8,128)(2,1)}, bf16[256,1024]{1,0:T(8,128)(2,1)}) custom-call(s32[5]{0:T(128)} %stack.23.place.refs_11_, bf16[256,1024]{1,0:T(8,128)(2,1)} %copy-done.12, bf16[256,1024]{1,0:T(8,128)(2,1)} %copy-done.21, bf16[256,1024]{1,0:T(8,128)(2,1)} %copy-done.22, ...), custom_call_target="tpu_custom_call" | custom-call | tf_op jit(solution)/shard_map/pallas_call | solution.py:364
  149.4 1.8 %collective-permute-start.28 = (bf16[256,1024]{1,0:T(8,128)(2,1)}, bf16[256,1024]{1,0:T(8,128)(2,1)S(1)}, u32[]{:S(2)}, u32[]{:S(2)}) collective-permute-start(bf16[256,1024]{1,0:T(8,128)(2,1)} %get-tuple-element.101), channel_id=1, source_target_pairs={{0,3},{64,76},{1,0},{65,77},{2,1},{66,78},{3,2},{67,79},{4,7},{68,... | collective-permute-start | bytes 1572872 | tf_op jit(solution)/shard_map/ppermute | solution.py:74
  151.2 1.8 %collective-permute-start.27 = (bf16[256,1024]{1,0:T(8,128)(2,1)}, bf16[256,1024]{1,0:T(8,128)(2,1)S(1)}, u32[]{:S(2)}, u32[]{:S(2)}) collective-permute-start(bf16[256,1024]{1,0:T(8,128)(2,1)} %get-tuple-element.100), channel_id=1, source_target_pairs={{0,2},{64,72},{1,3},{65,73},{2,0},{66,74},{3,1},{67,75},{4,6},{68,... | collective-permute-start | bytes 1572872 | tf_op jit(solution)/shard_map/ppermute | solution.py:74
  153.6 2.1 %collective-permute-done.31.refs_7_ = bf16[256,1024]{1,0:T(8,128)(2,1)} collective-permute-done((bf16[256,1024]{1,0:T(8,128)(2,1)S(1)}, bf16[256,1024]{1,0:T(8,128)(2,1)}, u32[]{:S(2)}, u32[]{:S(2)}) %collective-permute-start.31) | collective-permute-done | bytes 524320 | tf_op jit(solution)/shard_map/ppermute | solution.py:64
  155.7 3.6 %shard_map.101 = (bf16[80,1024]{1,0:T(8,128)(2,1)}, bf16[80,1024]{1,0:T(8,128)(2,1)}, bf16[80,1024]{1,0:T(8,128)(2,1)}, bf16[80,1024]{1,0:T(8,128)(2,1)}) custom-call(s32[5]{0:T(128)} %stack.23.place.refs_11_, bf16[320,256]{1,0:T(8,128)(2,1)} %copy-done.14, bf16[320,256]{1,0:T(8,128)(2,1)} %copy-done.27, bf16[320,256]{1,0:T(8,128)(2,1)} %copy-done.28, ...), custom_call_target="tpu_custom_call" | custom-call | tf_op jit(solution)/shard_map/pallas_call | solution.py:426
  159.3 1.4 collective-permute-start.34
  160.7 2.1 %collective-permute-start.33 = (bf16[80,1024]{1,0:T(8,128)(2,1)}, bf16[80,1024]{1,0:T(8,128)(2,1)S(1)}, u32[]{:S(2)}, u32[]{:S(2)}) collective-permute-start(bf16[80,1024]{1,0:T(8,128)(2,1)} %get-tuple-element.108), channel_id=1, source_target_pairs={{0,2},{64,72},{1,3},{65,73},{2,0},{66,74},{3,1},{67,75},{4,6},{68,... | collective-permute-start | bytes 491528 | tf_op jit(solution)/shard_map/ppermute | solution.py:74
  162.8 0.8 collective-permute-start.32
  163.6 4.1 %collective-permute-done.26 = bf16[256,1024]{1,0:T(8,128)(2,1)S(1)} collective-permute-done((bf16[256,1024]{1,0:T(8,128)(2,1)}, bf16[256,1024]{1,0:T(8,128)(2,1)S(1)}, u32[]{:S(2)}, u32[]{:S(2)}) %collective-permute-start.26) | collective-permute-done | bytes 524320 | tf_op jit(solution)/shard_map/ppermute | solution.py:74
  167.7 1.3 add_bitcast_fusion
  169.5 1.7 %collective-permute-done.32 = bf16[80,1024]{1,0:T(8,128)(2,1)S(1)} collective-permute-done((bf16[80,1024]{1,0:T(8,128)(2,1)}, bf16[80,1024]{1,0:T(8,128)(2,1)S(1)}, u32[]{:S(2)}, u32[]{:S(2)}) %collective-permute-start.32) | collective-permute-done | bytes 163872 | tf_op jit(solution)/shard_map/ppermute | solution.py:74
  171.3 0.8 convert_add_fusion.1
  (95 shorter events, 6.3 us)
Async XLA Ops:
  0.6 11.0 %copy-start.20 = (bf16[4,32,2560]{2,1,0:T(8,128)(2,1)S(1)}, bf16[4,32,2560]{2,1,0:T(8,128)(2,1)}, u32[]{:S(2)}) copy-start(bf16[4,32,2560]{2,1,0:T(8,128)(2,1)} %param.7) | copy-start | bytes 1966084
  0.6 30.7 %collective-permute-start.4 = (bf16[4096,1024]{1,0:T(8,128)(2,1)}, bf16[4096,1024]{1,0:T(8,128)(2,1)}, u32[]{:S(2)}, u32[]{:S(2)}) collective-permute-start(bf16[4096,1024]{1,0:T(8,128)(2,1)} %bitcast.19), channel_id=1, source_target_pairs={{0,64},{64,0},{1,65},{65,1},{2,66},{66,2},{3,67},{67,3},{4,68},{68... | collective-permute-start | bytes 25165832 | tf_op jit(solution)/shard_map/ppermute | solution.py:78
  3.5 27.8 %all-to-all-start = ((bf16[16,32,1024]{2,1,0:T(8,128)(2,1)}), bf16[16,32,1024]{2,1,0:T(8,128)(2,1)S(1)}, u32[]{:S(2)}, u32[]{:S(2)}) async-start(bf16[16,32,1024]{2,1,0:T(8,128)(2,1)} %shard_map.86), calls=%async_computation | async-start | bytes 2097152 | tf_op jit(solution)/shard_map/all_to_all | solution.py:523
  11.6 2.7 %copy-start.15 = (s32[5]{0:T(128)S(1)}, s32[5]{0:T(128)}, u32[]{:S(2)}) copy-start(s32[5]{0:T(128)} %stack.23.place.refs_11_) | copy-start | bytes 64
  12.5 1.9 %collective-permute-start = (bf16[1280,128]{1,0:T(8,128)(2,1)S(1)}, bf16[1280,128]{1,0:T(8,128)(2,1)S(1)}, u32[]{:S(2)}, u32[]{:S(2)}) collective-permute-start(bf16[1280,128]{1,0:T(8,128)(2,1)S(1)} %dynamic-slice_bitcast_fusion), channel_id=1, source_target_pairs={{0,64},{64,0},{1,65},{65,1},{2,66},{66,2},{3,67},{67,3},{4,68},{68... | collective-permute-start | bytes 983048 | tf_op jit(solution)/shard_map/ppermute | solution.py:78
  15.7 12.8 %collective-permute-start.1 = (bf16[320,256]{1,0:T(8,128)(2,1)S(1)}, bf16[320,256]{1,0:T(8,128)(2,1)S(1)}, u32[]{:S(2)}, u32[]{:S(2)}) collective-permute-start(bf16[320,256]{1,0:T(8,128)(2,1)S(1)} %get-tuple-element.57), channel_id=1, source_target_pairs={{0,4},{64,65},{1,5},{65,66},{2,6},{66,67},{3,7},{67,64},{4,8},{68,... | collective-permute-start | bytes 491528 | tf_op jit(solution)/shard_map/ppermute | solution.py:64
  17.7 13.6 %collective-permute-start.2 = (bf16[320,256]{1,0:T(8,128)(2,1)S(1)}, bf16[320,256]{1,0:T(8,128)(2,1)S(1)}, u32[]{:S(2)}, u32[]{:S(2)}) collective-permute-start(bf16[320,256]{1,0:T(8,128)(2,1)S(1)} %get-tuple-element.58), channel_id=1, source_target_pairs={{0,8},{64,66},{1,9},{65,67},{2,10},{66,64},{3,11},{67,65},{4,12},{... | collective-permute-start | bytes 491528 | tf_op jit(solution)/shard_map/ppermute | solution.py:64
  21.3 10.1 %collective-permute-start.3 = (bf16[320,256]{1,0:T(8,128)(2,1)S(1)}, bf16[320,256]{1,0:T(8,128)(2,1)S(1)}, u32[]{:S(2)}, u32[]{:S(2)}) collective-permute-start(bf16[320,256]{1,0:T(8,128)(2,1)S(1)} %get-tuple-element.59), channel_id=1, source_target_pairs={{0,12},{64,67},{1,13},{65,64},{2,14},{66,65},{3,15},{67,66},{4,0},... | collective-permute-start | bytes 491528 | tf_op jit(solution)/shard_map/ppermute | solution.py:64
  28.5 36.4 %copy-start.27 = (bf16[320,256]{1,0:T(8,128)(2,1)}, bf16[320,256]{1,0:T(8,128)(2,1)S(1)}, u32[]{:S(2)}) copy-start(bf16[320,256]{1,0:T(8,128)(2,1)S(1)} %collective-permute-done.1.refs_1_) | copy-start | bytes 491524
  31.3 33.5 %copy-start.28 = (bf16[320,256]{1,0:T(8,128)(2,1)}, bf16[320,256]{1,0:T(8,128)(2,1)S(1)}, u32[]{:S(2)}) copy-start(bf16[320,256]{1,0:T(8,128)(2,1)S(1)} %collective-permute-done.2.refs_2_) | copy-start | bytes 491524
  31.3 3.7 %copy-start.29 = (bf16[320,256]{1,0:T(8,128)(2,1)}, bf16[320,256]{1,0:T(8,128)(2,1)S(1)}, u32[]{:S(2)}) copy-start(bf16[320,256]{1,0:T(8,128)(2,1)S(1)} %collective-permute-done.3.refs_3_) | copy-start | bytes 491524
  31.3 1.0 copy-start.19
  35.0 5.3 %copy-start.1 = (bf16[4,32,1024]{2,1,0:T(8,128)(2,1)S(1)}, bf16[4,32,1024]{2,1,0:T(8,128)(2,1)}, u32[]{:S(2)}) copy-start(bf16[4,32,1024]{2,1,0:T(8,128)(2,1)} %shard_map.89) | copy-start | bytes 786436
  35.0 34.5 %all-to-all-start.1 = ((bf16[16,32,1024]{2,1,0:T(8,128)(2,1)}), bf16[16,32,1024]{2,1,0:T(8,128)(2,1)S(1)}, u32[]{:S(2)}, u32[]{:S(2)}) async-start(bf16[16,32,1024]{2,1,0:T(8,128)(2,1)} %shard_map.88), calls=%async_computation.1 | async-start | bytes 2097152 | tf_op jit(solution)/shard_map/all_to_all | solution.py:540
  40.3 29.2 %copy-start.16 = (s32[5]{0:T(128)S(1)}, s32[5]{0:T(128)}, u32[]{:S(2)}) copy-start(s32[5]{0:T(128)} %stack.23.place.refs_11_) | copy-start | bytes 64
  40.3 29.2 %copy-start.17 = (s32[128]{0:T(128)S(1)}, s32[128]{0:T(128)}, u32[]{:S(2)}) copy-start(s32[128]{0:T(128)} %routing.7) | copy-start | bytes 1540
  40.3 9.5 %collective-permute-start.5 = (bf16[128,1024]{1,0:T(8,128)(2,1)S(1)}, bf16[128,1024]{1,0:T(8,128)(2,1)S(1)}, u32[]{:S(2)}, u32[]{:S(2)}) collective-permute-start(bf16[128,1024]{1,0:T(8,128)(2,1)S(1)} %bitcast.24), channel_id=1, source_target_pairs={{0,16},{16,32},{32,48},{48,0},{1,17},{17,33},{33,49},{49,1},{2,18}... | collective-permute-start | bytes 786440 | tf_op jit(solution)/shard_map/ppermute | solution.py:40
  41.9 14.4 %collective-permute-start.6 = (bf16[128,1024]{1,0:T(8,128)(2,1)S(1)}, bf16[128,1024]{1,0:T(8,128)(2,1)S(1)}, u32[]{:S(2)}, u32[]{:S(2)}) collective-permute-start(bf16[128,1024]{1,0:T(8,128)(2,1)S(1)} %bitcast.25), channel_id=1, source_target_pairs={{0,32},{16,48},{32,0},{48,16},{1,33},{17,49},{33,1},{49,17},{2,34}... | collective-permute-start | bytes 786440 | tf_op jit(solution)/shard_map/ppermute | solution.py:40
  44.6 11.7 %collective-permute-start.7 = (bf16[128,1024]{1,0:T(8,128)(2,1)S(1)}, bf16[128,1024]{1,0:T(8,128)(2,1)S(1)}, u32[]{:S(2)}, u32[]{:S(2)}) collective-permute-start(bf16[128,1024]{1,0:T(8,128)(2,1)S(1)} %bitcast.26), channel_id=1, source_target_pairs={{0,48},{16,0},{32,16},{48,32},{1,49},{17,1},{33,17},{49,33},{2,50}... | collective-permute-start | bytes 786440 | tf_op jit(solution)/shard_map/ppermute | solution.py:40
  49.8 6.5 %copy-start.5 = (bf16[128,1024]{1,0:T(8,128)(2,1)}, bf16[128,1024]{1,0:T(8,128)(2,1)S(1)}, u32[]{:S(2)}) copy-start(bf16[128,1024]{1,0:T(8,128)(2,1)S(1)} %collective-permute-done.5.refs_1_) | copy-start | bytes 786436
  64.8 13.7 %collective-permute-start.8 = (bf16[128,1024]{1,0:T(8,128)(2,1)}, bf16[128,1024]{1,0:T(8,128)(2,1)S(1)}, u32[]{:S(2)}, u32[]{:S(2)}) collective-permute-start(bf16[128,1024]{1,0:T(8,128)(2,1)} %get-tuple-element.70.refs_4_), channel_id=1, source_target_pairs={{0,16},{16,32},{32,48},{48,0},{1,17},{17,33},{33,49},{49,1},{2,18}... | collective-permute-start | bytes 786440 | tf_op jit(solution)/shard_map/ppermute | solution.py:40
  65.6 13.8 %collective-permute-start.9 = (bf16[128,1024]{1,0:T(8,128)(2,1)}, bf16[128,1024]{1,0:T(8,128)(2,1)S(1)}, u32[]{:S(2)}, u32[]{:S(2)}) collective-permute-start(bf16[128,1024]{1,0:T(8,128)(2,1)} %get-tuple-element.70.refs_4_), channel_id=1, source_target_pairs={{0,32},{16,48},{32,0},{48,16},{1,33},{17,49},{33,1},{49,17},{2,34}... | collective-permute-start | bytes 786440 | tf_op jit(solution)/shard_map/ppermute | solution.py:40
  67.9 11.4 %collective-permute-start.10 = (bf16[128,1024]{1,0:T(8,128)(2,1)}, bf16[128,1024]{1,0:T(8,128)(2,1)S(1)}, u32[]{:S(2)}, u32[]{:S(2)}) collective-permute-start(bf16[128,1024]{1,0:T(8,128)(2,1)} %get-tuple-element.70.refs_4_), channel_id=1, source_target_pairs={{0,48},{16,0},{32,16},{48,32},{1,49},{17,1},{33,17},{49,33},{2,50}... | collective-permute-start | bytes 786440 | tf_op jit(solution)/shard_map/ppermute | solution.py:40
  70.5 3.4 %copy-start = (bf16[1,4096,1024]{2,1,0:T(8,128)(2,1)S(1)}, bf16[1,4096,1024]{2,1,0:T(8,128)(2,1)}, u32[]{:S(2)}) copy-start(bf16[1,4096,1024]{2,1,0:T(8,128)(2,1)} %param.12) | copy-start | bytes 25165828
  73.9 5.5 %copy-start.11 = (bf16[128,1024]{1,0:T(8,128)(2,1)S(1)}, bf16[128,1024]{1,0:T(8,128)(2,1)}, u32[]{:S(2)}) copy-start(bf16[128,1024]{1,0:T(8,128)(2,1)} %get-tuple-element.70.refs_4_) | copy-start | bytes 786436
  79.4 4.3 %copy-start.2 = (bf16[4,32,1024]{2,1,0:T(8,128)(2,1)S(1)}, bf16[4,32,1024]{2,1,0:T(8,128)(2,1)}, u32[]{:S(2)}) copy-start(bf16[4,32,1024]{2,1,0:T(8,128)(2,1)} %shard_map.89) | copy-start | bytes 786436
  79.4 4.3 %copy-start.6 = (bf16[128,1024]{1,0:T(8,128)(2,1)S(1)}, bf16[128,1024]{1,0:T(8,128)(2,1)}, u32[]{:S(2)}) copy-start(bf16[128,1024]{1,0:T(8,128)(2,1)} %copy-done.5) | copy-start | bytes 786436
  79.4 4.3 %copy-start.8 = (bf16[128,1024]{1,0:T(8,128)(2,1)S(1)}, bf16[128,1024]{1,0:T(8,128)(2,1)}, u32[]{:S(2)}) copy-start(bf16[128,1024]{1,0:T(8,128)(2,1)} %copy-done.7) | copy-start | bytes 786436
  79.4 4.3 %copy-start.10 = (bf16[128,1024]{1,0:T(8,128)(2,1)S(1)}, bf16[128,1024]{1,0:T(8,128)(2,1)}, u32[]{:S(2)}) copy-start(bf16[128,1024]{1,0:T(8,128)(2,1)} %copy-done.9) | copy-start | bytes 786436
  83.7 21.1 %copy-start.13 = (f32[128,1024]{1,0:T(8,128)S(1)}, f32[128,1024]{1,0:T(8,128)}, u32[]{:S(2)}) copy-start(f32[128,1024]{1,0:T(8,128)} %get-tuple-element.85.refs_9_) | copy-start | bytes 1572868
  84.7 2.7 %collective-permute-start.11 = (bf16[4,128,1024]{2,1,0:T(8,128)(2,1)S(1)}, bf16[4,128,1024]{2,1,0:T(8,128)(2,1)S(1)}, u32[]{:S(2)}, u32[]{:S(2)}) collective-permute-start(bf16[4,128,1024]{2,1,0:T(8,128)(2,1)S(1)} %get-tuple-element.74), channel_id=1, source_target_pairs={{0,64},{64,0},{1,65},{65,1},{2,66},{66,2},{3,67},{67,3},{4,68},{68... | collective-permute-start | bytes 3145736 | tf_op jit(solution)/shard_map/ppermute | solution.py:78
  84.8 11.2 %collective-permute-start.12 = (bf16[128,1024]{1,0:T(8,128)(2,1)S(1)}, bf16[128,1024]{1,0:T(8,128)(2,1)S(1)}, u32[]{:S(2)}, u32[]{:S(2)}) collective-permute-start(bf16[128,1024]{1,0:T(8,128)(2,1)S(1)} %get-tuple-element.81), channel_id=1, source_target_pairs={{0,16},{16,32},{32,48},{48,0},{1,17},{17,33},{33,49},{49,1},{2,18}... | collective-permute-start | bytes 786440 | tf_op jit(solution)/shard_map/ppermute | solution.py:40
  87.5 0.8 copy-start.12
  88.4 24.0 %collective-permute-start.18 = (bf16[256,1024]{1,0:T(8,128)(2,1)S(1)}, bf16[256,1024]{1,0:T(8,128)(2,1)S(1)}, u32[]{:S(2)}, u32[]{:S(2)}) collective-permute-start(bf16[256,1024]{1,0:T(8,128)(2,1)S(1)} %get-tuple-element.91), channel_id=1, source_target_pairs={{0,4},{64,65},{1,5},{65,66},{2,6},{66,67},{3,7},{67,64},{4,8},{68,... | collective-permute-start | bytes 1572872 | tf_op jit(solution)/shard_map/ppermute | solution.py:64
  90.0 11.0 %collective-permute-start.13 = (bf16[128,1024]{1,0:T(8,128)(2,1)S(1)}, bf16[128,1024]{1,0:T(8,128)(2,1)S(1)}, u32[]{:S(2)}, u32[]{:S(2)}) collective-permute-start(bf16[128,1024]{1,0:T(8,128)(2,1)S(1)} %get-tuple-element.82), channel_id=1, source_target_pairs={{0,32},{16,48},{32,0},{48,16},{1,33},{17,49},{33,1},{49,17},{2,34}... | collective-permute-start | bytes 786440 | tf_op jit(solution)/shard_map/ppermute | solution.py:40
  91.3 13.5 %collective-permute-start.14 = (bf16[128,1024]{1,0:T(8,128)(2,1)S(1)}, bf16[128,1024]{1,0:T(8,128)(2,1)S(1)}, u32[]{:S(2)}, u32[]{:S(2)}) collective-permute-start(bf16[128,1024]{1,0:T(8,128)(2,1)S(1)} %get-tuple-element.83), channel_id=1, source_target_pairs={{0,48},{16,0},{32,16},{48,32},{1,49},{17,1},{33,17},{49,33},{2,50}... | collective-permute-start | bytes 786440 | tf_op jit(solution)/shard_map/ppermute | solution.py:40
  93.3 19.3 %collective-permute-start.19 = (bf16[256,1024]{1,0:T(8,128)(2,1)S(1)}, bf16[256,1024]{1,0:T(8,128)(2,1)S(1)}, u32[]{:S(2)}, u32[]{:S(2)}) collective-permute-start(bf16[256,1024]{1,0:T(8,128)(2,1)S(1)} %get-tuple-element.92), channel_id=1, source_target_pairs={{0,8},{64,66},{1,9},{65,67},{2,10},{66,64},{3,11},{67,65},{4,12},{... | collective-permute-start | bytes 1572872 | tf_op jit(solution)/shard_map/ppermute | solution.py:64
  96.0 16.6 %collective-permute-start.20 = (bf16[256,1024]{1,0:T(8,128)(2,1)S(1)}, bf16[256,1024]{1,0:T(8,128)(2,1)S(1)}, u32[]{:S(2)}, u32[]{:S(2)}) collective-permute-start(bf16[256,1024]{1,0:T(8,128)(2,1)S(1)} %get-tuple-element.93), channel_id=1, source_target_pairs={{0,12},{64,67},{1,13},{65,64},{2,14},{66,65},{3,15},{67,66},{4,0},... | collective-permute-start | bytes 1572872 | tf_op jit(solution)/shard_map/ppermute | solution.py:64
  104.8 19.4 %copy-start.18 = (s32[128]{0:T(128)S(1)}, s32[128]{0:T(128)}, u32[]{:S(2)}) copy-start(s32[128]{0:T(128)} %counts.3) | copy-start | bytes 1540
  108.2 9.2 %collective-permute-start.15 = (bf16[128,1024]{1,0:T(8,128)(2,1)S(1)}, bf16[128,1024]{1,0:T(8,128)(2,1)S(1)}, u32[]{:S(2)}, u32[]{:S(2)}) collective-permute-start(bf16[128,1024]{1,0:T(8,128)(2,1)S(1)} %get-tuple-element.87), channel_id=1, source_target_pairs={{0,16},{16,32},{32,48},{48,0},{1,17},{17,33},{33,49},{49,1},{2,18}... | collective-permute-start | bytes 786440 | tf_op jit(solution)/shard_map/ppermute | solution.py:40
  109.3 14.9 %collective-permute-start.16 = (bf16[128,1024]{1,0:T(8,128)(2,1)S(1)}, bf16[128,1024]{1,0:T(8,128)(2,1)S(1)}, u32[]{:S(2)}, u32[]{:S(2)}) collective-permute-start(bf16[128,1024]{1,0:T(8,128)(2,1)S(1)} %get-tuple-element.88), channel_id=1, source_target_pairs={{0,32},{16,48},{32,0},{48,16},{1,33},{17,49},{33,1},{49,17},{2,34}... | collective-permute-start | bytes 786440 | tf_op jit(solution)/shard_map/ppermute | solution.py:40
  112.4 29.9 %copy-start.21 = (bf16[256,1024]{1,0:T(8,128)(2,1)}, bf16[256,1024]{1,0:T(8,128)(2,1)S(1)}, u32[]{:S(2)}) copy-start(bf16[256,1024]{1,0:T(8,128)(2,1)S(1)} %collective-permute-done.18.refs_1_) | copy-start | bytes 1572868
  112.4 11.8 %collective-permute-start.17 = (bf16[128,1024]{1,0:T(8,128)(2,1)S(1)}, bf16[128,1024]{1,0:T(8,128)(2,1)S(1)}, u32[]{:S(2)}, u32[]{:S(2)}) collective-permute-start(bf16[128,1024]{1,0:T(8,128)(2,1)S(1)} %get-tuple-element.89), channel_id=1, source_target_pairs={{0,48},{16,0},{32,16},{48,32},{1,49},{17,1},{33,17},{49,33},{2,50}... | collective-permute-start | bytes 786440 | tf_op jit(solution)/shard_map/ppermute | solution.py:40
  112.6 29.6 %copy-start.22 = (bf16[256,1024]{1,0:T(8,128)(2,1)}, bf16[256,1024]{1,0:T(8,128)(2,1)S(1)}, u32[]{:S(2)}) copy-start(bf16[256,1024]{1,0:T(8,128)(2,1)S(1)} %collective-permute-done.19.refs_2_) | copy-start | bytes 1572868
  112.6 12.4 %collective-permute-start.22 = (bf16[128,1024]{1,0:T(8,128)(2,1)S(1)}, bf16[128,1024]{1,0:T(8,128)(2,1)S(1)}, u32[]{:S(2)}, u32[]{:S(2)}) collective-permute-start(bf16[128,1024]{1,0:T(8,128)(2,1)S(1)} %get-tuple-element.97), channel_id=1, source_target_pairs={{0,64},{64,0},{1,65},{65,1},{2,66},{66,2},{3,67},{67,3},{4,68},{68... | collective-permute-start | bytes 786440 | tf_op jit(solution)/shard_map/ppermute | solution.py:78
  112.6 29.6 %copy-start.23 = (bf16[256,1024]{1,0:T(8,128)(2,1)}, bf16[256,1024]{1,0:T(8,128)(2,1)S(1)}, u32[]{:S(2)}) copy-start(bf16[256,1024]{1,0:T(8,128)(2,1)S(1)} %collective-permute-done.20.refs_3_) | copy-start | bytes 1572868
  124.9 5.8 %collective-permute-start.21 = (bf16[128,1024]{1,0:T(8,128)(2,1)S(1)}, bf16[128,1024]{1,0:T(8,128)(2,1)S(1)}, u32[]{:S(2)}, u32[]{:S(2)}) collective-permute-start(bf16[128,1024]{1,0:T(8,128)(2,1)S(1)} %shard_map.97.keep), channel_id=1, source_target_pairs={{0,64},{64,0},{1,65},{65,1},{2,66},{66,2},{3,67},{67,3},{4,68},{68... | collective-permute-start | bytes 786440 | tf_op jit(solution)/shard_map/ppermute | solution.py:78
  125.1 17.2 %copy-start.3 = (bf16[256,1024]{1,0:T(8,128)(2,1)}, bf16[256,1024]{1,0:T(8,128)(2,1)S(1)}, u32[]{:S(2)}) copy-start(bf16[256,1024]{1,0:T(8,128)(2,1)S(1)} %shard_map.99.refs_4_) | copy-start | bytes 1572868
  125.1 10.5 %collective-permute-start.23 = (bf16[256,1024]{1,0:T(8,128)(2,1)S(1)}, bf16[256,1024]{1,0:T(8,128)(2,1)S(1)}, u32[]{:S(2)}, u32[]{:S(2)}) collective-permute-start(bf16[256,1024]{1,0:T(8,128)(2,1)S(1)} %shard_map.99.refs_4_), channel_id=1, source_target_pairs={{0,4},{64,65},{1,5},{65,66},{2,6},{66,67},{3,7},{67,64},{4,8},{68,... | collective-permute-start | bytes 1572872 | tf_op jit(solution)/shard_map/ppermute | solution.py:64
  126.6 15.6 %collective-permute-start.24 = (bf16[256,1024]{1,0:T(8,128)(2,1)S(1)}, bf16[256,1024]{1,0:T(8,128)(2,1)S(1)}, u32[]{:S(2)}, u32[]{:S(2)}) collective-permute-start(bf16[256,1024]{1,0:T(8,128)(2,1)S(1)} %shard_map.99.refs_4_), channel_id=1, source_target_pairs={{0,8},{64,66},{1,9},{65,67},{2,10},{66,64},{3,11},{67,65},{4,12},{... | collective-permute-start | bytes 1572872 | tf_op jit(solution)/shard_map/ppermute | solution.py:64
  129.3 12.9 %collective-permute-start.25 = (bf16[256,1024]{1,0:T(8,128)(2,1)S(1)}, bf16[256,1024]{1,0:T(8,128)(2,1)}, u32[]{:S(2)}, u32[]{:S(2)}) collective-permute-start(bf16[256,1024]{1,0:T(8,128)(2,1)S(1)} %shard_map.99.refs_4_), channel_id=1, source_target_pairs={{0,12},{64,67},{1,13},{65,64},{2,14},{66,65},{3,15},{67,66},{4,0},... | collective-permute-start | bytes 1572872 | tf_op jit(solution)/shard_map/ppermute | solution.py:64
  130.8 18.6 %copy-start.4 = (bf16[256,1024]{1,0:T(8,128)(2,1)}, bf16[256,1024]{1,0:T(8,128)(2,1)S(1)}, u32[]{:S(2)}) copy-start(bf16[256,1024]{1,0:T(8,128)(2,1)S(1)} %shard_map.98.refs_4_) | copy-start | bytes 1572868
  130.8 22.2 %collective-permute-start.29 = (bf16[256,1024]{1,0:T(8,128)(2,1)S(1)}, bf16[256,1024]{1,0:T(8,128)(2,1)}, u32[]{:S(2)}, u32[]{:S(2)}) collective-permute-start(bf16[256,1024]{1,0:T(8,128)(2,1)S(1)} %shard_map.98.refs_4_), channel_id=1, source_target_pairs={{0,4},{64,65},{1,5},{65,66},{2,6},{66,67},{3,7},{67,64},{4,8},{68,... | collective-permute-start | bytes 1572872 | tf_op jit(solution)/shard_map/ppermute | solution.py:64
  131.5 22.1 %collective-permute-start.30 = (bf16[256,1024]{1,0:T(8,128)(2,1)S(1)}, bf16[256,1024]{1,0:T(8,128)(2,1)}, u32[]{:S(2)}, u32[]{:S(2)}) collective-permute-start(bf16[256,1024]{1,0:T(8,128)(2,1)S(1)} %shard_map.98.refs_4_), channel_id=1, source_target_pairs={{0,8},{64,66},{1,9},{65,67},{2,10},{66,64},{3,11},{67,65},{4,12},{... | collective-permute-start | bytes 1572872 | tf_op jit(solution)/shard_map/ppermute | solution.py:64
  135.5 6.7 %copy-start.24 = (bf16[256,1024]{1,0:T(8,128)(2,1)}, bf16[256,1024]{1,0:T(8,128)(2,1)S(1)}, u32[]{:S(2)}) copy-start(bf16[256,1024]{1,0:T(8,128)(2,1)S(1)} %collective-permute-done.23.refs_5_) | copy-start | bytes 1572868
  135.5 20.1 %collective-permute-start.31 = (bf16[256,1024]{1,0:T(8,128)(2,1)S(1)}, bf16[256,1024]{1,0:T(8,128)(2,1)}, u32[]{:S(2)}, u32[]{:S(2)}) collective-permute-start(bf16[256,1024]{1,0:T(8,128)(2,1)S(1)} %shard_map.98.refs_4_), channel_id=1, source_target_pairs={{0,12},{64,67},{1,13},{65,64},{2,14},{66,65},{3,15},{67,66},{4,0},... | collective-permute-start | bytes 1572872 | tf_op jit(solution)/shard_map/ppermute | solution.py:64
  149.4 18.3 %copy-start.26 = (bf16[256,1024]{1,0:T(8,128)(2,1)S(1)}, bf16[256,1024]{1,0:T(8,128)(2,1)}, u32[]{:S(2)}) copy-start(bf16[256,1024]{1,0:T(8,128)(2,1)} %get-tuple-element.98) | copy-start | bytes 1572868
  149.4 13.4 %collective-permute-start.28 = (bf16[256,1024]{1,0:T(8,128)(2,1)}, bf16[256,1024]{1,0:T(8,128)(2,1)S(1)}, u32[]{:S(2)}, u32[]{:S(2)}) collective-permute-start(bf16[256,1024]{1,0:T(8,128)(2,1)} %get-tuple-element.101), channel_id=1, source_target_pairs={{0,3},{64,76},{1,0},{65,77},{2,1},{66,78},{3,2},{67,79},{4,7},{68,... | collective-permute-start | bytes 1572872 | tf_op jit(solution)/shard_map/ppermute | solution.py:74
  151.2 12.4 %collective-permute-start.27 = (bf16[256,1024]{1,0:T(8,128)(2,1)}, bf16[256,1024]{1,0:T(8,128)(2,1)S(1)}, u32[]{:S(2)}, u32[]{:S(2)}) collective-permute-start(bf16[256,1024]{1,0:T(8,128)(2,1)} %get-tuple-element.100), channel_id=1, source_target_pairs={{0,2},{64,72},{1,3},{65,73},{2,0},{66,74},{3,1},{67,75},{4,6},{68,... | collective-permute-start | bytes 1572872 | tf_op jit(solution)/shard_map/ppermute | solution.py:74
  153.0 14.7 %collective-permute-start.26 = (bf16[256,1024]{1,0:T(8,128)(2,1)}, bf16[256,1024]{1,0:T(8,128)(2,1)S(1)}, u32[]{:S(2)}, u32[]{:S(2)}) collective-permute-start(bf16[256,1024]{1,0:T(8,128)(2,1)} %get-tuple-element.99), channel_id=1, source_target_pairs={{0,1},{64,68},{1,2},{65,69},{2,3},{66,70},{3,0},{67,71},{4,5},{68,... | collective-permute-start | bytes 1572872 | tf_op jit(solution)/shard_map/ppermute | solution.py:74
  159.3 12.0 %copy-start.30 = (bf16[80,1024]{1,0:T(8,128)(2,1)S(1)}, bf16[80,1024]{1,0:T(8,128)(2,1)}, u32[]{:S(2)}) copy-start(bf16[80,1024]{1,0:T(8,128)(2,1)} %get-tuple-element.106) | copy-start | bytes 491524
  159.3 9.8 %collective-permute-start.34 = (bf16[80,1024]{1,0:T(8,128)(2,1)}, bf16[80,1024]{1,0:T(8,128)(2,1)S(1)}, u32[]{:S(2)}, u32[]{:S(2)}) collective-permute-start(bf16[80,1024]{1,0:T(8,128)(2,1)} %get-tuple-element.109), channel_id=1, source_target_pairs={{0,3},{64,76},{1,0},{65,77},{2,1},{66,78},{3,2},{67,79},{4,7},{68,... | collective-permute-start | bytes 491528 | tf_op jit(solution)/shard_map/ppermute | solution.py:74
  160.7 8.9 %collective-permute-start.33 = (bf16[80,1024]{1,0:T(8,128)(2,1)}, bf16[80,1024]{1,0:T(8,128)(2,1)S(1)}, u32[]{:S(2)}, u32[]{:S(2)}) collective-permute-start(bf16[80,1024]{1,0:T(8,128)(2,1)} %get-tuple-element.108), channel_id=1, source_target_pairs={{0,2},{64,72},{1,3},{65,73},{2,0},{66,74},{3,1},{67,75},{4,6},{68,... | collective-permute-start | bytes 491528 | tf_op jit(solution)/shard_map/ppermute | solution.py:74
  162.8 8.5 %collective-permute-start.32 = (bf16[80,1024]{1,0:T(8,128)(2,1)}, bf16[80,1024]{1,0:T(8,128)(2,1)S(1)}, u32[]{:S(2)}, u32[]{:S(2)}) collective-permute-start(bf16[80,1024]{1,0:T(8,128)(2,1)} %get-tuple-element.107), channel_id=1, source_target_pairs={{0,1},{64,68},{1,2},{65,69},{2,3},{66,70},{3,0},{67,71},{4,5},{68,... | collective-permute-start | bytes 491528 | tf_op jit(solution)/shard_map/ppermute | solution.py:74
  (4 other events, 2.9 us)

commit v8 on v7

--- a/solution.py
+++ b/solution.py
@@ -564,9 +564,9 @@
         out_specs=WHOLE,
         out_shape=block,
         compiler_params=SMALL,
-    )(image_counts, place, *ends, after(cotangent, *rows[1:]))
+    )(image_counts, place, *ends, after(cotangent, *rows[1:], local[0]))
     grad = pair(grad, swap(grad))
-    going = grad
+    going = after(grad, local[1], local[3])
     grads = [grad] + [along_mine(going, e) for e in (1, 2, 3)]
 
     parts = weight_grad(place, [after(rows[0], grad)] + rows[1:], local)

time: 173 us -> 164 us (0.948)
  waiting for transfers between devices: 52.8 us -> 42.5 us
  starting transfers between devices: 62.7 us -> 65.1 us
    ppermute x12, waiting for transfers between devices: 29.8 us -> 23.7 us  [along_x(): lax.ppermute(block, 'mp', [(i, (i + distance) % SIDE) for i in range(SIDE)])]
    ppermute x12, waiting for transfers between devices: 13.3 us -> 9.18 us  [along_mine(): return lax.ppermute(block, ('segment', 'dp'), pairs)]
    ppermute x12, starting transfers between devices: 21.2 us -> 24.2 us  [along_mine(): return lax.ppermute(block, ('segment', 'dp'), pairs)]
  transfers between devices with their start and end apart: 37 -> 37, of which waited for: 16 -> 18; matrix products, arithmetic and copies ran while one was open for 4% -> 4% of each run, Pallas kernels for 19% -> 20%
where the time goes in v8:
time: 164 us; the launch traced here: 163 us
  starting transfers between devices  65.1 us (40%)
  waiting for transfers between devices  42.5 us (26%)
  Pallas kernels  39.8 us (24%)
  local copies, waits for them, and re-layouts  8.32 us (5%)
  matrix products  4.04 us (2%)
  other arithmetic  2.56 us (2%)
    ppermute x12, starting transfers between devices, along_mine(): return lax.ppermute(block, ('segment', 'dp'), pairs)  24.2 us
    ppermute x12, waiting for transfers between devices, along_x(): lax.ppermute(block, 'mp', [(i, (i + distance) % SIDE) for i in range(SIDE)])  23.7 us
    ppermute x12, starting transfers between devices, along_x(): lax.ppermute(block, 'mp', [(i, (i + distance) % SIDE) for i in range(SIDE)])  18.9 us
    ppermute x12, waiting for transfers between devices, along_mine(): return lax.ppermute(block, ('segment', 'dp'), pairs)  9.18 us
    all_to_all x1, starting transfers between devices, on_device(): arrived_text = lax.all_to_all(send_text, 'dp', 0, 0, tiled=True)  8.13 us
    ppermute x6, starting transfers between devices, along_other(): return lax.ppermute(block, ('segment', 'dp'), pairs)  7.96 us
    pallas_call x2, Pallas kernels, held_step(): pl.pallas_call(functools.partial(held_kernel, body, count, len(outs)), in...  7.65 us
    unnamed x62, local copies, waits for them, and re-layouts  7.37 us
  transfers between devices with their start and end apart: 37, of which 18 were waited for; matrix products, arithmetic and copies ran while one was open for 4% of the time, Pallas kernels for 20%

profile of v8, /device:TPU:0, one launch (start us, length us, event | category | flops | bytes accessed | tf_op | source)
XLA Modules:
  0.0 163.4 jit_solution(7684236935701022229)
XLA Ops:
  1.4 2.1 %shard_map.86 = bf16[16,32,1024]{2,1,0:T(8,128)(2,1)} custom-call(s32[128]{0:T(128)} %routing.7, s32[5]{0:T(128)} %stack.23.place.refs_11_, bf16[8,32,1024]{2,1,0:T(8,128)(2,1)} %bitcast.33), custom_call_target="tpu_custom_call" | custom-call | tf_op jit(solution)/shard_map/pallas_call | solution.py:97
  3.5 8.1 %all-to-all-start = ((bf16[16,32,1024]{2,1,0:T(8,128)(2,1)}), bf16[16,32,1024]{2,1,0:T(8,128)(2,1)S(1)}, u32[]{:S(2)}, u32[]{:S(2)}) async-start(bf16[16,32,1024]{2,1,0:T(8,128)(2,1)} %shard_map.86), calls=%async_computation | async-start | bytes 2097152 | tf_op jit(solution)/shard_map/all_to_all | solution.py:523
  12.8 1.6 collective-permute-done.far
  14.3 0.7 shard_map.87
  15.7 2.0 %collective-permute-start.1 = (bf16[320,256]{1,0:T(8,128)(2,1)S(1)}, bf16[320,256]{1,0:T(8,128)(2,1)S(1)}, u32[]{:S(2)}, u32[]{:S(2)}) collective-permute-start(bf16[320,256]{1,0:T(8,128)(2,1)S(1)} %get-tuple-element.58), channel_id=1, source_target_pairs={{0,4},{64,65},{1,5},{65,66},{2,6},{66,67},{3,7},{67,64},{4,8},{68,... | collective-permute-start | bytes 491528 | tf_op jit(solution)/shard_map/ppermute | solution.py:64
  17.7 3.6 %collective-permute-start.2 = (bf16[320,256]{1,0:T(8,128)(2,1)S(1)}, bf16[320,256]{1,0:T(8,128)(2,1)S(1)}, u32[]{:S(2)}, u32[]{:S(2)}) collective-permute-start(bf16[320,256]{1,0:T(8,128)(2,1)S(1)} %get-tuple-element.59), channel_id=1, source_target_pairs={{0,8},{64,66},{1,9},{65,67},{2,10},{66,64},{3,11},{67,65},{4,12},{... | collective-permute-start | bytes 491528 | tf_op jit(solution)/shard_map/ppermute | solution.py:64
  21.3 1.0 collective-permute-start.3
  22.3 4.0 %convolution_convert_fusion = bf16[128,1024]{1,0:T(8,128)(2,1)} fusion(bf16[128,2560]{1,0:T(8,128)(2,1)S(1)} %bitcast.31, bf16[2560,1024]{1,0:T(8,128)(2,1)} %param.8), kind=kOutput, calls=%fused_computation.10 | convolution fusion | flops 671219712 | bytes 6160384 | tf_op jit(solution)/shard_map/dot_general | solution.py:28
  26.3 2.1 %shard_map.88 = bf16[16,32,1024]{2,1,0:T(8,128)(2,1)} custom-call(s32[128]{0:T(128)} %routing.7, s32[5]{0:T(128)} %stack.23.place.refs_11_, bf16[8,32,1024]{2,1,0:T(8,128)(2,1)} %bitcast.34), custom_call_target="tpu_custom_call" | custom-call | tf_op jit(solution)/shard_map/pallas_call | solution.py:97
  28.5 2.9 %collective-permute-done.2.refs_2_ = bf16[320,256]{1,0:T(8,128)(2,1)S(1)} collective-permute-done((bf16[320,256]{1,0:T(8,128)(2,1)S(1)}, bf16[320,256]{1,0:T(8,128)(2,1)S(1)}, u32[]{:S(2)}, u32[]{:S(2)}) %collective-permute-start.2) | collective-permute-done | bytes 163872 | tf_op jit(solution)/shard_map/ppermute | solution.py:64
  31.4 1.0 copy-done.19
  32.3 2.7 %shard_map.89 = bf16[4,32,1024]{2,1,0:T(8,128)(2,1)} custom-call(s32[128]{0:T(128)} %routing.7, s32[128]{0:T(128)} %counts.3, s32[5]{0:T(128)} %stack.23.place.refs_11_, bf16[16,32,1024]{2,1,0:T(8,128)(2,1)} %copy-done.19, bf16[4,32,1024]{2,1,0:T(8,128)(2,1)} %bitcast.32), custom_call_target="tpu_custom_call" | custom-call | tf_op jit(solution)/shard_map/pallas_call | solution.py:122
  35.0 5.2 %all-to-all-start.1 = ((bf16[16,32,1024]{2,1,0:T(8,128)(2,1)}), bf16[16,32,1024]{2,1,0:T(8,128)(2,1)S(1)}, u32[]{:S(2)}, u32[]{:S(2)}) async-start(bf16[16,32,1024]{2,1,0:T(8,128)(2,1)} %shard_map.88), calls=%async_computation.1 | async-start | bytes 2097152 | tf_op jit(solution)/shard_map/all_to_all | solution.py:540
  40.3 1.6 collective-permute-start.5
  41.9 2.7 %collective-permute-start.6 = (bf16[128,1024]{1,0:T(8,128)(2,1)S(1)}, bf16[128,1024]{1,0:T(8,128)(2,1)S(1)}, u32[]{:S(2)}, u32[]{:S(2)}) collective-permute-start(bf16[128,1024]{1,0:T(8,128)(2,1)S(1)} %bitcast.25), channel_id=1, source_target_pairs={{0,32},{16,48},{32,0},{48,16},{1,33},{17,49},{33,1},{49,17},{2,34}... | collective-permute-start | bytes 786440 | tf_op jit(solution)/shard_map/ppermute | solution.py:40
  44.6 1.4 collective-permute-start.7
  46.0 3.8 %collective-permute-done.5.refs_1_ = bf16[128,1024]{1,0:T(8,128)(2,1)S(1)} collective-permute-done((bf16[128,1024]{1,0:T(8,128)(2,1)S(1)}, bf16[128,1024]{1,0:T(8,128)(2,1)S(1)}, u32[]{:S(2)}, u32[]{:S(2)}) %collective-permute-start.5) | collective-permute-done | bytes 262176 | tf_op jit(solution)/shard_map/ppermute | solution.py:40
  49.8 6.5 %collective-permute-done.6.refs_2_ = bf16[128,1024]{1,0:T(8,128)(2,1)S(1)} collective-permute-done((bf16[128,1024]{1,0:T(8,128)(2,1)S(1)}, bf16[128,1024]{1,0:T(8,128)(2,1)S(1)}, u32[]{:S(2)}, u32[]{:S(2)}) %collective-permute-start.6) | collective-permute-done | bytes 262176 | tf_op jit(solution)/shard_map/ppermute | solution.py:40
  56.3 0.7 copy-done.7
  57.0 0.7 copy-done.9
  57.7 7.1 %shard_map.92 = (bf16[128,1024]{1,0:T(8,128)(2,1)}, f32[128,1024]{1,0:T(8,128)}) custom-call(s32[5]{0:T(128)} %stack.23.place.refs_11_, bf16[4096,1024]{1,0:T(8,128)(2,1)} %bitcast.20, bf16[4096,1024]{1,0:T(8,128)(2,1)} %collective-permute-done.4.other, bf16[128,1024]{1,0:T(8,128)(2,1)} %bitcast.23, bf16[128,1024]{1,0:T(8,128)(2,1)} %copy-done.5, ...), custom_call_target="tpu_custom_call" | custom-call | tf_op jit(solution)/shard_map/pallas_call | solution.py:262
  64.8 0.7 collective-permute-start.8
  65.6 2.4 %collective-permute-start.9 = (bf16[128,1024]{1,0:T(8,128)(2,1)}, bf16[128,1024]{1,0:T(8,128)(2,1)S(1)}, u32[]{:S(2)}, u32[]{:S(2)}) collective-permute-start(bf16[128,1024]{1,0:T(8,128)(2,1)} %get-tuple-element.71.refs_4_), channel_id=1, source_target_pairs={{0,32},{16,48},{32,0},{48,16},{1,33},{17,49},{33,1},{49,17},{2,34}... | collective-permute-start | bytes 786440 | tf_op jit(solution)/shard_map/ppermute | solution.py:40
  67.9 1.6 collective-permute-start.10
  69.5 0.9 shard_map.90
  70.5 3.4 %copy-done = bf16[1,4096,1024]{2,1,0:T(8,128)(2,1)S(1)} copy-done((bf16[1,4096,1024]{2,1,0:T(8,128)(2,1)S(1)}, bf16[1,4096,1024]{2,1,0:T(8,128)(2,1)}, u32[]{:S(2)}) %copy-start) | copy-done | bytes 8388632
  73.9 4.7 %shard_map.91 = (bf16[1024,1024]{1,0:T(8,128)(2,1)S(1)}, bf16[1024,1024]{1,0:T(8,128)(2,1)S(1)}, bf16[1024,1024]{1,0:T(8,128)(2,1)S(1)}, bf16[1024,1024]{1,0:T(8...) custom-call(s32[5]{0:T(128)S(1)} %copy-done.16, ...), custom_call_target="tpu_custom_call" | custom-call | tf_op jit(solution)/shard_map/pallas_call | solution.py:304
  78.6 0.8 collective-permute-done.9.refs_6_
  79.4 4.2 %shard_map.93 = (bf16[128,1024]{1,0:T(8,128)(2,1)S(1)}, bf16[128,1024]{1,0:T(8,128)(2,1)S(1)}, bf16[128,1024]{1,0:T(8,128)(2,1)S(1)}, bf16[128,1024]{1,0:T(8,128)(2,1)S(1)}, bf16[128,1024]{1,0:T(8,128)(2,1)S(1)}) custom-call(bf16[1024,1024]{1,0:T(8,128)(2,1)S(1)} %get-tuple-element.67.refs_0_, bf16[1024,1024]{1,0:T(8,128)(2,1)S(1)} %get-tuple-element.68.refs_1_, ...), custom_call_target="tpu_custom_call" | custom-call | tf_op jit(solution)/shard_map/pallas_call | solution.py:326
  83.7 0.9 shard_map.94
  84.8 1.0 collective-permute-start.12
  85.7 3.1 %collective-permute-start.13 = (bf16[128,1024]{1,0:T(8,128)(2,1)S(1)}, bf16[128,1024]{1,0:T(8,128)(2,1)S(1)}, u32[]{:S(2)}, u32[]{:S(2)}) collective-permute-start(bf16[128,1024]{1,0:T(8,128)(2,1)S(1)} %get-tuple-element.83), channel_id=1, source_target_pairs={{0,32},{16,48},{32,0},{48,16},{1,33},{17,49},{33,1},{49,17},{2,34}... | collective-permute-start | bytes 786440 | tf_op jit(solution)/shard_map/ppermute | solution.py:40
  89.2 0.8 copy-done.12
  90.0 1.4 collective-permute-start.18
  91.4 2.7 %collective-permute-start.19 = (bf16[256,1024]{1,0:T(8,128)(2,1)S(1)}, bf16[256,1024]{1,0:T(8,128)(2,1)S(1)}, u32[]{:S(2)}, u32[]{:S(2)}) collective-permute-start(bf16[256,1024]{1,0:T(8,128)(2,1)S(1)} %get-tuple-element.93), channel_id=1, source_target_pairs={{0,8},{64,66},{1,9},{65,67},{2,10},{66,64},{3,11},{67,65},{4,12},{... | collective-permute-start | bytes 1572872 | tf_op jit(solution)/shard_map/ppermute | solution.py:64
  94.7 2.9 %collective-permute-start.20 = (bf16[256,1024]{1,0:T(8,128)(2,1)S(1)}, bf16[256,1024]{1,0:T(8,128)(2,1)S(1)}, u32[]{:S(2)}, u32[]{:S(2)}) collective-permute-start(bf16[256,1024]{1,0:T(8,128)(2,1)S(1)} %get-tuple-element.94), channel_id=1, source_target_pairs={{0,12},{64,67},{1,13},{65,64},{2,14},{66,65},{3,15},{67,66},{4,0},... | collective-permute-start | bytes 1572872 | tf_op jit(solution)/shard_map/ppermute | solution.py:64
  97.6 3.4 %collective-permute-done.13.refs_6_ = bf16[128,1024]{1,0:T(8,128)(2,1)S(1)} collective-permute-done((bf16[128,1024]{1,0:T(8,128)(2,1)S(1)}, bf16[128,1024]{1,0:T(8,128)(2,1)S(1)}, u32[]{:S(2)}, u32[]{:S(2)}) %collective-permute-start.13) | collective-permute-done | bytes 262176 | tf_op jit(solution)/shard_map/ppermute | solution.py:40
  101.1 3.4 %shard_map.96 = (bf16[128,1024]{1,0:T(8,128)(2,1)S(1)}, bf16[128,1024]{1,0:T(8,128)(2,1)S(1)}, bf16[128,1024]{1,0:T(8,128)(2,1)S(1)}, bf16[128,1024]{1,0:T(8,128...) custom-call(bf16[1024,1024]{1,0:T(8,128)(2,1)S(1)} %get-tuple-element.77.ref, ...), custom_call_target="tpu_custom_call" | custom-call | tf_op jit(solution)/shard_map/pallas_call | solution.py:326
  104.6 0.9 collective-permute-start.15
  105.4 0.7 collective-permute-done.21.far
  106.1 2.5 %collective-permute-start.16 = (bf16[128,1024]{1,0:T(8,128)(2,1)S(1)}, bf16[128,1024]{1,0:T(8,128)(2,1)S(1)}, u32[]{:S(2)}, u32[]{:S(2)}) collective-permute-start(bf16[128,1024]{1,0:T(8,128)(2,1)S(1)} %get-tuple-element.89), channel_id=1, source_target_pairs={{0,32},{16,48},{32,0},{48,16},{1,33},{17,49},{33,1},{49,17},{2,34}... | collective-permute-start | bytes 786440 | tf_op jit(solution)/shard_map/ppermute | solution.py:40
  108.6 0.9 collective-permute-start.17
  109.6 1.4 collective-permute-start.23
  111.1 1.9 %collective-permute-start.25 = (bf16[256,1024]{1,0:T(8,128)(2,1)S(1)}, bf16[256,1024]{1,0:T(8,128)(2,1)S(1)}, u32[]{:S(2)}, u32[]{:S(2)}) collective-permute-start(bf16[256,1024]{1,0:T(8,128)(2,1)S(1)} %shard_map.97.refs_4_), channel_id=1, source_target_pairs={{0,12},{64,67},{1,13},{65,64},{2,14},{66,65},{3,15},{67,66},{4,0},... | collective-permute-start | bytes 1572872 | tf_op jit(solution)/shard_map/ppermute | solution.py:64
  112.9 1.6 collective-permute-done.15.r1
  114.5 6.3 %collective-permute-done.16.r2 = bf16[128,1024]{1,0:T(8,128)(2,1)S(1)} collective-permute-done((bf16[128,1024]{1,0:T(8,128)(2,1)S(1)}, bf16[128,1024]{1,0:T(8,128)(2,1)S(1)}, u32[]{:S(2)}, u32[]{:S(2)}) %collective-permute-start.16) | collective-permute-done | bytes 262176 | tf_op jit(solution)/shard_map/ppermute | solution.py:40
  121.4 0.7 shard_map.98.keep
  122.3 3.2 %collective-permute-start.24 = (bf16[256,1024]{1,0:T(8,128)(2,1)S(1)}, bf16[256,1024]{1,0:T(8,128)(2,1)}, u32[]{:S(2)}, u32[]{:S(2)}) collective-permute-start(bf16[256,1024]{1,0:T(8,128)(2,1)S(1)} %shard_map.97.refs_4_), channel_id=1, source_target_pairs={{0,8},{64,66},{1,9},{65,67},{2,10},{66,64},{3,11},{67,65},{4,12},{... | collective-permute-start | bytes 1572872 | tf_op jit(solution)/shard_map/ppermute | solution.py:64
  126.2 2.1 %collective-permute-start.30 = (bf16[256,1024]{1,0:T(8,128)(2,1)S(1)}, bf16[256,1024]{1,0:T(8,128)(2,1)}, u32[]{:S(2)}, u32[]{:S(2)}) collective-permute-start(bf16[256,1024]{1,0:T(8,128)(2,1)S(1)} %shard_map.99.refs_4_), channel_id=1, source_target_pairs={{0,8},{64,66},{1,9},{65,67},{2,10},{66,64},{3,11},{67,65},{4,12},{... | collective-permute-start | bytes 1572872 | tf_op jit(solution)/shard_map/ppermute | solution.py:64
  128.3 1.4 collective-permute-start.31
  129.7 3.5 %collective-permute-done.24.refs_6_ = bf16[256,1024]{1,0:T(8,128)(2,1)} collective-permute-done((bf16[256,1024]{1,0:T(8,128)(2,1)S(1)}, bf16[256,1024]{1,0:T(8,128)(2,1)}, u32[]{:S(2)}, u32[]{:S(2)}) %collective-permute-start.24) | collective-permute-done | bytes 524320 | tf_op jit(solution)/shard_map/ppermute | solution.py:64
  133.3 6.3 %shard_map.100 = (bf16[256,1024]{1,0:T(8,128)(2,1)}, bf16[256,1024]{1,0:T(8,128)(2,1)}, bf16[256,1024]{1,0:T(8,128)(2,1)}, bf16[256,1024]{1,0:T(8,128)(2,1)}) custom-call(s32[5]{0:T(128)} %stack.23.place.refs_11_, bf16[256,1024]{1,0:T(8,128)(2,1)} %copy-done.12, bf16[256,1024]{1,0:T(8,128)(2,1)} %copy-done.21, bf16[256,1024]{1,0:T(8,128)(2,1)} %copy-done.22, ...), custom_call_target="tpu_custom_call" | custom-call | tf_op jit(solution)/shard_map/pallas_call | solution.py:364
  139.6 2.9 %collective-permute-start.28 = (bf16[256,1024]{1,0:T(8,128)(2,1)}, bf16[256,1024]{1,0:T(8,128)(2,1)S(1)}, u32[]{:S(2)}, u32[]{:S(2)}) collective-permute-start(bf16[256,1024]{1,0:T(8,128)(2,1)} %get-tuple-element.102), channel_id=1, source_target_pairs={{0,3},{64,76},{1,0},{65,77},{2,1},{66,78},{3,2},{67,79},{4,7},{68,... | collective-permute-start | bytes 1572872 | tf_op jit(solution)/shard_map/ppermute | solution.py:74
  142.5 0.9 collective-permute-start.27
  143.4 0.9 collective-permute-start.26
  144.4 2.6 %collective-permute-done.31.refs_7_ = bf16[256,1024]{1,0:T(8,128)(2,1)} collective-permute-done((bf16[256,1024]{1,0:T(8,128)(2,1)S(1)}, bf16[256,1024]{1,0:T(8,128)(2,1)}, u32[]{:S(2)}, u32[]{:S(2)}) %collective-permute-start.31) | collective-permute-done | bytes 524320 | tf_op jit(solution)/shard_map/ppermute | solution.py:64
  147.1 3.6 %shard_map.101 = (bf16[80,1024]{1,0:T(8,128)(2,1)}, bf16[80,1024]{1,0:T(8,128)(2,1)}, bf16[80,1024]{1,0:T(8,128)(2,1)}, bf16[80,1024]{1,0:T(8,128)(2,1)}) custom-call(s32[5]{0:T(128)} %stack.23.place.refs_11_, bf16[320,256]{1,0:T(8,128)(2,1)} %copy-done.14, bf16[320,256]{1,0:T(8,128)(2,1)} %copy-done.27, bf16[320,256]{1,0:T(8,128)(2,1)} %copy-done.28, ...), custom_call_target="tpu_custom_call" | custom-call | tf_op jit(solution)/shard_map/pallas_call | solution.py:426
  150.6 2.5 %collective-permute-start.34 = (bf16[80,1024]{1,0:T(8,128)(2,1)}, bf16[80,1024]{1,0:T(8,128)(2,1)S(1)}, u32[]{:S(2)}, u32[]{:S(2)}) collective-permute-start(bf16[80,1024]{1,0:T(8,128)(2,1)} %get-tuple-element.111), channel_id=1, source_target_pairs={{0,3},{64,76},{1,0},{65,77},{2,1},{66,78},{3,2},{67,79},{4,7},{68,... | collective-permute-start | bytes 491528 | tf_op jit(solution)/shard_map/ppermute | solution.py:74
  153.1 0.9 collective-permute-start.33
  154.0 1.2 collective-permute-done.28
  155.2 3.8 %collective-permute-done.26 = bf16[256,1024]{1,0:T(8,128)(2,1)S(1)} collective-permute-done((bf16[256,1024]{1,0:T(8,128)(2,1)}, bf16[256,1024]{1,0:T(8,128)(2,1)S(1)}, u32[]{:S(2)}, u32[]{:S(2)}) %collective-permute-start.26) | collective-permute-done | bytes 524320 | tf_op jit(solution)/shard_map/ppermute | solution.py:74
  159.1 1.3 add_bitcast_fusion
  160.9 1.7 %collective-permute-done.32 = bf16[80,1024]{1,0:T(8,128)(2,1)S(1)} collective-permute-done((bf16[80,1024]{1,0:T(8,128)(2,1)}, bf16[80,1024]{1,0:T(8,128)(2,1)S(1)}, u32[]{:S(2)}, u32[]{:S(2)}) %collective-permute-start.32) | collective-permute-done | bytes 163872 | tf_op jit(solution)/shard_map/ppermute | solution.py:74
  162.6 0.8 convert_add_fusion.1
  (95 shorter events, 5.8 us)
Async XLA Ops:
  0.6 11.0 %copy-start.20 = (bf16[4,32,2560]{2,1,0:T(8,128)(2,1)S(1)}, bf16[4,32,2560]{2,1,0:T(8,128)(2,1)}, u32[]{:S(2)}) copy-start(bf16[4,32,2560]{2,1,0:T(8,128)(2,1)} %param.7) | copy-start | bytes 1966084
  0.6 30.7 %collective-permute-start.4 = (bf16[4096,1024]{1,0:T(8,128)(2,1)}, bf16[4096,1024]{1,0:T(8,128)(2,1)}, u32[]{:S(2)}, u32[]{:S(2)}) collective-permute-start(bf16[4096,1024]{1,0:T(8,128)(2,1)} %bitcast.19), channel_id=1, source_target_pairs={{0,64},{64,0},{1,65},{65,1},{2,66},{66,2},{3,67},{67,3},{4,68},{68... | collective-permute-start | bytes 25165832 | tf_op jit(solution)/shard_map/ppermute | solution.py:78
  3.5 27.8 %all-to-all-start = ((bf16[16,32,1024]{2,1,0:T(8,128)(2,1)}), bf16[16,32,1024]{2,1,0:T(8,128)(2,1)S(1)}, u32[]{:S(2)}, u32[]{:S(2)}) async-start(bf16[16,32,1024]{2,1,0:T(8,128)(2,1)} %shard_map.86), calls=%async_computation | async-start | bytes 2097152 | tf_op jit(solution)/shard_map/all_to_all | solution.py:523
  11.6 2.7 %copy-start.15 = (s32[5]{0:T(128)S(1)}, s32[5]{0:T(128)}, u32[]{:S(2)}) copy-start(s32[5]{0:T(128)} %stack.23.place.refs_11_) | copy-start | bytes 64
  12.5 1.9 %collective-permute-start = (bf16[1280,128]{1,0:T(8,128)(2,1)S(1)}, bf16[1280,128]{1,0:T(8,128)(2,1)S(1)}, u32[]{:S(2)}, u32[]{:S(2)}) collective-permute-start(bf16[1280,128]{1,0:T(8,128)(2,1)S(1)} %dynamic-slice_bitcast_fusion), channel_id=1, source_target_pairs={{0,64},{64,0},{1,65},{65,1},{2,66},{66,2},{3,67},{67,3},{4,68},{68... | collective-permute-start | bytes 983048 | tf_op jit(solution)/shard_map/ppermute | solution.py:78
  15.7 12.8 %collective-permute-start.1 = (bf16[320,256]{1,0:T(8,128)(2,1)S(1)}, bf16[320,256]{1,0:T(8,128)(2,1)S(1)}, u32[]{:S(2)}, u32[]{:S(2)}) collective-permute-start(bf16[320,256]{1,0:T(8,128)(2,1)S(1)} %get-tuple-element.58), channel_id=1, source_target_pairs={{0,4},{64,65},{1,5},{65,66},{2,6},{66,67},{3,7},{67,64},{4,8},{68,... | collective-permute-start | bytes 491528 | tf_op jit(solution)/shard_map/ppermute | solution.py:64
  17.7 13.6 %collective-permute-start.2 = (bf16[320,256]{1,0:T(8,128)(2,1)S(1)}, bf16[320,256]{1,0:T(8,128)(2,1)S(1)}, u32[]{:S(2)}, u32[]{:S(2)}) collective-permute-start(bf16[320,256]{1,0:T(8,128)(2,1)S(1)} %get-tuple-element.59), channel_id=1, source_target_pairs={{0,8},{64,66},{1,9},{65,67},{2,10},{66,64},{3,11},{67,65},{4,12},{... | collective-permute-start | bytes 491528 | tf_op jit(solution)/shard_map/ppermute | solution.py:64
  21.3 10.1 %collective-permute-start.3 = (bf16[320,256]{1,0:T(8,128)(2,1)S(1)}, bf16[320,256]{1,0:T(8,128)(2,1)S(1)}, u32[]{:S(2)}, u32[]{:S(2)}) collective-permute-start(bf16[320,256]{1,0:T(8,128)(2,1)S(1)} %get-tuple-element.60), channel_id=1, source_target_pairs={{0,12},{64,67},{1,13},{65,64},{2,14},{66,65},{3,15},{67,66},{4,0},... | collective-permute-start | bytes 491528 | tf_op jit(solution)/shard_map/ppermute | solution.py:64
  28.5 36.4 %copy-start.27 = (bf16[320,256]{1,0:T(8,128)(2,1)}, bf16[320,256]{1,0:T(8,128)(2,1)S(1)}, u32[]{:S(2)}) copy-start(bf16[320,256]{1,0:T(8,128)(2,1)S(1)} %collective-permute-done.1.refs_1_) | copy-start | bytes 491524
  31.3 33.5 %copy-start.28 = (bf16[320,256]{1,0:T(8,128)(2,1)}, bf16[320,256]{1,0:T(8,128)(2,1)S(1)}, u32[]{:S(2)}) copy-start(bf16[320,256]{1,0:T(8,128)(2,1)S(1)} %collective-permute-done.2.refs_2_) | copy-start | bytes 491524
  31.3 3.7 %copy-start.29 = (bf16[320,256]{1,0:T(8,128)(2,1)}, bf16[320,256]{1,0:T(8,128)(2,1)S(1)}, u32[]{:S(2)}) copy-start(bf16[320,256]{1,0:T(8,128)(2,1)S(1)} %collective-permute-done.3.refs_3_) | copy-start | bytes 491524
  31.3 1.0 copy-start.19
  35.0 5.3 %copy-start.1 = (bf16[4,32,1024]{2,1,0:T(8,128)(2,1)S(1)}, bf16[4,32,1024]{2,1,0:T(8,128)(2,1)}, u32[]{:S(2)}) copy-start(bf16[4,32,1024]{2,1,0:T(8,128)(2,1)} %shard_map.89) | copy-start | bytes 786436
  35.0 34.5 %all-to-all-start.1 = ((bf16[16,32,1024]{2,1,0:T(8,128)(2,1)}), bf16[16,32,1024]{2,1,0:T(8,128)(2,1)S(1)}, u32[]{:S(2)}, u32[]{:S(2)}) async-start(bf16[16,32,1024]{2,1,0:T(8,128)(2,1)} %shard_map.88), calls=%async_computation.1 | async-start | bytes 2097152 | tf_op jit(solution)/shard_map/all_to_all | solution.py:540
  40.3 29.2 %copy-start.16 = (s32[5]{0:T(128)S(1)}, s32[5]{0:T(128)}, u32[]{:S(2)}) copy-start(s32[5]{0:T(128)} %stack.23.place.refs_11_) | copy-start | bytes 64
  40.3 29.2 %copy-start.17 = (s32[128]{0:T(128)S(1)}, s32[128]{0:T(128)}, u32[]{:S(2)}) copy-start(s32[128]{0:T(128)} %routing.7) | copy-start | bytes 1540
  40.3 9.5 %collective-permute-start.5 = (bf16[128,1024]{1,0:T(8,128)(2,1)S(1)}, bf16[128,1024]{1,0:T(8,128)(2,1)S(1)}, u32[]{:S(2)}, u32[]{:S(2)}) collective-permute-start(bf16[128,1024]{1,0:T(8,128)(2,1)S(1)} %bitcast.24), channel_id=1, source_target_pairs={{0,16},{16,32},{32,48},{48,0},{1,17},{17,33},{33,49},{49,1},{2,18}... | collective-permute-start | bytes 786440 | tf_op jit(solution)/shard_map/ppermute | solution.py:40
  41.9 14.4 %collective-permute-start.6 = (bf16[128,1024]{1,0:T(8,128)(2,1)S(1)}, bf16[128,1024]{1,0:T(8,128)(2,1)S(1)}, u32[]{:S(2)}, u32[]{:S(2)}) collective-permute-start(bf16[128,1024]{1,0:T(8,128)(2,1)S(1)} %bitcast.25), channel_id=1, source_target_pairs={{0,32},{16,48},{32,0},{48,16},{1,33},{17,49},{33,1},{49,17},{2,34}... | collective-permute-start | bytes 786440 | tf_op jit(solution)/shard_map/ppermute | solution.py:40
  44.6 11.7 %collective-permute-start.7 = (bf16[128,1024]{1,0:T(8,128)(2,1)S(1)}, bf16[128,1024]{1,0:T(8,128)(2,1)S(1)}, u32[]{:S(2)}, u32[]{:S(2)}) collective-permute-start(bf16[128,1024]{1,0:T(8,128)(2,1)S(1)} %bitcast.26), channel_id=1, source_target_pairs={{0,48},{16,0},{32,16},{48,32},{1,49},{17,1},{33,17},{49,33},{2,50}... | collective-permute-start | bytes 786440 | tf_op jit(solution)/shard_map/ppermute | solution.py:40
  49.8 6.5 %copy-start.5 = (bf16[128,1024]{1,0:T(8,128)(2,1)}, bf16[128,1024]{1,0:T(8,128)(2,1)S(1)}, u32[]{:S(2)}) copy-start(bf16[128,1024]{1,0:T(8,128)(2,1)S(1)} %collective-permute-done.5.refs_1_) | copy-start | bytes 786436
  64.8 13.7 %collective-permute-start.8 = (bf16[128,1024]{1,0:T(8,128)(2,1)}, bf16[128,1024]{1,0:T(8,128)(2,1)S(1)}, u32[]{:S(2)}, u32[]{:S(2)}) collective-permute-start(bf16[128,1024]{1,0:T(8,128)(2,1)} %get-tuple-element.71.refs_4_), channel_id=1, source_target_pairs={{0,16},{16,32},{32,48},{48,0},{1,17},{17,33},{33,49},{49,1},{2,18}... | collective-permute-start | bytes 786440 | tf_op jit(solution)/shard_map/ppermute | solution.py:40
  65.6 13.8 %collective-permute-start.9 = (bf16[128,1024]{1,0:T(8,128)(2,1)}, bf16[128,1024]{1,0:T(8,128)(2,1)S(1)}, u32[]{:S(2)}, u32[]{:S(2)}) collective-permute-start(bf16[128,1024]{1,0:T(8,128)(2,1)} %get-tuple-element.71.refs_4_), channel_id=1, source_target_pairs={{0,32},{16,48},{32,0},{48,16},{1,33},{17,49},{33,1},{49,17},{2,34}... | collective-permute-start | bytes 786440 | tf_op jit(solution)/shard_map/ppermute | solution.py:40
  67.9 11.4 %collective-permute-start.10 = (bf16[128,1024]{1,0:T(8,128)(2,1)}, bf16[128,1024]{1,0:T(8,128)(2,1)S(1)}, u32[]{:S(2)}, u32[]{:S(2)}) collective-permute-start(bf16[128,1024]{1,0:T(8,128)(2,1)} %get-tuple-element.71.refs_4_), channel_id=1, source_target_pairs={{0,48},{16,0},{32,16},{48,32},{1,49},{17,1},{33,17},{49,33},{2,50}... | collective-permute-start | bytes 786440 | tf_op jit(solution)/shard_map/ppermute | solution.py:40
  70.5 3.4 %copy-start = (bf16[1,4096,1024]{2,1,0:T(8,128)(2,1)S(1)}, bf16[1,4096,1024]{2,1,0:T(8,128)(2,1)}, u32[]{:S(2)}) copy-start(bf16[1,4096,1024]{2,1,0:T(8,128)(2,1)} %param.12) | copy-start | bytes 25165828
  73.9 5.5 %copy-start.11 = (bf16[128,1024]{1,0:T(8,128)(2,1)S(1)}, bf16[128,1024]{1,0:T(8,128)(2,1)}, u32[]{:S(2)}) copy-start(bf16[128,1024]{1,0:T(8,128)(2,1)} %get-tuple-element.71.refs_4_) | copy-start | bytes 786436
  79.4 4.3 %copy-start.2 = (bf16[4,32,1024]{2,1,0:T(8,128)(2,1)S(1)}, bf16[4,32,1024]{2,1,0:T(8,128)(2,1)}, u32[]{:S(2)}) copy-start(bf16[4,32,1024]{2,1,0:T(8,128)(2,1)} %shard_map.89) | copy-start | bytes 786436
  79.4 4.3 %copy-start.6 = (bf16[128,1024]{1,0:T(8,128)(2,1)S(1)}, bf16[128,1024]{1,0:T(8,128)(2,1)}, u32[]{:S(2)}) copy-start(bf16[128,1024]{1,0:T(8,128)(2,1)} %copy-done.5) | copy-start | bytes 786436
  79.4 4.3 %copy-start.8 = (bf16[128,1024]{1,0:T(8,128)(2,1)S(1)}, bf16[128,1024]{1,0:T(8,128)(2,1)}, u32[]{:S(2)}) copy-start(bf16[128,1024]{1,0:T(8,128)(2,1)} %copy-done.7) | copy-start | bytes 786436
  79.4 4.3 %copy-start.10 = (bf16[128,1024]{1,0:T(8,128)(2,1)S(1)}, bf16[128,1024]{1,0:T(8,128)(2,1)}, u32[]{:S(2)}) copy-start(bf16[128,1024]{1,0:T(8,128)(2,1)} %copy-done.9) | copy-start | bytes 786436
  83.7 17.4 %copy-start.13 = (f32[128,1024]{1,0:T(8,128)S(1)}, f32[128,1024]{1,0:T(8,128)}, u32[]{:S(2)}) copy-start(f32[128,1024]{1,0:T(8,128)} %get-tuple-element.86.refs_9_) | copy-start | bytes 1572868
  84.7 4.4 %collective-permute-start.11 = (bf16[4,128,1024]{2,1,0:T(8,128)(2,1)S(1)}, bf16[4,128,1024]{2,1,0:T(8,128)(2,1)S(1)}, u32[]{:S(2)}, u32[]{:S(2)}) collective-permute-start(bf16[4,128,1024]{2,1,0:T(8,128)(2,1)S(1)} %get-tuple-element.75), channel_id=1, source_target_pairs={{0,64},{64,0},{1,65},{65,1},{2,66},{66,2},{3,67},{67,3},{4,68},{68... | collective-permute-start | bytes 3145736 | tf_op jit(solution)/shard_map/ppermute | solution.py:78
  84.8 9.9 %collective-permute-start.12 = (bf16[128,1024]{1,0:T(8,128)(2,1)S(1)}, bf16[128,1024]{1,0:T(8,128)(2,1)S(1)}, u32[]{:S(2)}, u32[]{:S(2)}) collective-permute-start(bf16[128,1024]{1,0:T(8,128)(2,1)S(1)} %get-tuple-element.82), channel_id=1, source_target_pairs={{0,16},{16,32},{32,48},{48,0},{1,17},{17,33},{33,49},{49,1},{2,18}... | collective-permute-start | bytes 786440 | tf_op jit(solution)/shard_map/ppermute | solution.py:40
  85.7 15.3 %collective-permute-start.13 = (bf16[128,1024]{1,0:T(8,128)(2,1)S(1)}, bf16[128,1024]{1,0:T(8,128)(2,1)S(1)}, u32[]{:S(2)}, u32[]{:S(2)}) collective-permute-start(bf16[128,1024]{1,0:T(8,128)(2,1)S(1)} %get-tuple-element.83), channel_id=1, source_target_pairs={{0,32},{16,48},{32,0},{48,16},{1,33},{17,49},{33,1},{49,17},{2,34}... | collective-permute-start | bytes 786440 | tf_op jit(solution)/shard_map/ppermute | solution.py:40
  88.8 12.2 %collective-permute-start.14 = (bf16[128,1024]{1,0:T(8,128)(2,1)S(1)}, bf16[128,1024]{1,0:T(8,128)(2,1)S(1)}, u32[]{:S(2)}, u32[]{:S(2)}) collective-permute-start(bf16[128,1024]{1,0:T(8,128)(2,1)S(1)} %get-tuple-element.84), channel_id=1, source_target_pairs={{0,48},{16,0},{32,16},{48,32},{1,49},{17,1},{33,17},{49,33},{2,50}... | collective-permute-start | bytes 786440 | tf_op jit(solution)/shard_map/ppermute | solution.py:40
  90.0 18.6 %collective-permute-start.18 = (bf16[256,1024]{1,0:T(8,128)(2,1)S(1)}, bf16[256,1024]{1,0:T(8,128)(2,1)S(1)}, u32[]{:S(2)}, u32[]{:S(2)}) collective-permute-start(bf16[256,1024]{1,0:T(8,128)(2,1)S(1)} %get-tuple-element.92), channel_id=1, source_target_pairs={{0,4},{64,65},{1,5},{65,66},{2,6},{66,67},{3,7},{67,64},{4,8},{68,... | collective-permute-start | bytes 1572872 | tf_op jit(solution)/shard_map/ppermute | solution.py:64
  91.4 18.3 %collective-permute-start.19 = (bf16[256,1024]{1,0:T(8,128)(2,1)S(1)}, bf16[256,1024]{1,0:T(8,128)(2,1)S(1)}, u32[]{:S(2)}, u32[]{:S(2)}) collective-permute-start(bf16[256,1024]{1,0:T(8,128)(2,1)S(1)} %get-tuple-element.93), channel_id=1, source_target_pairs={{0,8},{64,66},{1,9},{65,67},{2,10},{66,64},{3,11},{67,65},{4,12},{... | collective-permute-start | bytes 1572872 | tf_op jit(solution)/shard_map/ppermute | solution.py:64
  94.7 16.4 %collective-permute-start.20 = (bf16[256,1024]{1,0:T(8,128)(2,1)S(1)}, bf16[256,1024]{1,0:T(8,128)(2,1)S(1)}, u32[]{:S(2)}, u32[]{:S(2)}) collective-permute-start(bf16[256,1024]{1,0:T(8,128)(2,1)S(1)} %get-tuple-element.94), channel_id=1, source_target_pairs={{0,12},{64,67},{1,13},{65,64},{2,14},{66,65},{3,15},{67,66},{4,0},... | collective-permute-start | bytes 1572872 | tf_op jit(solution)/shard_map/ppermute | solution.py:64
  101.1 20.4 %copy-start.18 = (s32[128]{0:T(128)S(1)}, s32[128]{0:T(128)}, u32[]{:S(2)}) copy-start(s32[128]{0:T(128)} %counts.3) | copy-start | bytes 1540
  104.5 1.6 collective-permute-start.21
  104.6 9.9 %collective-permute-start.15 = (bf16[128,1024]{1,0:T(8,128)(2,1)S(1)}, bf16[128,1024]{1,0:T(8,128)(2,1)S(1)}, u32[]{:S(2)}, u32[]{:S(2)}) collective-permute-start(bf16[128,1024]{1,0:T(8,128)(2,1)S(1)} %get-tuple-element.88), channel_id=1, source_target_pairs={{0,16},{16,32},{32,48},{48,0},{1,17},{17,33},{33,49},{49,1},{2,18}... | collective-permute-start | bytes 786440 | tf_op jit(solution)/shard_map/ppermute | solution.py:40
  106.1 14.8 %collective-permute-start.16 = (bf16[128,1024]{1,0:T(8,128)(2,1)S(1)}, bf16[128,1024]{1,0:T(8,128)(2,1)S(1)}, u32[]{:S(2)}, u32[]{:S(2)}) collective-permute-start(bf16[128,1024]{1,0:T(8,128)(2,1)S(1)} %get-tuple-element.89), channel_id=1, source_target_pairs={{0,32},{16,48},{32,0},{48,16},{1,33},{17,49},{33,1},{49,17},{2,34}... | collective-permute-start | bytes 786440 | tf_op jit(solution)/shard_map/ppermute | solution.py:40
  108.6 24.6 %copy-start.21 = (bf16[256,1024]{1,0:T(8,128)(2,1)}, bf16[256,1024]{1,0:T(8,128)(2,1)S(1)}, u32[]{:S(2)}) copy-start(bf16[256,1024]{1,0:T(8,128)(2,1)S(1)} %collective-permute-done.18.refs_1_) | copy-start | bytes 1572868
  108.6 12.8 %collective-permute-start.17 = (bf16[128,1024]{1,0:T(8,128)(2,1)S(1)}, bf16[128,1024]{1,0:T(8,128)(2,1)S(1)}, u32[]{:S(2)}, u32[]{:S(2)}) collective-permute-start(bf16[128,1024]{1,0:T(8,128)(2,1)S(1)} %get-tuple-element.90), channel_id=1, source_target_pairs={{0,48},{16,0},{32,16},{48,32},{1,49},{17,1},{33,17},{49,33},{2,50}... | collective-permute-start | bytes 786440 | tf_op jit(solution)/shard_map/ppermute | solution.py:40
  109.6 23.7 %copy-start.3 = (bf16[256,1024]{1,0:T(8,128)(2,1)}, bf16[256,1024]{1,0:T(8,128)(2,1)S(1)}, u32[]{:S(2)}) copy-start(bf16[256,1024]{1,0:T(8,128)(2,1)S(1)} %shard_map.97.refs_4_) | copy-start | bytes 1572868
  109.6 23.6 %copy-start.22 = (bf16[256,1024]{1,0:T(8,128)(2,1)}, bf16[256,1024]{1,0:T(8,128)(2,1)S(1)}, u32[]{:S(2)}) copy-start(bf16[256,1024]{1,0:T(8,128)(2,1)S(1)} %collective-permute-done.19.refs_2_) | copy-start | bytes 1572868
  109.6 15.9 %collective-permute-start.23 = (bf16[256,1024]{1,0:T(8,128)(2,1)S(1)}, bf16[256,1024]{1,0:T(8,128)(2,1)S(1)}, u32[]{:S(2)}, u32[]{:S(2)}) collective-permute-start(bf16[256,1024]{1,0:T(8,128)(2,1)S(1)} %shard_map.97.refs_4_), channel_id=1, source_target_pairs={{0,4},{64,65},{1,5},{65,66},{2,6},{66,67},{3,7},{67,64},{4,8},{68,... | collective-permute-start | bytes 1572872 | tf_op jit(solution)/shard_map/ppermute | solution.py:64
  111.1 22.2 %copy-start.23 = (bf16[256,1024]{1,0:T(8,128)(2,1)}, bf16[256,1024]{1,0:T(8,128)(2,1)S(1)}, u32[]{:S(2)}) copy-start(bf16[256,1024]{1,0:T(8,128)(2,1)S(1)} %collective-permute-done.20.refs_3_) | copy-start | bytes 1572868
  111.1 14.5 %collective-permute-start.25 = (bf16[256,1024]{1,0:T(8,128)(2,1)S(1)}, bf16[256,1024]{1,0:T(8,128)(2,1)S(1)}, u32[]{:S(2)}, u32[]{:S(2)}) collective-permute-start(bf16[256,1024]{1,0:T(8,128)(2,1)S(1)} %shard_map.97.refs_4_), channel_id=1, source_target_pairs={{0,12},{64,67},{1,13},{65,64},{2,14},{66,65},{3,15},{67,66},{4,0},... | collective-permute-start | bytes 1572872 | tf_op jit(solution)/shard_map/ppermute | solution.py:64
  122.2 3.3 %collective-permute-start.22 = (bf16[128,1024]{1,0:T(8,128)(2,1)S(1)}, bf16[128,1024]{1,0:T(8,128)(2,1)S(1)}, u32[]{:S(2)}, u32[]{:S(2)}) collective-permute-start(bf16[128,1024]{1,0:T(8,128)(2,1)S(1)} %shard_map.98.keep), channel_id=1, source_target_pairs={{0,64},{64,0},{1,65},{65,1},{2,66},{66,2},{3,67},{67,3},{4,68},{68... | collective-permute-start | bytes 786440 | tf_op jit(solution)/shard_map/ppermute | solution.py:78
  122.3 11.0 %collective-permute-start.24 = (bf16[256,1024]{1,0:T(8,128)(2,1)S(1)}, bf16[256,1024]{1,0:T(8,128)(2,1)}, u32[]{:S(2)}, u32[]{:S(2)}) collective-permute-start(bf16[256,1024]{1,0:T(8,128)(2,1)S(1)} %shard_map.97.refs_4_), channel_id=1, source_target_pairs={{0,8},{64,66},{1,9},{65,67},{2,10},{66,64},{3,11},{67,65},{4,12},{... | collective-permute-start | bytes 1572872 | tf_op jit(solution)/shard_map/ppermute | solution.py:64
  125.5 14.1 %copy-start.4 = (bf16[256,1024]{1,0:T(8,128)(2,1)}, bf16[256,1024]{1,0:T(8,128)(2,1)S(1)}, u32[]{:S(2)}) copy-start(bf16[256,1024]{1,0:T(8,128)(2,1)S(1)} %shard_map.99.refs_4_) | copy-start | bytes 1572868
  125.6 7.7 %copy-start.24 = (bf16[256,1024]{1,0:T(8,128)(2,1)}, bf16[256,1024]{1,0:T(8,128)(2,1)S(1)}, u32[]{:S(2)}) copy-start(bf16[256,1024]{1,0:T(8,128)(2,1)S(1)} %collective-permute-done.23.refs_5_) | copy-start | bytes 1572868
  125.6 7.7 %copy-start.25 = (bf16[256,1024]{1,0:T(8,128)(2,1)}, bf16[256,1024]{1,0:T(8,128)(2,1)S(1)}, u32[]{:S(2)}) copy-start(bf16[256,1024]{1,0:T(8,128)(2,1)S(1)} %collective-permute-done.25.refs_7_) | copy-start | bytes 1572868
  125.6 17.8 %collective-permute-start.29 = (bf16[256,1024]{1,0:T(8,128)(2,1)S(1)}, bf16[256,1024]{1,0:T(8,128)(2,1)}, u32[]{:S(2)}, u32[]{:S(2)}) collective-permute-start(bf16[256,1024]{1,0:T(8,128)(2,1)S(1)} %shard_map.99.refs_4_), channel_id=1, source_target_pairs={{0,4},{64,65},{1,5},{65,66},{2,6},{66,67},{3,7},{67,64},{4,8},{68,... | collective-permute-start | bytes 1572872 | tf_op jit(solution)/shard_map/ppermute | solution.py:64
  126.2 18.2 %collective-permute-start.30 = (bf16[256,1024]{1,0:T(8,128)(2,1)S(1)}, bf16[256,1024]{1,0:T(8,128)(2,1)}, u32[]{:S(2)}, u32[]{:S(2)}) collective-permute-start(bf16[256,1024]{1,0:T(8,128)(2,1)S(1)} %shard_map.99.refs_4_), channel_id=1, source_target_pairs={{0,8},{64,66},{1,9},{65,67},{2,10},{66,64},{3,11},{67,65},{4,12},{... | collective-permute-start | bytes 1572872 | tf_op jit(solution)/shard_map/ppermute | solution.py:64
  128.3 18.8 %collective-permute-start.31 = (bf16[256,1024]{1,0:T(8,128)(2,1)S(1)}, bf16[256,1024]{1,0:T(8,128)(2,1)}, u32[]{:S(2)}, u32[]{:S(2)}) collective-permute-start(bf16[256,1024]{1,0:T(8,128)(2,1)S(1)} %shard_map.99.refs_4_), channel_id=1, source_target_pairs={{0,12},{64,67},{1,13},{65,64},{2,14},{66,65},{3,15},{67,66},{4,0},... | collective-permute-start | bytes 1572872 | tf_op jit(solution)/shard_map/ppermute | solution.py:64
  139.6 19.4 %copy-start.26 = (bf16[256,1024]{1,0:T(8,128)(2,1)S(1)}, bf16[256,1024]{1,0:T(8,128)(2,1)}, u32[]{:S(2)}) copy-start(bf16[256,1024]{1,0:T(8,128)(2,1)} %get-tuple-element.99) | copy-start | bytes 1572868
  139.6 15.6 %collective-permute-start.28 = (bf16[256,1024]{1,0:T(8,128)(2,1)}, bf16[256,1024]{1,0:T(8,128)(2,1)S(1)}, u32[]{:S(2)}, u32[]{:S(2)}) collective-permute-start(bf16[256,1024]{1,0:T(8,128)(2,1)} %get-tuple-element.102), channel_id=1, source_target_pairs={{0,3},{64,76},{1,0},{65,77},{2,1},{66,78},{3,2},{67,79},{4,7},{68,... | collective-permute-start | bytes 1572872 | tf_op jit(solution)/shard_map/ppermute | solution.py:74
  142.5 12.7 %collective-permute-start.27 = (bf16[256,1024]{1,0:T(8,128)(2,1)}, bf16[256,1024]{1,0:T(8,128)(2,1)S(1)}, u32[]{:S(2)}, u32[]{:S(2)}) collective-permute-start(bf16[256,1024]{1,0:T(8,128)(2,1)} %get-tuple-element.101), channel_id=1, source_target_pairs={{0,2},{64,72},{1,3},{65,73},{2,0},{66,74},{3,1},{67,75},{4,6},{68,... | collective-permute-start | bytes 1572872 | tf_op jit(solution)/shard_map/ppermute | solution.py:74
  143.4 15.7 %collective-permute-start.26 = (bf16[256,1024]{1,0:T(8,128)(2,1)}, bf16[256,1024]{1,0:T(8,128)(2,1)S(1)}, u32[]{:S(2)}, u32[]{:S(2)}) collective-permute-start(bf16[256,1024]{1,0:T(8,128)(2,1)} %get-tuple-element.100), channel_id=1, source_target_pairs={{0,1},{64,68},{1,2},{65,69},{2,3},{66,70},{3,0},{67,71},{4,5},{68,... | collective-permute-start | bytes 1572872 | tf_op jit(solution)/shard_map/ppermute | solution.py:74
  150.6 12.0 %copy-start.30 = (bf16[80,1024]{1,0:T(8,128)(2,1)S(1)}, bf16[80,1024]{1,0:T(8,128)(2,1)}, u32[]{:S(2)}) copy-start(bf16[80,1024]{1,0:T(8,128)(2,1)} %get-tuple-element.108) | copy-start | bytes 491524
  150.6 9.7 %collective-permute-start.34 = (bf16[80,1024]{1,0:T(8,128)(2,1)}, bf16[80,1024]{1,0:T(8,128)(2,1)S(1)}, u32[]{:S(2)}, u32[]{:S(2)}) collective-permute-start(bf16[80,1024]{1,0:T(8,128)(2,1)} %get-tuple-element.111), channel_id=1, source_target_pairs={{0,3},{64,76},{1,0},{65,77},{2,1},{66,78},{3,2},{67,79},{4,7},{68,... | collective-permute-start | bytes 491528 | tf_op jit(solution)/shard_map/ppermute | solution.py:74
  153.1 7.8 %collective-permute-start.33 = (bf16[80,1024]{1,0:T(8,128)(2,1)}, bf16[80,1024]{1,0:T(8,128)(2,1)S(1)}, u32[]{:S(2)}, u32[]{:S(2)}) collective-permute-start(bf16[80,1024]{1,0:T(8,128)(2,1)} %get-tuple-element.110), channel_id=1, source_target_pairs={{0,2},{64,72},{1,3},{65,73},{2,0},{66,74},{3,1},{67,75},{4,6},{68,... | collective-permute-start | bytes 491528 | tf_op jit(solution)/shard_map/ppermute | solution.py:74
  155.2 7.4 %collective-permute-start.32 = (bf16[80,1024]{1,0:T(8,128)(2,1)}, bf16[80,1024]{1,0:T(8,128)(2,1)S(1)}, u32[]{:S(2)}, u32[]{:S(2)}) collective-permute-start(bf16[80,1024]{1,0:T(8,128)(2,1)} %get-tuple-element.109), channel_id=1, source_target_pairs={{0,1},{64,68},{1,2},{65,69},{2,3},{66,70},{3,0},{67,71},{4,5},{68,... | collective-permute-start | bytes 491528 | tf_op jit(solution)/shard_map/ppermute | solution.py:74
  (4 other events, 2.9 us)

commit v9 on v8

--- a/solution.py
+++ b/solution.py
@@ -285,7 +285,7 @@
         start = pl.multiple_of(block * size, size)
         return pltpu.make_async_copy(source.at[pl.ds(start, size)], outs[n], sems.at[n])
 
-    for n in range(2 * SIDE):
+    for n in range(len(outs)):
 
         @pl.when(core == n // SIDE)
         def _():
@@ -295,19 +295,19 @@
         def _():
             copy(other, n).start()
 
-    for n in range(2 * SIDE):
+    for n in range(len(outs)):
         copy(own, n).wait()
 
 
-def turn(place, own, other):
+def turn(place, own, other, sections=2, limit=8):
     rows, columns = own.shape
     blocks = pl.pallas_call(
         turn_kernel,
         in_specs=[pl.BlockSpec(memory_space=pltpu.SMEM), ANY, ANY],
-        out_specs=[pl.BlockSpec(memory_space=pltpu.VMEM)] * (2 * SIDE),
-        scratch_shapes=[pltpu.SemaphoreType.DMA((2 * SIDE,))],
-        out_shape=[pltpu.VMEM((rows // SIDE, columns), own.dtype)] * (2 * SIDE),
-        compiler_params=SMALL,
+        out_specs=[pl.BlockSpec(memory_space=pltpu.VMEM)] * (sections * SIDE),
+        scratch_shapes=[pltpu.SemaphoreType.DMA((sections * SIDE,))],
+        out_shape=[pltpu.VMEM((rows // SIDE, columns), own.dtype)] * (sections * SIDE),
+        compiler_params=pltpu.CompilerParams(vmem_limit_bytes=limit * 1024 * 1024),
     )(place, own, other)
     return (blocks[:SIDE], blocks[SIDE:])
 
@@ -538,8 +538,9 @@
 
     blocks0 = [start] + [along_x(start, d) for d in (1, 2, 3)]
     arrived_ups = lax.all_to_all(after(send_ups, start), "dp", 0, 0, tiled=True)
-    hidden, slope = step(
-        forward_body, 0, place, own, other, blocks0, [block, jax.ShapeDtypeStruct(block.shape, F32)]
+    first_weights, _ = turn(place, own, after(other, start), 1, 50)
+    hidden, slope = held_step(
+        forward_body, first_weights, blocks0, [block, jax.ShapeDtypeStruct(block.shape, F32)]
     )
 
     blocks1 = [hidden] + [along_x(hidden, d) for d in (1, 2, 3)]

time: 164 us -> 160 us (0.976)
  starting transfers between devices: 65.1 us -> 58.6 us
  waiting for transfers between devices: 42.5 us -> 46.9 us
    pallas_call x1 -> x0, Pallas kernels: 7.08 us -> none  [step(): pl.pallas_call(functools.partial(step_kernel, body, section, count, len(o...]
    ppermute x12, waiting for transfers between devices: 23.7 us -> 30.5 us  [along_x(): lax.ppermute(block, 'mp', [(i, (i + distance) % SIDE) for i in range(SIDE)])]
    ppermute x12, starting transfers between devices: 18.9 us -> 12.2 us  [along_x(): lax.ppermute(block, 'mp', [(i, (i + distance) % SIDE) for i in range(SIDE)])]
    pallas_call x1 -> x2, Pallas kernels: 4.68 us -> 8.85 us  [turn(): pl.pallas_call(turn_kernel, in_specs=[pl.BlockSpec(memory_space=pltpu.SME...]
    ppermute x6, starting transfers between devices: 7.96 us -> 11.2 us  [along_other(): return lax.ppermute(block, ('segment', 'dp'), pairs)]
    ppermute x12, starting transfers between devices: 24.2 us -> 21 us  [along_mine(): return lax.ppermute(block, ('segment', 'dp'), pairs)]
    ppermute x6, waiting for transfers between devices: 7.32 us -> 4.44 us  [along_other(): return lax.ppermute(block, ('segment', 'dp'), pairs)]
    pallas_call x2 -> x3, Pallas kernels: 7.65 us -> 9.18 us  [held_step(): pl.pallas_call(functools.partial(held_kernel, body, count, len(outs)), in...]
  transfers between devices with their start and end apart: 37 -> 37, of which waited for: 18 -> 15; matrix products, arithmetic and copies ran while one was open for 4% -> 4% of each run, Pallas kernels for 20% -> 19%
where the time goes in v9:
time: 160 us; the launch traced here: 159 us
  starting transfers between devices  58.6 us (37%)
  waiting for transfers between devices  46.9 us (29%)
  Pallas kernels  38.2 us (24%)
  local copies, waits for them, and re-layouts  7.68 us (5%)
  matrix products  4.04 us (3%)
  other arithmetic  2.56 us (2%)
    ppermute x12, waiting for transfers between devices, along_x(): lax.ppermute(block, 'mp', [(i, (i + distance) % SIDE) for i in range(SIDE)])  30.5 us
    ppermute x12, starting transfers between devices, along_mine(): return lax.ppermute(block, ('segment', 'dp'), pairs)  21 us
    ppermute x12, starting transfers between devices, along_x(): lax.ppermute(block, 'mp', [(i, (i + distance) % SIDE) for i in range(SIDE)])  12.2 us
    ppermute x6, starting transfers between devices, along_other(): return lax.ppermute(block, ('segment', 'dp'), pairs)  11.2 us
    pallas_call x3, Pallas kernels, held_step(): pl.pallas_call(functools.partial(held_kernel, body, count, len(outs)), in...  9.18 us
    ppermute x12, waiting for transfers between devices, along_mine(): return lax.ppermute(block, ('segment', 'dp'), pairs)  8.86 us
    pallas_call x2, Pallas kernels, turn(): pl.pallas_call(turn_kernel, in_specs=[pl.BlockSpec(memory_space=pltpu.SME...  8.85 us
    all_to_all x1, starting transfers between devices, on_device(): arrived_text = lax.all_to_all(send_text, 'dp', 0, 0, tiled=True)  8.13 us
  transfers between devices with their start and end apart: 37, of which 15 were waited for; matrix products, arithmetic and copies ran while one was open for 4% of the time, Pallas kernels for 19%

profile of v9, /device:TPU:0, one launch (start us, length us, event | category | flops | bytes accessed | tf_op | source)
XLA Modules:
  0.0 159.0 jit_solution(11102774234018865125)
XLA Ops:
  0.8 0.6 stack.23.place.refs_11_
  1.4 2.1 %shard_map.86 = bf16[16,32,1024]{2,1,0:T(8,128)(2,1)} custom-call(s32[128]{0:T(128)} %routing.7, s32[5]{0:T(128)} %stack.23.place.refs_11_, bf16[8,32,1024]{2,1,0:T(8,128)(2,1)} %bitcast.33), custom_call_target="tpu_custom_call" | custom-call | tf_op jit(solution)/shard_map/pallas_call | solution.py:97
  3.5 8.1 %all-to-all-start = ((bf16[16,32,1024]{2,1,0:T(8,128)(2,1)}), bf16[16,32,1024]{2,1,0:T(8,128)(2,1)S(1)}, u32[]{:S(2)}, u32[]{:S(2)}) async-start(bf16[16,32,1024]{2,1,0:T(8,128)(2,1)} %shard_map.86), calls=%async_computation | async-start | bytes 2097152 | tf_op jit(solution)/shard_map/all_to_all | solution.py:523
  11.7 0.5 fusion.5
  12.8 1.6 collective-permute-done.far
  14.3 0.7 shard_map.87
  15.0 0.7 copy-done.7
  15.7 2.0 %collective-permute-start.1 = (bf16[320,256]{1,0:T(8,128)(2,1)S(1)}, bf16[320,256]{1,0:T(8,128)(2,1)S(1)}, u32[]{:S(2)}, u32[]{:S(2)}) collective-permute-start(bf16[320,256]{1,0:T(8,128)(2,1)S(1)} %get-tuple-element.63), channel_id=1, source_target_pairs={{0,4},{64,65},{1,5},{65,66},{2,6},{66,67},{3,7},{67,64},{4,8},{68,... | collective-permute-start | bytes 491528 | tf_op jit(solution)/shard_map/ppermute | solution.py:64
  17.7 3.6 %collective-permute-start.2 = (bf16[320,256]{1,0:T(8,128)(2,1)S(1)}, bf16[320,256]{1,0:T(8,128)(2,1)S(1)}, u32[]{:S(2)}, u32[]{:S(2)}) collective-permute-start(bf16[320,256]{1,0:T(8,128)(2,1)S(1)} %get-tuple-element.64), channel_id=1, source_target_pairs={{0,8},{64,66},{1,9},{65,67},{2,10},{66,64},{3,11},{67,65},{4,12},{... | collective-permute-start | bytes 491528 | tf_op jit(solution)/shard_map/ppermute | solution.py:64
  21.3 1.0 collective-permute-start.3
  22.3 4.0 %convolution_convert_fusion = bf16[128,1024]{1,0:T(8,128)(2,1)} fusion(bf16[128,2560]{1,0:T(8,128)(2,1)S(1)} %bitcast.31, bf16[2560,1024]{1,0:T(8,128)(2,1)} %param.8), kind=kOutput, calls=%fused_computation.10 | convolution fusion | flops 671219712 | bytes 6160384 | tf_op jit(solution)/shard_map/dot_general | solution.py:28
  26.3 2.1 %shard_map.88 = bf16[16,32,1024]{2,1,0:T(8,128)(2,1)} custom-call(s32[128]{0:T(128)} %routing.7, s32[5]{0:T(128)} %stack.23.place.refs_11_, bf16[8,32,1024]{2,1,0:T(8,128)(2,1)} %bitcast.34), custom_call_target="tpu_custom_call" | custom-call | tf_op jit(solution)/shard_map/pallas_call | solution.py:97
  28.5 2.9 %collective-permute-done.2.refs_2_ = bf16[320,256]{1,0:T(8,128)(2,1)S(1)} collective-permute-done((bf16[320,256]{1,0:T(8,128)(2,1)S(1)}, bf16[320,256]{1,0:T(8,128)(2,1)S(1)}, u32[]{:S(2)}, u32[]{:S(2)}) %collective-permute-start.2) | collective-permute-done | bytes 163872 | tf_op jit(solution)/shard_map/ppermute | solution.py:64
  31.4 1.0 copy-done.12
  32.4 2.7 %shard_map.89 = bf16[4,32,1024]{2,1,0:T(8,128)(2,1)} custom-call(s32[128]{0:T(128)} %routing.7, s32[128]{0:T(128)} %counts.3, s32[5]{0:T(128)} %stack.23.place.refs_11_, bf16[16,32,1024]{2,1,0:T(8,128)(2,1)} %copy-done.12, bf16[4,32,1024]{2,1,0:T(8,128)(2,1)} %bitcast.32), custom_call_target="tpu_custom_call" | custom-call | tf_op jit(solution)/shard_map/pallas_call | solution.py:122
  35.1 5.2 %all-to-all-start.1 = ((bf16[16,32,1024]{2,1,0:T(8,128)(2,1)}), bf16[16,32,1024]{2,1,0:T(8,128)(2,1)S(1)}, u32[]{:S(2)}, u32[]{:S(2)}) async-start(bf16[16,32,1024]{2,1,0:T(8,128)(2,1)} %shard_map.88), calls=%async_computation.1 | async-start | bytes 2097152 | tf_op jit(solution)/shard_map/all_to_all | solution.py:540
  40.3 2.8 %collective-permute-start.7 = (bf16[128,1024]{1,0:T(8,128)(2,1)S(1)}, bf16[128,1024]{1,0:T(8,128)(2,1)S(1)}, u32[]{:S(2)}, u32[]{:S(2)}) collective-permute-start(bf16[128,1024]{1,0:T(8,128)(2,1)S(1)} %bitcast.23), channel_id=1, source_target_pairs={{0,48},{16,0},{32,16},{48,32},{1,49},{17,1},{33,17},{49,33},{2,50}... | collective-permute-start | bytes 786440 | tf_op jit(solution)/shard_map/ppermute | solution.py:40
  43.2 0.8 collective-permute-start.6
  44.0 0.9 collective-permute-start.5
  44.9 4.2 %shard_map.92 = (bf16[1024,1024]{1,0:T(8,128)(2,1)S(1)}, bf16[1024,1024]{1,0:T(8,128)(2,1)S(1)}, bf16[1024,1024]{1,0:T(8,128)(2,1)S(1)}, bf16[1024,1024]{1,0:T(8,128)(2,1)S(1)}) custom-call(s32[5]{0:T(128)} %stack.23.place.refs_11_, bf16[4096,1024]{1,0:T(8,128)(2,1)} %bitcast.20, bf16[4096,1024]{1,0:T(8,128)(2,1)} %collective-permute-done.4.other), custom_call_target="tpu_custom_call" | custom-call | tf_op jit(solution)/shard_map/pallas_call | solution.py:304
  49.0 5.4 %collective-permute-done.7.refs_7_.refs_3_ = bf16[128,1024]{1,0:T(8,128)(2,1)S(1)} collective-permute-done((bf16[128,1024]{1,0:T(8,128)(2,1)S(1)}, bf16[128,1024]{1,0:T(8,128)(2,1)S(1)}, u32[]{:S(2)}, u32[]{:S(2)}) %collective-permute-start.7) | collective-permute-done | bytes 262176 | tf_op jit(solution)/shard_map/ppermute | solution.py:40
  54.4 3.7 %collective-permute-done.5.refs_5_.refs_1_ = bf16[128,1024]{1,0:T(8,128)(2,1)S(1)} collective-permute-done((bf16[128,1024]{1,0:T(8,128)(2,1)S(1)}, bf16[128,1024]{1,0:T(8,128)(2,1)S(1)}, u32[]{:S(2)}, u32[]{:S(2)}) %collective-permute-start.5) | collective-permute-done | bytes 262176 | tf_op jit(solution)/shard_map/ppermute | solution.py:40
  58.1 1.5 shard_map.93
  59.7 0.8 copy-done.5
  60.5 0.6 collective-permute-start.10
  61.1 0.8 collective-permute-start.9
  61.9 0.8 collective-permute-start.8
  62.7 0.9 shard_map.90
  63.7 3.4 %copy-done = bf16[1,4096,1024]{2,1,0:T(8,128)(2,1)S(1)} copy-done((bf16[1,4096,1024]{2,1,0:T(8,128)(2,1)S(1)}, bf16[1,4096,1024]{2,1,0:T(8,128)(2,1)}, u32[]{:S(2)}) %copy-start) | copy-done | bytes 8388632
  67.0 4.7 %shard_map.91 = (bf16[1024,1024]{1,0:T(8,128)(2,1)S(1)}, bf16[1024,1024]{1,0:T(8,128)(2,1)S(1)}, bf16[1024,1024]{1,0:T(8,128)(2,1)S(1)}, bf16[1024,1024]{1,0:T(8...) custom-call(s32[5]{0:T(128)S(1)} %copy-done.9, ...), custom_call_target="tpu_custom_call" | custom-call | tf_op jit(solution)/shard_map/pallas_call | solution.py:304
  71.9 3.9 %collective-permute-done.8.refs_5_ = bf16[128,1024]{1,0:T(8,128)(2,1)S(1)} collective-permute-done((bf16[128,1024]{1,0:T(8,128)(2,1)S(1)}, bf16[128,1024]{1,0:T(8,128)(2,1)S(1)}, u32[]{:S(2)}, u32[]{:S(2)}) %collective-permute-start.8) | collective-permute-done | bytes 262176 | tf_op jit(solution)/shard_map/ppermute | solution.py:40
  75.8 4.2 %shard_map.94 = (bf16[128,1024]{1,0:T(8,128)(2,1)S(1)}, bf16[128,1024]{1,0:T(8,128)(2,1)S(1)}, bf16[128,1024]{1,0:T(8,128)(2,1)S(1)}, bf16[128,1024]{1,0:T(8,128)(2,1)S(1)}, bf16[128,1024]{1,0:T(8,128)(2,1)S(1)}) custom-call(bf16[1024,1024]{1,0:T(8,128)(2,1)S(1)} %get-tuple-element.72.refs_0_, bf16[1024,1024]{1,0:T(8,128)(2,1)S(1)} %get-tuple-element.73.refs_1_, ...), custom_call_target="tpu_custom_call" | custom-call | tf_op jit(solution)/shard_map/pallas_call | solution.py:326
  80.1 0.8 shard_map.95
  81.2 2.6 %collective-permute-start.13 = (bf16[128,1024]{1,0:T(8,128)(2,1)S(1)}, bf16[128,1024]{1,0:T(8,128)(2,1)S(1)}, u32[]{:S(2)}, u32[]{:S(2)}) collective-permute-start(bf16[128,1024]{1,0:T(8,128)(2,1)S(1)} %get-tuple-element.93), channel_id=1, source_target_pairs={{0,32},{16,48},{32,0},{48,16},{1,33},{17,49},{33,1},{49,17},{2,34}... | collective-permute-start | bytes 786440 | tf_op jit(solution)/shard_map/ppermute | solution.py:40
  83.8 0.8 collective-permute-start.14
  84.8 0.8 copy-done.4
  85.6 1.6 %collective-permute-start.18 = (bf16[256,1024]{1,0:T(8,128)(2,1)S(1)}, bf16[256,1024]{1,0:T(8,128)(2,1)S(1)}, u32[]{:S(2)}, u32[]{:S(2)}) collective-permute-start(bf16[256,1024]{1,0:T(8,128)(2,1)S(1)} %get-tuple-element.102), channel_id=1, source_target_pairs={{0,4},{64,65},{1,5},{65,66},{2,6},{66,67},{3,7},{67,64},{4,8},{68,... | collective-permute-start | bytes 1572872 | tf_op jit(solution)/shard_map/ppermute | solution.py:64
  87.2 2.7 %collective-permute-start.19 = (bf16[256,1024]{1,0:T(8,128)(2,1)S(1)}, bf16[256,1024]{1,0:T(8,128)(2,1)S(1)}, u32[]{:S(2)}, u32[]{:S(2)}) collective-permute-start(bf16[256,1024]{1,0:T(8,128)(2,1)S(1)} %get-tuple-element.103), channel_id=1, source_target_pairs={{0,8},{64,66},{1,9},{65,67},{2,10},{66,64},{3,11},{67,65},{4,12},{... | collective-permute-start | bytes 1572872 | tf_op jit(solution)/shard_map/ppermute | solution.py:64
  89.9 6.8 %collective-permute-done.12.refs_5_ = bf16[128,1024]{1,0:T(8,128)(2,1)S(1)} collective-permute-done((bf16[128,1024]{1,0:T(8,128)(2,1)S(1)}, bf16[128,1024]{1,0:T(8,128)(2,1)S(1)}, u32[]{:S(2)}, u32[]{:S(2)}) %collective-permute-start.12) | collective-permute-done | bytes 262176 | tf_op jit(solution)/shard_map/ppermute | solution.py:40
  96.7 2.9 %collective-permute-start.20 = (bf16[256,1024]{1,0:T(8,128)(2,1)S(1)}, bf16[256,1024]{1,0:T(8,128)(2,1)S(1)}, u32[]{:S(2)}, u32[]{:S(2)}) collective-permute-start(bf16[256,1024]{1,0:T(8,128)(2,1)S(1)} %get-tuple-element.104), channel_id=1, source_target_pairs={{0,12},{64,67},{1,13},{65,64},{2,14},{66,65},{3,15},{67,66},{4,0},... | collective-permute-start | bytes 1572872 | tf_op jit(solution)/shard_map/ppermute | solution.py:64
  99.6 3.4 %shard_map.97 = (bf16[128,1024]{1,0:T(8,128)(2,1)S(1)}, bf16[128,1024]{1,0:T(8,128)(2,1)S(1)}, bf16[128,1024]{1,0:T(8,128)(2,1)S(1)}, bf16[128,1024]{1,0:T(8,128...) custom-call(bf16[1024,1024]{1,0:T(8,128)(2,1)S(1)} %get-tuple-element.87.ref, ...), custom_call_target="tpu_custom_call" | custom-call | tf_op jit(solution)/shard_map/pallas_call | solution.py:326
  103.2 1.4 collective-permute-done.21.far
  104.7 1.8 %collective-permute-start.17 = (bf16[128,1024]{1,0:T(8,128)(2,1)S(1)}, bf16[128,1024]{1,0:T(8,128)(2,1)S(1)}, u32[]{:S(2)}, u32[]{:S(2)}) collective-permute-start(bf16[128,1024]{1,0:T(8,128)(2,1)S(1)} %get-tuple-element.100), channel_id=1, source_target_pairs={{0,48},{16,0},{32,16},{48,32},{1,49},{17,1},{33,17},{49,33},{2,50}... | collective-permute-start | bytes 786440 | tf_op jit(solution)/shard_map/ppermute | solution.py:40
  106.6 2.0 %collective-permute-start.25 = (bf16[256,1024]{1,0:T(8,128)(2,1)S(1)}, bf16[256,1024]{1,0:T(8,128)(2,1)S(1)}, u32[]{:S(2)}, u32[]{:S(2)}) collective-permute-start(bf16[256,1024]{1,0:T(8,128)(2,1)S(1)} %shard_map.98.refs_4_), channel_id=1, source_target_pairs={{0,12},{64,67},{1,13},{65,64},{2,14},{66,65},{3,15},{67,66},{4,0},... | collective-permute-start | bytes 1572872 | tf_op jit(solution)/shard_map/ppermute | solution.py:64
  108.7 10.0 %collective-permute-done.15.r1 = bf16[128,1024]{1,0:T(8,128)(2,1)S(1)} collective-permute-done((bf16[128,1024]{1,0:T(8,128)(2,1)S(1)}, bf16[128,1024]{1,0:T(8,128)(2,1)S(1)}, u32[]{:S(2)}, u32[]{:S(2)}) %collective-permute-start.15) | collective-permute-done | bytes 262176 | tf_op jit(solution)/shard_map/ppermute | solution.py:40
  118.6 0.6 collective-permute-done.17.r3
  119.3 0.7 shard_map.99.keep
  120.1 2.0 %collective-permute-start.24 = (bf16[256,1024]{1,0:T(8,128)(2,1)S(1)}, bf16[256,1024]{1,0:T(8,128)(2,1)}, u32[]{:S(2)}, u32[]{:S(2)}) collective-permute-start(bf16[256,1024]{1,0:T(8,128)(2,1)S(1)} %shard_map.98.refs_4_), channel_id=1, source_target_pairs={{0,8},{64,66},{1,9},{65,67},{2,10},{66,64},{3,11},{67,65},{4,12},{... | collective-permute-start | bytes 1572872 | tf_op jit(solution)/shard_map/ppermute | solution.py:64
  122.2 1.2 collective-permute-start.31
  123.4 1.5 collective-permute-start.30
  124.9 0.4 collective-permute-start.29
  125.3 5.8 %collective-permute-done.24.refs_6_ = bf16[256,1024]{1,0:T(8,128)(2,1)} collective-permute-done((bf16[256,1024]{1,0:T(8,128)(2,1)S(1)}, bf16[256,1024]{1,0:T(8,128)(2,1)}, u32[]{:S(2)}, u32[]{:S(2)}) %collective-permute-start.24) | collective-permute-done | bytes 524320 | tf_op jit(solution)/shard_map/ppermute | solution.py:64
  131.1 6.3 %shard_map.101 = (bf16[256,1024]{1,0:T(8,128)(2,1)}, bf16[256,1024]{1,0:T(8,128)(2,1)}, bf16[256,1024]{1,0:T(8,128)(2,1)}, bf16[256,1024]{1,0:T(8,128)(2,1)}) custom-call(s32[5]{0:T(128)} %stack.23.place.refs_11_, bf16[256,1024]{1,0:T(8,128)(2,1)} %copy-done.4, bf16[256,1024]{1,0:T(8,128)(2,1)} %copy-done.14, bf16[256,1024]{1,0:T(8,128)(2,1)} %copy-done.15, ...), custom_call_target="tpu_custom_call" | custom-call | tf_op jit(solution)/shard_map/pallas_call | solution.py:364
  137.4 1.5 collective-permute-start.26
  139.0 2.7 %collective-permute-start.27 = (bf16[256,1024]{1,0:T(8,128)(2,1)}, bf16[256,1024]{1,0:T(8,128)(2,1)S(1)}, u32[]{:S(2)}, u32[]{:S(2)}) collective-permute-start(bf16[256,1024]{1,0:T(8,128)(2,1)} %get-tuple-element.111), channel_id=1, source_target_pairs={{0,2},{64,72},{1,3},{65,73},{2,0},{66,74},{3,1},{67,75},{4,6},{68,... | collective-permute-start | bytes 1572872 | tf_op jit(solution)/shard_map/ppermute | solution.py:74
  141.6 1.5 collective-permute-start.28
  143.3 3.6 %shard_map.102 = (bf16[80,1024]{1,0:T(8,128)(2,1)}, bf16[80,1024]{1,0:T(8,128)(2,1)}, bf16[80,1024]{1,0:T(8,128)(2,1)}, bf16[80,1024]{1,0:T(8,128)(2,1)}) custom-call(s32[5]{0:T(128)} %stack.23.place.refs_11_, bf16[320,256]{1,0:T(8,128)(2,1)} %copy-done.7, bf16[320,256]{1,0:T(8,128)(2,1)} %copy-done.20, bf16[320,256]{1,0:T(8,128)(2,1)} %copy-done.21, ...), custom_call_target="tpu_custom_call" | custom-call | tf_op jit(solution)/shard_map/pallas_call | solution.py:426
  146.9 1.4 collective-permute-start.32
  148.3 2.7 %collective-permute-start.33 = (bf16[80,1024]{1,0:T(8,128)(2,1)}, bf16[80,1024]{1,0:T(8,128)(2,1)S(1)}, u32[]{:S(2)}, u32[]{:S(2)}) collective-permute-start(bf16[80,1024]{1,0:T(8,128)(2,1)} %get-tuple-element.120), channel_id=1, source_target_pairs={{0,2},{64,72},{1,3},{65,73},{2,0},{66,74},{3,1},{67,75},{4,6},{68,... | collective-permute-start | bytes 491528 | tf_op jit(solution)/shard_map/ppermute | solution.py:74
  150.9 1.5 collective-permute-start.34
  152.4 2.3 %collective-permute-done.27 = bf16[256,1024]{1,0:T(8,128)(2,1)S(1)} collective-permute-done((bf16[256,1024]{1,0:T(8,128)(2,1)}, bf16[256,1024]{1,0:T(8,128)(2,1)S(1)}, u32[]{:S(2)}, u32[]{:S(2)}) %collective-permute-start.27) | collective-permute-done | bytes 524320 | tf_op jit(solution)/shard_map/ppermute | solution.py:74
  154.7 1.3 add_bitcast_fusion
  156.4 1.8 %collective-permute-done.33 = bf16[80,1024]{1,0:T(8,128)(2,1)S(1)} collective-permute-done((bf16[80,1024]{1,0:T(8,128)(2,1)}, bf16[80,1024]{1,0:T(8,128)(2,1)S(1)}, u32[]{:S(2)}, u32[]{:S(2)}) %collective-permute-start.33) | collective-permute-done | bytes 163872 | tf_op jit(solution)/shard_map/ppermute | solution.py:74
  158.2 0.8 convert_add_fusion.1
  (82 shorter events, 2.5 us)
Async XLA Ops:
  0.6 11.0 %copy-start.13 = (bf16[4,32,2560]{2,1,0:T(8,128)(2,1)S(1)}, bf16[4,32,2560]{2,1,0:T(8,128)(2,1)}, u32[]{:S(2)}) copy-start(bf16[4,32,2560]{2,1,0:T(8,128)(2,1)} %param.7) | copy-start | bytes 1966084
  0.6 30.7 %collective-permute-start.4 = (bf16[4096,1024]{1,0:T(8,128)(2,1)}, bf16[4096,1024]{1,0:T(8,128)(2,1)}, u32[]{:S(2)}, u32[]{:S(2)}) collective-permute-start(bf16[4096,1024]{1,0:T(8,128)(2,1)} %bitcast.19), channel_id=1, source_target_pairs={{0,64},{64,0},{1,65},{65,1},{2,66},{66,2},{3,67},{67,3},{4,68},{68... | collective-permute-start | bytes 25165832 | tf_op jit(solution)/shard_map/ppermute | solution.py:78
  3.5 27.8 %all-to-all-start = ((bf16[16,32,1024]{2,1,0:T(8,128)(2,1)}), bf16[16,32,1024]{2,1,0:T(8,128)(2,1)S(1)}, u32[]{:S(2)}, u32[]{:S(2)}) async-start(bf16[16,32,1024]{2,1,0:T(8,128)(2,1)} %shard_map.86), calls=%async_computation | async-start | bytes 2097152 | tf_op jit(solution)/shard_map/all_to_all | solution.py:523
  11.7 2.7 %copy-start.8 = (s32[5]{0:T(128)S(1)}, s32[5]{0:T(128)}, u32[]{:S(2)}) copy-start(s32[5]{0:T(128)} %stack.23.place.refs_11_) | copy-start | bytes 64
  12.5 1.8 %collective-permute-start = (bf16[1280,128]{1,0:T(8,128)(2,1)S(1)}, bf16[1280,128]{1,0:T(8,128)(2,1)S(1)}, u32[]{:S(2)}, u32[]{:S(2)}) collective-permute-start(bf16[1280,128]{1,0:T(8,128)(2,1)S(1)} %dynamic-slice_bitcast_fusion), channel_id=1, source_target_pairs={{0,64},{64,0},{1,65},{65,1},{2,66},{66,2},{3,67},{67,3},{4,68},{68... | collective-permute-start | bytes 983048 | tf_op jit(solution)/shard_map/ppermute | solution.py:78
  15.0 0.7 copy-start.7
  15.7 12.8 %collective-permute-start.1 = (bf16[320,256]{1,0:T(8,128)(2,1)S(1)}, bf16[320,256]{1,0:T(8,128)(2,1)S(1)}, u32[]{:S(2)}, u32[]{:S(2)}) collective-permute-start(bf16[320,256]{1,0:T(8,128)(2,1)S(1)} %get-tuple-element.63), channel_id=1, source_target_pairs={{0,4},{64,65},{1,5},{65,66},{2,6},{66,67},{3,7},{67,64},{4,8},{68,... | collective-permute-start | bytes 491528 | tf_op jit(solution)/shard_map/ppermute | solution.py:64
  17.7 13.6 %collective-permute-start.2 = (bf16[320,256]{1,0:T(8,128)(2,1)S(1)}, bf16[320,256]{1,0:T(8,128)(2,1)S(1)}, u32[]{:S(2)}, u32[]{:S(2)}) collective-permute-start(bf16[320,256]{1,0:T(8,128)(2,1)S(1)} %get-tuple-element.64), channel_id=1, source_target_pairs={{0,8},{64,66},{1,9},{65,67},{2,10},{66,64},{3,11},{67,65},{4,12},{... | collective-permute-start | bytes 491528 | tf_op jit(solution)/shard_map/ppermute | solution.py:64
  21.3 10.1 %collective-permute-start.3 = (bf16[320,256]{1,0:T(8,128)(2,1)S(1)}, bf16[320,256]{1,0:T(8,128)(2,1)S(1)}, u32[]{:S(2)}, u32[]{:S(2)}) collective-permute-start(bf16[320,256]{1,0:T(8,128)(2,1)S(1)} %get-tuple-element.65), channel_id=1, source_target_pairs={{0,12},{64,67},{1,13},{65,64},{2,14},{66,65},{3,15},{67,66},{4,0},... | collective-permute-start | bytes 491528 | tf_op jit(solution)/shard_map/ppermute | solution.py:64
  28.5 6.6 %copy-start.20 = (bf16[320,256]{1,0:T(8,128)(2,1)}, bf16[320,256]{1,0:T(8,128)(2,1)S(1)}, u32[]{:S(2)}) copy-start(bf16[320,256]{1,0:T(8,128)(2,1)S(1)} %collective-permute-done.1.refs_1_) | copy-start | bytes 491524
  31.4 3.7 %copy-start.21 = (bf16[320,256]{1,0:T(8,128)(2,1)}, bf16[320,256]{1,0:T(8,128)(2,1)S(1)}, u32[]{:S(2)}) copy-start(bf16[320,256]{1,0:T(8,128)(2,1)S(1)} %collective-permute-done.2.refs_2_) | copy-start | bytes 491524
  31.4 3.7 %copy-start.22 = (bf16[320,256]{1,0:T(8,128)(2,1)}, bf16[320,256]{1,0:T(8,128)(2,1)S(1)}, u32[]{:S(2)}) copy-start(bf16[320,256]{1,0:T(8,128)(2,1)S(1)} %collective-permute-done.3.refs_3_) | copy-start | bytes 491524
  31.4 1.0 copy-start.12
  35.0 5.3 %copy-start.1 = (bf16[4,32,1024]{2,1,0:T(8,128)(2,1)S(1)}, bf16[4,32,1024]{2,1,0:T(8,128)(2,1)}, u32[]{:S(2)}) copy-start(bf16[4,32,1024]{2,1,0:T(8,128)(2,1)} %shard_map.89) | copy-start | bytes 786436
  35.1 27.6 %all-to-all-start.1 = ((bf16[16,32,1024]{2,1,0:T(8,128)(2,1)}), bf16[16,32,1024]{2,1,0:T(8,128)(2,1)S(1)}, u32[]{:S(2)}, u32[]{:S(2)}) async-start(bf16[16,32,1024]{2,1,0:T(8,128)(2,1)} %shard_map.88), calls=%async_computation.1 | async-start | bytes 2097152 | tf_op jit(solution)/shard_map/all_to_all | solution.py:540
  40.3 14.1 %collective-permute-start.7 = (bf16[128,1024]{1,0:T(8,128)(2,1)S(1)}, bf16[128,1024]{1,0:T(8,128)(2,1)S(1)}, u32[]{:S(2)}, u32[]{:S(2)}) collective-permute-start(bf16[128,1024]{1,0:T(8,128)(2,1)S(1)} %bitcast.23), channel_id=1, source_target_pairs={{0,48},{16,0},{32,16},{48,32},{1,49},{17,1},{33,17},{49,33},{2,50}... | collective-permute-start | bytes 786440 | tf_op jit(solution)/shard_map/ppermute | solution.py:40
  43.2 11.3 %collective-permute-start.6 = (bf16[128,1024]{1,0:T(8,128)(2,1)S(1)}, bf16[128,1024]{1,0:T(8,128)(2,1)S(1)}, u32[]{:S(2)}, u32[]{:S(2)}) collective-permute-start(bf16[128,1024]{1,0:T(8,128)(2,1)S(1)} %bitcast.24), channel_id=1, source_target_pairs={{0,32},{16,48},{32,0},{48,16},{1,33},{17,49},{33,1},{49,17},{2,34}... | collective-permute-start | bytes 786440 | tf_op jit(solution)/shard_map/ppermute | solution.py:40
  44.0 14.1 %collective-permute-start.5 = (bf16[128,1024]{1,0:T(8,128)(2,1)S(1)}, bf16[128,1024]{1,0:T(8,128)(2,1)S(1)}, u32[]{:S(2)}, u32[]{:S(2)}) collective-permute-start(bf16[128,1024]{1,0:T(8,128)(2,1)S(1)} %bitcast.25), channel_id=1, source_target_pairs={{0,16},{16,32},{32,48},{48,0},{1,17},{17,33},{33,49},{49,1},{2,18}... | collective-permute-start | bytes 786440 | tf_op jit(solution)/shard_map/ppermute | solution.py:40
  58.1 4.6 %copy-start.9 = (s32[5]{0:T(128)S(1)}, s32[5]{0:T(128)}, u32[]{:S(2)}) copy-start(s32[5]{0:T(128)} %stack.23.place.refs_11_) | copy-start | bytes 64
  58.1 4.6 %copy-start.10 = (s32[128]{0:T(128)S(1)}, s32[128]{0:T(128)}, u32[]{:S(2)}) copy-start(s32[128]{0:T(128)} %routing.7) | copy-start | bytes 1540
  59.6 0.8 copy-start.5
  60.5 11.3 %collective-permute-start.10 = (bf16[128,1024]{1,0:T(8,128)(2,1)S(1)}, bf16[128,1024]{1,0:T(8,128)(2,1)S(1)}, u32[]{:S(2)}, u32[]{:S(2)}) collective-permute-start(bf16[128,1024]{1,0:T(8,128)(2,1)S(1)} %get-tuple-element.81.refs_4_), channel_id=1, source_target_pairs={{0,48},{16,0},{32,16},{48,32},{1,49},{17,1},{33,17},{49,33},{2,50}... | collective-permute-start | bytes 786440 | tf_op jit(solution)/shard_map/ppermute | solution.py:40
  61.1 10.8 %collective-permute-start.9 = (bf16[128,1024]{1,0:T(8,128)(2,1)S(1)}, bf16[128,1024]{1,0:T(8,128)(2,1)S(1)}, u32[]{:S(2)}, u32[]{:S(2)}) collective-permute-start(bf16[128,1024]{1,0:T(8,128)(2,1)S(1)} %get-tuple-element.81.refs_4_), channel_id=1, source_target_pairs={{0,32},{16,48},{32,0},{48,16},{1,33},{17,49},{33,1},{49,17},{2,34}... | collective-permute-start | bytes 786440 | tf_op jit(solution)/shard_map/ppermute | solution.py:40
  61.9 13.9 %collective-permute-start.8 = (bf16[128,1024]{1,0:T(8,128)(2,1)S(1)}, bf16[128,1024]{1,0:T(8,128)(2,1)S(1)}, u32[]{:S(2)}, u32[]{:S(2)}) collective-permute-start(bf16[128,1024]{1,0:T(8,128)(2,1)S(1)} %get-tuple-element.81.refs_4_), channel_id=1, source_target_pairs={{0,16},{16,32},{32,48},{48,0},{1,17},{17,33},{33,49},{49,1},{2,18}... | collective-permute-start | bytes 786440 | tf_op jit(solution)/shard_map/ppermute | solution.py:40
  63.7 3.4 %copy-start = (bf16[1,4096,1024]{2,1,0:T(8,128)(2,1)S(1)}, bf16[1,4096,1024]{2,1,0:T(8,128)(2,1)}, u32[]{:S(2)}) copy-start(bf16[1,4096,1024]{2,1,0:T(8,128)(2,1)} %param.12) | copy-start | bytes 25165828
  80.1 19.5 %copy-start.6 = (f32[128,1024]{1,0:T(8,128)S(1)}, f32[128,1024]{1,0:T(8,128)}, u32[]{:S(2)}) copy-start(f32[128,1024]{1,0:T(8,128)} %copy-done.5) | copy-start | bytes 1572868
  80.9 3.8 %collective-permute-start.11 = (bf16[4,128,1024]{2,1,0:T(8,128)(2,1)S(1)}, bf16[4,128,1024]{2,1,0:T(8,128)(2,1)S(1)}, u32[]{:S(2)}, u32[]{:S(2)}) collective-permute-start(bf16[4,128,1024]{2,1,0:T(8,128)(2,1)S(1)} %get-tuple-element.85), channel_id=1, source_target_pairs={{0,64},{64,0},{1,65},{65,1},{2,66},{66,2},{3,67},{67,3},{4,68},{68... | collective-permute-start | bytes 3145736 | tf_op jit(solution)/shard_map/ppermute | solution.py:78
  81.1 15.5 %collective-permute-start.12 = (bf16[128,1024]{1,0:T(8,128)(2,1)S(1)}, bf16[128,1024]{1,0:T(8,128)(2,1)S(1)}, u32[]{:S(2)}, u32[]{:S(2)}) collective-permute-start(bf16[128,1024]{1,0:T(8,128)(2,1)S(1)} %get-tuple-element.92), channel_id=1, source_target_pairs={{0,16},{16,32},{32,48},{48,0},{1,17},{17,33},{33,49},{49,1},{2,18}... | collective-permute-start | bytes 786440 | tf_op jit(solution)/shard_map/ppermute | solution.py:40
  81.2 18.3 %collective-permute-start.13 = (bf16[128,1024]{1,0:T(8,128)(2,1)S(1)}, bf16[128,1024]{1,0:T(8,128)(2,1)S(1)}, u32[]{:S(2)}, u32[]{:S(2)}) collective-permute-start(bf16[128,1024]{1,0:T(8,128)(2,1)S(1)} %get-tuple-element.93), channel_id=1, source_target_pairs={{0,32},{16,48},{32,0},{48,16},{1,33},{17,49},{33,1},{49,17},{2,34}... | collective-permute-start | bytes 786440 | tf_op jit(solution)/shard_map/ppermute | solution.py:40
  83.8 15.7 %collective-permute-start.14 = (bf16[128,1024]{1,0:T(8,128)(2,1)S(1)}, bf16[128,1024]{1,0:T(8,128)(2,1)S(1)}, u32[]{:S(2)}, u32[]{:S(2)}) collective-permute-start(bf16[128,1024]{1,0:T(8,128)(2,1)S(1)} %get-tuple-element.94), channel_id=1, source_target_pairs={{0,48},{16,0},{32,16},{48,32},{1,49},{17,1},{33,17},{49,33},{2,50}... | collective-permute-start | bytes 786440 | tf_op jit(solution)/shard_map/ppermute | solution.py:40
  84.8 0.8 copy-start.4
  85.6 19.1 %collective-permute-start.18 = (bf16[256,1024]{1,0:T(8,128)(2,1)S(1)}, bf16[256,1024]{1,0:T(8,128)(2,1)S(1)}, u32[]{:S(2)}, u32[]{:S(2)}) collective-permute-start(bf16[256,1024]{1,0:T(8,128)(2,1)S(1)} %get-tuple-element.102), channel_id=1, source_target_pairs={{0,4},{64,65},{1,5},{65,66},{2,6},{66,67},{3,7},{67,64},{4,8},{68,... | collective-permute-start | bytes 1572872 | tf_op jit(solution)/shard_map/ppermute | solution.py:64
  87.2 19.3 %collective-permute-start.19 = (bf16[256,1024]{1,0:T(8,128)(2,1)S(1)}, bf16[256,1024]{1,0:T(8,128)(2,1)S(1)}, u32[]{:S(2)}, u32[]{:S(2)}) collective-permute-start(bf16[256,1024]{1,0:T(8,128)(2,1)S(1)} %get-tuple-element.103), channel_id=1, source_target_pairs={{0,8},{64,66},{1,9},{65,67},{2,10},{66,64},{3,11},{67,65},{4,12},{... | collective-permute-start | bytes 1572872 | tf_op jit(solution)/shard_map/ppermute | solution.py:64
  96.7 11.9 %collective-permute-start.20 = (bf16[256,1024]{1,0:T(8,128)(2,1)S(1)}, bf16[256,1024]{1,0:T(8,128)(2,1)S(1)}, u32[]{:S(2)}, u32[]{:S(2)}) collective-permute-start(bf16[256,1024]{1,0:T(8,128)(2,1)S(1)} %get-tuple-element.104), channel_id=1, source_target_pairs={{0,12},{64,67},{1,13},{65,64},{2,14},{66,65},{3,15},{67,66},{4,0},... | collective-permute-start | bytes 1572872 | tf_op jit(solution)/shard_map/ppermute | solution.py:64
  99.6 19.7 %copy-start.11 = (s32[128]{0:T(128)S(1)}, s32[128]{0:T(128)}, u32[]{:S(2)}) copy-start(s32[128]{0:T(128)} %counts.3) | copy-start | bytes 1540
  103.0 1.6 %collective-permute-start.21 = (bf16[128,1024]{1,0:T(8,128)(2,1)S(1)}, bf16[128,1024]{1,0:T(8,128)(2,1)S(1)}, u32[]{:S(2)}, u32[]{:S(2)}) collective-permute-start(bf16[128,1024]{1,0:T(8,128)(2,1)S(1)} %get-tuple-element.106), channel_id=1, source_target_pairs={{0,64},{64,0},{1,65},{65,1},{2,66},{66,2},{3,67},{67,3},{4,68},{68... | collective-permute-start | bytes 786440 | tf_op jit(solution)/shard_map/ppermute | solution.py:78
  103.1 15.6 %collective-permute-start.15 = (bf16[128,1024]{1,0:T(8,128)(2,1)S(1)}, bf16[128,1024]{1,0:T(8,128)(2,1)S(1)}, u32[]{:S(2)}, u32[]{:S(2)}) collective-permute-start(bf16[128,1024]{1,0:T(8,128)(2,1)S(1)} %get-tuple-element.98), channel_id=1, source_target_pairs={{0,16},{16,32},{32,48},{48,0},{1,17},{17,33},{33,49},{49,1},{2,18}... | collective-permute-start | bytes 786440 | tf_op jit(solution)/shard_map/ppermute | solution.py:40
  104.6 14.0 %collective-permute-start.16 = (bf16[128,1024]{1,0:T(8,128)(2,1)S(1)}, bf16[128,1024]{1,0:T(8,128)(2,1)S(1)}, u32[]{:S(2)}, u32[]{:S(2)}) collective-permute-start(bf16[128,1024]{1,0:T(8,128)(2,1)S(1)} %get-tuple-element.99), channel_id=1, source_target_pairs={{0,32},{16,48},{32,0},{48,16},{1,33},{17,49},{33,1},{49,17},{2,34}... | collective-permute-start | bytes 786440 | tf_op jit(solution)/shard_map/ppermute | solution.py:40
  104.7 26.4 %copy-start.14 = (bf16[256,1024]{1,0:T(8,128)(2,1)}, bf16[256,1024]{1,0:T(8,128)(2,1)S(1)}, u32[]{:S(2)}) copy-start(bf16[256,1024]{1,0:T(8,128)(2,1)S(1)} %collective-permute-done.18.refs_1_) | copy-start | bytes 1572868
  104.7 14.6 %collective-permute-start.17 = (bf16[128,1024]{1,0:T(8,128)(2,1)S(1)}, bf16[128,1024]{1,0:T(8,128)(2,1)S(1)}, u32[]{:S(2)}, u32[]{:S(2)}) collective-permute-start(bf16[128,1024]{1,0:T(8,128)(2,1)S(1)} %get-tuple-element.100), channel_id=1, source_target_pairs={{0,48},{16,0},{32,16},{48,32},{1,49},{17,1},{33,17},{49,33},{2,50}... | collective-permute-start | bytes 786440 | tf_op jit(solution)/shard_map/ppermute | solution.py:40
  106.5 24.6 %copy-start.2 = (bf16[256,1024]{1,0:T(8,128)(2,1)}, bf16[256,1024]{1,0:T(8,128)(2,1)S(1)}, u32[]{:S(2)}) copy-start(bf16[256,1024]{1,0:T(8,128)(2,1)S(1)} %shard_map.98.refs_4_) | copy-start | bytes 1572868
  106.6 24.5 %copy-start.15 = (bf16[256,1024]{1,0:T(8,128)(2,1)}, bf16[256,1024]{1,0:T(8,128)(2,1)S(1)}, u32[]{:S(2)}) copy-start(bf16[256,1024]{1,0:T(8,128)(2,1)S(1)} %collective-permute-done.19.refs_2_) | copy-start | bytes 1572868
  106.6 15.6 %collective-permute-start.25 = (bf16[256,1024]{1,0:T(8,128)(2,1)S(1)}, bf16[256,1024]{1,0:T(8,128)(2,1)S(1)}, u32[]{:S(2)}, u32[]{:S(2)}) collective-permute-start(bf16[256,1024]{1,0:T(8,128)(2,1)S(1)} %shard_map.98.refs_4_), channel_id=1, source_target_pairs={{0,12},{64,67},{1,13},{65,64},{2,14},{66,65},{3,15},{67,66},{4,0},... | collective-permute-start | bytes 1572872 | tf_op jit(solution)/shard_map/ppermute | solution.py:64
  108.6 22.5 %copy-start.16 = (bf16[256,1024]{1,0:T(8,128)(2,1)}, bf16[256,1024]{1,0:T(8,128)(2,1)S(1)}, u32[]{:S(2)}) copy-start(bf16[256,1024]{1,0:T(8,128)(2,1)S(1)} %collective-permute-done.20.refs_3_) | copy-start | bytes 1572868
  108.6 13.6 %collective-permute-start.23 = (bf16[256,1024]{1,0:T(8,128)(2,1)S(1)}, bf16[256,1024]{1,0:T(8,128)(2,1)S(1)}, u32[]{:S(2)}, u32[]{:S(2)}) collective-permute-start(bf16[256,1024]{1,0:T(8,128)(2,1)S(1)} %shard_map.98.refs_4_), channel_id=1, source_target_pairs={{0,4},{64,65},{1,5},{65,66},{2,6},{66,67},{3,7},{67,64},{4,8},{68,... | collective-permute-start | bytes 1572872 | tf_op jit(solution)/shard_map/ppermute | solution.py:64
  120.0 2.1 %collective-permute-start.22 = (bf16[128,1024]{1,0:T(8,128)(2,1)S(1)}, bf16[128,1024]{1,0:T(8,128)(2,1)S(1)}, u32[]{:S(2)}, u32[]{:S(2)}) collective-permute-start(bf16[128,1024]{1,0:T(8,128)(2,1)S(1)} %shard_map.99.keep), channel_id=1, source_target_pairs={{0,64},{64,0},{1,65},{65,1},{2,66},{66,2},{3,67},{67,3},{4,68},{68... | collective-permute-start | bytes 786440 | tf_op jit(solution)/shard_map/ppermute | solution.py:78
  120.1 11.0 %collective-permute-start.24 = (bf16[256,1024]{1,0:T(8,128)(2,1)S(1)}, bf16[256,1024]{1,0:T(8,128)(2,1)}, u32[]{:S(2)}, u32[]{:S(2)}) collective-permute-start(bf16[256,1024]{1,0:T(8,128)(2,1)S(1)} %shard_map.98.refs_4_), channel_id=1, source_target_pairs={{0,8},{64,66},{1,9},{65,67},{2,10},{66,64},{3,11},{67,65},{4,12},{... | collective-permute-start | bytes 1572872 | tf_op jit(solution)/shard_map/ppermute | solution.py:64
  122.1 15.3 %copy-start.3 = (bf16[256,1024]{1,0:T(8,128)(2,1)}, bf16[256,1024]{1,0:T(8,128)(2,1)S(1)}, u32[]{:S(2)}) copy-start(bf16[256,1024]{1,0:T(8,128)(2,1)S(1)} %shard_map.100.refs_4_) | copy-start | bytes 1572868
  122.1 9.0 %copy-start.17 = (bf16[256,1024]{1,0:T(8,128)(2,1)}, bf16[256,1024]{1,0:T(8,128)(2,1)S(1)}, u32[]{:S(2)}) copy-start(bf16[256,1024]{1,0:T(8,128)(2,1)S(1)} %collective-permute-done.25.refs_7_) | copy-start | bytes 1572868
  122.1 9.0 %copy-start.18 = (bf16[256,1024]{1,0:T(8,128)(2,1)}, bf16[256,1024]{1,0:T(8,128)(2,1)S(1)}, u32[]{:S(2)}) copy-start(bf16[256,1024]{1,0:T(8,128)(2,1)S(1)} %collective-permute-done.23.refs_5_) | copy-start | bytes 1572868
  122.2 19.5 %collective-permute-start.31 = (bf16[256,1024]{1,0:T(8,128)(2,1)S(1)}, bf16[256,1024]{1,0:T(8,128)(2,1)}, u32[]{:S(2)}, u32[]{:S(2)}) collective-permute-start(bf16[256,1024]{1,0:T(8,128)(2,1)S(1)} %shard_map.100.refs_4_), channel_id=1, source_target_pairs={{0,12},{64,67},{1,13},{65,64},{2,14},{66,65},{3,15},{67,66},{4,0},... | collective-permute-start | bytes 1572872 | tf_op jit(solution)/shard_map/ppermute | solution.py:64
  123.4 19.7 %collective-permute-start.30 = (bf16[256,1024]{1,0:T(8,128)(2,1)S(1)}, bf16[256,1024]{1,0:T(8,128)(2,1)}, u32[]{:S(2)}, u32[]{:S(2)}) collective-permute-start(bf16[256,1024]{1,0:T(8,128)(2,1)S(1)} %shard_map.100.refs_4_), channel_id=1, source_target_pairs={{0,8},{64,66},{1,9},{65,67},{2,10},{66,64},{3,11},{67,65},{4,12},{... | collective-permute-start | bytes 1572872 | tf_op jit(solution)/shard_map/ppermute | solution.py:64
  124.9 18.4 %collective-permute-start.29 = (bf16[256,1024]{1,0:T(8,128)(2,1)S(1)}, bf16[256,1024]{1,0:T(8,128)(2,1)}, u32[]{:S(2)}, u32[]{:S(2)}) collective-permute-start(bf16[256,1024]{1,0:T(8,128)(2,1)S(1)} %shard_map.100.refs_4_), channel_id=1, source_target_pairs={{0,4},{64,65},{1,5},{65,66},{2,6},{66,67},{3,7},{67,64},{4,8},{68,... | collective-permute-start | bytes 1572872 | tf_op jit(solution)/shard_map/ppermute | solution.py:64
  137.4 17.3 %copy-start.19 = (bf16[256,1024]{1,0:T(8,128)(2,1)S(1)}, bf16[256,1024]{1,0:T(8,128)(2,1)}, u32[]{:S(2)}) copy-start(bf16[256,1024]{1,0:T(8,128)(2,1)} %get-tuple-element.109) | copy-start | bytes 1572868
  137.4 13.5 %collective-permute-start.26 = (bf16[256,1024]{1,0:T(8,128)(2,1)}, bf16[256,1024]{1,0:T(8,128)(2,1)S(1)}, u32[]{:S(2)}, u32[]{:S(2)}) collective-permute-start(bf16[256,1024]{1,0:T(8,128)(2,1)} %get-tuple-element.110), channel_id=1, source_target_pairs={{0,1},{64,68},{1,2},{65,69},{2,3},{66,70},{3,0},{67,71},{4,5},{68,... | collective-permute-start | bytes 1572872 | tf_op jit(solution)/shard_map/ppermute | solution.py:74
  139.0 15.8 %collective-permute-start.27 = (bf16[256,1024]{1,0:T(8,128)(2,1)}, bf16[256,1024]{1,0:T(8,128)(2,1)S(1)}, u32[]{:S(2)}, u32[]{:S(2)}) collective-permute-start(bf16[256,1024]{1,0:T(8,128)(2,1)} %get-tuple-element.111), channel_id=1, source_target_pairs={{0,2},{64,72},{1,3},{65,73},{2,0},{66,74},{3,1},{67,75},{4,6},{68,... | collective-permute-start | bytes 1572872 | tf_op jit(solution)/shard_map/ppermute | solution.py:74
  141.6 13.1 %collective-permute-start.28 = (bf16[256,1024]{1,0:T(8,128)(2,1)}, bf16[256,1024]{1,0:T(8,128)(2,1)S(1)}, u32[]{:S(2)}, u32[]{:S(2)}) collective-permute-start(bf16[256,1024]{1,0:T(8,128)(2,1)} %get-tuple-element.112), channel_id=1, source_target_pairs={{0,3},{64,76},{1,0},{65,77},{2,1},{66,78},{3,2},{67,79},{4,7},{68,... | collective-permute-start | bytes 1572872 | tf_op jit(solution)/shard_map/ppermute | solution.py:74
  146.8 11.3 %copy-start.23 = (bf16[80,1024]{1,0:T(8,128)(2,1)S(1)}, bf16[80,1024]{1,0:T(8,128)(2,1)}, u32[]{:S(2)}) copy-start(bf16[80,1024]{1,0:T(8,128)(2,1)} %get-tuple-element.118) | copy-start | bytes 491524
  146.9 9.5 %collective-permute-start.32 = (bf16[80,1024]{1,0:T(8,128)(2,1)}, bf16[80,1024]{1,0:T(8,128)(2,1)S(1)}, u32[]{:S(2)}, u32[]{:S(2)}) collective-permute-start(bf16[80,1024]{1,0:T(8,128)(2,1)} %get-tuple-element.119), channel_id=1, source_target_pairs={{0,1},{64,68},{1,2},{65,69},{2,3},{66,70},{3,0},{67,71},{4,5},{68,... | collective-permute-start | bytes 491528 | tf_op jit(solution)/shard_map/ppermute | solution.py:74
  148.3 9.9 %collective-permute-start.33 = (bf16[80,1024]{1,0:T(8,128)(2,1)}, bf16[80,1024]{1,0:T(8,128)(2,1)S(1)}, u32[]{:S(2)}, u32[]{:S(2)}) collective-permute-start(bf16[80,1024]{1,0:T(8,128)(2,1)} %get-tuple-element.120), channel_id=1, source_target_pairs={{0,2},{64,72},{1,3},{65,73},{2,0},{66,74},{3,1},{67,75},{4,6},{68,... | collective-permute-start | bytes 491528 | tf_op jit(solution)/shard_map/ppermute | solution.py:74
  150.9 7.2 %collective-permute-start.34 = (bf16[80,1024]{1,0:T(8,128)(2,1)}, bf16[80,1024]{1,0:T(8,128)(2,1)S(1)}, u32[]{:S(2)}, u32[]{:S(2)}) collective-permute-start(bf16[80,1024]{1,0:T(8,128)(2,1)} %get-tuple-element.121), channel_id=1, source_target_pairs={{0,3},{64,76},{1,0},{65,77},{2,1},{66,78},{3,2},{67,79},{4,7},{68,... | collective-permute-start | bytes 491528 | tf_op jit(solution)/shard_map/ppermute | solution.py:74
